TPU v7x, 32 devices: a whole 2x2x4 slice. The times are simulated.
32 devices in a mesh: gx: 4 (over y, x), gy: 2 (over core), col: 4 (over z).
Axes of the slice: x: 2, y: 2, z: 4, core: 2. Of those that a mesh axis runs over, the one named last changes fastest.
Arguments:
- iterate: float32 [3, 32, 16, 16, 512], P(None, None, 'gx', 'gy', 'col'), may hold values from -0.75 to 0.75
- residual: float32 [3, 32, 16, 16, 512], P(None, None, 'gx', 'gy', 'col'), may hold values from -8 to 8
- cell_ids: int32 [16, 16, 512], P('gx', 'gy', 'col'), may hold values from 0 to 15
- materials: float32 [2, 16], replicated, may hold values from 0.2 to 2
- eigen_counts: int32 [32], P(('gx', 'gy', 'col')), may hold values from 8 to 48, as said below
- coarse_rank: int32 [32], P(('gx', 'gy', 'col')), may hold values from 0 to 31, each once
- eigen_basis: float32 [48, 3, 16, 16, 512], P(None, None, 'gx', 'gy', 'col'), may hold values from -0.0546875 to 0.0546875
- coarse_inverse: bfloat16 [1024, 1024], P(('gx', 'col'))
Outputs:
- new_iterate: float32 [3, 32, 16, 16, 512], P(None, None, 'gx', 'gy', 'col')
- new_residual: float32 [3, 32, 16, 16, 512], P(None, None, 'gx', 'gy', 'col')
Inputs may be any that keep to these rules, and one draw needn't show every extreme that they name: `eigen_counts`: the counts sum to 1024. `coarse_rank`: each subdomain has one position.
All inputs are finite; a program needn't handle non-finite values.
Results may differ from a plain program's by a relative error of at most 0.0027.
Values may be sent and summed in bfloat16 or wider, within the bound.
No kernel may reach another device: no remote copies, remote signals or barrier semaphores. Data moves between devices by JAX's collectives and lax.ppermute only.
A program may use at most 128 MiB of HBM per device.

v0:
```python
import jax
import jax.numpy as jnp
from jax import lax
from jax.sharding import PartitionSpec as P

SWEEPS = 4


damping = 0.6


def extended(x, sides, width):
    for axis, dim in sides:
        devices, length = (lax.axis_size(axis), x.shape[dim])
        up = [(i, (i + 1) % devices) for i in range(devices - 1)]
        down = [(j, i) for i, j in up]
        last = lax.slice_in_dim(x, length - width, length, axis=dim)
        first = lax.slice_in_dim(x, 0, width, axis=dim)
        before = lax.ppermute(last, axis, up)
        after = lax.ppermute(first, axis, down)
        x = jnp.concatenate([before, x, after], axis=dim)
    return x


def face_coefs(mu_padded):
    center = mu_padded[1:-1, 1:-1, 1:-1]
    result = []
    for axis_pick in range(3):
        for side_pick in (0, 2):
            window_cut = [slice(1, -1)] * 3
            window_cut[axis_pick] = slice(side_pick, side_pick + center.shape[axis_pick])
            result.append(0.5 * (center + mu_padded[tuple(window_cut)]))
    return result


def apply_op(padded_field, coefs, lam_field):
    center = padded_field[:, :, 1:-1, 1:-1, 1:-1]
    result = center + lam_field * jnp.sum(center, axis=0, keepdims=True)
    shape_cells = center.shape[2:]
    position = 0
    for axis_pick in range(3):
        for side_pick in (0, 2):
            window_cut = [slice(1, -1)] * 3
            window_cut[axis_pick] = slice(side_pick, side_pick + shape_cells[axis_pick])
            neighbour = padded_field[(slice(None), slice(None)) + tuple(window_cut)]
            result = result + coefs[position] * (center - neighbour)
            position = position + 1
    return result


def pad_cells(field_value):
    return jnp.pad(field_value, ((0, 0), (0, 0), (1, 1), (1, 1), (1, 1)))


def local_solve(res_box, coefs, lam_box):
    diag_inv = damping / (1.0 + lam_box + sum(coefs))
    field_value = diag_inv * res_box
    for sweep_step in range(SWEEPS - 1):
        field_value = field_value + diag_inv * (
            res_box - apply_op(pad_cells(field_value), coefs, lam_box)
        )
    return field_value[:, :, 1:-1, 1:-1, 1:-1]


def lookup(ids_plus, materials):
    table_rows = materials.shape[1]
    onehot = (ids_plus[..., None] == jnp.arange(1, table_rows + 1, dtype=jnp.int32)).astype(
        jnp.float32
    )
    values = jnp.dot(onehot.reshape(-1, table_rows), materials.T, precision=lax.Precision.HIGHEST)
    values = values.reshape(ids_plus.shape + (2,))
    return (values[..., 0], values[..., 1])


def body(
    iterate, residual, cell_ids, materials, eigen_counts, coarse_rank, eigen_basis, coarse_inverse
):
    highest = lax.Precision.HIGHEST
    ids_wide = extended(cell_ids + 1, (("gx", 0), ("gy", 1), ("col", 2)), 2)
    mu_wide, lam_wide = lookup(ids_wide, materials)
    lam_box = lam_wide[1:-1, 1:-1, 1:-1]
    res_box = extended(residual, (("gx", 2), ("gy", 3), ("col", 4)), 1)
    box_coefs = face_coefs(mu_wide)
    near_part = local_solve(res_box, box_coefs, lam_box)
    slot_count = eigen_basis.shape[0]
    load_count = residual.shape[1]
    total_rows = coarse_inverse.shape[1]
    slot_ids = jnp.arange(slot_count, dtype=jnp.int32)
    live_slots = slot_ids < eigen_counts[0]
    pieces = jnp.einsum("ecxyz,ckxyz->ek", eigen_basis, residual, precision=highest)
    pieces = jnp.where(live_slots[:, None], pieces, 0.0)
    all_counts, all_ranks = (
        lax.all_gather(eigen_counts, ("gx", "gy", "col"), axis=0, tiled=True),
        lax.all_gather(coarse_rank, ("gx", "gy", "col"), axis=0, tiled=True),
    )
    my_start = jnp.sum(all_counts * (all_ranks < coarse_rank[0]).astype(jnp.int32))
    starts = jnp.sum(
        all_counts[None, :] * (all_ranks[None, :] < all_ranks[:, None]).astype(jnp.int32), axis=1
    )
    gathered = lax.all_gather(
        pieces.astype(jnp.bfloat16)[None], ("gx", "gy", "col"), axis=0, tiled=True
    )
    target = jnp.where(
        slot_ids[None, :] < all_counts[:, None],
        starts[:, None] + slot_ids[None, :],
        total_rows + slot_ids[None, :],
    )
    assembled = (
        jnp.zeros((total_rows + slot_count, load_count), jnp.bfloat16)
        .at[target.reshape(-1)]
        .add(gathered.reshape(-1, load_count))
    )
    coarse_vector = assembled[:total_rows]
    partial_coef = jnp.dot(coarse_inverse, coarse_vector, preferred_element_type=jnp.float32)
    coarse_coef = lax.all_gather(partial_coef, ("gx", "col"), axis=0, tiled=True)
    padded_coef = jnp.concatenate(
        [coarse_coef, jnp.zeros((slot_count, load_count), jnp.float32)], axis=0
    )
    own_coef = lax.dynamic_slice_in_dim(padded_coef, my_start, slot_count, 0)
    own_coef = jnp.where(live_slots[:, None], own_coef, 0.0)
    direction = near_part + jnp.einsum("ecxyz,ek->ckxyz", eigen_basis, own_coef, precision=highest)
    inner_coefs = [coef_item[1:-1, 1:-1, 1:-1] for coef_item in box_coefs]
    lam_own = lam_box[1:-1, 1:-1, 1:-1]
    local_loads = jnp.einsum("cjxyz,ckxyz->jk", direction, residual, precision=highest)
    direction_pad = extended(direction, (("gx", 2), ("gy", 3), ("col", 4)), 1)
    image_field = apply_op(direction_pad, inner_coefs, lam_own)
    local_energy = jnp.einsum("cjxyz,ckxyz->jk", direction, image_field, precision=highest)
    energy, load_products = lax.psum((local_energy, local_loads), ("gx", "gy", "col"))
    factor = jnp.linalg.cholesky(energy)
    step_coef = jax.scipy.linalg.cho_solve((factor, True), load_products)
    new_iterate = iterate + jnp.einsum("cjxyz,jk->ckxyz", direction, step_coef, precision=highest)
    new_residual = residual - jnp.einsum(
        "cjxyz,jk->ckxyz", image_field, step_coef, precision=highest
    )
    return (new_iterate, new_residual)


def solution(mesh):
    placed = (
        P(None, None, "gx", "gy", "col"),
        P(None, None, "gx", "gy", "col"),
        P("gx", "gy", "col"),
        P(),
        P(("gx", "gy", "col")),
        P(("gx", "gy", "col")),
        P(None, None, "gx", "gy", "col"),
        P(("gx", "col"), None),
    )
    return jax.shard_map(
        body,
        mesh=mesh,
        in_specs=placed,
        out_specs=(P(None, None, "gx", "gy", "col"), P(None, None, "gx", "gy", "col")),
        check_vma=False,
    )
```

profile of v0, /device:TPU:0, one launch (start us, length us, event | category | flops | bytes accessed | tf_op | source)
XLA Modules:
  0.0 447.1 jit_solution(9138449706740287763)
XLA Ops:
  1.5 4.8 %collective-permute-start = (s32[2,8,128]{2,1,0:T(8,128)S(1)}, s32[2,8,128]{2,1,0:T(8,128)S(1)}, u32[]{:S(2)}, u32[]{:S(2)}) collective-permute-start(s32[2,8,128]{2,1,0:T(8,128)S(1)} %get-tuple-element.53), channel_id=1, source_target_pairs={{0,8},{8,16},{16,24},{1,9},{9,17},{17,25},{2,10},{10,18},{18,26},{... | collective-permute-start | bytes 24584 | tf_op jit(solution)/shard_map/ppermute | solution.py:19
  6.3 1.3 collective-permute-start.1
  7.6 1.2 fusion.141
  9.6 5.3 %collective-permute-start.6 = (f32[3,32,1,8,128]{4,1,3,2,0:T(8,128)}, f32[3,32,1,8,128]{4,1,3,2,0:T(8,128)}, u32[]{:S(2)}, u32[]{:S(2)}) collective-permute-start(f32[3,32,1,8,128]{4,1,3,2,0:T(8,128)} %copy.205), channel_id=1, source_target_pairs={{0,8},{8,16},{16,24},{1,9},{9,17},{17,25},{2,10},{10,18},{18,26},{... | collective-permute-start | bytes 1179656 | tf_op jit(solution)/shard_map/ppermute | solution.py:19
  15.0 1.3 collective-permute-start.7
  17.9 48.7 %all-reduce.6 = (s32[32]{0:T(128)S(1)}, s32[32]{0:T(128)S(1)}) all-reduce(s32[32]{0:T(128)S(1)} %dynamic-update-slice.3, s32[32]{0:T(128)S(1)} %dynamic-update-slice.4), channel_id=1, replica_groups=mesh['gx'=4,'gy'=2,'col'=4] {'gx','gy','col'}, use_global_device_ids=true, to_apply=%add.4 | all-reduce | flops 64 | bytes 512
  66.9 5.6 %fusion.95 = bf16[1,48,32]{1,2,0:T(8,128)(2,1)S(1)} fusion(f32[48,3,4,8,128]{4,3,2,1,0:T(8,128)} %param.14, pred[48]{0:T(512)(128)(4,1)S(1)} %iota_compare_fusion.3, f32[3,32,4,8,128]{4,3,2,1,0:T(8,128)S(1)} %copy-done.2), kind=kOutput, calls=%fused_computation.138 | convolution fusion | flops 226495488 | bytes 3935280 | tf_op jit(solution)/shard_map/ecxyz,ckxyz->ek/dot_general | solution.py:90
  72.6 67.2 %all-gather.1 = bf16[32,48,32]{1,2,0:T(8,128)(2,1)S(1)} all-gather(bf16[1,48,32]{1,2,0:T(8,128)(2,1)S(1)} %fusion.95), channel_id=2, replica_groups=mesh['gx'=4,'gy'=2,'col'=4] {'gx','gy','col'}, dimensions={0}, use_global_device_ids=true | all-gather | bytes 101376 | tf_op jit(solution)/shard_map/all_gather | solution.py:100
  140.1 8.9 %scatter_custom_fusion = bf16[1072,32]{1,0:T(8,128)(2,1)S(1)} fusion(s32[1536]{0:T(1024)S(1)} %fusion.119, bf16[1536,32]{1,0:T(8,128)(2,1)S(1)} %bitcast.78, bf16[]{:T(256)} %constant.66.clone.1), kind=kCustom, calls=%fused_computation.150 | custom fusion | flops 49152 | bytes 68610 | tf_op jit(solution)/shard_map/scatter-add | solution.py:111
  149.8 1.3 collective-permute-start.2
  151.1 1.3 collective-permute-start.3
  152.4 1.7 collective-permute-done.3
  154.3 2.3 collective-permute-start.4
  156.6 1.3 collective-permute-start.5
  157.9 40.6 %all-gather.2 = f32[16,64,32]{1,2,0:T(8,128)S(1)} all-gather(f32[1,64,32]{1,2,0:T(8,128)S(1)} %convolution_bitcast_fusion.3), channel_id=1, replica_groups=mesh['gx'=4,'gy'=2,'col'=4] {'gx','col'}, dimensions={0}, use_global_device_ids=true | all-gather | bytes 139264 | tf_op jit(solution)/shard_map/all_gather | solution.py:115
  201.6 1.0 constant_dynamic-update-slice_fusion.2
  203.6 1.3 collective-permute-start.8
  204.9 1.5 collective-permute-start.9
  206.6 1.8 collective-permute-done.9
  208.8 3.5 fusion.138
  212.4 3.2 copy.134
  215.5 2.6 copy.135
  218.1 1.3 collective-permute-start.11
  219.4 5.2 %collective-permute-start.10 = (f32[3,32,6,10,1]{1,4,3,2,0:T(1,128)}, f32[3,32,6,10,1]{1,4,3,2,0:T(1,128)}, u32[]{:S(2)}, u32[]{:S(2)}) collective-permute-start(f32[3,32,6,10,1]{1,4,3,2,0:T(1,128)} %copy.134), channel_id=1, source_target_pairs={{0,1},{1,2},{2,3},{4,5},{5,6},{6,7},{8,9},{9,10},{10,11},{12,13},{... | collective-permute-start | bytes 69128 | tf_op jit(solution)/shard_map/ppermute | solution.py:19
  226.4 3.1 copy.136
  229.6 2.3 copy.137
  231.9 8.4 %fusion.130 = (f32[32,6,10,130]{3,0,2,1:T(8,128)S(1)}, f32[3,32,6,10,130]{4,1,3,2,0:T(8,128)}, f32[3,32,6,10,130]{4,1,3,2,0:T(8,128)}) fusion(f32[6,10,130]{2,1,0:T(8,128)S(1)} %copy.130, f32[3,32,6,10,1]{4,1,3,2,0:T(8,128)} %copy.137, f32[3,32,6,1,128]{4,1,3,2,0:T(8,128)S(1)} %collective-permute-done.9, f32[3,32,6,8,128]{4,1,3,2,0:T(8,128)} %copy-done.4, ...), kind=kLoop, calls=%fused_computation.208 | loop fusion | flops 4243200 | bytes 10015200 | tf_op jit(solution)/shard_map/reduce_sum | solution.py:38
  240.4 1.6 broadcast_multiply_fusion.3
  242.0 20.9 %fusion.128 = (f32[32,6,10,130]{3,0,2,1:T(8,128)}, f32[3,32,6,10,130]{4,1,3,2,0:T(8,128)}) fusion(f32[3,32,6,10,130]{4,1,3,2,0:T(8,128)} %get-tuple-element.21, f32[3,32,6,10,130]{4,1,3,2,0:T(8,128)} %get-tuple-element.22, f32[6,10,130]{2,1,0:T(8,128)S(1)} %copy.144, f32[6,10,130]{2,1,0:T(8,128)S(1)} %copy.143, f32[6,10,130]{2,1,0:T(8,128)S(1)} %copy.142, ...), kind=kLoop, calls=%fused_computation.207 | loop fusion | flops 16972800 | bytes 11200800 | tf_op jit(solution)/shard_map/reduce_sum | solution.py:38
  262.9 3.3 broadcast_multiply_fusion.2
  266.2 20.7 %fusion.126 = (f32[32,6,10,130]{3,0,2,1:T(8,128)}, f32[3,32,6,10,130]{4,1,3,2,0:T(8,128)}) fusion(f32[3,32,6,10,130]{4,1,3,2,0:T(8,128)} %get-tuple-element.19, f32[3,32,6,10,130]{4,1,3,2,0:T(8,128)} %get-tuple-element.22, f32[6,10,130]{2,1,0:T(8,128)S(1)} %copy.144, f32[6,10,130]{2,1,0:T(8,128)S(1)} %copy.143, f32[6,10,130]{2,1,0:T(8,128)S(1)} %copy.142, ...), kind=kLoop, calls=%fused_computation.206 | loop fusion | flops 16972800 | bytes 11200800 | tf_op jit(solution)/shard_map/reduce_sum | solution.py:38
  287.0 3.3 broadcast_multiply_fusion.1
  290.3 23.3 %fusion.46 = (f32[3,32,6,10,130]{4,1,3,2,0:T(8,128)}, f32[3,32,6,10,130]{4,1,3,2,0:T(8,128)}, f32[3,32,6,10,130]{4,1,3,2,0:T(8,128)}, f32[3,32,6,10,130]{4,1,3,2,0:T(8,128)}) fusion(f32[3,32,6,10,130]{4,1,3,2,0:T(8,128)} %get-tuple-element.17, f32[32,6,10,130]{3,0,2,1:T(8,128)} %broadcast_multiply_fusion.1, f32[6,10,130]{2,1,0:T(8,128)S(1)} %copy.141, ...), kind=kLoop, calls=%fused_computation.65 | loop fusion | flops 9734400 | bytes 16099200 | tf_op jit(solution)/shard_map/add | solution.py:46
  313.6 11.6 %fusion.145 = (f32[32,4,8,128]{3,0,2,1:T(8,128)S(1)}, f32[3,32,4,8,128]{4,1,3,2,0:T(8,128)S(1)}) fusion(f32[48,3,4,8,128]{4,3,2,1,0:T(8,128)} %param.14, s32[]{:T(128)S(6)} %select_n.43, f32[1024,32]{0,1:T(8,128)S(1)} %reshape.169, pred[48]{0:T(512)(128)(4,1)S(1)} %iota_compare_fusion.3, f32[3,32,6,10,130]{4,1,3,2,0:T(8,128)} %get-tuple-element.33, ...), kind=kOutput, calls=%fused_computation.217 | convolution fusion | flops 230688256 | bytes 14073908 | tf_op jit(solution)/shard_map/ecxyz,ek->ckxyz/dot_general | solution.py:121
  325.2 1.3 collective-permute-start.12
  326.6 1.3 collective-permute-start.13
  327.9 6.5 %collective-permute-done.12 = f32[3,32,1,8,128]{4,1,3,2,0:T(8,128)S(1)} collective-permute-done((f32[3,32,1,8,128]{4,1,3,2,0:T(8,128)S(1)}, f32[3,32,1,8,128]{4,1,3,2,0:T(8,128)S(1)}, u32[]{:S(2)}, u32[]{:S(2)}) %collective-permute-start.12) | collective-permute-done | bytes 393248 | tf_op jit(solution)/shard_map/ppermute | solution.py:19
  334.3 12.7 %collective-permute-done.13 = f32[3,32,1,8,128]{4,1,3,2,0:T(8,128)S(1)} collective-permute-done((f32[3,32,1,8,128]{4,1,3,2,0:T(8,128)S(1)}, f32[3,32,1,8,128]{4,1,3,2,0:T(8,128)S(1)}, u32[]{:S(2)}, u32[]{:S(2)}) %collective-permute-start.13) | collective-permute-done | bytes 393248 | tf_op jit(solution)/shard_map/ppermute | solution.py:20
  347.1 1.3 collective-permute-start.14
  348.4 1.3 collective-permute-start.15
  349.7 0.9 slice.302
  350.7 0.9 slice.305
  351.6 0.9 slice.303
  352.5 0.9 slice.307
  353.4 0.9 slice.308
  354.3 0.9 slice.309
  358.0 3.5 fusion.137
  361.6 2.6 copy.157
  364.1 2.6 copy.160
  366.7 1.3 collective-permute-start.17
  368.0 5.3 %collective-permute-start.16 = (f32[3,32,6,10,1]{1,4,3,2,0:T(1,128)S(1)}, f32[3,32,6,10,1]{1,4,3,2,0:T(1,128)}, u32[]{:S(2)}, u32[]{:S(2)}) collective-permute-start(f32[3,32,6,10,1]{1,4,3,2,0:T(1,128)S(1)} %copy.157), channel_id=1, source_target_pairs={{0,1},{1,2},{2,3},{4,5},{5,6},{6,7},{8,9},{9,10},{10,11},{12,13},{... | collective-permute-start | bytes 69128 | tf_op jit(solution)/shard_map/ppermute | solution.py:19
  373.3 2.2 convolution_bitcast_fusion.1
  375.5 3.4 copy.158
  378.9 2.4 copy.161
  381.3 4.2 fusion.60
  385.5 1.1 copy-done.3
  386.6 1.4 convolution_bitcast_fusion.2
  388.1 41.3 %all-reduce.7 = (f32[32,32]{1,0:T(8,128)S(1)}, f32[32,32]{0,1:T(8,128)S(1)}) all-reduce(f32[32,32]{1,0:T(8,128)S(1)} %convolution_bitcast_fusion.1, f32[32,32]{0,1:T(8,128)S(1)} %convolution_bitcast_fusion.2), channel_id=1, replica_groups=mesh['gx'=4,'gy'=2,'col'=4] {'gx','gy','col'}, use_global_device_ids=true, to_apply=%region_10.11 | all-reduce | flops 2048 | bytes 16384 | tf_op jit(solution)/shard_map/psum | solution.py:128
  429.4 2.9 cholesky.16
  433.7 2.4 custom-call.10
  436.6 3.7 bitcast_subtract_fusion
  440.3 2.2 bitcast_add_fusion
  442.5 2.1 copy.169
  444.6 2.1 copy.170
  (109 shorter events, 12.6 us)
Async XLA Ops:
  0.6 148.3 %copy-start = (bf16[64,1024]{1,0:T(8,128)(2,1)S(1)}, bf16[64,1024]{1,0:T(8,128)(2,1)}, u32[]{:S(2)}) copy-start(bf16[64,1024]{1,0:T(8,128)(2,1)} %param.15) | copy-start | bytes 393220
  0.6 66.3 %copy-start.2 = (f32[3,32,4,8,128]{4,3,2,1,0:T(8,128)S(1)}, f32[3,32,4,8,128]{4,3,2,1,0:T(8,128)}, u32[]{:S(2)}) copy-start(f32[3,32,4,8,128]{4,3,2,1,0:T(8,128)} %param.9) | copy-start | bytes 4718596
  1.5 148.3 %collective-permute-start = (s32[2,8,128]{2,1,0:T(8,128)S(1)}, s32[2,8,128]{2,1,0:T(8,128)S(1)}, u32[]{:S(2)}, u32[]{:S(2)}) collective-permute-start(s32[2,8,128]{2,1,0:T(8,128)S(1)} %get-tuple-element.53), channel_id=1, source_target_pairs={{0,8},{8,16},{16,24},{1,9},{9,17},{17,25},{2,10},{10,18},{18,26},{... | collective-permute-start | bytes 24584 | tf_op jit(solution)/shard_map/ppermute | solution.py:19
  6.3 143.5 %collective-permute-start.1 = (s32[2,8,128]{2,1,0:T(8,128)S(1)}, s32[2,8,128]{2,1,0:T(8,128)S(1)}, u32[]{:S(2)}, u32[]{:S(2)}) collective-permute-start(s32[2,8,128]{2,1,0:T(8,128)S(1)} %get-tuple-element.54), channel_id=1, source_target_pairs={{8,0},{16,8},{24,16},{9,1},{17,9},{25,17},{10,2},{18,10},{26,18},{... | collective-permute-start | bytes 24584 | tf_op jit(solution)/shard_map/ppermute | solution.py:20
  9.6 191.9 %collective-permute-start.6 = (f32[3,32,1,8,128]{4,1,3,2,0:T(8,128)}, f32[3,32,1,8,128]{4,1,3,2,0:T(8,128)}, u32[]{:S(2)}, u32[]{:S(2)}) collective-permute-start(f32[3,32,1,8,128]{4,1,3,2,0:T(8,128)} %copy.205), channel_id=1, source_target_pairs={{0,8},{8,16},{16,24},{1,9},{9,17},{17,25},{2,10},{10,18},{18,26},{... | collective-permute-start | bytes 1179656 | tf_op jit(solution)/shard_map/ppermute | solution.py:19
  15.0 188.5 %collective-permute-start.7 = (f32[3,32,1,8,128]{4,1,3,2,0:T(8,128)S(1)}, f32[3,32,1,8,128]{4,1,3,2,0:T(8,128)S(1)}, u32[]{:S(2)}, u32[]{:S(2)}) collective-permute-start(f32[3,32,1,8,128]{4,1,3,2,0:T(8,128)S(1)} %copy.206), channel_id=1, source_target_pairs={{8,0},{16,8},{24,16},{9,1},{17,9},{25,17},{10,2},{18,10},{26,18},{... | collective-permute-start | bytes 1179656 | tf_op jit(solution)/shard_map/ppermute | solution.py:20
  72.6 128.3 %copy-start.16 = (f32[2,16]{1,0:T(2,128)S(1)}, f32[2,16]{1,0:T(2,128)}, u32[]{:S(2)}) copy-start(f32[2,16]{1,0:T(2,128)} %param.11) | copy-start | bytes 388
  149.8 2.6 collective-permute-start.2
  151.1 3.1 collective-permute-start.3
  154.3 46.4 %collective-permute-start.4 = (s32[8,12,2]{2,1,0:T(8,128)S(1)}, s32[8,12,2]{2,1,0:T(8,128)S(1)}, u32[]{:S(2)}, u32[]{:S(2)}) collective-permute-start(s32[8,12,2]{2,1,0:T(8,128)S(1)} %get-tuple-element.49), channel_id=1, source_target_pairs={{0,1},{1,2},{2,3},{4,5},{5,6},{6,7},{8,9},{9,10},{10,11},{12,13},{... | collective-permute-start | bytes 2312 | tf_op jit(solution)/shard_map/ppermute | solution.py:19
  156.6 44.2 %collective-permute-start.5 = (s32[8,12,2]{2,1,0:T(8,128)S(1)}, s32[8,12,2]{2,1,0:T(8,128)S(1)}, u32[]{:S(2)}, u32[]{:S(2)}) collective-permute-start(s32[8,12,2]{2,1,0:T(8,128)S(1)} %get-tuple-element.50), channel_id=1, source_target_pairs={{1,0},{2,1},{3,2},{5,4},{6,5},{7,6},{9,8},{10,9},{11,10},{13,12},{... | collective-permute-start | bytes 2312 | tf_op jit(solution)/shard_map/ppermute | solution.py:20
  203.5 4.9 %copy-start.4 = (f32[3,32,6,8,128]{4,1,3,2,0:T(8,128)}, f32[3,32,6,8,128]{4,1,3,2,0:T(8,128)S(1)}, u32[]{:S(2)}) copy-start(f32[3,32,6,8,128]{4,1,3,2,0:T(8,128)S(1)} %constant_dynamic-update-slice_fusion) | copy-start | bytes 7077892
  203.6 3.0 collective-permute-start.8
  204.9 3.5 collective-permute-start.9
  206.6 18.0 %copy-start.15 = (f32[8,12,132]{2,0,1:T(8,128)}, f32[8,12,132]{2,0,1:T(8,128)S(1)}, u32[]{:S(2)}) copy-start(f32[8,12,132]{2,0,1:T(8,128)S(1)} %get-tuple-element.58) | copy-start | bytes 152068
  218.1 11.5 %collective-permute-start.11 = (f32[3,32,6,10,1]{1,4,3,2,0:T(1,128)S(1)}, f32[3,32,6,10,1]{1,4,3,2,0:T(1,128)S(1)}, u32[]{:S(2)}, u32[]{:S(2)}) collective-permute-start(f32[3,32,6,10,1]{1,4,3,2,0:T(1,128)S(1)} %copy.135), channel_id=1, source_target_pairs={{1,0},{2,1},{3,2},{5,4},{6,5},{7,6},{9,8},{10,9},{11,10},{13,12},{... | collective-permute-start | bytes 69128 | tf_op jit(solution)/shard_map/ppermute | solution.py:20
  219.4 7.0 %collective-permute-start.10 = (f32[3,32,6,10,1]{1,4,3,2,0:T(1,128)}, f32[3,32,6,10,1]{1,4,3,2,0:T(1,128)}, u32[]{:S(2)}, u32[]{:S(2)}) collective-permute-start(f32[3,32,6,10,1]{1,4,3,2,0:T(1,128)} %copy.134), channel_id=1, source_target_pairs={{0,1},{1,2},{2,3},{4,5},{5,6},{6,7},{8,9},{9,10},{10,11},{12,13},{... | collective-permute-start | bytes 69128 | tf_op jit(solution)/shard_map/ppermute | solution.py:19
  224.8 0.6 copy-start.14
  224.8 0.7 copy-start.13
  224.9 0.7 copy-start.12
  224.9 0.7 copy-start.11
  224.9 0.8 copy-start.10
  325.2 9.1 %collective-permute-start.12 = (f32[3,32,1,8,128]{4,1,3,2,0:T(8,128)S(1)}, f32[3,32,1,8,128]{4,1,3,2,0:T(8,128)S(1)}, u32[]{:S(2)}, u32[]{:S(2)}) collective-permute-start(f32[3,32,1,8,128]{4,1,3,2,0:T(8,128)S(1)} %get-tuple-element.42), channel_id=1, source_target_pairs={{0,8},{8,16},{16,24},{1,9},{9,17},{17,25},{2,10},{10,18},{18,26},{... | collective-permute-start | bytes 1179656 | tf_op jit(solution)/shard_map/ppermute | solution.py:19
  326.6 20.5 %collective-permute-start.13 = (f32[3,32,1,8,128]{4,1,3,2,0:T(8,128)S(1)}, f32[3,32,1,8,128]{4,1,3,2,0:T(8,128)S(1)}, u32[]{:S(2)}, u32[]{:S(2)}) collective-permute-start(f32[3,32,1,8,128]{4,1,3,2,0:T(8,128)S(1)} %get-tuple-element.43), channel_id=1, source_target_pairs={{8,0},{16,8},{24,16},{9,1},{17,9},{25,17},{10,2},{18,10},{26,18},{... | collective-permute-start | bytes 1179656 | tf_op jit(solution)/shard_map/ppermute | solution.py:20
  334.3 21.9 %copy-start.5 = (f32[3,32,1,8,128]{4,1,3,2,0:T(8,128)}, f32[3,32,1,8,128]{4,1,3,2,0:T(8,128)S(1)}, u32[]{:S(2)}) copy-start(f32[3,32,1,8,128]{4,1,3,2,0:T(8,128)S(1)} %collective-permute-done.12) | copy-start | bytes 1179652
  347.1 9.2 %copy-start.6 = (f32[3,32,1,8,128]{4,1,3,2,0:T(8,128)}, f32[3,32,1,8,128]{4,1,3,2,0:T(8,128)S(1)}, u32[]{:S(2)}) copy-start(f32[3,32,1,8,128]{4,1,3,2,0:T(8,128)S(1)} %collective-permute-done.13) | copy-start | bytes 1179652
  347.1 9.1 %collective-permute-start.14 = (f32[3,32,6,1,128]{4,1,3,2,0:T(8,128)S(1)}, f32[3,32,6,1,128]{4,1,3,2,0:T(8,128)S(1)}, u32[]{:S(2)}, u32[]{:S(2)}) collective-permute-start(f32[3,32,6,1,128]{4,1,3,2,0:T(8,128)S(1)} %get-tuple-element.38), channel_id=1, source_target_pairs={{0,4},{1,5},{2,6},{3,7},{8,12},{9,13},{10,14},{11,15},{16,20},{17,... | collective-permute-start | bytes 884744 | tf_op jit(solution)/shard_map/ppermute | solution.py:19
  348.4 7.8 %collective-permute-start.15 = (f32[3,32,6,1,128]{4,1,3,2,0:T(8,128)S(1)}, f32[3,32,6,1,128]{4,1,3,2,0:T(8,128)S(1)}, u32[]{:S(2)}, u32[]{:S(2)}) collective-permute-start(f32[3,32,6,1,128]{4,1,3,2,0:T(8,128)S(1)} %get-tuple-element.39), channel_id=1, source_target_pairs={{4,0},{5,1},{6,2},{7,3},{12,8},{13,9},{14,10},{15,11},{20,16},{21,... | collective-permute-start | bytes 884744 | tf_op jit(solution)/shard_map/ppermute | solution.py:20
  356.3 0.7 copy-start.8
  357.0 0.7 copy-start.9
  366.7 12.2 %collective-permute-start.17 = (f32[3,32,6,10,1]{1,4,3,2,0:T(1,128)S(1)}, f32[3,32,6,10,1]{1,4,3,2,0:T(1,128)S(1)}, u32[]{:S(2)}, u32[]{:S(2)}) collective-permute-start(f32[3,32,6,10,1]{1,4,3,2,0:T(1,128)S(1)} %copy.160), channel_id=1, source_target_pairs={{1,0},{2,1},{3,2},{5,4},{6,5},{7,6},{9,8},{10,9},{11,10},{13,12},{... | collective-permute-start | bytes 69128 | tf_op jit(solution)/shard_map/ppermute | solution.py:20
  368.0 7.5 %collective-permute-start.16 = (f32[3,32,6,10,1]{1,4,3,2,0:T(1,128)S(1)}, f32[3,32,6,10,1]{1,4,3,2,0:T(1,128)}, u32[]{:S(2)}, u32[]{:S(2)}) collective-permute-start(f32[3,32,6,10,1]{1,4,3,2,0:T(1,128)S(1)} %copy.157), channel_id=1, source_target_pairs={{0,1},{1,2},{2,3},{4,5},{5,6},{6,7},{8,9},{9,10},{10,11},{12,13},{... | collective-permute-start | bytes 69128 | tf_op jit(solution)/shard_map/ppermute | solution.py:19
  385.5 1.1 copy-start.3
  436.6 3.7 copy-start.7
  442.5 4.1 copy-start.1
where the time goes:
time: 456 us; the launch traced here: 447 us
  blocking collectives  198 us (43%)
  other arithmetic  105 us (23%)
  local copies, waits for them, and re-layouts  47.7 us (10%)
  starting transfers between devices  39.9 us (9%)
  matrix products  28 us (6%)
  waiting for transfers between devices  23.4 us (5%)
  between operations  5.09 us (1%)
    all_gather x1, blocking collectives, body(): lax.all_gather(pieces.astype(jnp.bfloat16)[None], ('gx', 'gy', 'col'), ax...  67.2 us
    reduce_sum x3, other arithmetic, apply_op(): result = center + lam_field * jnp.sum(center, axis=0, keepdims=True)  50.1 us
    unnamed x1, blocking collectives  48.7 us
    psum x1, blocking collectives, body(): lax.psum((local_energy, local_loads), ('gx', 'gy', 'col'))  41.3 us
    all_gather x1, blocking collectives, body(): lax.all_gather(partial_coef, ('gx', 'col'), axis=0, tiled=True)  40.6 us
    ppermute x9, starting transfers between devices, extended(): before = lax.ppermute(last, axis, up)  28.1 us
    add x2, other arithmetic, apply_op(): result = result + coefs[position] * (center - neighbour)  27.5 us
    ppermute x9, waiting for transfers between devices, extended(): after = lax.ppermute(first, axis, down)  16.3 us
  transfers between devices with their start and end apart: 18, of which 6 were waited for; matrix products, arithmetic and copies ran while one was open for 8% of the time, Pallas kernels for 0%

commit v1 on v0

v1 whole, which is shorter than its diff:
```python
import jax
import jax.numpy as jnp
from jax import lax
from jax.experimental import pallas as pl
from jax.experimental.pallas import tpu as pltpu
from jax.sharding import PartitionSpec as P

DAMPING = 0.6
F32 = jnp.float32
BF16 = jnp.bfloat16
LANES = 128
HALO_IDS = 16
AXES = ("gx", "gy", "col")
TRANSPOSED = (((1,), (1,)), ((), ()))


def split_hi_lo(value):
    hi = value.astype(BF16)
    return hi, (value - hi.astype(F32)).astype(BF16)


def paired_left(value, width, parts):
    rows = value.shape[0]
    hi, lo = split_hi_lo(value)
    parts[pl.ds(0, rows), :] = hi
    parts[pl.ds(rows, rows), :] = lo
    high = parts[pl.ds(0, rows), :].astype(F32)
    low = parts[pl.ds(rows, rows), :].astype(F32)
    return jnp.concatenate([high + roll_lanes(high, width), low], axis=0).astype(BF16)


def lane_ids(rows):
    return lax.broadcasted_iota(jnp.int32, (rows, LANES), 1)


def roll_lanes(value, shift):
    if isinstance(shift, int):
        shift = shift % LANES
        if shift == 0:
            return value
    return pltpu.roll(value, shift, axis=1)


def vmem_call(name, kernel, outs, scratch, limit_mib, flops, moved, operands, spaces=None):
    spaces = spaces or [pltpu.VMEM] * len(operands)
    return pl.pallas_call(
        kernel,
        name=name,
        out_shape=outs,
        in_specs=[pl.BlockSpec(memory_space=space) for space in spaces],
        out_specs=jax.tree.map(lambda _: pl.BlockSpec(memory_space=pltpu.VMEM), outs),
        scratch_shapes=scratch,
        compiler_params=pltpu.CompilerParams(vmem_limit_bytes=limit_mib << 20),
        cost_estimate=pl.CostEstimate(flops=flops, bytes_accessed=moved, transcendentals=0),
    )(*operands)


class Sizes:
    def __init__(self, residual, eigen_basis, coarse_inverse):
        self.comps, self.loads, self.cx, self.cy, _ = residual.shape
        self.slots = eigen_basis.shape[0]
        self.block_rows, self.total_rows = coarse_inverse.shape
        self.cells = self.cx * self.cy
        self.bx, self.by = self.cx + 2, self.cy + 2
        self.box = self.bx * self.by
        self.tiles = self.comps * self.cells
        self.face_x = self.comps * self.cy * self.loads
        self.face_y = self.comps * self.bx * self.loads
        self.inner_y = self.comps * self.cx * self.loads
        self.face_z = self.comps * self.loads
        self.pitch = 16


def own_rows(sz, ref, comp, cell):
    start = comp * sz.loads * sz.cells + cell
    return ref[pl.ds(start, sz.loads, stride=sz.cells), :]


def pack_x(sz, res, ids, lo, hi):
    for comp in range(sz.comps):
        for y in range(sz.cy):
            rows = pl.ds((comp * sz.cy + y) * sz.loads, sz.loads)
            lo[rows, :] = own_rows(sz, res, comp, y).astype(BF16)
            hi[rows, :] = own_rows(sz, res, comp, (sz.cx - 1) * sz.cy + y).astype(BF16)
    two = 2 * sz.cy
    lo[pl.ds(sz.face_x, two), :] = (ids[pl.ds(0, two), :] + 1).astype(F32).astype(BF16)
    hi[pl.ds(sz.face_x, two), :] = (
        (ids[pl.ds(sz.cells - two, two), :] + 1).astype(F32).astype(BF16)
    )


def make_pieces(sz, count, rank, basis, res, message, split, wide):
    slots, loads = sz.slots, sz.loads

    def step(index, carry):
        both, low = carry
        basis_hi, basis_lo, res_hi, res_both = [], [], [], []
        for half in range(2):
            tile = index * 2 + half
            comp = tile // sz.cells
            hi, lo = split_hi_lo(basis[pl.ds(tile, slots, stride=sz.tiles), :])
            split[tile, pl.ds(0, slots), :] = hi
            split[tile, pl.ds(slots, slots), :] = lo
            value_hi, value_lo = split_hi_lo(own_rows(sz, res, comp, tile - comp * sz.cells))
            basis_hi.append(hi)
            basis_lo.append(lo)
            res_hi.append(value_hi)
            res_both.append(jnp.concatenate([value_hi, value_lo], axis=0))
        both = both + lax.dot_general(
            jnp.concatenate(res_both, axis=1),
            jnp.concatenate(basis_hi, axis=1),
            TRANSPOSED,
            preferred_element_type=F32,
        )
        low = low + lax.dot_general(
            jnp.concatenate(res_hi, axis=1),
            jnp.concatenate(basis_lo, axis=1),
            TRANSPOSED,
            preferred_element_type=F32,
        )
        return both, low

    both, low = lax.fori_loop(
        0,
        sz.tiles // 2,
        step,
        (jnp.zeros((2 * loads, slots), F32), jnp.zeros((loads, slots), F32)),
        unroll=4,
    )
    pieces = both[:loads] + both[loads:] + low
    slot = lax.broadcasted_iota(jnp.int32, pieces.shape, 1)
    wide[...] = jnp.zeros_like(wide)
    wide[:, pl.ds(0, slots)] = jnp.where(slot < count[0], pieces, 0.0)
    half = loads // 2
    lane = lane_ids(half)
    packed = jnp.where(lane < 64, wide[:half, :], roll_lanes(wide[half:, :], 64))
    packed = jnp.where(lane == slots, count[0].astype(F32), packed)
    packed = jnp.where(lane == slots + 1, rank[0].astype(F32), packed).astype(BF16)
    for device in range(message.shape[0]):
        message[device] = packed


def pack_y(sz, swap, res, ids, below, above, *refs):
    outs, side = refs[:-1], refs[-1]
    last = sz.cy - 1
    if swap:
        faces = [jnp.where(lax.axis_index("gy") == 0, last, 0)]
    else:
        faces = [0, last]
    ids_below = below[pl.ds(sz.face_x, 2 * sz.cy), :].astype(F32)
    ids_above = above[pl.ds(sz.face_x, 2 * sz.cy), :].astype(F32)
    for out, y in zip(outs, faces):
        dynamic = not isinstance(y, int)
        for comp in range(sz.comps):
            for x in range(sz.bx):
                rows = pl.ds((comp * sz.bx + x) * sz.loads, sz.loads)
                if 0 < x < sz.bx - 1:
                    value = own_rows(sz, res, comp, (x - 1) * sz.cy + y).astype(BF16)
                else:
                    source = below if x == 0 else above
                    start = (comp * sz.cy + y) * sz.loads
                    if dynamic:
                        start = pl.multiple_of(start, sz.loads)
                    value = source[pl.ds(start, sz.loads), :]
                out[rows, :] = value
        for x in range(sz.cx + 4):
            for j in range(2):
                if 2 <= x < sz.cx + 2:
                    first = (ids[pl.ds((x - 2) * sz.cy + j, 1), :] + 1).astype(F32)
                    end = (ids[pl.ds((x - 2) * sz.cy + last - 1 + j, 1), :] + 1).astype(F32)
                else:
                    source, base = (ids_below, x * sz.cy) if x < 2 else (
                        ids_above, (x - sz.cx - 2) * sz.cy)
                    first = source[base + j : base + j + 1]
                    end = source[base + last - 1 + j : base + last + j]
                if dynamic:
                    row = jnp.where(y == 0, first, end)
                else:
                    row = first if y == 0 else end
                side[pl.ds(x * 2 + j, 1), :] = row
        out[pl.ds(sz.face_y, HALO_IDS), :] = side[...].astype(BF16)


def side_flags(swap):
    if not swap:
        return None, None
    upper = lax.axis_index("gy") == 1
    return jnp.where(upper, 1.0, 0.0).astype(F32), jnp.where(upper, 0.0, 1.0).astype(F32)


def flagged(value, flag):
    value = value.astype(F32)
    return value if flag is None else value * flag


def box_tile(sz, res, below, above, ylow, yhigh, flags, comp, x, y):
    if y == 0 or y == sz.by - 1:
        source, flag = (ylow, flags[0]) if y == 0 else (yhigh, flags[1])
        return flagged(source[pl.ds((comp * sz.bx + x) * sz.loads, sz.loads), :], flag)
    if x == 0 or x == sz.bx - 1:
        source = below if x == 0 else above
        return source[pl.ds((comp * sz.cy + y - 1) * sz.loads, sz.loads), :].astype(F32)
    return own_rows(sz, res, comp, (x - 1) * sz.cy + y - 1)


def pack_z(sz, swap, res, ids, below, above, ylow, yhigh, out, id_box, star, outer):
    flags = side_flags(swap)
    pitch = sz.pitch
    id_box[...] = jnp.zeros_like(id_box)
    two = 2 * sz.cy
    ids_below = below[pl.ds(sz.face_x, two), :].astype(F32)
    ids_above = above[pl.ds(sz.face_x, two), :].astype(F32)
    ids_low = flagged(ylow[pl.ds(sz.face_y, HALO_IDS), :], flags[0])
    ids_high = flagged(yhigh[pl.ds(sz.face_y, HALO_IDS), :], flags[1])
    for x in range(sz.cx + 4):
        if x < 2:
            rows = ids_below[x * sz.cy : (x + 1) * sz.cy]
        elif x >= sz.cx + 2:
            rows = ids_above[(x - sz.cx - 2) * sz.cy : (x - sz.cx - 1) * sz.cy]
        else:
            rows = (ids[pl.ds((x - 2) * sz.cy, sz.cy), :] + 1).astype(F32)
        id_box[pl.ds(x * pitch + 2, sz.cy), :] = rows
        id_box[pl.ds(x * pitch, 2), :] = ids_low[2 * x : 2 * x + 2]
        id_box[pl.ds(x * pitch + sz.cy + 2, 2), :] = ids_high[2 * x : 2 * x + 2]
    values = id_box[...]
    lane = lane_ids(values.shape[0])
    outer[...] = jnp.where(lane == LANES - 1, roll_lanes(values, 1), roll_lanes(values, -1))
    star[...] = jnp.zeros_like(star)
    lane8 = lane_ids(8)
    taken = jnp.zeros((8, LANES), F32)
    for x in range(sz.bx):
        for y in range(sz.by):
            place = x * sz.by + y
            row = (x + 1) * pitch + y + 1
            for j, shift in enumerate((0, -pitch, pitch, -1, 1)):
                star[pl.ds(place * 8 + j, 1), :] = id_box[pl.ds(row + shift, 1), :]
            star[pl.ds(place * 8 + 5, 1), :] = outer[pl.ds(row, 1), :]
    for place in range(sz.box):
        picked = roll_lanes(star[pl.ds(place * 8, 8), :], 2 * place + 1)
        taken = jnp.where((lane8 >> 1) == place, picked, taken)
    out[pl.ds(sz.face_z, HALO_IDS), :] = jnp.concatenate(
        [taken, jnp.zeros((HALO_IDS - 8, LANES), F32)], axis=0
    ).astype(BF16)
    lane_k = lane_ids(sz.loads)
    for comp in range(sz.comps):
        total = jnp.zeros((sz.loads, LANES), F32)
        for x in range(sz.bx):
            for y in range(sz.by):
                place = x * sz.by + y
                tile = box_tile(sz, res, below, above, ylow, yhigh, flags, comp, x, y)
                total = jnp.where(
                    (lane_k >> 1) == place, roll_lanes(tile, 2 * place + 1), total
                )
        out[pl.ds(comp * sz.loads, sz.loads), :] = total.astype(BF16)


def place_pieces(sz, starts, gathered, inverse, message, vector, wide):
    half = sz.loads // 2
    lane = lane_ids(half)
    vector[...] = jnp.zeros_like(vector)

    def place(device, carry):
        start = starts[device]
        block = start // LANES
        offset = start - block * LANES
        packed = gathered[device].astype(F32)
        low = jnp.where(lane < sz.slots, packed, 0.0)
        high = jnp.where((lane >= 64) & (lane < 64 + sz.slots), packed, 0.0)
        both = jnp.concatenate(
            [
                pltpu.roll(low, offset, axis=1),
                pltpu.roll(high, lax.rem(offset + 64, LANES), axis=1),
            ],
            axis=0,
        )
        wide_lane = lane_ids(sz.loads)
        vector[block] = vector[block] + jnp.where(wide_lane >= offset, both, 0.0)
        vector[block + 1] = vector[block + 1] + jnp.where(wide_lane < offset, both, 0.0)
        return carry

    lax.fori_loop(0, gathered.shape[0], place, 0)
    total = jnp.zeros((sz.loads, sz.block_rows), F32)
    for block in range(sz.total_rows // LANES):
        total = total + lax.dot_general(
            vector[block].astype(BF16),
            inverse[:, pl.ds(block * LANES, LANES)],
            TRANSPOSED,
            preferred_element_type=F32,
        )
    if sz.block_rows == 64:
        wide[...] = jnp.zeros_like(wide)
        wide[:, pl.ds(0, 64)] = total
        packed = jnp.where(lane < 64, wide[:half, :], roll_lanes(wide[half:, :], 64))
        for device in range(message.shape[0]):
            message[device, 0] = packed
    else:
        for device in range(message.shape[0]):
            for block in range(sz.block_rows // LANES):
                message[device, block] = total[:, block * LANES : (block + 1) * LANES]


def own_coefs(sz, coefs, start):
    if sz.block_rows == 64:
        half = sz.loads // 2
        block = start // 64
        offset = start - block * 64
        first = coefs[block]
        second = coefs[jnp.minimum(block + 1, coefs.shape[0] - 1)]
        lane = lane_ids(half)
        top = jnp.where(lane < 64, first, roll_lanes(second, 64))
        bottom = jnp.where(lane < 64, roll_lanes(first, 64), second)
        both = jnp.concatenate([top, bottom], axis=0)
    else:
        block = start // LANES
        offset = start - block * LANES
        first = coefs[block]
        second = coefs[jnp.minimum(block + 1, coefs.shape[0] - 1)]
        both = jnp.where(lane_ids(sz.loads) >= offset, first, second)
    return pltpu.roll(both, lax.rem(LANES - offset, LANES), axis=1)


def look_up(table, row, ids):
    result = jnp.zeros_like(ids)
    for material in range(table.shape[1]):
        result = jnp.where(ids == material + 1, table[row, material], result)
    return result


DINV, KEEP, DLAM, WXM, WXP, WYM, WYP, WZM, WZP = range(9)


def spread_row(ref, index, row):
    return jnp.broadcast_to(ref[index, pl.ds(row, 1), :], (8, LANES))


def make_coefs(sz, table, id_box, halo_ids, coefs, halo_coefs, own, mu_box, halo_mu):
    pitch = sz.pitch
    mu_box[...] = look_up(table, 0, id_box[...])
    lam_box = look_up(table, 1, id_box[...])
    mu_halo = look_up(table, 0, halo_ids)
    lam_halo = look_up(table, 1, halo_ids)
    lane8 = lane_ids(8)
    center = jnp.broadcast_to(mu_halo[0:1], (8, LANES))
    inner = jnp.zeros((8, LANES), F32)
    for place in range(sz.box):
        row = (place // sz.by + 1) * pitch + place % sz.by + 1
        halo_mu[pl.ds(row, 1), :] = roll_lanes(center, -2 * place)[0:1]
        spread = jnp.broadcast_to(mu_box[pl.ds(row, 1), :], (8, LANES))
        here = (((lane8 + 1) >> 1) & 63) == place
        inner = jnp.where(here, roll_lanes(spread, 2 * place), inner)
    rows_id = lax.broadcasted_iota(jnp.int32, (pitch, LANES), 0)
    lane = lane_ids(pitch)
    for x in range(1, sz.bx + 1):
        mu = mu_box[pl.ds(x * pitch, pitch), :]
        edge = halo_mu[pl.ds(x * pitch, pitch), :]
        lam = lam_box[x * pitch : (x + 1) * pitch]
        faces = [
            0.5 * (mu + mu_box[pl.ds((x - 1) * pitch, pitch), :]),
            0.5 * (mu + mu_box[pl.ds((x + 1) * pitch, pitch), :]),
            0.5 * (mu + mu_box[pl.ds(x * pitch - 1, pitch), :]),
            0.5 * (mu + mu_box[pl.ds(x * pitch + 1, pitch), :]),
            0.5 * (mu + jnp.where(lane == 0, edge, roll_lanes(mu, 1))),
            0.5 * (mu + jnp.where(lane == LANES - 1, edge, roll_lanes(mu, -1))),
        ]
        diag = 1.0 + sum(faces)
        dinv = DAMPING / (diag + lam)
        rows = pl.ds(x * pitch, pitch)
        coefs[DINV, rows, :] = dinv
        coefs[KEEP, rows, :] = (1.0 - DAMPING) + dinv * lam
        coefs[DLAM, rows, :] = dinv * lam
        weights = [dinv * face for face in faces]
        if x == 1:
            weights[0] = jnp.zeros_like(dinv)
        if x == sz.bx:
            weights[1] = jnp.zeros_like(dinv)
        weights[2] = jnp.where(rows_id == 1, 0.0, weights[2])
        weights[3] = jnp.where(rows_id == sz.by, 0.0, weights[3])
        for j in range(6):
            coefs[WXM + j, rows, :] = weights[j]
        if 2 <= x <= sz.cx + 1:
            target = pl.ds((x - 2) * sz.cy, sz.cy)
            for j, value in enumerate([diag, lam] + faces):
                own[j, target, :] = value[2 : 2 + sz.cy]
    place = ((lane8 + 1) >> 1) & 63
    column = jnp.zeros_like(place)
    for x in range(1, sz.bx):
        column = column + (place >= x * sz.by).astype(jnp.int32)
    y_place = place - column * sz.by
    others = [jnp.broadcast_to(mu_halo[j : j + 1], (8, LANES)) for j in range(1, 6)]
    faces = [0.5 * (center + other) for other in others] + [0.5 * (center + inner)]
    lam = jnp.broadcast_to(lam_halo[0:1], (8, LANES))
    dinv = DAMPING / (1.0 + lam + sum(faces))
    live = place < sz.box
    keep = [
        live & (column > 0),
        live & (column < sz.bx - 1),
        live & (y_place > 0),
        live & (y_place < sz.by - 1),
        None,
        live,
    ]
    halo_coefs[DINV] = dinv
    halo_coefs[KEEP] = (1.0 - DAMPING) + dinv * lam
    halo_coefs[DLAM] = dinv * lam
    for j, target in ((0, WXM), (1, WXP), (2, WYM), (3, WYP), (5, WZM)):
        halo_coefs[target] = jnp.where(keep[j], dinv * faces[j], 0.0)


def solve_and_direct(
    sz, swap, start, count, table, res, below, above, ylow, yhigh, zdown, zup, id_box, coarse,
    split, *rest,
):
    if swap:
        direction, xlo, xhi, yface, zface, own = rest[:6]
        yfaces = [yface]
        rest = rest[6:]
    else:
        direction, xlo, xhi, ylo_out, yhi_out, zface, own = rest[:7]
        yfaces = [ylo_out, yhi_out]
        rest = rest[7:]
    first, second, third, halos, inner, coefs, halo_coefs, mu_box, halo_mu, left = rest
    loads, comps = sz.loads, sz.comps
    groups = loads // 8
    flags = side_flags(swap)
    lane8 = lane_ids(8)
    even8 = (lane8 & 1) == 0

    def halo_rows(row, size):
        down = zdown[pl.ds(row, size), :].astype(F32)
        up = zup[pl.ds(row, size), :].astype(F32)
        even = (lane_ids(size) & 1) == 0
        return jnp.where(even, down, roll_lanes(up, -2))

    halo_mu[...] = jnp.zeros_like(halo_mu)
    inner[1] = jnp.zeros((comps, loads, LANES), F32)
    make_coefs(
        sz, table, id_box, halo_rows(sz.face_z, HALO_IDS)[:8], coefs, halo_coefs, own, mu_box,
        halo_mu,
    )
    here_of = lambda place: (((lane8 + 1) >> 1) & 63) == place

    for comp in range(comps):
        halo = halo_rows(comp * loads, loads)
        dinv = jnp.concatenate([halo_coefs[DINV]] * groups, axis=0)
        halos[0, comp] = dinv * halo
        total = jnp.zeros((loads, LANES), F32)
        lane_k = lane_ids(loads)
        for x in range(sz.bx):
            for y in range(sz.by):
                place = x * sz.by + y
                row = (x + 1) * sz.pitch + y + 1
                tile = box_tile(sz, res, below, above, ylow, yhigh, flags, comp, x, y)
                value = tile * jnp.broadcast_to(coefs[DINV, pl.ds(row, 1), :], (loads, LANES))
                first[comp, place] = value
                here = (((lane_k + 1) >> 1) & 63) == place
                total = jnp.where(here, roll_lanes(value, 2 * place), total)
        inner[0, comp] = total

    def relax(source, level, place, row):
        coef = [spread_row(coefs, j, row) for j in range(9)]
        xm, xp = jnp.maximum(place - sz.by, 0), jnp.minimum(place + sz.by, sz.box - 1)
        ym, yp = jnp.maximum(place - 1, 0), jnp.minimum(place + 1, sz.box - 1)
        back = lax.rem(LANES - 2 * place + LANES, LANES)
        result = {}
        for group in range(groups):
            rows = pl.ds(group * 8, 8)
            center = [source[comp, place, rows, :] for comp in range(comps)]
            coupled = coef[DLAM] * sum(center)
            for comp in range(comps):
                value = center[comp]
                edge = pltpu.roll(halos[level, comp, rows, :], back, axis=1)
                zm = jnp.where(lane8 == 0, edge, roll_lanes(value, 1))
                zp = jnp.where(lane8 == LANES - 1, edge, roll_lanes(value, -1))
                out = (first[comp, place, rows, :] - coupled) + coef[KEEP] * value
                out = out + coef[WXM] * source[comp, xm, rows, :]
                out = out + coef[WXP] * source[comp, xp, rows, :]
                out = out + coef[WYM] * source[comp, ym, rows, :]
                out = out + coef[WYP] * source[comp, yp, rows, :]
                out = out + coef[WZM] * zm
                out = out + coef[WZP] * zp
                result[comp, group] = out
        return result

    def sweep(source, target, level):
        def at(place, carry):
            x = place // sz.by
            row = (x + 1) * sz.pitch + place - x * sz.by + 1
            result = relax(source, level, place, row)
            for (comp, group), out in result.items():
                rows = pl.ds(group * 8, 8)
                target[comp, place, rows, :] = out
                if level == 0:
                    inner[1, comp, rows, :] = jnp.where(
                        here_of(place), pltpu.roll(out, 2 * place, axis=1),
                        inner[1, comp, rows, :],
                    )
            return carry

        lax.fori_loop(0, sz.box, at, 0)
        coef = [halo_coefs[j] for j in range(8)]
        for group in range(groups):
            rows = pl.ds(group * 8, 8)
            center = [halos[level, comp, rows, :] for comp in range(comps)]
            coupled = coef[DLAM] * sum(center)
            for comp in range(comps):
                value = center[comp]
                out = (halos[0, comp, rows, :] - coupled) + coef[KEEP] * value
                out = out + coef[WXM] * roll_lanes(value, 2 * sz.by)
                out = out + coef[WXP] * roll_lanes(value, -2 * sz.by)
                out = out + coef[WYM] * roll_lanes(value, 2)
                out = out + coef[WYP] * roll_lanes(value, -2)
                out = out + coef[WZM] * inner[level, comp, rows, :]
                halos[level + 1, comp, rows, :] = out

    sweep(first, second, 0)
    sweep(second, third, 1)

    mine = own_coefs(sz, coarse, start[0])
    mine = jnp.where(lane_ids(loads) < jnp.minimum(count[0], sz.slots), mine, 0.0)
    left[...] = paired_left(mine, sz.slots, left)
    zface[...] = jnp.zeros_like(zface)

    def final(cell, carry):
        x = cell // sz.cy
        y = cell - x * sz.cy
        place = (x + 1) * sz.by + y + 1
        result = relax(third, 2, place, (x + 2) * sz.pitch + y + 2)
        for comp in range(comps):
            tile = comp * sz.cells + cell
            part = jnp.dot(
                left[:, : 2 * sz.slots], split[tile], preferred_element_type=F32
            )
            for group in range(groups):
                rows = pl.ds(group * 8, 8)
                value = result[comp, group] + (
                    part[group * 8 : group * 8 + 8]
                    + part[loads + group * 8 : loads + group * 8 + 8]
                )
                direction[comp, cell, rows, :] = value
                zrows = pl.ds(comp * loads + group * 8, 8)
                zface[zrows, :] = jnp.where(
                    (lane8 >> 1) == place,
                    pltpu.roll(value, 2 * place + 1, axis=1),
                    zface[zrows, :],
                )
        return carry

    lax.fori_loop(0, sz.cells, final, 0)
    for comp in range(comps):
        for y in range(sz.cy):
            rows = pl.ds((comp * sz.cy + y) * loads, loads)
            xlo[rows, :] = direction[comp, y].astype(BF16)
            xhi[rows, :] = direction[comp, (sz.cx - 1) * sz.cy + y].astype(BF16)
        for x in range(sz.cx):
            rows = pl.ds((comp * sz.cx + x) * loads, loads)
            if swap:
                y = jnp.where(lax.axis_index("gy") == 0, sz.cy - 1, 0)
                yfaces[0][rows, :] = direction[comp, x * sz.cy + y].astype(BF16)
            else:
                yfaces[0][rows, :] = direction[comp, x * sz.cy].astype(BF16)
                yfaces[1][rows, :] = direction[comp, x * sz.cy + sz.cy - 1].astype(BF16)


def make_image(
    sz, swap, res, own, direction, below, above, ylow, yhigh, zdown, zup, dir_split,
    image_split, message, box, halo, sem,
):
    loads, comps = sz.loads, sz.comps
    groups = loads // 8
    copies = []
    for comp in range(comps):
        for x in range(sz.cx):
            copies.append(
                pltpu.make_async_copy(
                    direction.at[comp, pl.ds(x * sz.cy, sz.cy)],
                    box.at[comp, pl.ds((x + 1) * sz.by + 1, sz.cy)],
                    sem.at[comp, x],
                )
            )
    for copy in copies:
        copy.start()
    flags = side_flags(swap)
    for comp in range(comps):
        for y in range(sz.cy):
            rows = pl.ds((comp * sz.cy + y) * loads, loads)
            box[comp, y + 1] = below[rows, :].astype(F32)
            box[comp, (sz.bx - 1) * sz.by + y + 1] = above[rows, :].astype(F32)
        for x in range(sz.cx):
            rows = pl.ds((comp * sz.cx + x) * loads, loads)
            box[comp, (x + 1) * sz.by] = flagged(ylow[rows, :], flags[0])
            box[comp, (x + 1) * sz.by + sz.by - 1] = flagged(yhigh[rows, :], flags[1])
        rows = pl.ds(comp * loads, loads)
        even = (lane_ids(loads) & 1) == 0
        halo[comp] = jnp.where(
            even, zdown[rows, :].astype(F32), roll_lanes(zup[rows, :].astype(F32), -2)
        )
    for copy in copies:
        copy.wait()
    lane8 = lane_ids(8)

    def at(cell, total):
        x = cell // sz.cy
        y = cell - x * sz.cy
        place = (x + 1) * sz.by + y + 1
        back = lax.rem(LANES - 2 * place + LANES, LANES)
        coef = [spread_row(own, j, cell) for j in range(8)]
        parts = {}
        for group in range(groups):
            rows = pl.ds(group * 8, 8)
            center = [box[comp, place, rows, :] for comp in range(comps)]
            coupled = coef[1] * sum(center)
            for comp in range(comps):
                value = center[comp]
                edge = pltpu.roll(halo[comp, rows, :], back, axis=1)
                zm = jnp.where(lane8 == 0, edge, roll_lanes(value, 1))
                zp = jnp.where(lane8 == LANES - 1, edge, roll_lanes(value, -1))
                out = coef[0] * value + coupled
                out = out - coef[2] * box[comp, place - sz.by, rows, :]
                out = out - coef[3] * box[comp, place + sz.by, rows, :]
                out = out - coef[4] * box[comp, place - 1, rows, :]
                out = out - coef[5] * box[comp, place + 1, rows, :]
                out = out - coef[6] * zm
                parts[comp, group] = out - coef[7] * zp
        for comp in range(comps):
            tile = comp * sz.cells + cell
            dir_hi, dir_lo = split_hi_lo(box[comp, place])
            field = jnp.concatenate([parts[comp, group] for group in range(groups)], axis=0)
            field_hi, field_lo = split_hi_lo(field)
            res_hi, res_lo = split_hi_lo(own_rows(sz, res, comp, cell))
            left = jnp.concatenate([dir_hi, dir_lo], axis=0)
            field_both = jnp.concatenate([field_hi, field_lo], axis=0)
            dir_split[tile] = left
            image_split[tile] = field_both
            total = total + lax.dot_general(
                left,
                jnp.concatenate([field_both, res_hi, res_lo], axis=0),
                TRANSPOSED,
                preferred_element_type=F32,
            )
        return total

    total = lax.fori_loop(0, sz.cells, at, jnp.zeros((2 * loads, 4 * loads), F32))
    high, low = total[:loads], total[loads:]
    sums = high + roll_lanes(high, -loads) + low
    half = loads // 2
    lane = lane_ids(half)
    packed = jnp.where((lane & (2 * loads - 1)) < loads, sums[:half], roll_lanes(sums[half:], loads))
    for device in range(message.shape[0]):
        message[device] = packed


def finish(
    sz, sums, iterate, res, dir_split, image_split, new_iterate, new_residual, parts
):
    loads = sz.loads
    half = loads // 2
    total = sums[0]
    for device in range(1, sums.shape[0]):
        total = total + sums[device]
    system = jnp.concatenate([total, roll_lanes(total, -loads)], axis=0)
    lane = lane_ids(loads)
    system = jnp.where((lane & (2 * loads - 1)) < loads, system, 0.0)
    row_ids = lax.broadcasted_iota(jnp.int32, (loads, LANES), 0)
    for i in range(loads):
        row = system[i : i + 1, :]
        row = row / row[:, i : i + 1]
        system = jnp.where(row_ids == i, row, system - system[:, i : i + 1] * row)
    step = jnp.transpose(system)[2 * loads : 3 * loads, :]
    padded = jnp.concatenate([step, jnp.zeros((loads, LANES - loads), F32)], axis=1) if (
        step.shape[1] < LANES
    ) else step
    left = paired_left(padded, loads, parts)[:, : 2 * loads]

    def at(cell, carry):
        for comp in range(sz.comps):
            tile = comp * sz.cells + cell
            right = jnp.concatenate([dir_split[tile], image_split[tile]], axis=1)
            part = jnp.dot(left, right, preferred_element_type=F32)
            part = part[:loads] + part[loads:]
            rows = pl.ds(comp * loads * sz.cells + cell, loads, stride=sz.cells)
            new_iterate[rows, :] = iterate[rows, :] + part[:, :LANES]
            new_residual[rows, :] = res[rows, :] - part[:, LANES:]
        return carry

    lax.fori_loop(0, sz.cells, at, 0, unroll=2)


def exchange(low, high, axis):
    devices = lax.axis_size(axis)
    up = [(i, i + 1) for i in range(devices - 1)]
    down = [(j, i) for i, j in up]
    return lax.ppermute(high, axis, up), lax.ppermute(low, axis, down)


def exchange_y(faces, swap):
    if swap:
        got = lax.ppermute(faces[0], "gy", [(0, 1), (1, 0)])
        return got, got
    return exchange(faces[0], faces[1], "gy")


def body(
    iterate, residual, cell_ids, materials, eigen_counts, coarse_rank, eigen_basis, coarse_inverse
):
    sz = Sizes(residual, eigen_basis, coarse_inverse)
    shape = jax.ShapeDtypeStruct
    swap = lax.axis_size("gy") == 2
    devices = 1
    for axis in AXES:
        devices = devices * lax.axis_size(axis)
    blocks = sz.total_rows // sz.block_rows
    smem, vmem = pltpu.SMEM, pltpu.VMEM
    res = residual.reshape(-1, LANES)
    old = iterate.reshape(-1, LANES)
    basis = eigen_basis.reshape(-1, LANES)
    ids = cell_ids.reshape(-1, LANES)

    def call(name, kernel, *args, **kwargs):
        return vmem_call(name, lambda *refs: kernel(sz, *refs), *args, **kwargs)

    def call_swap(name, kernel, *args, **kwargs):
        return vmem_call(name, lambda *refs: kernel(sz, swap, *refs), *args, **kwargs)

    face = shape((sz.face_x + 2 * sz.cy, LANES), BF16)
    xlo, xhi = call("pack_x", pack_x, [face, face], [], 16, 1 << 20, 2 << 20, [res, ids])
    below, above = exchange(xlo, xhi, "gx")

    message, split = call(
        "pieces",
        make_pieces,
        [
            shape((devices, sz.loads // 2, LANES), BF16),
            shape((sz.tiles, 2 * sz.slots, LANES), BF16),
        ],
        [pltpu.VMEM((sz.loads, LANES), F32)],
        20,
        1 << 27,
        7 << 20,
        [eigen_counts, coarse_rank, basis, res],
        spaces=[smem, smem, vmem, vmem],
    )
    gathered = lax.all_to_all(message, AXES, 0, 0, tiled=True)
    all_counts = gathered[:, 0, sz.slots].astype(jnp.int32)
    all_ranks = gathered[:, 0, sz.slots + 1].astype(jnp.int32)
    starts = jnp.sum(
        all_counts[None, :] * (all_ranks[None, :] < all_ranks[:, None]).astype(jnp.int32), axis=1
    )
    my_start = jnp.sum(
        all_counts * (all_ranks < coarse_rank[0]).astype(jnp.int32), keepdims=True
    )

    side = [pltpu.VMEM((HALO_IDS, LANES), F32)]
    yface = shape((sz.face_y + HALO_IDS, LANES), BF16)
    faces = call_swap(
        "pack_y", pack_y, [yface] * (1 if swap else 2), side, 16, 1 << 20, 2 << 20,
        [res, ids, below, above],
    )
    ylow, yhigh = exchange_y(faces, swap)
    rows = (sz.cx + 4) * sz.pitch
    zmessage, id_box = call_swap(
        "pack_z",
        pack_z,
        [shape((sz.face_z + HALO_IDS, LANES), BF16), shape((rows, LANES), F32)],
        [pltpu.VMEM((sz.box * 8, LANES), F32), pltpu.VMEM((rows, LANES), F32)],
        16,
        1 << 22,
        3 << 20,
        [res, ids, below, above, ylow, yhigh],
    )
    zdown, zup = exchange(zmessage, zmessage, "col")

    packed = sz.block_rows == 64
    tile = (1, sz.loads // 2, LANES) if packed else (sz.block_rows // LANES, sz.loads, LANES)
    partial = call(
        "coarse",
        place_pieces,
        shape((blocks,) + tile, F32),
        [
            pltpu.VMEM((sz.total_rows // LANES + 1, sz.loads, LANES), F32),
            pltpu.VMEM((sz.loads, LANES), F32),
        ],
        20,
        1 << 23,
        1 << 20,
        [starts, gathered, coarse_inverse],
        spaces=[smem, vmem, vmem],
    )
    coarse = lax.all_to_all(partial, ("gx", "col"), 0, 0, tiled=True)
    coarse = coarse.reshape((-1,) + tile[1:])

    dface = shape((sz.face_x, LANES), BF16)
    dyface = shape((sz.inner_y, LANES), BF16)
    field = pltpu.VMEM((sz.comps, sz.box, sz.loads, LANES), F32)
    results = call_swap(
        "solve",
        solve_and_direct,
        [shape((sz.comps, sz.cells, sz.loads, LANES), F32), dface, dface]
        + [dyface] * (1 if swap else 2)
        + [shape((sz.face_z, LANES), F32), shape((8, sz.cells, LANES), F32)],
        [
            field,
            field,
            field,
            pltpu.VMEM((3, sz.comps, sz.loads, LANES), F32),
            pltpu.VMEM((2, sz.comps, sz.loads, LANES), F32),
            pltpu.VMEM((9, rows, LANES), F32),
            pltpu.VMEM((9, 8, LANES), F32),
            pltpu.VMEM((rows, LANES), F32),
            pltpu.VMEM((rows, LANES), F32),
            pltpu.VMEM((2 * sz.loads, LANES), BF16),
        ],
        40,
        1 << 28,
        8 << 20,
        [
            my_start, eigen_counts, materials, res, below, above, ylow, yhigh, zdown, zup, id_box,
            coarse, split,
        ],
        spaces=[smem, smem, smem] + [vmem] * 10,
    )
    direction, dxlo, dxhi = results[:3]
    dfaces, zface, own = results[3:-2], results[-2], results[-1]
    dbelow, dabove = exchange(dxlo, dxhi, "gx")
    dylow, dyhigh = exchange_y(dfaces, swap)
    dzdown, dzup = exchange(zface, zface, "col")

    dir_split, image_split, energy = call_swap(
        "image",
        make_image,
        [
            shape((sz.tiles, 2 * sz.loads, LANES), BF16),
            shape((sz.tiles, 2 * sz.loads, LANES), BF16),
            shape((devices, sz.loads // 2, LANES), F32),
        ],
        [
            field,
            pltpu.VMEM((sz.comps, sz.loads, LANES), F32),
            pltpu.SemaphoreType.DMA((sz.comps, sz.cx)),
        ],
        32,
        1 << 28,
        8 << 20,
        [res, own, direction, dbelow, dabove, dylow, dyhigh, dzdown, dzup],
        spaces=[vmem, vmem, pl.ANY] + [vmem] * 6,
    )
    sums = lax.all_to_all(energy, AXES, 0, 0, tiled=True)
    flat = shape(res.shape, F32)
    new_iterate, new_residual = call(
        "finish",
        finish,
        [flat, flat],
        [pltpu.VMEM((2 * sz.loads, LANES), BF16)],
        32,
        1 << 27,
        9 << 20,
        [sums, old, res, dir_split, image_split],
    )
    return (new_iterate.reshape(iterate.shape), new_residual.reshape(residual.shape))


def solution(mesh):
    placed = (
        P(None, None, "gx", "gy", "col"),
        P(None, None, "gx", "gy", "col"),
        P("gx", "gy", "col"),
        P(),
        P(("gx", "gy", "col")),
        P(("gx", "gy", "col")),
        P(None, None, "gx", "gy", "col"),
        P(("gx", "col"), None),
    )
    return jax.shard_map(
        body,
        mesh=mesh,
        in_specs=placed,
        out_specs=(P(None, None, "gx", "gy", "col"), P(None, None, "gx", "gy", "col")),
        check_vma=False,
    )
```

time: 456 us -> 137 us (0.30); the launches traced: 447 us -> 136 us
  blocking collectives: 198 us -> 18 us
  other arithmetic: 105 us -> 2.18 us
  Pallas kernels: 0 us -> 60.7 us
  local copies, waits for them, and re-layouts: 47.7 us -> 6.18 us
  matrix products: 28 us -> 0 us
  waiting for transfers between devices: 23.4 us -> 12.4 us
  starting transfers between devices: 39.9 us -> 34.9 us
    all_gather x2 -> x0, blocking collectives: 108 us -> none  [the longest x1 67.2 us: body(): lax.all_gather(pieces.astype(jnp.bfloat16)[None], ('gx', 'gy', 'col'), ax...]
    pallas_call x0 -> x8, Pallas kernels: none -> 60.7 us  [vmem_call(): pl.pallas_call(kernel, name=name, out_shape=outs, in_specs=[pl.BlockSpec(...]
    reduce_sum x4 -> x1, other arithmetic: 50.8 us -> 0.69 us  [body(): jnp.sum(all_counts * (all_ranks < coarse_rank[0]).astype(jnp.int32), keep...]
    unnamed x1 -> x0, blocking collectives: 48.7 us -> none
    psum x1 -> x0, blocking collectives: 41.3 us -> none  [body(): lax.psum((local_energy, local_loads), ('gx', 'gy', 'col'))]
    add x5 -> x0, other arithmetic: 28.3 us -> none  [the longest x2 27.5 us: apply_op(): result = result + coefs[position] * (center - neighbour)]
    dot_general x8 -> x0, matrix products: 27.5 us -> none  [the longest x1 11.6 us: body(): jnp.einsum('ecxyz,ek->ckxyz', eigen_basis, own_coef, precision=highest)]
    slice x30 -> x0, local copies, waits for them, and re-layouts: 25.3 us -> none  [the longest x8 13 us: extended(): last = lax.slice_in_dim(x, length - width, length, axis=dim)]
  transfers between devices with their start and end apart: 18 -> 12, of which waited for: 6 -> 5; matrix products, arithmetic and copies ran while one was open for 8% -> 2% of each run, Pallas kernels for 0% -> 4%
where the time goes in v1:
time: 137 us; the launch traced here: 136 us
  Pallas kernels  60.7 us (44%)
  starting transfers between devices  34.9 us (25%)
  blocking collectives  18 us (13%)
  waiting for transfers between devices  12.4 us (9%)
  local copies, waits for them, and re-layouts  6.18 us (5%)
  other arithmetic  2.18 us (2%)
  between operations  2.13 us (2%)
    pallas_call x8, Pallas kernels, vmem_call(): pl.pallas_call(kernel, name=name, out_shape=outs, in_specs=[pl.BlockSpec(...  60.7 us
    ppermute x8, starting transfers between devices, exchange(): return (lax.ppermute(high, axis, up), lax.ppermute(low, axis, down))  22.1 us
    all_to_all x1, blocking collectives, body(): sums = lax.all_to_all(energy, AXES, 0, 0, tiled=True)  18 us
    ppermute x8, waiting for transfers between devices, exchange(): return (lax.ppermute(high, axis, up), lax.ppermute(low, axis, down))  12.4 us
    all_to_all x1, starting transfers between devices, body(): gathered = lax.all_to_all(message, AXES, 0, 0, tiled=True)  7.3 us
    unnamed x18, local copies, waits for them, and re-layouts  6.18 us
    all_to_all x1, starting transfers between devices, body(): coarse = lax.all_to_all(partial, ('gx', 'col'), 0, 0, tiled=True)  5.34 us
  transfers between devices with their start and end apart: 12, of which 5 were waited for; matrix products, arithmetic and copies ran while one was open for 2% of the time, Pallas kernels for 4%

profile of v1, /device:TPU:0, one launch (start us, length us, event | category | flops | bytes accessed | tf_op | source)
XLA Modules:
  0.0 136.4 jit_solution(3826440506138159592)
XLA Ops:
  1.9 0.0 copy-start
  1.9 1.4 %copy-done = f32[3,32,4,8,128]{4,3,2,1,0:T(8,128)S(1)} copy-done((f32[3,32,4,8,128]{4,3,2,1,0:T(8,128)S(1)}, f32[3,32,4,8,128]{4,3,2,1,0:T(8,128)}, u32[]{:S(2)}) %copy-start) | copy-done | bytes 1572888
  3.3 0.0 copy-start.2
  3.3 1.7 %copy-done.2 = f32[48,3,4,8,128]{4,3,2,1,0:T(8,128)S(1)} copy-done((f32[48,3,4,8,128]{4,3,2,1,0:T(8,128)S(1)}, f32[48,3,4,8,128]{4,3,2,1,0:T(8,128)}, u32[]{:S(2)}) %copy-start.2) | copy-done | bytes 2359320
  5.0 0.0 copy-start.1
  5.0 0.0 copy-start.6
  5.0 5.0 %pieces.1 = (bf16[32,16,128]{2,1,0:T(8,128)(2,1)}, bf16[96,96,128]{2,1,0:T(8,128)(2,1)S(1)}) custom-call(s32[1]{0:T(128)S(6)} %copy.12.refs_0_.refs_1_, s32[1]{0:T(128)} %copy.13.refs_1_, f32[4608,128]{1,0:T(8,128)S(1)} %bitcast.17, f32[3072,128]{1,0:T(8,128)S(1)} %bitcast.10), custom_call_target="tpu_custom_call" | custom-call | flops 134217728 | bytes 7340032 | tf_op jit(solution)/shard_map/pieces/pallas_call | solution.py:46
  10.0 0.0 copy-start.3
  10.0 1.4 %copy-done.3 = bf16[96,96,128]{2,1,0:T(8,128)(2,1)} copy-done((bf16[96,96,128]{2,1,0:T(8,128)(2,1)}, bf16[96,96,128]{2,1,0:T(8,128)(2,1)S(1)}, u32[]{:S(2)}) %copy-start.3) | copy-done | bytes 2359320
  11.4 7.3 %all-to-all-start = ((bf16[32,16,128]{2,1,0:T(8,128)(2,1)}), bf16[32,16,128]{2,1,0:T(8,128)(2,1)S(1)}, u32[]{:S(2)}, u32[]{:S(2)}) async-start(bf16[32,16,128]{2,1,0:T(8,128)(2,1)} %get-tuple-element.19), calls=%async_computation | async-start | bytes 262144 | tf_op jit(solution)/shard_map/all_to_all | solution.py:742
  18.7 0.0 copy-done.1
  18.7 0.0 copy-done.6
  18.8 0.0 copy-start.7
  18.8 0.4 pack_x.1
  19.2 3.7 %collective-permute-start = (bf16[784,128]{1,0:T(8,128)(2,1)S(1)}, bf16[784,128]{1,0:T(8,128)(2,1)S(1)}, u32[]{:S(2)}, u32[]{:S(2)}) collective-permute-start(bf16[784,128]{1,0:T(8,128)(2,1)S(1)} %get-tuple-element.20), channel_id=1, source_target_pairs={{0,8},{8,16},{16,24},{1,9},{9,17},{17,25},{2,10},{10,18},{18,26},{... | collective-permute-start | bytes 602120 | tf_op jit(solution)/shard_map/ppermute | solution.py:692
  22.9 1.3 collective-permute-start.1
  24.2 3.6 %collective-permute-done.refs_2_.refs_4_ = bf16[784,128]{1,0:T(8,128)(2,1)S(1)} collective-permute-done((bf16[784,128]{1,0:T(8,128)(2,1)S(1)}, bf16[784,128]{1,0:T(8,128)(2,1)S(1)}, u32[]{:S(2)}, u32[]{:S(2)}) %collective-permute-start) | collective-permute-done | bytes 200736 | tf_op jit(solution)/shard_map/ppermute | solution.py:692
  27.8 6.2 %collective-permute-done.1.refs_3_.refs_5_ = bf16[784,128]{1,0:T(8,128)(2,1)S(1)} collective-permute-done((bf16[784,128]{1,0:T(8,128)(2,1)S(1)}, bf16[784,128]{1,0:T(8,128)(2,1)S(1)}, u32[]{:S(2)}, u32[]{:S(2)}) %collective-permute-start.1) | collective-permute-done | bytes 200736 | tf_op jit(solution)/shard_map/ppermute | solution.py:692
  34.0 0.1 pack_y.1
  34.1 0.0 copy-start.8
  34.1 0.1 collective-permute-start.2
  34.2 0.0 all-to-all-done.refs_1_
  34.2 1.3 fusion.1
  35.5 0.2 select_reduce_fusion.refs_0_
  35.7 0.0 copy-done.7
  35.7 4.0 %coarse.1 = f32[16,1,16,128]{3,2,1,0:T(8,128)} custom-call(s32[32]{0:T(128)S(1)} %select_reduce_fusion.refs_0_, bf16[32,16,128]{2,1,0:T(8,128)(2,1)S(1)} %all-to-all-done.refs_1_, bf16[64,1024]{1,0:T(8,128)(2,1)S(1)} %copy-done.7), custom_call_target="tpu_custom_call" | custom-call | flops 8388608 | bytes 1048576 | tf_op jit(solution)/shard_map/coarse/pallas_call | solution.py:46
  39.7 5.3 %all-to-all-start.1 = ((f32[16,1,16,128]{3,2,1,0:T(8,128)}), f32[16,1,16,128]{3,2,1,0:T(8,128)S(1)}, u32[]{:S(2)}, u32[]{:S(2)}) async-start(f32[16,1,16,128]{3,2,1,0:T(8,128)} %coarse.1), calls=%async_computation.1 | async-start | bytes 262144 | tf_op jit(solution)/shard_map/all_to_all | solution.py:788
  45.0 0.0 collective-permute-done.2.refs_4_.refs_5_.refs_6_.refs_7_
  45.0 1.3 pack_z.1
  46.3 1.3 collective-permute-start.4
  47.6 4.5 %collective-permute-start.3 = (bf16[112,128]{1,0:T(8,128)(2,1)S(1)}, bf16[112,128]{1,0:T(8,128)(2,1)S(1)}, u32[]{:S(2)}, u32[]{:S(2)}) collective-permute-start(bf16[112,128]{1,0:T(8,128)(2,1)S(1)} %get-tuple-element.22), channel_id=1, source_target_pairs={{0,1},{1,2},{2,3},{4,5},{5,6},{6,7},{8,9},{9,10},{10,11},{12,13},{... | collective-permute-start | bytes 86024 | tf_op jit(solution)/shard_map/ppermute | solution.py:692
  52.2 0.7 fusion.2
  52.9 0.0 collective-permute-done.4.refs_9_
  52.9 0.8 collective-permute-done.3.refs_8_
  53.7 0.0 all-to-all-done.1
  53.7 0.0 copy-done.8
  53.7 0.0 copy-start.4
  53.7 1.7 %copy-done.4 = bf16[96,96,128]{2,1,0:T(8,128)(2,1)S(1)} copy-done((bf16[96,96,128]{2,1,0:T(8,128)(2,1)S(1)}, bf16[96,96,128]{2,1,0:T(8,128)(2,1)}, u32[]{:S(2)}) %copy-start.4) | copy-done | bytes 2359320
  55.4 27.5 %solve.1 = (f32[3,32,32,128]{3,2,1,0:T(8,128)S(1)}, bf16[768,128]{1,0:T(8,128)(2,1)S(1)}, bf16[768,128]{1,0:T(8,128)(2,1)S(1)}, bf16[384,128]{1,0:T(8,128)(2,1)S...) custom-call(s32[1]{0:T(128)} %bitcast.3.refs_0_, s32[1]{0:T(128)S(6)} %copy.12.refs_0_.refs_1_, ...), custom_call_target="tpu_custom_call" | custom-call | flops 268435456 | bytes 8388608 | tf_op jit(solution)/shard_map/solve/pallas_call | solution.py:46
  82.9 3.8 %collective-permute-start.5 = (bf16[768,128]{1,0:T(8,128)(2,1)S(1)}, bf16[768,128]{1,0:T(8,128)(2,1)S(1)}, u32[]{:S(2)}, u32[]{:S(2)}) collective-permute-start(bf16[768,128]{1,0:T(8,128)(2,1)S(1)} %get-tuple-element.27), channel_id=1, source_target_pairs={{0,8},{8,16},{16,24},{1,9},{9,17},{17,25},{2,10},{10,18},{18,26},{... | collective-permute-start | bytes 589832 | tf_op jit(solution)/shard_map/ppermute | solution.py:692
  86.7 1.3 collective-permute-start.6
  88.0 0.1 collective-permute-start.7
  88.1 1.3 collective-permute-start.9
  89.4 4.8 %collective-permute-start.8 = (f32[96,128]{1,0:T(8,128)S(1)}, f32[96,128]{1,0:T(8,128)S(1)}, u32[]{:S(2)}, u32[]{:S(2)}) collective-permute-start(f32[96,128]{1,0:T(8,128)S(1)} %get-tuple-element.30), channel_id=1, source_target_pairs={{0,1},{1,2},{2,3},{4,5},{5,6},{6,7},{8,9},{9,10},{10,11},{12,13},{... | collective-permute-start | bytes 147464 | tf_op jit(solution)/shard_map/ppermute | solution.py:692
  94.3 0.4 collective-permute-done.9.refs_8_
  94.7 1.3 collective-permute-done.8.refs_7_
  96.0 0.0 collective-permute-done.7.refs_5_.refs_6_
  96.0 0.0 collective-permute-done.5.refs_3_
  96.0 0.0 collective-permute-done.6.refs_4_
  96.0 0.0 copy-start.5
  96.0 11.7 %image.1 = (bf16[96,64,128]{2,1,0:T(8,128)(2,1)S(1)}, bf16[96,64,128]{2,1,0:T(8,128)(2,1)S(1)}, f32[32,16,128]{2,1,0:T(8,128)S(1)}) custom-call(f32[3072,128]{1,0:T(8,128)S(1)} %bitcast.15, f32[8,32,128]{2,1,0:T(8,128)S(1)} %get-tuple-element.25.refs_1_, f32[3,32,32,128]{3,2,1,0:T(8,128)S(1)} %get-tuple-element.26.refs_2_, ...), custom_call_target="tpu_custom_call" | custom-call | flops 268435456 | bytes 8388608 | tf_op jit(solution)/shard_map/image/pallas_call | solution.py:46
  107.7 18.0 %all_to_all.15.refs_0_ = f32[32,16,128]{2,1,0:T(8,128)S(1)} all-to-all(f32[32,16,128]{2,1,0:T(8,128)S(1)} %get-tuple-element.31), channel_id=1, replica_groups=mesh['gx'=4,'gy'=2,'col'=4] {'gx','gy','col'}, dimensions={0} | all-to-all | bytes 524288 | tf_op jit(solution)/shard_map/all_to_all | solution.py:846
  125.8 0.0 copy-done.5
  125.8 10.6 %finish.1 = (f32[3072,128]{1,0:T(8,128)}, f32[3072,128]{1,0:T(8,128)}) custom-call(f32[32,16,128]{2,1,0:T(8,128)S(1)} %all_to_all.15.refs_0_, f32[3072,128]{1,0:T(8,128)S(1)} %bitcast.18, f32[3072,128]{1,0:T(8,128)S(1)} %bitcast.16, bf16[96,64,128]{2,1,0:T(8,128)(2,1)S(1)} %get-tuple-element.32.refs_3_, bf16[96,64,128]{2,1,0:T(8,128)(2,1)S(1)} %get-tuple-element.33.refs_4_), custom_call_target="tpu_custom_call" | custom-call | flops 134217728 | bytes 9437184 | tf_op jit(solution)/shard_map/finish/pallas_call | solution.py:46
Async XLA Ops:
  1.9 1.4 %copy-start = (f32[3,32,4,8,128]{4,3,2,1,0:T(8,128)S(1)}, f32[3,32,4,8,128]{4,3,2,1,0:T(8,128)}, u32[]{:S(2)}) copy-start(f32[3,32,4,8,128]{4,3,2,1,0:T(8,128)} %param.9) | copy-start | bytes 4718596
  3.3 1.7 %copy-start.2 = (f32[48,3,4,8,128]{4,3,2,1,0:T(8,128)S(1)}, f32[48,3,4,8,128]{4,3,2,1,0:T(8,128)}, u32[]{:S(2)}) copy-start(f32[48,3,4,8,128]{4,3,2,1,0:T(8,128)} %param.14) | copy-start | bytes 7077892
  5.0 13.7 %copy-start.1 = (f32[3,32,4,8,128]{4,3,2,1,0:T(8,128)S(1)}, f32[3,32,4,8,128]{4,3,2,1,0:T(8,128)}, u32[]{:S(2)}) copy-start(f32[3,32,4,8,128]{4,3,2,1,0:T(8,128)} %param.9) | copy-start | bytes 4718596
  5.0 13.7 %copy-start.6 = (s32[4,8,128]{2,1,0:T(8,128)S(1)}, s32[4,8,128]{2,1,0:T(8,128)}, u32[]{:S(2)}) copy-start(s32[4,8,128]{2,1,0:T(8,128)} %param.10) | copy-start | bytes 49156
  10.0 1.4 %copy-start.3 = (bf16[96,96,128]{2,1,0:T(8,128)(2,1)}, bf16[96,96,128]{2,1,0:T(8,128)(2,1)S(1)}, u32[]{:S(2)}) copy-start(bf16[96,96,128]{2,1,0:T(8,128)(2,1)S(1)} %get-tuple-element.24.refs_12_) | copy-start | bytes 7077892
  11.4 22.8 %all-to-all-start = ((bf16[32,16,128]{2,1,0:T(8,128)(2,1)}), bf16[32,16,128]{2,1,0:T(8,128)(2,1)S(1)}, u32[]{:S(2)}, u32[]{:S(2)}) async-start(bf16[32,16,128]{2,1,0:T(8,128)(2,1)} %get-tuple-element.19), calls=%async_computation | async-start | bytes 262144 | tf_op jit(solution)/shard_map/all_to_all | solution.py:742
  18.8 16.9 %copy-start.7 = (bf16[64,1024]{1,0:T(8,128)(2,1)S(1)}, bf16[64,1024]{1,0:T(8,128)(2,1)}, u32[]{:S(2)}) copy-start(bf16[64,1024]{1,0:T(8,128)(2,1)} %refs_2_.2) | copy-start | bytes 393220
  19.2 8.5 %collective-permute-start = (bf16[784,128]{1,0:T(8,128)(2,1)S(1)}, bf16[784,128]{1,0:T(8,128)(2,1)S(1)}, u32[]{:S(2)}, u32[]{:S(2)}) collective-permute-start(bf16[784,128]{1,0:T(8,128)(2,1)S(1)} %get-tuple-element.20), channel_id=1, source_target_pairs={{0,8},{8,16},{16,24},{1,9},{9,17},{17,25},{2,10},{10,18},{18,26},{... | collective-permute-start | bytes 602120 | tf_op jit(solution)/shard_map/ppermute | solution.py:692
  22.9 11.1 %collective-permute-start.1 = (bf16[784,128]{1,0:T(8,128)(2,1)S(1)}, bf16[784,128]{1,0:T(8,128)(2,1)S(1)}, u32[]{:S(2)}, u32[]{:S(2)}) collective-permute-start(bf16[784,128]{1,0:T(8,128)(2,1)S(1)} %get-tuple-element.21), channel_id=1, source_target_pairs={{8,0},{16,8},{24,16},{9,1},{17,9},{25,17},{10,2},{18,10},{26,18},{... | collective-permute-start | bytes 602120 | tf_op jit(solution)/shard_map/ppermute | solution.py:692
  34.1 19.6 %copy-start.8 = (f32[2,16]{1,0:T(2,128)S(1)}, f32[2,16]{1,0:T(2,128)}, u32[]{:S(2)}) copy-start(f32[2,16]{1,0:T(2,128)} %refs_2_.3) | copy-start | bytes 388
  34.1 10.9 %collective-permute-start.2 = (bf16[592,128]{1,0:T(8,128)(2,1)S(1)}, bf16[592,128]{1,0:T(8,128)(2,1)S(1)}, u32[]{:S(2)}, u32[]{:S(2)}) collective-permute-start(bf16[592,128]{1,0:T(8,128)(2,1)S(1)} %pack_y.1), channel_id=1, source_target_pairs={{0,4},{4,0},{1,5},{5,1},{2,6},{6,2},{3,7},{7,3},{8,12},{12,8},{9,1... | collective-permute-start | bytes 454664 | tf_op jit(solution)/shard_map/ppermute | solution.py:697
  39.7 14.0 %all-to-all-start.1 = ((f32[16,1,16,128]{3,2,1,0:T(8,128)}), f32[16,1,16,128]{3,2,1,0:T(8,128)S(1)}, u32[]{:S(2)}, u32[]{:S(2)}) async-start(f32[16,1,16,128]{3,2,1,0:T(8,128)} %coarse.1), calls=%async_computation.1 | async-start | bytes 262144 | tf_op jit(solution)/shard_map/all_to_all | solution.py:788
  46.3 6.6 %collective-permute-start.4 = (bf16[112,128]{1,0:T(8,128)(2,1)S(1)}, bf16[112,128]{1,0:T(8,128)(2,1)S(1)}, u32[]{:S(2)}, u32[]{:S(2)}) collective-permute-start(bf16[112,128]{1,0:T(8,128)(2,1)S(1)} %get-tuple-element.22), channel_id=1, source_target_pairs={{1,0},{2,1},{3,2},{5,4},{6,5},{7,6},{9,8},{10,9},{11,10},{13,12},{... | collective-permute-start | bytes 86024 | tf_op jit(solution)/shard_map/ppermute | solution.py:692
  47.6 6.1 %collective-permute-start.3 = (bf16[112,128]{1,0:T(8,128)(2,1)S(1)}, bf16[112,128]{1,0:T(8,128)(2,1)S(1)}, u32[]{:S(2)}, u32[]{:S(2)}) collective-permute-start(bf16[112,128]{1,0:T(8,128)(2,1)S(1)} %get-tuple-element.22), channel_id=1, source_target_pairs={{0,1},{1,2},{2,3},{4,5},{5,6},{6,7},{8,9},{9,10},{10,11},{12,13},{... | collective-permute-start | bytes 86024 | tf_op jit(solution)/shard_map/ppermute | solution.py:692
  53.7 1.7 %copy-start.4 = (bf16[96,96,128]{2,1,0:T(8,128)(2,1)S(1)}, bf16[96,96,128]{2,1,0:T(8,128)(2,1)}, u32[]{:S(2)}) copy-start(bf16[96,96,128]{2,1,0:T(8,128)(2,1)} %copy-done.3) | copy-start | bytes 7077892
  82.9 13.1 %collective-permute-start.5 = (bf16[768,128]{1,0:T(8,128)(2,1)S(1)}, bf16[768,128]{1,0:T(8,128)(2,1)S(1)}, u32[]{:S(2)}, u32[]{:S(2)}) collective-permute-start(bf16[768,128]{1,0:T(8,128)(2,1)S(1)} %get-tuple-element.27), channel_id=1, source_target_pairs={{0,8},{8,16},{16,24},{1,9},{9,17},{17,25},{2,10},{10,18},{18,26},{... | collective-permute-start | bytes 589832 | tf_op jit(solution)/shard_map/ppermute | solution.py:692
  86.7 9.3 %collective-permute-start.6 = (bf16[768,128]{1,0:T(8,128)(2,1)S(1)}, bf16[768,128]{1,0:T(8,128)(2,1)S(1)}, u32[]{:S(2)}, u32[]{:S(2)}) collective-permute-start(bf16[768,128]{1,0:T(8,128)(2,1)S(1)} %get-tuple-element.28), channel_id=1, source_target_pairs={{8,0},{16,8},{24,16},{9,1},{17,9},{25,17},{10,2},{18,10},{26,18},{... | collective-permute-start | bytes 589832 | tf_op jit(solution)/shard_map/ppermute | solution.py:692
  88.0 8.0 %collective-permute-start.7 = (bf16[384,128]{1,0:T(8,128)(2,1)S(1)}, bf16[384,128]{1,0:T(8,128)(2,1)S(1)}, u32[]{:S(2)}, u32[]{:S(2)}) collective-permute-start(bf16[384,128]{1,0:T(8,128)(2,1)S(1)} %get-tuple-element.29), channel_id=1, source_target_pairs={{0,4},{4,0},{1,5},{5,1},{2,6},{6,2},{3,7},{7,3},{8,12},{12,8},{9,1... | collective-permute-start | bytes 294920 | tf_op jit(solution)/shard_map/ppermute | solution.py:697
  88.1 6.6 %collective-permute-start.9 = (f32[96,128]{1,0:T(8,128)S(1)}, f32[96,128]{1,0:T(8,128)S(1)}, u32[]{:S(2)}, u32[]{:S(2)}) collective-permute-start(f32[96,128]{1,0:T(8,128)S(1)} %get-tuple-element.30), channel_id=1, source_target_pairs={{1,0},{2,1},{3,2},{5,4},{6,5},{7,6},{9,8},{10,9},{11,10},{13,12},{... | collective-permute-start | bytes 147464 | tf_op jit(solution)/shard_map/ppermute | solution.py:692
  89.4 6.6 %collective-permute-start.8 = (f32[96,128]{1,0:T(8,128)S(1)}, f32[96,128]{1,0:T(8,128)S(1)}, u32[]{:S(2)}, u32[]{:S(2)}) collective-permute-start(f32[96,128]{1,0:T(8,128)S(1)} %get-tuple-element.30), channel_id=1, source_target_pairs={{0,1},{1,2},{2,3},{4,5},{5,6},{6,7},{8,9},{9,10},{10,11},{12,13},{... | collective-permute-start | bytes 147464 | tf_op jit(solution)/shard_map/ppermute | solution.py:692
  96.0 29.8 %copy-start.5 = (f32[3,32,4,8,128]{4,3,2,1,0:T(8,128)S(1)}, f32[3,32,4,8,128]{4,3,2,1,0:T(8,128)}, u32[]{:S(2)}) copy-start(f32[3,32,4,8,128]{4,3,2,1,0:T(8,128)} %param.8) | copy-start | bytes 4718596

commit v2 on v1

--- a/solution.py
+++ b/solution.py
@@ -53,6 +53,13 @@
         compiler_params=pltpu.CompilerParams(vmem_limit_bytes=limit_mib << 20),
         cost_estimate=pl.CostEstimate(flops=flops, bytes_accessed=moved, transcendentals=0),
     )(*operands)
+
+
+def own_index():
+    index = 0
+    for axis in AXES:
+        index = index * lax.axis_size(axis) + lax.axis_index(axis)
+    return index
 
 
 class Sizes:
@@ -89,7 +96,8 @@
     )
 
 
-def make_pieces(sz, count, rank, basis, res, message, split, wide):
+def make_pieces(sz, count, rank, basis, res, after, message, split, wide):
+    del after
     slots, loads = sz.slots, sz.loads
 
     def step(index, carry):
@@ -278,7 +286,7 @@
         vector[block + 1] = vector[block + 1] + jnp.where(wide_lane < offset, both, 0.0)
         return carry
 
-    lax.fori_loop(0, gathered.shape[0], place, 0)
+    lax.fori_loop(0, gathered.shape[0], place, 0, unroll=8)
     total = jnp.zeros((sz.loads, sz.block_rows), F32)
     for block in range(sz.total_rows // LANES):
         total = total + lax.dot_general(
@@ -292,11 +300,11 @@
         wide[:, pl.ds(0, 64)] = total
         packed = jnp.where(lane < 64, wide[:half, :], roll_lanes(wide[half:, :], 64))
         for device in range(message.shape[0]):
-            message[device, 0] = packed
+            message[device, 0] = packed.astype(BF16)
     else:
         for device in range(message.shape[0]):
             for block in range(sz.block_rows // LANES):
-                message[device, block] = total[:, block * LANES : (block + 1) * LANES]
+                message[device, block] = total[:, block * LANES : (block + 1) * LANES].astype(BF16)
 
 
 def own_coefs(sz, coefs, start):
@@ -304,8 +312,8 @@
         half = sz.loads // 2
         block = start // 64
         offset = start - block * 64
-        first = coefs[block]
-        second = coefs[jnp.minimum(block + 1, coefs.shape[0] - 1)]
+        first = coefs[block].astype(F32)
+        second = coefs[jnp.minimum(block + 1, coefs.shape[0] - 1)].astype(F32)
         lane = lane_ids(half)
         top = jnp.where(lane < 64, first, roll_lanes(second, 64))
         bottom = jnp.where(lane < 64, roll_lanes(first, 64), second)
@@ -313,8 +321,8 @@
     else:
         block = start // LANES
         offset = start - block * LANES
-        first = coefs[block]
-        second = coefs[jnp.minimum(block + 1, coefs.shape[0] - 1)]
+        first = coefs[block].astype(F32)
+        second = coefs[jnp.minimum(block + 1, coefs.shape[0] - 1)].astype(F32)
         both = jnp.where(lane_ids(sz.loads) >= offset, first, second)
     return pltpu.roll(both, lax.rem(LANES - offset, LANES), axis=1)
 
@@ -407,7 +415,7 @@
 
 
 def solve_and_direct(
-    sz, swap, start, count, table, res, below, above, ylow, yhigh, zdown, zup, id_box, coarse,
+    sz, swap, starts, count, table, res, below, above, ylow, yhigh, zdown, zup, id_box, coarse,
     split, *rest,
 ):
     if swap:
@@ -418,7 +426,7 @@
         direction, xlo, xhi, ylo_out, yhi_out, zface, own = rest[:7]
         yfaces = [ylo_out, yhi_out]
         rest = rest[7:]
-    first, second, third, halos, inner, coefs, halo_coefs, mu_box, halo_mu, left = rest
+    first, second, third, halos, inner, coefs, halo_coefs, mu_box, halo_mu, left, zedge = rest
     loads, comps = sz.loads, sz.comps
     groups = loads // 8
     flags = side_flags(swap)
@@ -490,13 +498,14 @@
                 rows = pl.ds(group * 8, 8)
                 target[comp, place, rows, :] = out
                 if level == 0:
-                    inner[1, comp, rows, :] = jnp.where(
-                        here_of(place), pltpu.roll(out, 2 * place, axis=1),
-                        inner[1, comp, rows, :],
+                    pltpu.store(
+                        inner.at[1, comp, rows, :],
+                        pltpu.roll(out, 2 * place, axis=1),
+                        mask=here_of(place),
                     )
             return carry
 
-        lax.fori_loop(0, sz.box, at, 0)
+        lax.fori_loop(0, sz.box, at, 0, unroll=4)
         coef = [halo_coefs[j] for j in range(8)]
         for group in range(groups):
             rows = pl.ds(group * 8, 8)
@@ -515,10 +524,10 @@
     sweep(first, second, 0)
     sweep(second, third, 1)
 
-    mine = own_coefs(sz, coarse, start[0])
+    mine = own_coefs(sz, coarse, starts[own_index()])
     mine = jnp.where(lane_ids(loads) < jnp.minimum(count[0], sz.slots), mine, 0.0)
     left[...] = paired_left(mine, sz.slots, left)
-    zface[...] = jnp.zeros_like(zface)
+    zedge[...] = jnp.zeros_like(zedge)
 
     def final(cell, carry):
         x = cell // sz.cy
@@ -538,14 +547,15 @@
                 )
                 direction[comp, cell, rows, :] = value
                 zrows = pl.ds(comp * loads + group * 8, 8)
-                zface[zrows, :] = jnp.where(
-                    (lane8 >> 1) == place,
+                pltpu.store(
+                    zedge.at[zrows, :],
                     pltpu.roll(value, 2 * place + 1, axis=1),
-                    zface[zrows, :],
+                    mask=(lane8 >> 1) == place,
                 )
         return carry
 
-    lax.fori_loop(0, sz.cells, final, 0)
+    lax.fori_loop(0, sz.cells, final, 0, unroll=4)
+    zface[...] = zedge[...].astype(BF16)
     for comp in range(comps):
         for y in range(sz.cy):
             rows = pl.ds((comp * sz.cy + y) * loads, loads)
@@ -639,32 +649,53 @@
             )
         return total
 
-    total = lax.fori_loop(0, sz.cells, at, jnp.zeros((2 * loads, 4 * loads), F32))
+    total = lax.fori_loop(
+        0, sz.cells, at, jnp.zeros((2 * loads, 4 * loads), F32), unroll=4
+    )
     high, low = total[:loads], total[loads:]
     sums = high + roll_lanes(high, -loads) + low
-    half = loads // 2
-    lane = lane_ids(half)
-    packed = jnp.where((lane & (2 * loads - 1)) < loads, sums[:half], roll_lanes(sums[half:], loads))
+    if message.shape[1] == 1:
+        for device in range(message.shape[0]):
+            message[device] = sums[device : device + 1]
+    else:
+        for device in range(message.shape[0]):
+            message[device] = sums
+
+
+def add_rows(sz, parts, message):
+    total = parts[0]
+    for device in range(1, parts.shape[0]):
+        total = total + parts[device]
     for device in range(message.shape[0]):
-        message[device] = packed
+        message[device] = total
 
 
 def finish(
     sz, sums, iterate, res, dir_split, image_split, new_iterate, new_residual, parts
 ):
     loads = sz.loads
-    half = loads // 2
-    total = sums[0]
-    for device in range(1, sums.shape[0]):
-        total = total + sums[device]
-    system = jnp.concatenate([total, roll_lanes(total, -loads)], axis=0)
+    if sums.shape[1] == 1:
+        system = jnp.concatenate([sums[device] for device in range(sums.shape[0])], axis=0)
+    else:
+        system = sums[0]
+        for device in range(1, sums.shape[0]):
+            system = system + sums[device]
     lane = lane_ids(loads)
     system = jnp.where((lane & (2 * loads - 1)) < loads, system, 0.0)
     row_ids = lax.broadcasted_iota(jnp.int32, (loads, LANES), 0)
-    for i in range(loads):
-        row = system[i : i + 1, :]
-        row = row / row[:, i : i + 1]
-        system = jnp.where(row_ids == i, row, system - system[:, i : i + 1] * row)
+    for base in range(0, loads, 8):
+        columns = [
+            jnp.broadcast_to(system[:, i : i + 1], (loads, LANES)) for i in range(base, base + 8)
+        ]
+        for j in range(8):
+            i = base + j
+            here = row_ids == i
+            scale = 1.0 / columns[j][i : i + 1, :]
+            row = system[i : i + 1, :] * scale
+            system = jnp.where(here, row, system - columns[j] * row)
+            for other in range(j + 1, 8):
+                entry = columns[other][i : i + 1, :] * scale
+                columns[other] = jnp.where(here, entry, columns[other] - columns[j] * entry)
     step = jnp.transpose(system)[2 * loads : 3 * loads, :]
     padded = jnp.concatenate([step, jnp.zeros((loads, LANES - loads), F32)], axis=1) if (
         step.shape[1] < LANES
@@ -682,7 +713,7 @@
             new_residual[rows, :] = res[rows, :] - part[:, LANES:]
         return carry
 
-    lax.fori_loop(0, sz.cells, at, 0, unroll=2)
+    lax.fori_loop(0, sz.cells, at, 0, unroll=4)
 
 
 def exchange(low, high, axis):
@@ -709,6 +740,7 @@
     for axis in AXES:
         devices = devices * lax.axis_size(axis)
     blocks = sz.total_rows // sz.block_rows
+    scatter = devices == sz.loads
     smem, vmem = pltpu.SMEM, pltpu.VMEM
     res = residual.reshape(-1, LANES)
     old = iterate.reshape(-1, LANES)
@@ -736,17 +768,14 @@
         20,
         1 << 27,
         7 << 20,
-        [eigen_counts, coarse_rank, basis, res],
-        spaces=[smem, smem, vmem, vmem],
+        [eigen_counts, coarse_rank, basis, res, xhi],
+        spaces=[smem, smem, vmem, vmem, pl.ANY],
     )
     gathered = lax.all_to_all(message, AXES, 0, 0, tiled=True)
     all_counts = gathered[:, 0, sz.slots].astype(jnp.int32)
     all_ranks = gathered[:, 0, sz.slots + 1].astype(jnp.int32)
     starts = jnp.sum(
         all_counts[None, :] * (all_ranks[None, :] < all_ranks[:, None]).astype(jnp.int32), axis=1
-    )
-    my_start = jnp.sum(
-        all_counts * (all_ranks < coarse_rank[0]).astype(jnp.int32), keepdims=True
     )
 
     side = [pltpu.VMEM((HALO_IDS, LANES), F32)]
@@ -774,7 +803,7 @@
     partial = call(
         "coarse",
         place_pieces,
-        shape((blocks,) + tile, F32),
+        shape((blocks,) + tile, BF16),
         [
             pltpu.VMEM((sz.total_rows // LANES + 1, sz.loads, LANES), F32),
             pltpu.VMEM((sz.loads, LANES), F32),
@@ -796,7 +825,7 @@
         solve_and_direct,
         [shape((sz.comps, sz.cells, sz.loads, LANES), F32), dface, dface]
         + [dyface] * (1 if swap else 2)
-        + [shape((sz.face_z, LANES), F32), shape((8, sz.cells, LANES), F32)],
+        + [shape((sz.face_z, LANES), BF16), shape((8, sz.cells, LANES), F32)],
         [
             field,
             field,
@@ -808,12 +837,13 @@
             pltpu.VMEM((rows, LANES), F32),
             pltpu.VMEM((rows, LANES), F32),
             pltpu.VMEM((2 * sz.loads, LANES), BF16),
+            pltpu.VMEM((sz.face_z, LANES), F32),
         ],
-        40,
+        28,
         1 << 28,
         8 << 20,
         [
-            my_start, eigen_counts, materials, res, below, above, ylow, yhigh, zdown, zup, id_box,
+            starts, eigen_counts, materials, res, below, above, ylow, yhigh, zdown, zup, id_box,
             coarse, split,
         ],
         spaces=[smem, smem, smem] + [vmem] * 10,
@@ -830,27 +860,32 @@
         [
             shape((sz.tiles, 2 * sz.loads, LANES), BF16),
             shape((sz.tiles, 2 * sz.loads, LANES), BF16),
-            shape((devices, sz.loads // 2, LANES), F32),
+            shape((devices, 1 if scatter else sz.loads, LANES), F32),
         ],
         [
             field,
             pltpu.VMEM((sz.comps, sz.loads, LANES), F32),
             pltpu.SemaphoreType.DMA((sz.comps, sz.cx)),
         ],
-        32,
+        20,
         1 << 28,
         8 << 20,
         [res, own, direction, dbelow, dabove, dylow, dyhigh, dzdown, dzup],
         spaces=[vmem, vmem, pl.ANY] + [vmem] * 6,
     )
     sums = lax.all_to_all(energy, AXES, 0, 0, tiled=True)
+    if scatter:
+        whole = call(
+            "add_rows", add_rows, shape(sums.shape, F32), [], 4, 1 << 12, 1 << 15, [sums]
+        )
+        sums = lax.all_to_all(whole, AXES, 0, 0, tiled=True)
     flat = shape(res.shape, F32)
     new_iterate, new_residual = call(
         "finish",
         finish,
         [flat, flat],
         [pltpu.VMEM((2 * sz.loads, LANES), BF16)],
-        32,
+        20,
         1 << 27,
         9 << 20,
         [sums, old, res, dir_split, image_split],

time: 137 us -> 122 us (0.89)
  Pallas kernels: 60.7 us -> 37.9 us
  blocking collectives: 18 us -> 23.6 us
  starting transfers between devices: 34.9 us -> 40.2 us
  waiting for transfers between devices: 12.4 us -> 7.65 us
  local copies, waits for them, and re-layouts: 6.18 us -> 7.88 us
    pallas_call x8 -> x9, Pallas kernels: 60.7 us -> 37.9 us  [vmem_call(): pl.pallas_call(kernel, name=name, out_shape=outs, in_specs=[pl.BlockSpec(...]
    all_to_all x0 -> x1, blocking collectives: none -> 8.87 us  [body(): sums = lax.all_to_all(whole, AXES, 0, 0, tiled=True)]
    ppermute x8, waiting for transfers between devices: 12.4 us -> 7.35 us  [exchange(): return (lax.ppermute(high, axis, up), lax.ppermute(low, axis, down))]
    all_to_all x1, starting transfers between devices: 5.34 us -> 9.83 us  [body(): coarse = lax.all_to_all(partial, ('gx', 'col'), 0, 0, tiled=True)]
    all_to_all x1, blocking collectives: 18 us -> 14.8 us  [body(): sums = lax.all_to_all(energy, AXES, 0, 0, tiled=True)]
    unnamed x18 -> x20, local copies, waits for them, and re-layouts: 6.18 us -> 7.88 us
  transfers between devices with their start and end apart: 12 -> 12, of which waited for: 5 -> 5; matrix products, arithmetic and copies ran while one was open for 2% -> 1% of each run, Pallas kernels for 4% -> 3%
where the time goes in v2:
time: 122 us; the launch traced here: 121 us
  starting transfers between devices  40.2 us (33%)
  Pallas kernels  37.9 us (31%)
  blocking collectives  23.6 us (19%)
  local copies, waits for them, and re-layouts  7.88 us (6%)
  waiting for transfers between devices  7.65 us (6%)
  between operations  2.11 us (2%)
  other arithmetic  1.48 us (1%)
    pallas_call x9, Pallas kernels, vmem_call(): pl.pallas_call(kernel, name=name, out_shape=outs, in_specs=[pl.BlockSpec(...  37.9 us
    ppermute x8, starting transfers between devices, exchange(): return (lax.ppermute(high, axis, up), lax.ppermute(low, axis, down))  23 us
    all_to_all x1, blocking collectives, body(): sums = lax.all_to_all(energy, AXES, 0, 0, tiled=True)  14.8 us
    all_to_all x1, starting transfers between devices, body(): coarse = lax.all_to_all(partial, ('gx', 'col'), 0, 0, tiled=True)  9.83 us
    all_to_all x1, blocking collectives, body(): sums = lax.all_to_all(whole, AXES, 0, 0, tiled=True)  8.87 us
    unnamed x20, local copies, waits for them, and re-layouts  7.88 us
    ppermute x8, waiting for transfers between devices, exchange(): return (lax.ppermute(high, axis, up), lax.ppermute(low, axis, down))  7.35 us
    all_to_all x1, starting transfers between devices, body(): gathered = lax.all_to_all(message, AXES, 0, 0, tiled=True)  7.3 us
  transfers between devices with their start and end apart: 12, of which 5 were waited for; matrix products, arithmetic and copies ran while one was open for 1% of the time, Pallas kernels for 3%

profile of v2, /device:TPU:0, one launch (start us, length us, event | category | flops | bytes accessed | tf_op | source)
XLA Modules:
  0.0 120.9 jit_solution(7090120081739938283)
XLA Ops:
  1.9 0.0 copy-start
  1.9 1.4 %copy-done = f32[3,32,4,8,128]{4,3,2,1,0:T(8,128)S(1)} copy-done((f32[3,32,4,8,128]{4,3,2,1,0:T(8,128)S(1)}, f32[3,32,4,8,128]{4,3,2,1,0:T(8,128)}, u32[]{:S(2)}) %copy-start) | copy-done | bytes 1572888
  3.3 0.0 copy-start.6
  3.3 0.7 copy-done.6
  4.0 0.0 copy-start.1
  4.1 0.4 pack_x.1
  4.5 1.0 copy-done.1
  5.5 0.0 copy-start.4
  5.5 1.7 %copy-done.4 = f32[48,3,4,8,128]{4,3,2,1,0:T(8,128)S(1)} copy-done((f32[48,3,4,8,128]{4,3,2,1,0:T(8,128)S(1)}, f32[48,3,4,8,128]{4,3,2,1,0:T(8,128)}, u32[]{:S(2)}) %copy-start.4) | copy-done | bytes 2359320
  7.1 0.0 copy-start.7
  7.1 5.0 %pieces.1 = (bf16[32,16,128]{2,1,0:T(8,128)(2,1)}, bf16[96,96,128]{2,1,0:T(8,128)(2,1)S(1)}) custom-call(s32[1]{0:T(128)S(6)} %copy.12.refs_0_.refs_1_, s32[1]{0:T(128)S(6)} %copy.13.refs_1_, f32[4608,128]{1,0:T(8,128)S(1)} %bitcast.14, f32[3072,128]{1,0:T(8,128)S(1)} %bitcast.8, bf16[784,128]{1,0:T(8,128)(2,1)S(1)} %get-tuple-element.19.refs_4_), custom_call_target="tpu_custom_call" | custom-call | flops 134217728 | bytes 7340032 | tf_op jit(solution)/shard_map/pieces/pallas_call | solution.py:46
  12.1 0.0 copy-start.2
  12.1 1.4 %copy-done.2 = bf16[96,96,128]{2,1,0:T(8,128)(2,1)} copy-done((bf16[96,96,128]{2,1,0:T(8,128)(2,1)}, bf16[96,96,128]{2,1,0:T(8,128)(2,1)S(1)}, u32[]{:S(2)}) %copy-start.2) | copy-done | bytes 2359320
  13.6 0.0 copy-start.8
  13.6 7.3 %all-to-all-start = ((bf16[32,16,128]{2,1,0:T(8,128)(2,1)}), bf16[32,16,128]{2,1,0:T(8,128)(2,1)S(1)}, u32[]{:S(2)}, u32[]{:S(2)}) async-start(bf16[32,16,128]{2,1,0:T(8,128)(2,1)} %get-tuple-element.20), calls=%async_computation | async-start | bytes 262144 | tf_op jit(solution)/shard_map/all_to_all | solution.py:774
  20.9 1.3 %collective-permute-start.1 = (bf16[784,128]{1,0:T(8,128)(2,1)S(1)}, bf16[784,128]{1,0:T(8,128)(2,1)S(1)}, u32[]{:S(2)}, u32[]{:S(2)}) collective-permute-start(bf16[784,128]{1,0:T(8,128)(2,1)S(1)} %get-tuple-element.21), channel_id=1, source_target_pairs={{8,0},{16,8},{24,16},{9,1},{17,9},{25,17},{10,2},{18,10},{26,18},{... | collective-permute-start | bytes 602120 | tf_op jit(solution)/shard_map/ppermute | solution.py:723
  22.2 4.6 %collective-permute-start = (bf16[784,128]{1,0:T(8,128)(2,1)S(1)}, bf16[784,128]{1,0:T(8,128)(2,1)S(1)}, u32[]{:S(2)}, u32[]{:S(2)}) collective-permute-start(bf16[784,128]{1,0:T(8,128)(2,1)S(1)} %get-tuple-element.19.refs_4_), channel_id=1, source_target_pairs={{0,8},{8,16},{16,24},{1,9},{9,17},{17,25},{2,10},{10,18},{18,26},{... | collective-permute-start | bytes 602120 | tf_op jit(solution)/shard_map/ppermute | solution.py:723
  26.7 4.3 %collective-permute-done.1.refs_3_.refs_5_ = bf16[784,128]{1,0:T(8,128)(2,1)S(1)} collective-permute-done((bf16[784,128]{1,0:T(8,128)(2,1)S(1)}, bf16[784,128]{1,0:T(8,128)(2,1)S(1)}, u32[]{:S(2)}, u32[]{:S(2)}) %collective-permute-start.1) | collective-permute-done | bytes 200736 | tf_op jit(solution)/shard_map/ppermute | solution.py:723
  31.1 0.0 collective-permute-done.refs_2_.refs_4_
  31.1 0.0 copy-done.7
  31.1 0.1 pack_y.1
  31.2 0.0 copy-start.9
  31.2 0.1 collective-permute-start.2
  31.3 0.0 all-to-all-done.refs_1_
  31.3 1.3 %fusion.1 = (s32[32]{0:T(128)S(1)}, s32[32]{0:T(128)S(1)}) fusion(bf16[32,16,128]{2,1,0:T(8,128)(2,1)S(1)} %all-to-all-done.refs_1_), kind=kLoop, calls=%fused_computation.3 | loop fusion | flops 64 | bytes 384 | tf_op jit(solution)/shard_map/convert_element_type | solution.py:776
  32.6 0.2 select_reduce_fusion.refs_0_
  32.8 0.0 copy-done.8
  32.8 2.0 %coarse.1 = bf16[16,1,16,128]{3,2,1,0:T(8,128)(2,1)} custom-call(s32[32]{0:T(128)S(1)} %select_reduce_fusion.refs_0_, bf16[32,16,128]{2,1,0:T(8,128)(2,1)S(1)} %all-to-all-done.refs_1_, bf16[64,1024]{1,0:T(8,128)(2,1)S(1)} %copy-done.8), custom_call_target="tpu_custom_call" | custom-call | flops 8388608 | bytes 1048576 | tf_op jit(solution)/shard_map/coarse/pallas_call | solution.py:46
  34.8 9.8 %all-to-all-start.1 = ((bf16[16,1,16,128]{3,2,1,0:T(8,128)(2,1)}), bf16[16,1,16,128]{3,2,1,0:T(8,128)(2,1)S(1)}, u32[]{:S(2)}, u32[]{:S(2)}) async-start(bf16[16,1,16,128]{3,2,1,0:T(8,128)(2,1)} %coarse.1), calls=%async_computation.1 | async-start | bytes 131072 | tf_op jit(solution)/shard_map/all_to_all | solution.py:817
  44.6 0.0 collective-permute-done.2.refs_4_.refs_5_.refs_6_.refs_7_
  44.7 1.3 %pack_z.1 = (bf16[112,128]{1,0:T(8,128)(2,1)S(1)}, f32[128,128]{1,0:T(8,128)S(1)}) custom-call(f32[3072,128]{1,0:T(8,128)S(1)} %bitcast.10, s32[32,128]{1,0:T(8,128)S(1)} %bitcast.19, bf16[784,128]{1,0:T(8,128)(2,1)S(1)} %collective-permute-done.refs_2_.refs_4_, bf16[784,128]{1,0:T(8,128)(2,1)S(1)} %collective-permute-done.1.refs_3_.refs_5_, ...), custom_call_target="tpu_custom_call" | custom-call | flops 4194304 | bytes 3145728 | tf_op jit(solution)/shard_map/pack_z/pallas_call | solution.py:46
  45.9 1.3 %collective-permute-start.4 = (bf16[112,128]{1,0:T(8,128)(2,1)S(1)}, bf16[112,128]{1,0:T(8,128)(2,1)S(1)}, u32[]{:S(2)}, u32[]{:S(2)}) collective-permute-start(bf16[112,128]{1,0:T(8,128)(2,1)S(1)} %get-tuple-element.22), channel_id=1, source_target_pairs={{1,0},{2,1},{3,2},{5,4},{6,5},{7,6},{9,8},{10,9},{11,10},{13,12},{... | collective-permute-start | bytes 86024 | tf_op jit(solution)/shard_map/ppermute | solution.py:723
  47.2 4.5 %collective-permute-start.3 = (bf16[112,128]{1,0:T(8,128)(2,1)S(1)}, bf16[112,128]{1,0:T(8,128)(2,1)S(1)}, u32[]{:S(2)}, u32[]{:S(2)}) collective-permute-start(bf16[112,128]{1,0:T(8,128)(2,1)S(1)} %get-tuple-element.22), channel_id=1, source_target_pairs={{0,1},{1,2},{2,3},{4,5},{5,6},{6,7},{8,9},{9,10},{10,11},{12,13},{... | collective-permute-start | bytes 86024 | tf_op jit(solution)/shard_map/ppermute | solution.py:723
  51.8 0.3 all-to-all-done.1
  52.1 0.0 collective-permute-done.4.refs_9_
  52.1 1.2 %collective-permute-done.3.refs_8_ = bf16[112,128]{1,0:T(8,128)(2,1)S(1)} collective-permute-done((bf16[112,128]{1,0:T(8,128)(2,1)S(1)}, bf16[112,128]{1,0:T(8,128)(2,1)S(1)}, u32[]{:S(2)}, u32[]{:S(2)}) %collective-permute-start.3) | collective-permute-done | bytes 28704 | tf_op jit(solution)/shard_map/ppermute | solution.py:723
  53.3 0.0 copy-done.9
  53.3 0.0 copy-start.3
  53.3 1.7 %copy-done.3 = bf16[96,96,128]{2,1,0:T(8,128)(2,1)S(1)} copy-done((bf16[96,96,128]{2,1,0:T(8,128)(2,1)S(1)}, bf16[96,96,128]{2,1,0:T(8,128)(2,1)}, u32[]{:S(2)}) %copy-start.3) | copy-done | bytes 2359320
  55.0 14.9 %solve.1 = (f32[3,32,32,128]{3,2,1,0:T(8,128)S(1)}, bf16[768,128]{1,0:T(8,128)(2,1)S(1)}, bf16[768,128]{1,0:T(8,128)(2,1)S(1)}, bf16[384,128]{1,0:T(8,128)(2,1)S...) custom-call(s32[32]{0:T(128)S(1)} %select_reduce_fusion.refs_0_, s32[1]{0:T(128)S(6)} %copy.12.refs_0_.refs_1_, ...), custom_call_target="tpu_custom_call" | custom-call | flops 268435456 | bytes 8388608 | tf_op jit(solution)/shard_map/solve/pallas_call | solution.py:46
  69.9 3.8 %collective-permute-start.5 = (bf16[768,128]{1,0:T(8,128)(2,1)S(1)}, bf16[768,128]{1,0:T(8,128)(2,1)S(1)}, u32[]{:S(2)}, u32[]{:S(2)}) collective-permute-start(bf16[768,128]{1,0:T(8,128)(2,1)S(1)} %get-tuple-element.27), channel_id=1, source_target_pairs={{0,8},{8,16},{16,24},{1,9},{9,17},{17,25},{2,10},{10,18},{18,26},{... | collective-permute-start | bytes 589832 | tf_op jit(solution)/shard_map/ppermute | solution.py:723
  73.8 1.3 %collective-permute-start.6 = (bf16[768,128]{1,0:T(8,128)(2,1)S(1)}, bf16[768,128]{1,0:T(8,128)(2,1)S(1)}, u32[]{:S(2)}, u32[]{:S(2)}) collective-permute-start(bf16[768,128]{1,0:T(8,128)(2,1)S(1)} %get-tuple-element.28), channel_id=1, source_target_pairs={{8,0},{16,8},{24,16},{9,1},{17,9},{25,17},{10,2},{18,10},{26,18},{... | collective-permute-start | bytes 589832 | tf_op jit(solution)/shard_map/ppermute | solution.py:723
  75.1 0.1 collective-permute-start.7
  75.2 1.3 %collective-permute-start.9 = (bf16[96,128]{1,0:T(8,128)(2,1)S(1)}, bf16[96,128]{1,0:T(8,128)(2,1)S(1)}, u32[]{:S(2)}, u32[]{:S(2)}) collective-permute-start(bf16[96,128]{1,0:T(8,128)(2,1)S(1)} %get-tuple-element.30), channel_id=1, source_target_pairs={{1,0},{2,1},{3,2},{5,4},{6,5},{7,6},{9,8},{10,9},{11,10},{13,12},{... | collective-permute-start | bytes 73736 | tf_op jit(solution)/shard_map/ppermute | solution.py:723
  76.5 4.8 %collective-permute-start.8 = (bf16[96,128]{1,0:T(8,128)(2,1)S(1)}, bf16[96,128]{1,0:T(8,128)(2,1)S(1)}, u32[]{:S(2)}, u32[]{:S(2)}) collective-permute-start(bf16[96,128]{1,0:T(8,128)(2,1)S(1)} %get-tuple-element.30), channel_id=1, source_target_pairs={{0,1},{1,2},{2,3},{4,5},{5,6},{6,7},{8,9},{9,10},{10,11},{12,13},{... | collective-permute-start | bytes 73736 | tf_op jit(solution)/shard_map/ppermute | solution.py:723
  81.3 0.0 collective-permute-done.9.refs_8_
  81.3 1.5 %collective-permute-done.8.refs_7_ = bf16[96,128]{1,0:T(8,128)(2,1)S(1)} collective-permute-done((bf16[96,128]{1,0:T(8,128)(2,1)S(1)}, bf16[96,128]{1,0:T(8,128)(2,1)S(1)}, u32[]{:S(2)}, u32[]{:S(2)}) %collective-permute-start.8) | collective-permute-done | bytes 24608 | tf_op jit(solution)/shard_map/ppermute | solution.py:723
  82.8 0.0 collective-permute-done.7.refs_5_.refs_6_
  82.8 0.0 collective-permute-done.5.refs_3_
  82.8 0.3 collective-permute-done.6.refs_4_
  83.1 0.0 copy-start.5
  83.1 6.3 %image.1 = (bf16[96,64,128]{2,1,0:T(8,128)(2,1)S(1)}, bf16[96,64,128]{2,1,0:T(8,128)(2,1)S(1)}, f32[32,1,128]{2,1,0:T(1,128)S(1)}) custom-call(f32[3072,128]{1,0:T(8,128)S(1)} %bitcast.12, f32[8,32,128]{2,1,0:T(8,128)S(1)} %get-tuple-element.25.refs_1_, f32[3,32,32,128]{3,2,1,0:T(8,128)S(1)} %get-tuple-element.26.refs_2_, ...), custom_call_target="tpu_custom_call" | custom-call | flops 268435456 | bytes 8388608 | tf_op jit(solution)/shard_map/image/pallas_call | solution.py:46
  89.4 14.8 %all_to_all.20.refs_0_ = f32[32,1,128]{2,1,0:T(1,128)S(1)} all-to-all(f32[32,1,128]{2,1,0:T(1,128)S(1)} %get-tuple-element.31), channel_id=1, replica_groups=mesh['gx'=4,'gy'=2,'col'=4] {'gx','gy','col'}, dimensions={0} | all-to-all | bytes 32768 | tf_op jit(solution)/shard_map/all_to_all | solution.py:876
  104.2 8.9 %all_to_all.21.refs_0_ = f32[32,1,128]{2,1,0:T(1,128)S(1)} all-to-all(f32[32,1,128]{2,1,0:T(1,128)S(1)} %add_rows.1), channel_id=1, replica_groups=mesh['gx'=4,'gy'=2,'col'=4] {'gx','gy','col'}, dimensions={0} | all-to-all | bytes 32768 | tf_op jit(solution)/shard_map/all_to_all | solution.py:881
  113.1 0.0 copy-done.5
  113.1 7.8 %finish.1 = (f32[3072,128]{1,0:T(8,128)}, f32[3072,128]{1,0:T(8,128)}) custom-call(f32[32,1,128]{2,1,0:T(1,128)S(1)} %all_to_all.21.refs_0_, f32[3072,128]{1,0:T(8,128)S(1)} %bitcast.15, f32[3072,128]{1,0:T(8,128)S(1)} %bitcast.13, bf16[96,64,128]{2,1,0:T(8,128)(2,1)S(1)} %get-tuple-element.32.refs_3_, bf16[96,64,128]{2,1,0:T(8,128)(2,1)S(1)} %get-tuple-element.33.refs_4_), custom_call_target="tpu_custom_call" | custom-call | flops 134217728 | bytes 9437184 | tf_op jit(solution)/shard_map/finish/pallas_call | solution.py:46
  (1 shorter events, 0.0 us)
Async XLA Ops:
  1.9 1.4 %copy-start = (f32[3,32,4,8,128]{4,3,2,1,0:T(8,128)S(1)}, f32[3,32,4,8,128]{4,3,2,1,0:T(8,128)}, u32[]{:S(2)}) copy-start(f32[3,32,4,8,128]{4,3,2,1,0:T(8,128)} %param.9) | copy-start | bytes 4718596
  3.3 0.7 copy-start.6
  4.0 1.4 %copy-start.1 = (f32[3,32,4,8,128]{4,3,2,1,0:T(8,128)S(1)}, f32[3,32,4,8,128]{4,3,2,1,0:T(8,128)}, u32[]{:S(2)}) copy-start(f32[3,32,4,8,128]{4,3,2,1,0:T(8,128)} %param.9) | copy-start | bytes 4718596
  5.5 1.7 %copy-start.4 = (f32[48,3,4,8,128]{4,3,2,1,0:T(8,128)S(1)}, f32[48,3,4,8,128]{4,3,2,1,0:T(8,128)}, u32[]{:S(2)}) copy-start(f32[48,3,4,8,128]{4,3,2,1,0:T(8,128)} %param.14) | copy-start | bytes 7077892
  7.1 24.0 %copy-start.7 = (s32[4,8,128]{2,1,0:T(8,128)S(1)}, s32[4,8,128]{2,1,0:T(8,128)}, u32[]{:S(2)}) copy-start(s32[4,8,128]{2,1,0:T(8,128)} %param.10) | copy-start | bytes 49156
  12.1 1.4 %copy-start.2 = (bf16[96,96,128]{2,1,0:T(8,128)(2,1)}, bf16[96,96,128]{2,1,0:T(8,128)(2,1)S(1)}, u32[]{:S(2)}) copy-start(bf16[96,96,128]{2,1,0:T(8,128)(2,1)S(1)} %get-tuple-element.24.refs_12_) | copy-start | bytes 7077892
  13.6 19.2 %copy-start.8 = (bf16[64,1024]{1,0:T(8,128)(2,1)S(1)}, bf16[64,1024]{1,0:T(8,128)(2,1)}, u32[]{:S(2)}) copy-start(bf16[64,1024]{1,0:T(8,128)(2,1)} %refs_2_.2) | copy-start | bytes 393220
  13.6 17.7 %all-to-all-start = ((bf16[32,16,128]{2,1,0:T(8,128)(2,1)}), bf16[32,16,128]{2,1,0:T(8,128)(2,1)S(1)}, u32[]{:S(2)}, u32[]{:S(2)}) async-start(bf16[32,16,128]{2,1,0:T(8,128)(2,1)} %get-tuple-element.20), calls=%async_computation | async-start | bytes 262144 | tf_op jit(solution)/shard_map/all_to_all | solution.py:774
  20.9 10.2 %collective-permute-start.1 = (bf16[784,128]{1,0:T(8,128)(2,1)S(1)}, bf16[784,128]{1,0:T(8,128)(2,1)S(1)}, u32[]{:S(2)}, u32[]{:S(2)}) collective-permute-start(bf16[784,128]{1,0:T(8,128)(2,1)S(1)} %get-tuple-element.21), channel_id=1, source_target_pairs={{8,0},{16,8},{24,16},{9,1},{17,9},{25,17},{10,2},{18,10},{26,18},{... | collective-permute-start | bytes 602120 | tf_op jit(solution)/shard_map/ppermute | solution.py:723
  22.2 8.9 %collective-permute-start = (bf16[784,128]{1,0:T(8,128)(2,1)S(1)}, bf16[784,128]{1,0:T(8,128)(2,1)S(1)}, u32[]{:S(2)}, u32[]{:S(2)}) collective-permute-start(bf16[784,128]{1,0:T(8,128)(2,1)S(1)} %get-tuple-element.19.refs_4_), channel_id=1, source_target_pairs={{0,8},{8,16},{16,24},{1,9},{9,17},{17,25},{2,10},{10,18},{18,26},{... | collective-permute-start | bytes 602120 | tf_op jit(solution)/shard_map/ppermute | solution.py:723
  31.2 22.1 %copy-start.9 = (f32[2,16]{1,0:T(2,128)S(1)}, f32[2,16]{1,0:T(2,128)}, u32[]{:S(2)}) copy-start(f32[2,16]{1,0:T(2,128)} %refs_2_.3) | copy-start | bytes 388
  31.2 13.4 %collective-permute-start.2 = (bf16[592,128]{1,0:T(8,128)(2,1)S(1)}, bf16[592,128]{1,0:T(8,128)(2,1)S(1)}, u32[]{:S(2)}, u32[]{:S(2)}) collective-permute-start(bf16[592,128]{1,0:T(8,128)(2,1)S(1)} %pack_y.1), channel_id=1, source_target_pairs={{0,4},{4,0},{1,5},{5,1},{2,6},{6,2},{3,7},{7,3},{8,12},{12,8},{9,1... | collective-permute-start | bytes 454664 | tf_op jit(solution)/shard_map/ppermute | solution.py:728
  34.8 17.3 %all-to-all-start.1 = ((bf16[16,1,16,128]{3,2,1,0:T(8,128)(2,1)}), bf16[16,1,16,128]{3,2,1,0:T(8,128)(2,1)S(1)}, u32[]{:S(2)}, u32[]{:S(2)}) async-start(bf16[16,1,16,128]{3,2,1,0:T(8,128)(2,1)} %coarse.1), calls=%async_computation.1 | async-start | bytes 131072 | tf_op jit(solution)/shard_map/all_to_all | solution.py:817
  45.9 6.2 %collective-permute-start.4 = (bf16[112,128]{1,0:T(8,128)(2,1)S(1)}, bf16[112,128]{1,0:T(8,128)(2,1)S(1)}, u32[]{:S(2)}, u32[]{:S(2)}) collective-permute-start(bf16[112,128]{1,0:T(8,128)(2,1)S(1)} %get-tuple-element.22), channel_id=1, source_target_pairs={{1,0},{2,1},{3,2},{5,4},{6,5},{7,6},{9,8},{10,9},{11,10},{13,12},{... | collective-permute-start | bytes 86024 | tf_op jit(solution)/shard_map/ppermute | solution.py:723
  47.2 6.1 %collective-permute-start.3 = (bf16[112,128]{1,0:T(8,128)(2,1)S(1)}, bf16[112,128]{1,0:T(8,128)(2,1)S(1)}, u32[]{:S(2)}, u32[]{:S(2)}) collective-permute-start(bf16[112,128]{1,0:T(8,128)(2,1)S(1)} %get-tuple-element.22), channel_id=1, source_target_pairs={{0,1},{1,2},{2,3},{4,5},{5,6},{6,7},{8,9},{9,10},{10,11},{12,13},{... | collective-permute-start | bytes 86024 | tf_op jit(solution)/shard_map/ppermute | solution.py:723
  53.3 1.7 %copy-start.3 = (bf16[96,96,128]{2,1,0:T(8,128)(2,1)S(1)}, bf16[96,96,128]{2,1,0:T(8,128)(2,1)}, u32[]{:S(2)}) copy-start(bf16[96,96,128]{2,1,0:T(8,128)(2,1)} %copy-done.2) | copy-start | bytes 7077892
  69.9 12.9 %collective-permute-start.5 = (bf16[768,128]{1,0:T(8,128)(2,1)S(1)}, bf16[768,128]{1,0:T(8,128)(2,1)S(1)}, u32[]{:S(2)}, u32[]{:S(2)}) collective-permute-start(bf16[768,128]{1,0:T(8,128)(2,1)S(1)} %get-tuple-element.27), channel_id=1, source_target_pairs={{0,8},{8,16},{16,24},{1,9},{9,17},{17,25},{2,10},{10,18},{18,26},{... | collective-permute-start | bytes 589832 | tf_op jit(solution)/shard_map/ppermute | solution.py:723
  73.8 9.3 %collective-permute-start.6 = (bf16[768,128]{1,0:T(8,128)(2,1)S(1)}, bf16[768,128]{1,0:T(8,128)(2,1)S(1)}, u32[]{:S(2)}, u32[]{:S(2)}) collective-permute-start(bf16[768,128]{1,0:T(8,128)(2,1)S(1)} %get-tuple-element.28), channel_id=1, source_target_pairs={{8,0},{16,8},{24,16},{9,1},{17,9},{25,17},{10,2},{18,10},{26,18},{... | collective-permute-start | bytes 589832 | tf_op jit(solution)/shard_map/ppermute | solution.py:723
  75.1 7.7 %collective-permute-start.7 = (bf16[384,128]{1,0:T(8,128)(2,1)S(1)}, bf16[384,128]{1,0:T(8,128)(2,1)S(1)}, u32[]{:S(2)}, u32[]{:S(2)}) collective-permute-start(bf16[384,128]{1,0:T(8,128)(2,1)S(1)} %get-tuple-element.29), channel_id=1, source_target_pairs={{0,4},{4,0},{1,5},{5,1},{2,6},{6,2},{3,7},{7,3},{8,12},{12,8},{9,1... | collective-permute-start | bytes 294920 | tf_op jit(solution)/shard_map/ppermute | solution.py:728
  75.2 6.2 %collective-permute-start.9 = (bf16[96,128]{1,0:T(8,128)(2,1)S(1)}, bf16[96,128]{1,0:T(8,128)(2,1)S(1)}, u32[]{:S(2)}, u32[]{:S(2)}) collective-permute-start(bf16[96,128]{1,0:T(8,128)(2,1)S(1)} %get-tuple-element.30), channel_id=1, source_target_pairs={{1,0},{2,1},{3,2},{5,4},{6,5},{7,6},{9,8},{10,9},{11,10},{13,12},{... | collective-permute-start | bytes 73736 | tf_op jit(solution)/shard_map/ppermute | solution.py:723
  76.5 6.4 %collective-permute-start.8 = (bf16[96,128]{1,0:T(8,128)(2,1)S(1)}, bf16[96,128]{1,0:T(8,128)(2,1)S(1)}, u32[]{:S(2)}, u32[]{:S(2)}) collective-permute-start(bf16[96,128]{1,0:T(8,128)(2,1)S(1)} %get-tuple-element.30), channel_id=1, source_target_pairs={{0,1},{1,2},{2,3},{4,5},{5,6},{6,7},{8,9},{9,10},{10,11},{12,13},{... | collective-permute-start | bytes 73736 | tf_op jit(solution)/shard_map/ppermute | solution.py:723
  83.1 30.0 %copy-start.5 = (f32[3,32,4,8,128]{4,3,2,1,0:T(8,128)S(1)}, f32[3,32,4,8,128]{4,3,2,1,0:T(8,128)}, u32[]{:S(2)}) copy-start(f32[3,32,4,8,128]{4,3,2,1,0:T(8,128)} %param.8) | copy-start | bytes 4718596

commit v3 on v2

--- a/solution.py
+++ b/solution.py
@@ -78,27 +78,102 @@
         self.pitch = 16
 
 
+class Halo:
+    def __init__(self, axis, refs):
+        self.refs = refs
+        self.even = lax.rem(lax.axis_index(axis), 2) == 0
+
+    def side(self, rows, first):
+        value = self.refs[0][rows, :].astype(F32)
+        other = self.refs[1][rows, :].astype(F32) if len(self.refs) > 1 else jnp.zeros_like(value)
+        return jnp.where(self.even, value, other) if first else jnp.where(self.even, other, value)
+
+    def below(self, rows):
+        return self.side(rows, False)
+
+    def above(self, rows):
+        return self.side(rows, True)
+
+    def send(self, rows, low, high):
+        self.refs[0][rows, :] = jnp.where(self.even, high, low).astype(BF16)
+        if len(self.refs) > 1:
+            self.refs[1][rows, :] = jnp.where(self.even, low, high).astype(BF16)
+
+
+def swaps(axis):
+    return 1 if lax.axis_size(axis) == 2 else 2
+
+
+def exchange(faces, axis):
+    devices = lax.axis_size(axis)
+    result = []
+    for parity in range(swaps(axis)):
+        pairs = []
+        for low in range(parity, devices - 1, 2):
+            pairs += [(low, low + 1), (low + 1, low)]
+        result.append(lax.ppermute(faces[parity], axis, pairs))
+    return result
+
+
+def take_halos(refs, *axes):
+    refs = list(refs)
+    halos = []
+    for axis in axes:
+        count = swaps(axis)
+        halos.append(Halo(axis, refs[:count]))
+        refs = refs[count:]
+    return halos + [refs]
+
+
 def own_rows(sz, ref, comp, cell):
     start = comp * sz.loads * sz.cells + cell
     return ref[pl.ds(start, sz.loads, stride=sz.cells), :]
 
 
-def pack_x(sz, res, ids, lo, hi):
+def pack_x(sz, res, ids, *refs):
+    xsend, (low, high, id_rows, sem) = take_halos(refs, "gx")
+    copies = [
+        pltpu.make_async_copy(res.at[:, pl.ds(0, sz.cy)], low, sem.at[0]),
+        pltpu.make_async_copy(res.at[:, pl.ds(sz.cells - sz.cy, sz.cy)], high, sem.at[1]),
+        pltpu.make_async_copy(ids, id_rows, sem.at[2]),
+    ]
+    for copy in copies:
+        copy.start()
+    for copy in copies:
+        copy.wait()
+    low, high = (ref.reshape(sz.comps * sz.loads * sz.cy, LANES) for ref in (low, high))
     for comp in range(sz.comps):
         for y in range(sz.cy):
             rows = pl.ds((comp * sz.cy + y) * sz.loads, sz.loads)
-            lo[rows, :] = own_rows(sz, res, comp, y).astype(BF16)
-            hi[rows, :] = own_rows(sz, res, comp, (sz.cx - 1) * sz.cy + y).astype(BF16)
+            taken = pl.ds(comp * sz.loads * sz.cy + y, sz.loads, stride=sz.cy)
+            xsend.send(rows, low[taken, :], high[taken, :])
     two = 2 * sz.cy
-    lo[pl.ds(sz.face_x, two), :] = (ids[pl.ds(0, two), :] + 1).astype(F32).astype(BF16)
-    hi[pl.ds(sz.face_x, two), :] = (
-        (ids[pl.ds(sz.cells - two, two), :] + 1).astype(F32).astype(BF16)
-    )
-
-
-def make_pieces(sz, count, rank, basis, res, after, message, split, wide):
+    first = (id_rows[pl.ds(0, two), :] + 1).astype(F32)
+    last = (id_rows[pl.ds(sz.cells - two, two), :] + 1).astype(F32)
+    xsend.send(pl.ds(sz.face_x, two), first, last)
+
+
+def make_pieces(
+    sz, count, rank, basis_in, res_in, after, message, split, wide, basis_rows, res_rows, sem
+):
     del after
     slots, loads = sz.slots, sz.loads
+    copies = []
+    for comp in range(sz.comps):
+        part = pl.ds(comp * sz.cells, sz.cells)
+        copies.append(
+            (
+                pltpu.make_async_copy(
+                    basis_in.at[:, part], basis_rows.at[:, part], sem.at[0, comp]
+                ),
+                pltpu.make_async_copy(res_in.at[comp], res_rows.at[comp], sem.at[1, comp]),
+            )
+        )
+    for pair in copies:
+        for copy in pair:
+            copy.start()
+    basis = basis_rows.reshape(slots * sz.tiles, LANES)
+    res = res_rows.reshape(sz.tiles * loads, LANES)
 
     def step(index, carry):
         both, low = carry
@@ -128,13 +203,14 @@
         )
         return both, low
 
-    both, low = lax.fori_loop(
-        0,
-        sz.tiles // 2,
-        step,
-        (jnp.zeros((2 * loads, slots), F32), jnp.zeros((loads, slots), F32)),
-        unroll=4,
-    )
+    carry = (jnp.zeros((2 * loads, slots), F32), jnp.zeros((loads, slots), F32))
+    for comp in range(sz.comps):
+        for copy in copies[comp]:
+            copy.wait()
+        carry = lax.fori_loop(
+            comp * sz.cells // 2, (comp + 1) * sz.cells // 2, step, carry, unroll=4
+        )
+    both, low = carry
     pieces = both[:loads] + both[loads:] + low
     slot = lax.broadcasted_iota(jnp.int32, pieces.shape, 1)
     wide[...] = jnp.zeros_like(wide)
@@ -143,83 +219,61 @@
     lane = lane_ids(half)
     packed = jnp.where(lane < 64, wide[:half, :], roll_lanes(wide[half:, :], 64))
     packed = jnp.where(lane == slots, count[0].astype(F32), packed)
-    packed = jnp.where(lane == slots + 1, rank[0].astype(F32), packed).astype(BF16)
+    packed = jnp.where(lane == slots + 1, rank[0].astype(F32), packed)
+    message[...] = packed.astype(BF16)
+
+
+def pack_y(sz, res, ids, packed, *refs):
+    xhalo, refs = take_halos(refs, "gx")
+    message = refs[0]
+    ysend, (side_low, side_high) = take_halos(refs[1:], "gy")
     for device in range(message.shape[0]):
-        message[device] = packed
-
-
-def pack_y(sz, swap, res, ids, below, above, *refs):
-    outs, side = refs[:-1], refs[-1]
+        message[device] = packed[...]
     last = sz.cy - 1
-    if swap:
-        faces = [jnp.where(lax.axis_index("gy") == 0, last, 0)]
-    else:
-        faces = [0, last]
-    ids_below = below[pl.ds(sz.face_x, 2 * sz.cy), :].astype(F32)
-    ids_above = above[pl.ds(sz.face_x, 2 * sz.cy), :].astype(F32)
-    for out, y in zip(outs, faces):
-        dynamic = not isinstance(y, int)
-        for comp in range(sz.comps):
-            for x in range(sz.bx):
-                rows = pl.ds((comp * sz.bx + x) * sz.loads, sz.loads)
-                if 0 < x < sz.bx - 1:
-                    value = own_rows(sz, res, comp, (x - 1) * sz.cy + y).astype(BF16)
-                else:
-                    source = below if x == 0 else above
-                    start = (comp * sz.cy + y) * sz.loads
-                    if dynamic:
-                        start = pl.multiple_of(start, sz.loads)
-                    value = source[pl.ds(start, sz.loads), :]
-                out[rows, :] = value
-        for x in range(sz.cx + 4):
-            for j in range(2):
-                if 2 <= x < sz.cx + 2:
-                    first = (ids[pl.ds((x - 2) * sz.cy + j, 1), :] + 1).astype(F32)
-                    end = (ids[pl.ds((x - 2) * sz.cy + last - 1 + j, 1), :] + 1).astype(F32)
-                else:
-                    source, base = (ids_below, x * sz.cy) if x < 2 else (
-                        ids_above, (x - sz.cx - 2) * sz.cy)
-                    first = source[base + j : base + j + 1]
-                    end = source[base + last - 1 + j : base + last + j]
-                if dynamic:
-                    row = jnp.where(y == 0, first, end)
-                else:
-                    row = first if y == 0 else end
-                side[pl.ds(x * 2 + j, 1), :] = row
-        out[pl.ds(sz.face_y, HALO_IDS), :] = side[...].astype(BF16)
-
-
-def side_flags(swap):
-    if not swap:
-        return None, None
-    upper = lax.axis_index("gy") == 1
-    return jnp.where(upper, 1.0, 0.0).astype(F32), jnp.where(upper, 0.0, 1.0).astype(F32)
-
-
-def flagged(value, flag):
-    value = value.astype(F32)
-    return value if flag is None else value * flag
-
-
-def box_tile(sz, res, below, above, ylow, yhigh, flags, comp, x, y):
+    for comp in range(sz.comps):
+        for x in range(sz.bx):
+            rows = pl.ds((comp * sz.bx + x) * sz.loads, sz.loads)
+            if 0 < x < sz.bx - 1:
+                low, high = (own_rows(sz, res, comp, (x - 1) * sz.cy + y) for y in (0, last))
+            else:
+                side = xhalo.below if x == 0 else xhalo.above
+                low, high = (
+                    side(pl.ds((comp * sz.cy + y) * sz.loads, sz.loads)) for y in (0, last)
+                )
+            ysend.send(rows, low, high)
+    ids_below = xhalo.below(pl.ds(sz.face_x, 2 * sz.cy))
+    ids_above = xhalo.above(pl.ds(sz.face_x, 2 * sz.cy))
+    for x in range(sz.cx + 4):
+        if x < 2:
+            rows = ids_below[x * sz.cy : (x + 1) * sz.cy]
+        elif x >= sz.cx + 2:
+            rows = ids_above[(x - sz.cx - 2) * sz.cy : (x - sz.cx - 1) * sz.cy]
+        else:
+            rows = (ids[pl.ds((x - 2) * sz.cy, sz.cy), :] + 1).astype(F32)
+        side_low[pl.ds(2 * x, 2), :] = rows[:2]
+        side_high[pl.ds(2 * x, 2), :] = rows[sz.cy - 2 :]
+    ysend.send(pl.ds(sz.face_y, HALO_IDS), side_low[...], side_high[...])
+
+
+def box_tile(sz, res, xhalo, yhalo, comp, x, y):
     if y == 0 or y == sz.by - 1:
-        source, flag = (ylow, flags[0]) if y == 0 else (yhigh, flags[1])
-        return flagged(source[pl.ds((comp * sz.bx + x) * sz.loads, sz.loads), :], flag)
+        side = yhalo.below if y == 0 else yhalo.above
+        return side(pl.ds((comp * sz.bx + x) * sz.loads, sz.loads))
     if x == 0 or x == sz.bx - 1:
-        source = below if x == 0 else above
-        return source[pl.ds((comp * sz.cy + y - 1) * sz.loads, sz.loads), :].astype(F32)
+        side = xhalo.below if x == 0 else xhalo.above
+        return side(pl.ds((comp * sz.cy + y - 1) * sz.loads, sz.loads))
     return own_rows(sz, res, comp, (x - 1) * sz.cy + y - 1)
 
 
-def pack_z(sz, swap, res, ids, below, above, ylow, yhigh, out, id_box, star, outer):
-    flags = side_flags(swap)
+def pack_z(sz, res, ids, *refs):
+    xhalo, yhalo, (out, id_box, star, outer) = take_halos(refs, "gx", "gy")
     pitch = sz.pitch
     id_box[...] = jnp.zeros_like(id_box)
     two = 2 * sz.cy
-    ids_below = below[pl.ds(sz.face_x, two), :].astype(F32)
-    ids_above = above[pl.ds(sz.face_x, two), :].astype(F32)
-    ids_low = flagged(ylow[pl.ds(sz.face_y, HALO_IDS), :], flags[0])
-    ids_high = flagged(yhigh[pl.ds(sz.face_y, HALO_IDS), :], flags[1])
+    ids_below = xhalo.below(pl.ds(sz.face_x, two))
+    ids_above = xhalo.above(pl.ds(sz.face_x, two))
+    ids_low = yhalo.below(pl.ds(sz.face_y, HALO_IDS))
+    ids_high = yhalo.above(pl.ds(sz.face_y, HALO_IDS))
     for x in range(sz.cx + 4):
         if x < 2:
             rows = ids_below[x * sz.cy : (x + 1) * sz.cy]
@@ -255,7 +309,7 @@
         for x in range(sz.bx):
             for y in range(sz.by):
                 place = x * sz.by + y
-                tile = box_tile(sz, res, below, above, ylow, yhigh, flags, comp, x, y)
+                tile = box_tile(sz, res, xhalo, yhalo, comp, x, y)
                 total = jnp.where(
                     (lane_k >> 1) == place, roll_lanes(tile, 2 * place + 1), total
                 )
@@ -300,11 +354,11 @@
         wide[:, pl.ds(0, 64)] = total
         packed = jnp.where(lane < 64, wide[:half, :], roll_lanes(wide[half:, :], 64))
         for device in range(message.shape[0]):
-            message[device, 0] = packed.astype(BF16)
+            message[device, 0] = packed
     else:
         for device in range(message.shape[0]):
             for block in range(sz.block_rows // LANES):
-                message[device, block] = total[:, block * LANES : (block + 1) * LANES].astype(BF16)
+                message[device, block] = total[:, block * LANES : (block + 1) * LANES]
 
 
 def own_coefs(sz, coefs, start):
@@ -312,8 +366,8 @@
         half = sz.loads // 2
         block = start // 64
         offset = start - block * 64
-        first = coefs[block].astype(F32)
-        second = coefs[jnp.minimum(block + 1, coefs.shape[0] - 1)].astype(F32)
+        first = coefs[block]
+        second = coefs[jnp.minimum(block + 1, coefs.shape[0] - 1)]
         lane = lane_ids(half)
         top = jnp.where(lane < 64, first, roll_lanes(second, 64))
         bottom = jnp.where(lane < 64, roll_lanes(first, 64), second)
@@ -321,8 +375,8 @@
     else:
         block = start // LANES
         offset = start - block * LANES
-        first = coefs[block].astype(F32)
-        second = coefs[jnp.minimum(block + 1, coefs.shape[0] - 1)].astype(F32)
+        first = coefs[block]
+        second = coefs[jnp.minimum(block + 1, coefs.shape[0] - 1)]
         both = jnp.where(lane_ids(sz.loads) >= offset, first, second)
     return pltpu.roll(both, lax.rem(LANES - offset, LANES), axis=1)
 
@@ -414,41 +468,33 @@
         halo_coefs[target] = jnp.where(keep[j], dinv * faces[j], 0.0)
 
 
-def solve_and_direct(
-    sz, swap, starts, count, table, res, below, above, ylow, yhigh, zdown, zup, id_box, coarse,
-    split, *rest,
-):
-    if swap:
-        direction, xlo, xhi, yface, zface, own = rest[:6]
-        yfaces = [yface]
-        rest = rest[6:]
-    else:
-        direction, xlo, xhi, ylo_out, yhi_out, zface, own = rest[:7]
-        yfaces = [ylo_out, yhi_out]
-        rest = rest[7:]
-    first, second, third, halos, inner, coefs, halo_coefs, mu_box, halo_mu, left, zedge = rest
+def z_halo(zhalo, rows):
+    down, up = zhalo.below(rows), zhalo.above(rows)
+    even = (lane_ids(down.shape[0]) & 1) == 0
+    return jnp.where(even, down, roll_lanes(up, -2))
+
+
+def solve_and_direct(sz, starts, count, table, res, id_box, coarse, split, *refs):
+    xhalo, yhalo, zhalo, refs = take_halos(refs, "gx", "gy", "col")
+    direction, own, zface = refs[:3]
+    xsend, ysend, refs = take_halos(refs[3:], "gx", "gy")
+    first, second, third, halos, inner, coefs, halo_coefs, mu_box, halo_mu, left, zedge = refs
     loads, comps = sz.loads, sz.comps
     groups = loads // 8
-    flags = side_flags(swap)
     lane8 = lane_ids(8)
-    even8 = (lane8 & 1) == 0
-
-    def halo_rows(row, size):
-        down = zdown[pl.ds(row, size), :].astype(F32)
-        up = zup[pl.ds(row, size), :].astype(F32)
-        even = (lane_ids(size) & 1) == 0
-        return jnp.where(even, down, roll_lanes(up, -2))
 
     halo_mu[...] = jnp.zeros_like(halo_mu)
     inner[1] = jnp.zeros((comps, loads, LANES), F32)
     make_coefs(
-        sz, table, id_box, halo_rows(sz.face_z, HALO_IDS)[:8], coefs, halo_coefs, own, mu_box,
-        halo_mu,
-    )
-    here_of = lambda place: (((lane8 + 1) >> 1) & 63) == place
+        sz, table, id_box, z_halo(zhalo, pl.ds(sz.face_z, HALO_IDS))[:8], coefs, halo_coefs, own,
+        mu_box, halo_mu,
+    )
+
+    def here_of(place):
+        return (((lane8 + 1) >> 1) & 63) == place
 
     for comp in range(comps):
-        halo = halo_rows(comp * loads, loads)
+        halo = z_halo(zhalo, pl.ds(comp * loads, loads))
         dinv = jnp.concatenate([halo_coefs[DINV]] * groups, axis=0)
         halos[0, comp] = dinv * halo
         total = jnp.zeros((loads, LANES), F32)
@@ -457,7 +503,7 @@
             for y in range(sz.by):
                 place = x * sz.by + y
                 row = (x + 1) * sz.pitch + y + 1
-                tile = box_tile(sz, res, below, above, ylow, yhigh, flags, comp, x, y)
+                tile = box_tile(sz, res, xhalo, yhalo, comp, x, y)
                 value = tile * jnp.broadcast_to(coefs[DINV, pl.ds(row, 1), :], (loads, LANES))
                 first[comp, place] = value
                 here = (((lane_k + 1) >> 1) & 63) == place
@@ -505,7 +551,7 @@
                     )
             return carry
 
-        lax.fori_loop(0, sz.box, at, 0, unroll=4)
+        lax.fori_loop(0, sz.box, at, 0, unroll=6)
         coef = [halo_coefs[j] for j in range(8)]
         for group in range(groups):
             rows = pl.ds(group * 8, 8)
@@ -559,22 +605,15 @@
     for comp in range(comps):
         for y in range(sz.cy):
             rows = pl.ds((comp * sz.cy + y) * loads, loads)
-            xlo[rows, :] = direction[comp, y].astype(BF16)
-            xhi[rows, :] = direction[comp, (sz.cx - 1) * sz.cy + y].astype(BF16)
+            xsend.send(rows, direction[comp, y], direction[comp, (sz.cx - 1) * sz.cy + y])
         for x in range(sz.cx):
             rows = pl.ds((comp * sz.cx + x) * loads, loads)
-            if swap:
-                y = jnp.where(lax.axis_index("gy") == 0, sz.cy - 1, 0)
-                yfaces[0][rows, :] = direction[comp, x * sz.cy + y].astype(BF16)
-            else:
-                yfaces[0][rows, :] = direction[comp, x * sz.cy].astype(BF16)
-                yfaces[1][rows, :] = direction[comp, x * sz.cy + sz.cy - 1].astype(BF16)
-
-
-def make_image(
-    sz, swap, res, own, direction, below, above, ylow, yhigh, zdown, zup, dir_split,
-    image_split, message, box, halo, sem,
-):
+            ysend.send(rows, direction[comp, x * sz.cy], direction[comp, (x + 1) * sz.cy - 1])
+
+
+def make_image(sz, res, own, direction, *refs):
+    xhalo, yhalo, zhalo, refs = take_halos(refs, "gx", "gy", "col")
+    dir_split, image_split, message, box, halo, sem = refs
     loads, comps = sz.loads, sz.comps
     groups = loads // 8
     copies = []
@@ -589,21 +628,16 @@
             )
     for copy in copies:
         copy.start()
-    flags = side_flags(swap)
     for comp in range(comps):
         for y in range(sz.cy):
             rows = pl.ds((comp * sz.cy + y) * loads, loads)
-            box[comp, y + 1] = below[rows, :].astype(F32)
-            box[comp, (sz.bx - 1) * sz.by + y + 1] = above[rows, :].astype(F32)
+            box[comp, y + 1] = xhalo.below(rows)
+            box[comp, (sz.bx - 1) * sz.by + y + 1] = xhalo.above(rows)
         for x in range(sz.cx):
             rows = pl.ds((comp * sz.cx + x) * loads, loads)
-            box[comp, (x + 1) * sz.by] = flagged(ylow[rows, :], flags[0])
-            box[comp, (x + 1) * sz.by + sz.by - 1] = flagged(yhigh[rows, :], flags[1])
-        rows = pl.ds(comp * loads, loads)
-        even = (lane_ids(loads) & 1) == 0
-        halo[comp] = jnp.where(
-            even, zdown[rows, :].astype(F32), roll_lanes(zup[rows, :].astype(F32), -2)
-        )
+            box[comp, (x + 1) * sz.by] = yhalo.below(rows)
+            box[comp, (x + 1) * sz.by + sz.by - 1] = yhalo.above(rows)
+        halo[comp] = z_halo(zhalo, pl.ds(comp * loads, loads))
     for copy in copies:
         copy.wait()
     lane8 = lane_ids(8)
@@ -654,18 +688,17 @@
     )
     high, low = total[:loads], total[loads:]
     sums = high + roll_lanes(high, -loads) + low
-    if message.shape[1] == 1:
-        for device in range(message.shape[0]):
-            message[device] = sums[device : device + 1]
-    else:
-        for device in range(message.shape[0]):
-            message[device] = sums
-
-
-def add_rows(sz, parts, message):
-    total = parts[0]
-    for device in range(1, parts.shape[0]):
-        total = total + parts[device]
+    half = loads // 2
+    lane = lane_ids(half)
+    packed = jnp.where((lane & (2 * loads - 1)) < loads, sums[:half], roll_lanes(sums[half:], loads))
+    message[...] = packed
+
+
+def share_sums(sz, mine, *refs):
+    message = refs[-1]
+    total = mine[...]
+    for other in refs[:-1]:
+        total = total + other[...]
     for device in range(message.shape[0]):
         message[device] = total
 
@@ -674,12 +707,10 @@
     sz, sums, iterate, res, dir_split, image_split, new_iterate, new_residual, parts
 ):
     loads = sz.loads
-    if sums.shape[1] == 1:
-        system = jnp.concatenate([sums[device] for device in range(sums.shape[0])], axis=0)
-    else:
-        system = sums[0]
-        for device in range(1, sums.shape[0]):
-            system = system + sums[device]
+    total = sums[0]
+    for device in range(1, sums.shape[0]):
+        total = total + sums[device]
+    system = jnp.concatenate([total, roll_lanes(total, -loads)], axis=0)
     lane = lane_ids(loads)
     system = jnp.where((lane & (2 * loads - 1)) < loads, system, 0.0)
     row_ids = lax.broadcasted_iota(jnp.int32, (loads, LANES), 0)
@@ -716,99 +747,107 @@
     lax.fori_loop(0, sz.cells, at, 0, unroll=4)
 
 
-def exchange(low, high, axis):
-    devices = lax.axis_size(axis)
-    up = [(i, i + 1) for i in range(devices - 1)]
-    down = [(j, i) for i, j in up]
-    return lax.ppermute(high, axis, up), lax.ppermute(low, axis, down)
-
-
-def exchange_y(faces, swap):
-    if swap:
-        got = lax.ppermute(faces[0], "gy", [(0, 1), (1, 0)])
-        return got, got
-    return exchange(faces[0], faces[1], "gy")
-
-
 def body(
     iterate, residual, cell_ids, materials, eigen_counts, coarse_rank, eigen_basis, coarse_inverse
 ):
     sz = Sizes(residual, eigen_basis, coarse_inverse)
     shape = jax.ShapeDtypeStruct
-    swap = lax.axis_size("gy") == 2
     devices = 1
     for axis in AXES:
         devices = devices * lax.axis_size(axis)
     blocks = sz.total_rows // sz.block_rows
-    scatter = devices == sz.loads
-    smem, vmem = pltpu.SMEM, pltpu.VMEM
+    smem, vmem, scratch, dma = pltpu.SMEM, pltpu.VMEM, pltpu.VMEM, pltpu.SemaphoreType.DMA
     res = residual.reshape(-1, LANES)
     old = iterate.reshape(-1, LANES)
-    basis = eigen_basis.reshape(-1, LANES)
     ids = cell_ids.reshape(-1, LANES)
 
     def call(name, kernel, *args, **kwargs):
         return vmem_call(name, lambda *refs: kernel(sz, *refs), *args, **kwargs)
 
-    def call_swap(name, kernel, *args, **kwargs):
-        return vmem_call(name, lambda *refs: kernel(sz, swap, *refs), *args, **kwargs)
-
     face = shape((sz.face_x + 2 * sz.cy, LANES), BF16)
-    xlo, xhi = call("pack_x", pack_x, [face, face], [], 16, 1 << 20, 2 << 20, [res, ids])
-    below, above = exchange(xlo, xhi, "gx")
-
-    message, split = call(
+    faces = call(
+        "pack_x",
+        pack_x,
+        [face] * swaps("gx"),
+        [scratch((sz.comps * sz.loads, sz.cy, LANES), F32)] * 2
+        + [scratch((sz.cells, LANES), jnp.int32), dma((3,))],
+        8,
+        1 << 20,
+        2 << 20,
+        [residual.reshape(-1, sz.cells, LANES), ids],
+        spaces=[pl.ANY, pl.ANY],
+    )
+    xhalo = exchange(faces, "gx")
+
+    packed, split = call(
         "pieces",
         make_pieces,
         [
-            shape((devices, sz.loads // 2, LANES), BF16),
+            shape((sz.loads // 2, LANES), BF16),
             shape((sz.tiles, 2 * sz.slots, LANES), BF16),
         ],
-        [pltpu.VMEM((sz.loads, LANES), F32)],
-        20,
+        [
+            scratch((sz.loads, LANES), F32),
+            scratch((sz.slots, sz.tiles, LANES), F32),
+            scratch((sz.comps, sz.loads * sz.cells, LANES), F32),
+            dma((2, sz.comps)),
+        ],
+        12,
         1 << 27,
         7 << 20,
-        [eigen_counts, coarse_rank, basis, res, xhi],
-        spaces=[smem, smem, vmem, vmem, pl.ANY],
-    )
+        [
+            eigen_counts,
+            coarse_rank,
+            eigen_basis.reshape(sz.slots, sz.tiles, LANES),
+            residual.reshape(sz.comps, -1, LANES),
+            faces[0],
+        ],
+        spaces=[smem, smem, pl.ANY, pl.ANY, pl.ANY],
+    )
+
+    yface = shape((sz.face_y + HALO_IDS, LANES), BF16)
+    message, *faces = call(
+        "pack_y",
+        pack_y,
+        [shape((devices,) + packed.shape, BF16)] + [yface] * swaps("gy"),
+        [scratch((HALO_IDS, LANES), F32)] * 2,
+        8,
+        1 << 20,
+        2 << 20,
+        [res, ids, packed] + xhalo,
+    )
+    yhalo = exchange(faces, "gy")
     gathered = lax.all_to_all(message, AXES, 0, 0, tiled=True)
     all_counts = gathered[:, 0, sz.slots].astype(jnp.int32)
     all_ranks = gathered[:, 0, sz.slots + 1].astype(jnp.int32)
     starts = jnp.sum(
         all_counts[None, :] * (all_ranks[None, :] < all_ranks[:, None]).astype(jnp.int32), axis=1
     )
-
-    side = [pltpu.VMEM((HALO_IDS, LANES), F32)]
-    yface = shape((sz.face_y + HALO_IDS, LANES), BF16)
-    faces = call_swap(
-        "pack_y", pack_y, [yface] * (1 if swap else 2), side, 16, 1 << 20, 2 << 20,
-        [res, ids, below, above],
-    )
-    ylow, yhigh = exchange_y(faces, swap)
     rows = (sz.cx + 4) * sz.pitch
-    zmessage, id_box = call_swap(
+    zmessage, id_box = call(
         "pack_z",
         pack_z,
         [shape((sz.face_z + HALO_IDS, LANES), BF16), shape((rows, LANES), F32)],
-        [pltpu.VMEM((sz.box * 8, LANES), F32), pltpu.VMEM((rows, LANES), F32)],
-        16,
+        [scratch((sz.box * 8, LANES), F32), scratch((rows, LANES), F32)],
+        8,
         1 << 22,
         3 << 20,
-        [res, ids, below, above, ylow, yhigh],
-    )
-    zdown, zup = exchange(zmessage, zmessage, "col")
-
-    packed = sz.block_rows == 64
-    tile = (1, sz.loads // 2, LANES) if packed else (sz.block_rows // LANES, sz.loads, LANES)
+        [res, ids] + xhalo + yhalo,
+    )
+    zhalo = exchange([zmessage] * 2, "col")
+
+    tile = (1, sz.loads // 2, LANES)
+    if sz.block_rows != 64:
+        tile = (sz.block_rows // LANES, sz.loads, LANES)
     partial = call(
         "coarse",
         place_pieces,
-        shape((blocks,) + tile, BF16),
+        shape((blocks,) + tile, F32),
         [
-            pltpu.VMEM((sz.total_rows // LANES + 1, sz.loads, LANES), F32),
-            pltpu.VMEM((sz.loads, LANES), F32),
+            scratch((sz.total_rows // LANES + 1, sz.loads, LANES), F32),
+            scratch((sz.loads, LANES), F32),
         ],
-        20,
+        12,
         1 << 23,
         1 << 20,
         [starts, gathered, coarse_inverse],
@@ -817,75 +856,72 @@
     coarse = lax.all_to_all(partial, ("gx", "col"), 0, 0, tiled=True)
     coarse = coarse.reshape((-1,) + tile[1:])
 
-    dface = shape((sz.face_x, LANES), BF16)
-    dyface = shape((sz.inner_y, LANES), BF16)
-    field = pltpu.VMEM((sz.comps, sz.box, sz.loads, LANES), F32)
-    results = call_swap(
+    field = scratch((sz.comps, sz.box, sz.loads, LANES), F32)
+    direction, own, zface, *faces = call(
         "solve",
         solve_and_direct,
-        [shape((sz.comps, sz.cells, sz.loads, LANES), F32), dface, dface]
-        + [dyface] * (1 if swap else 2)
-        + [shape((sz.face_z, LANES), BF16), shape((8, sz.cells, LANES), F32)],
+        [
+            shape((sz.comps, sz.cells, sz.loads, LANES), F32),
+            shape((8, sz.cells, LANES), F32),
+            shape((sz.face_z, LANES), BF16),
+        ]
+        + [shape((sz.face_x, LANES), BF16)] * swaps("gx")
+        + [shape((sz.inner_y, LANES), BF16)] * swaps("gy"),
         [
             field,
             field,
             field,
-            pltpu.VMEM((3, sz.comps, sz.loads, LANES), F32),
-            pltpu.VMEM((2, sz.comps, sz.loads, LANES), F32),
-            pltpu.VMEM((9, rows, LANES), F32),
-            pltpu.VMEM((9, 8, LANES), F32),
-            pltpu.VMEM((rows, LANES), F32),
-            pltpu.VMEM((rows, LANES), F32),
-            pltpu.VMEM((2 * sz.loads, LANES), BF16),
-            pltpu.VMEM((sz.face_z, LANES), F32),
+            scratch((3, sz.comps, sz.loads, LANES), F32),
+            scratch((2, sz.comps, sz.loads, LANES), F32),
+            scratch((9, rows, LANES), F32),
+            scratch((9, 8, LANES), F32),
+            scratch((rows, LANES), F32),
+            scratch((rows, LANES), F32),
+            scratch((2 * sz.loads, LANES), BF16),
+            scratch((sz.face_z, LANES), F32),
         ],
-        28,
+        20,
         1 << 28,
         8 << 20,
-        [
-            starts, eigen_counts, materials, res, below, above, ylow, yhigh, zdown, zup, id_box,
-            coarse, split,
-        ],
-        spaces=[smem, smem, smem] + [vmem] * 10,
-    )
-    direction, dxlo, dxhi = results[:3]
-    dfaces, zface, own = results[3:-2], results[-2], results[-1]
-    dbelow, dabove = exchange(dxlo, dxhi, "gx")
-    dylow, dyhigh = exchange_y(dfaces, swap)
-    dzdown, dzup = exchange(zface, zface, "col")
-
-    dir_split, image_split, energy = call_swap(
+        [starts, eigen_counts, materials, res, id_box, coarse, split] + xhalo + yhalo + zhalo,
+        spaces=[smem, smem, smem] + [vmem] * (4 + len(xhalo + yhalo + zhalo)),
+    )
+    xhalo = exchange(faces[: swaps("gx")], "gx")
+    yhalo = exchange(faces[swaps("gx") :], "gy")
+    zhalo = exchange([zface] * 2, "col")
+    sums_shape = (sz.loads // 2, LANES)
+    dir_split, image_split, sums = call(
         "image",
         make_image,
         [
             shape((sz.tiles, 2 * sz.loads, LANES), BF16),
             shape((sz.tiles, 2 * sz.loads, LANES), BF16),
-            shape((devices, 1 if scatter else sz.loads, LANES), F32),
+            shape(sums_shape, F32),
         ],
-        [
-            field,
-            pltpu.VMEM((sz.comps, sz.loads, LANES), F32),
-            pltpu.SemaphoreType.DMA((sz.comps, sz.cx)),
-        ],
-        20,
+        [field, scratch((sz.comps, sz.loads, LANES), F32), dma((sz.comps, sz.cx))],
+        16,
         1 << 28,
         8 << 20,
-        [res, own, direction, dbelow, dabove, dylow, dyhigh, dzdown, dzup],
-        spaces=[vmem, vmem, pl.ANY] + [vmem] * 6,
-    )
-    sums = lax.all_to_all(energy, AXES, 0, 0, tiled=True)
-    if scatter:
-        whole = call(
-            "add_rows", add_rows, shape(sums.shape, F32), [], 4, 1 << 12, 1 << 15, [sums]
-        )
-        sums = lax.all_to_all(whole, AXES, 0, 0, tiled=True)
+        [res, own, direction] + xhalo + yhalo + zhalo,
+        spaces=[vmem, vmem, pl.ANY] + [vmem] * len(xhalo + yhalo + zhalo),
+    )
+    over, operands = AXES, [sums]
+    if lax.axis_size("gy") == 2:
+        over = ("gx", "col")
+        operands += exchange([sums], "gy")
+        devices = devices // 2
+    spread = call(
+        "share_sums", share_sums, shape((devices,) + sums_shape, F32), [], 4, 1 << 12, 1 << 17,
+        operands,
+    )
+    sums = lax.all_to_all(spread, over, 0, 0, tiled=True)
     flat = shape(res.shape, F32)
     new_iterate, new_residual = call(
         "finish",
         finish,
         [flat, flat],
-        [pltpu.VMEM((2 * sz.loads, LANES), BF16)],
-        20,
+        [scratch((2 * sz.loads, LANES), BF16)],
+        16,
         1 << 27,
         9 << 20,
         [sums, old, res, dir_split, image_split],

time: 122 us -> 106 us (0.87)
  starting transfers between devices: 40.2 us -> 22.2 us
  blocking collectives: 23.6 us -> 29 us
  waiting for transfers between devices: 7.65 us -> 6.19 us
    all_to_all x1 -> x0, starting transfers between devices: 7.3 us -> none  [body(): gathered = lax.all_to_all(message, AXES, 0, 0, tiled=True)]
    all_to_all x1, starting transfers between devices: 9.83 us -> 3.51 us  [body(): coarse = lax.all_to_all(partial, ('gx', 'col'), 0, 0, tiled=True)]
    all_to_all x2, blocking collectives: 23.6 us -> 29 us  [the longest x1 16 us: body(): sums = lax.all_to_all(spread, over, 0, 0, tiled=True)]
    ppermute x10 -> x11, starting transfers between devices: 23.1 us -> 18.7 us  [exchange(): result.append(lax.ppermute(faces[parity], axis, pairs))]
    ppermute x10 -> x11, waiting for transfers between devices: 7.35 us -> 6.19 us  [exchange(): result.append(lax.ppermute(faces[parity], axis, pairs))]
  transfers between devices with their start and end apart: 12 -> 12, of which waited for: 5 -> 4; matrix products, arithmetic and copies ran while one was open for 1% -> 0% of each run, Pallas kernels for 3% -> 6%
where the time goes in v3:
time: 106 us; the launch traced here: 105 us
  Pallas kernels  37.6 us (35%)
  blocking collectives  29 us (27%)
  starting transfers between devices  22.2 us (21%)
  local copies, waits for them, and re-layouts  6.9 us (7%)
  waiting for transfers between devices  6.19 us (6%)
  between operations  2.13 us (2%)
  other arithmetic  1.48 us (1%)
    pallas_call x9, Pallas kernels, vmem_call(): pl.pallas_call(kernel, name=name, out_shape=outs, in_specs=[pl.BlockSpec(...  37.6 us
    ppermute x11, starting transfers between devices, exchange(): result.append(lax.ppermute(faces[parity], axis, pairs))  18.7 us
    all_to_all x1, blocking collectives, body(): sums = lax.all_to_all(spread, over, 0, 0, tiled=True)  16 us
    all_to_all x1, blocking collectives, body(): gathered = lax.all_to_all(message, AXES, 0, 0, tiled=True)  13 us
    unnamed x20, local copies, waits for them, and re-layouts  6.9 us
    ppermute x11, waiting for transfers between devices, exchange(): result.append(lax.ppermute(faces[parity], axis, pairs))  6.19 us
    all_to_all x1, starting transfers between devices, body(): coarse = lax.all_to_all(partial, ('gx', 'col'), 0, 0, tiled=True)  3.51 us
  transfers between devices with their start and end apart: 12, of which 4 were waited for; matrix products, arithmetic and copies ran while one was open for 0% of the time, Pallas kernels for 6%

profile of v3, /device:TPU:0, one launch (start us, length us, event | category | flops | bytes accessed | tf_op | source)
XLA Modules:
  0.0 105.5 jit_solution(3773484463941022464)
XLA Ops:
  0.6 0.0 copy-start
  0.6 1.4 %copy-done = f32[3,32,4,8,128]{4,3,2,1,0:T(8,128)S(1)} copy-done((f32[3,32,4,8,128]{4,3,2,1,0:T(8,128)S(1)}, f32[3,32,4,8,128]{4,3,2,1,0:T(8,128)}, u32[]{:S(2)}) %copy-start) | copy-done | bytes 1572888
  2.0 0.0 copy-start.6
  2.0 0.7 copy-done.6
  2.8 0.0 copy-start.1
  2.8 0.3 pack_x.1
  3.0 0.8 collective-permute-start.1
  3.9 5.7 %collective-permute-start = (bf16[784,128]{1,0:T(8,128)(2,1)S(1)}, bf16[784,128]{1,0:T(8,128)(2,1)S(1)}, u32[]{:S(2)}, u32[]{:S(2)}) collective-permute-start(bf16[784,128]{1,0:T(8,128)(2,1)S(1)} %get-tuple-element.21.refs_4_), channel_id=1, source_target_pairs={{0,8},{8,0},{16,24},{24,16},{1,9},{9,1},{17,25},{25,17},{2,10},{10... | collective-permute-start | bytes 602120 | tf_op jit(solution)/shard_map/ppermute | solution.py:114
  10.9 0.0 copy-done.1
  10.9 0.0 copy-start.4
  10.9 1.7 %copy-done.4 = f32[48,3,4,8,128]{4,3,2,1,0:T(8,128)S(1)} copy-done((f32[48,3,4,8,128]{4,3,2,1,0:T(8,128)S(1)}, f32[48,3,4,8,128]{4,3,2,1,0:T(8,128)}, u32[]{:S(2)}) %copy-start.4) | copy-done | bytes 2359320
  12.6 0.0 copy-start.7
  12.6 4.5 %pieces.1 = (bf16[16,128]{1,0:T(8,128)(2,1)S(1)}, bf16[96,96,128]{2,1,0:T(8,128)(2,1)S(1)}) custom-call(s32[1]{0:T(128)S(6)} %copy.12.refs_0_.refs_1_, s32[1]{0:T(128)S(6)} %copy.13.refs_1_, f32[48,96,128]{2,1,0:T(8,128)S(1)} %bitcast.16, f32[3,1024,128]{2,1,0:T(8,128)S(1)} %bitcast.10, bf16[784,128]{1,0:T(8,128)(2,1)S(1)} %get-tuple-element.21.refs_4_), custom_call_target="tpu_custom_call" | custom-call | flops 134217728 | bytes 7340032 | tf_op jit(solution)/shard_map/pieces/pallas_call | solution.py:46
  17.1 0.0 copy-start.2
  17.1 1.4 %copy-done.2 = bf16[96,96,128]{2,1,0:T(8,128)(2,1)} copy-done((bf16[96,96,128]{2,1,0:T(8,128)(2,1)}, bf16[96,96,128]{2,1,0:T(8,128)(2,1)S(1)}, u32[]{:S(2)}) %copy-start.2) | copy-done | bytes 2359320
  18.6 0.0 copy-start.8
  18.6 0.0 collective-permute-done.1.refs_4_.refs_3_.refs_8_
  18.6 0.0 collective-permute-done.refs_3_.refs_2_.refs_7_
  18.6 0.0 copy-done.7
  18.6 0.3 pack_y.1
  18.8 0.0 copy-start.9
  18.9 13.0 %all_to_all.15.refs_1_ = bf16[32,16,128]{2,1,0:T(8,128)(2,1)S(1)} all-to-all(bf16[32,16,128]{2,1,0:T(8,128)(2,1)S(1)} %get-tuple-element.24), channel_id=1, replica_groups=mesh['gx'=4,'gy'=2,'col'=4] {'gx','gy','col'}, dimensions={0} | all-to-all | bytes 262144 | tf_op jit(solution)/shard_map/all_to_all | solution.py:820
  31.9 1.3 %fusion.1 = (s32[32]{0:T(128)S(1)}, s32[32]{0:T(128)S(1)}) fusion(bf16[32,16,128]{2,1,0:T(8,128)(2,1)S(1)} %all_to_all.15.refs_1_), kind=kLoop, calls=%fused_computation.3 | loop fusion | flops 64 | bytes 384 | tf_op jit(solution)/shard_map/convert_element_type | solution.py:822
  33.2 0.2 select_reduce_fusion.refs_0_
  33.4 0.0 copy-done.8
  33.4 2.0 %coarse.1 = f32[16,1,16,128]{3,2,1,0:T(8,128)} custom-call(s32[32]{0:T(128)S(1)} %select_reduce_fusion.refs_0_, bf16[32,16,128]{2,1,0:T(8,128)(2,1)S(1)} %all_to_all.15.refs_1_, bf16[64,1024]{1,0:T(8,128)(2,1)S(1)} %copy-done.8), custom_call_target="tpu_custom_call" | custom-call | flops 8388608 | bytes 1048576 | tf_op jit(solution)/shard_map/coarse/pallas_call | solution.py:46
  35.4 3.5 %all-to-all-start.1 = ((f32[16,1,16,128]{3,2,1,0:T(8,128)}), f32[16,1,16,128]{3,2,1,0:T(8,128)S(1)}, u32[]{:S(2)}, u32[]{:S(2)}) async-start(f32[16,1,16,128]{3,2,1,0:T(8,128)} %coarse.1), calls=%async_computation.1 | async-start | bytes 262144 | tf_op jit(solution)/shard_map/all_to_all | solution.py:856
  39.0 0.1 collective-permute-start.2
  39.0 1.4 %collective-permute-done.2.refs_4_.refs_9_ = bf16[592,128]{1,0:T(8,128)(2,1)S(1)} collective-permute-done((bf16[592,128]{1,0:T(8,128)(2,1)S(1)}, bf16[592,128]{1,0:T(8,128)(2,1)S(1)}, u32[]{:S(2)}, u32[]{:S(2)}) %collective-permute-start.2) | collective-permute-done | bytes 151584 | tf_op jit(solution)/shard_map/ppermute | solution.py:114
  40.4 1.3 %pack_z.1 = (bf16[112,128]{1,0:T(8,128)(2,1)S(1)}, f32[128,128]{1,0:T(8,128)S(1)}) custom-call(f32[3072,128]{1,0:T(8,128)S(1)} %bitcast.12, s32[32,128]{1,0:T(8,128)S(1)} %bitcast.21, bf16[784,128]{1,0:T(8,128)(2,1)S(1)} %collective-permute-done.refs_3_.refs_2_.refs_7_, bf16[784,128]{1,0:T(8,128)(2,1)S(1)} %collective-permute-done.1.refs_4_.refs_3_.refs_8_, ...), custom_call_target="tpu_custom_call" | custom-call | flops 4194304 | bytes 3145728 | tf_op jit(solution)/shard_map/pack_z/pallas_call | solution.py:46
  41.7 0.7 collective-permute-start.4
  42.4 4.5 %collective-permute-start.3 = (bf16[112,128]{1,0:T(8,128)(2,1)S(1)}, bf16[112,128]{1,0:T(8,128)(2,1)S(1)}, u32[]{:S(2)}, u32[]{:S(2)}) collective-permute-start(bf16[112,128]{1,0:T(8,128)(2,1)S(1)} %get-tuple-element.28), channel_id=1, source_target_pairs={{0,1},{1,0},{2,3},{3,2},{4,5},{5,4},{6,7},{7,6},{8,9},{9,8},{10,11... | collective-permute-start | bytes 86024 | tf_op jit(solution)/shard_map/ppermute | solution.py:114
  46.9 0.0 collective-permute-done.4.refs_11_
  46.9 1.8 %collective-permute-done.3.refs_10_ = bf16[112,128]{1,0:T(8,128)(2,1)S(1)} collective-permute-done((bf16[112,128]{1,0:T(8,128)(2,1)S(1)}, bf16[112,128]{1,0:T(8,128)(2,1)S(1)}, u32[]{:S(2)}, u32[]{:S(2)}) %collective-permute-start.3) | collective-permute-done | bytes 28704 | tf_op jit(solution)/shard_map/ppermute | solution.py:114
  48.8 0.0 all-to-all-done.1
  48.8 0.0 copy-done.9
  48.8 0.0 copy-start.3
  48.8 1.7 %copy-done.3 = bf16[96,96,128]{2,1,0:T(8,128)(2,1)S(1)} copy-done((bf16[96,96,128]{2,1,0:T(8,128)(2,1)S(1)}, bf16[96,96,128]{2,1,0:T(8,128)(2,1)}, u32[]{:S(2)}) %copy-start.3) | copy-done | bytes 2359320
  50.4 14.8 %solve.1 = (f32[3,32,32,128]{3,2,1,0:T(8,128)S(1)}, f32[8,32,128]{2,1,0:T(8,128)S(1)}, bf16[96,128]{1,0:T(8,128)(2,1)S(1)}, bf16[768,128]{1,0:T(8,128)(2,1)S(1)}...) custom-call(s32[32]{0:T(128)S(1)} %select_reduce_fusion.refs_0_, s32[1]{0:T(128)S(6)} %copy.12.refs_0_.refs_1_, ...), custom_call_target="tpu_custom_call" | custom-call | flops 268435456 | bytes 8388608 | tf_op jit(solution)/shard_map/solve/pallas_call | solution.py:46
  65.2 1.6 %collective-permute-start.5 = (bf16[768,128]{1,0:T(8,128)(2,1)S(1)}, bf16[768,128]{1,0:T(8,128)(2,1)S(1)}, u32[]{:S(2)}, u32[]{:S(2)}) collective-permute-start(bf16[768,128]{1,0:T(8,128)(2,1)S(1)} %get-tuple-element.31), channel_id=1, source_target_pairs={{0,8},{8,0},{16,24},{24,16},{1,9},{9,1},{17,25},{25,17},{2,10},{10... | collective-permute-start | bytes 589832 | tf_op jit(solution)/shard_map/ppermute | solution.py:114
  66.8 0.7 collective-permute-start.6
  67.4 0.1 collective-permute-start.7
  67.5 0.7 collective-permute-start.9
  68.2 3.9 %collective-permute-start.8 = (bf16[96,128]{1,0:T(8,128)(2,1)S(1)}, bf16[96,128]{1,0:T(8,128)(2,1)S(1)}, u32[]{:S(2)}, u32[]{:S(2)}) collective-permute-start(bf16[96,128]{1,0:T(8,128)(2,1)S(1)} %get-tuple-element.34), channel_id=1, source_target_pairs={{0,1},{1,0},{2,3},{3,2},{4,5},{5,4},{6,7},{7,6},{8,9},{9,8},{10,11... | collective-permute-start | bytes 73736 | tf_op jit(solution)/shard_map/ppermute | solution.py:114
  72.1 0.0 collective-permute-done.9.refs_7_
  72.1 1.8 %collective-permute-done.8.refs_6_ = bf16[96,128]{1,0:T(8,128)(2,1)S(1)} collective-permute-done((bf16[96,128]{1,0:T(8,128)(2,1)S(1)}, bf16[96,128]{1,0:T(8,128)(2,1)S(1)}, u32[]{:S(2)}, u32[]{:S(2)}) %collective-permute-start.8) | collective-permute-done | bytes 24608 | tf_op jit(solution)/shard_map/ppermute | solution.py:114
  73.9 0.0 collective-permute-done.7.refs_5_
  73.9 0.0 collective-permute-done.5.refs_3_
  73.9 0.0 collective-permute-done.6.refs_4_
  73.9 0.0 copy-start.5
  73.9 6.5 %image.1 = (bf16[96,64,128]{2,1,0:T(8,128)(2,1)S(1)}, bf16[96,64,128]{2,1,0:T(8,128)(2,1)S(1)}, f32[16,128]{1,0:T(8,128)S(1)}) custom-call(f32[3072,128]{1,0:T(8,128)S(1)} %bitcast.14, f32[8,32,128]{2,1,0:T(8,128)S(1)} %get-tuple-element.29.refs_1_, f32[3,32,32,128]{3,2,1,0:T(8,128)S(1)} %get-tuple-element.30.refs_2_, ...), custom_call_target="tpu_custom_call" | custom-call | flops 268435456 | bytes 8388608 | tf_op jit(solution)/shard_map/image/pallas_call | solution.py:46
  80.4 0.1 collective-permute-start.10
  80.5 1.2 %collective-permute-done.10.refs_1_ = f32[16,128]{1,0:T(8,128)S(1)} collective-permute-done((f32[16,128]{1,0:T(8,128)S(1)}, f32[16,128]{1,0:T(8,128)S(1)}, u32[]{:S(2)}, u32[]{:S(2)}) %collective-permute-start.10) | collective-permute-done | bytes 8224 | tf_op jit(solution)/shard_map/ppermute | solution.py:114
  81.7 16.0 %all_to_all.16.refs_0_ = f32[16,16,128]{2,1,0:T(8,128)S(1)} all-to-all(f32[16,16,128]{2,1,0:T(8,128)S(1)} %share_sums.1), channel_id=1, replica_groups=mesh['gx'=4,'gy'=2,'col'=4] {'gx','col'}, dimensions={0} | all-to-all | bytes 262144 | tf_op jit(solution)/shard_map/all_to_all | solution.py:917
  97.6 0.0 copy-done.5
  97.6 7.9 %finish.1 = (f32[3072,128]{1,0:T(8,128)}, f32[3072,128]{1,0:T(8,128)}) custom-call(f32[16,16,128]{2,1,0:T(8,128)S(1)} %all_to_all.16.refs_0_, f32[3072,128]{1,0:T(8,128)S(1)} %bitcast.17, f32[3072,128]{1,0:T(8,128)S(1)} %bitcast.15, bf16[96,64,128]{2,1,0:T(8,128)(2,1)S(1)} %get-tuple-element.36.refs_3_, bf16[96,64,128]{2,1,0:T(8,128)(2,1)S(1)} %get-tuple-element.37.refs_4_), custom_call_target="tpu_custom_call" | custom-call | flops 134217728 | bytes 9437184 | tf_op jit(solution)/shard_map/finish/pallas_call | solution.py:46
  (1 shorter events, 0.0 us)
Async XLA Ops:
  0.6 1.4 %copy-start = (f32[3,32,4,8,128]{4,3,2,1,0:T(8,128)S(1)}, f32[3,32,4,8,128]{4,3,2,1,0:T(8,128)}, u32[]{:S(2)}) copy-start(f32[3,32,4,8,128]{4,3,2,1,0:T(8,128)} %param.9) | copy-start | bytes 4718596
  2.0 0.7 copy-start.6
  2.8 8.1 %copy-start.1 = (f32[3,32,4,8,128]{4,3,2,1,0:T(8,128)S(1)}, f32[3,32,4,8,128]{4,3,2,1,0:T(8,128)}, u32[]{:S(2)}) copy-start(f32[3,32,4,8,128]{4,3,2,1,0:T(8,128)} %param.9) | copy-start | bytes 4718596
  3.0 15.5 %collective-permute-start.1 = (bf16[784,128]{1,0:T(8,128)(2,1)S(1)}, bf16[784,128]{1,0:T(8,128)(2,1)S(1)}, u32[]{:S(2)}, u32[]{:S(2)}) collective-permute-start(bf16[784,128]{1,0:T(8,128)(2,1)S(1)} %get-tuple-element.23), channel_id=1, source_target_pairs={{8,16},{16,8},{9,17},{17,9},{10,18},{18,10},{11,19},{19,11},{12,20... | collective-permute-start | bytes 602120 | tf_op jit(solution)/shard_map/ppermute | solution.py:114
  3.9 14.7 %collective-permute-start = (bf16[784,128]{1,0:T(8,128)(2,1)S(1)}, bf16[784,128]{1,0:T(8,128)(2,1)S(1)}, u32[]{:S(2)}, u32[]{:S(2)}) collective-permute-start(bf16[784,128]{1,0:T(8,128)(2,1)S(1)} %get-tuple-element.21.refs_4_), channel_id=1, source_target_pairs={{0,8},{8,0},{16,24},{24,16},{1,9},{9,1},{17,25},{25,17},{2,10},{10... | collective-permute-start | bytes 602120 | tf_op jit(solution)/shard_map/ppermute | solution.py:114
  10.9 1.7 %copy-start.4 = (f32[48,3,4,8,128]{4,3,2,1,0:T(8,128)S(1)}, f32[48,3,4,8,128]{4,3,2,1,0:T(8,128)}, u32[]{:S(2)}) copy-start(f32[48,3,4,8,128]{4,3,2,1,0:T(8,128)} %param.14) | copy-start | bytes 7077892
  12.6 6.0 %copy-start.7 = (s32[4,8,128]{2,1,0:T(8,128)S(1)}, s32[4,8,128]{2,1,0:T(8,128)}, u32[]{:S(2)}) copy-start(s32[4,8,128]{2,1,0:T(8,128)} %param.10) | copy-start | bytes 49156
  17.1 1.4 %copy-start.2 = (bf16[96,96,128]{2,1,0:T(8,128)(2,1)}, bf16[96,96,128]{2,1,0:T(8,128)(2,1)S(1)}, u32[]{:S(2)}) copy-start(bf16[96,96,128]{2,1,0:T(8,128)(2,1)S(1)} %get-tuple-element.27.refs_6_) | copy-start | bytes 7077892
  18.6 14.8 %copy-start.8 = (bf16[64,1024]{1,0:T(8,128)(2,1)S(1)}, bf16[64,1024]{1,0:T(8,128)(2,1)}, u32[]{:S(2)}) copy-start(bf16[64,1024]{1,0:T(8,128)(2,1)} %refs_2_.2) | copy-start | bytes 393220
  18.8 29.9 %copy-start.9 = (f32[2,16]{1,0:T(2,128)S(1)}, f32[2,16]{1,0:T(2,128)}, u32[]{:S(2)}) copy-start(f32[2,16]{1,0:T(2,128)} %refs_2_.3) | copy-start | bytes 388
  35.4 13.3 %all-to-all-start.1 = ((f32[16,1,16,128]{3,2,1,0:T(8,128)}), f32[16,1,16,128]{3,2,1,0:T(8,128)S(1)}, u32[]{:S(2)}, u32[]{:S(2)}) async-start(f32[16,1,16,128]{3,2,1,0:T(8,128)} %coarse.1), calls=%async_computation.1 | async-start | bytes 262144 | tf_op jit(solution)/shard_map/all_to_all | solution.py:856
  39.0 1.4 %collective-permute-start.2 = (bf16[592,128]{1,0:T(8,128)(2,1)S(1)}, bf16[592,128]{1,0:T(8,128)(2,1)S(1)}, u32[]{:S(2)}, u32[]{:S(2)}) collective-permute-start(bf16[592,128]{1,0:T(8,128)(2,1)S(1)} %get-tuple-element.25), channel_id=1, source_target_pairs={{0,4},{4,0},{1,5},{5,1},{2,6},{6,2},{3,7},{7,3},{8,12},{12,8},{9,1... | collective-permute-start | bytes 454664 | tf_op jit(solution)/shard_map/ppermute | solution.py:114
  41.7 5.2 %collective-permute-start.4 = (bf16[112,128]{1,0:T(8,128)(2,1)S(1)}, bf16[112,128]{1,0:T(8,128)(2,1)S(1)}, u32[]{:S(2)}, u32[]{:S(2)}) collective-permute-start(bf16[112,128]{1,0:T(8,128)(2,1)S(1)} %get-tuple-element.28), channel_id=1, source_target_pairs={{1,2},{2,1},{5,6},{6,5},{9,10},{10,9},{13,14},{14,13},{17,18},{18,... | collective-permute-start | bytes 86024 | tf_op jit(solution)/shard_map/ppermute | solution.py:114
  42.4 6.4 %collective-permute-start.3 = (bf16[112,128]{1,0:T(8,128)(2,1)S(1)}, bf16[112,128]{1,0:T(8,128)(2,1)S(1)}, u32[]{:S(2)}, u32[]{:S(2)}) collective-permute-start(bf16[112,128]{1,0:T(8,128)(2,1)S(1)} %get-tuple-element.28), channel_id=1, source_target_pairs={{0,1},{1,0},{2,3},{3,2},{4,5},{5,4},{6,7},{7,6},{8,9},{9,8},{10,11... | collective-permute-start | bytes 86024 | tf_op jit(solution)/shard_map/ppermute | solution.py:114
  48.8 1.7 %copy-start.3 = (bf16[96,96,128]{2,1,0:T(8,128)(2,1)S(1)}, bf16[96,96,128]{2,1,0:T(8,128)(2,1)}, u32[]{:S(2)}) copy-start(bf16[96,96,128]{2,1,0:T(8,128)(2,1)} %copy-done.2) | copy-start | bytes 7077892
  65.2 8.7 %collective-permute-start.5 = (bf16[768,128]{1,0:T(8,128)(2,1)S(1)}, bf16[768,128]{1,0:T(8,128)(2,1)S(1)}, u32[]{:S(2)}, u32[]{:S(2)}) collective-permute-start(bf16[768,128]{1,0:T(8,128)(2,1)S(1)} %get-tuple-element.31), channel_id=1, source_target_pairs={{0,8},{8,0},{16,24},{24,16},{1,9},{9,1},{17,25},{25,17},{2,10},{10... | collective-permute-start | bytes 589832 | tf_op jit(solution)/shard_map/ppermute | solution.py:114
  66.8 7.1 %collective-permute-start.6 = (bf16[768,128]{1,0:T(8,128)(2,1)S(1)}, bf16[768,128]{1,0:T(8,128)(2,1)S(1)}, u32[]{:S(2)}, u32[]{:S(2)}) collective-permute-start(bf16[768,128]{1,0:T(8,128)(2,1)S(1)} %get-tuple-element.32), channel_id=1, source_target_pairs={{8,16},{16,8},{9,17},{17,9},{10,18},{18,10},{11,19},{19,11},{12,20... | collective-permute-start | bytes 589832 | tf_op jit(solution)/shard_map/ppermute | solution.py:114
  67.4 6.4 %collective-permute-start.7 = (bf16[384,128]{1,0:T(8,128)(2,1)S(1)}, bf16[384,128]{1,0:T(8,128)(2,1)S(1)}, u32[]{:S(2)}, u32[]{:S(2)}) collective-permute-start(bf16[384,128]{1,0:T(8,128)(2,1)S(1)} %get-tuple-element.33), channel_id=1, source_target_pairs={{0,4},{4,0},{1,5},{5,1},{2,6},{6,2},{3,7},{7,3},{8,12},{12,8},{9,1... | collective-permute-start | bytes 294920 | tf_op jit(solution)/shard_map/ppermute | solution.py:114
  67.5 4.6 %collective-permute-start.9 = (bf16[96,128]{1,0:T(8,128)(2,1)S(1)}, bf16[96,128]{1,0:T(8,128)(2,1)S(1)}, u32[]{:S(2)}, u32[]{:S(2)}) collective-permute-start(bf16[96,128]{1,0:T(8,128)(2,1)S(1)} %get-tuple-element.34), channel_id=1, source_target_pairs={{1,2},{2,1},{5,6},{6,5},{9,10},{10,9},{13,14},{14,13},{17,18},{18,... | collective-permute-start | bytes 73736 | tf_op jit(solution)/shard_map/ppermute | solution.py:114
  68.2 5.7 %collective-permute-start.8 = (bf16[96,128]{1,0:T(8,128)(2,1)S(1)}, bf16[96,128]{1,0:T(8,128)(2,1)S(1)}, u32[]{:S(2)}, u32[]{:S(2)}) collective-permute-start(bf16[96,128]{1,0:T(8,128)(2,1)S(1)} %get-tuple-element.34), channel_id=1, source_target_pairs={{0,1},{1,0},{2,3},{3,2},{4,5},{5,4},{6,7},{7,6},{8,9},{9,8},{10,11... | collective-permute-start | bytes 73736 | tf_op jit(solution)/shard_map/ppermute | solution.py:114
  73.9 23.7 %copy-start.5 = (f32[3,32,4,8,128]{4,3,2,1,0:T(8,128)S(1)}, f32[3,32,4,8,128]{4,3,2,1,0:T(8,128)}, u32[]{:S(2)}) copy-start(f32[3,32,4,8,128]{4,3,2,1,0:T(8,128)} %param.8) | copy-start | bytes 4718596
  80.4 1.2 %collective-permute-start.10 = (f32[16,128]{1,0:T(8,128)S(1)}, f32[16,128]{1,0:T(8,128)S(1)}, u32[]{:S(2)}, u32[]{:S(2)}) collective-permute-start(f32[16,128]{1,0:T(8,128)S(1)} %get-tuple-element.35.refs_0_), channel_id=1, source_target_pairs={{0,4},{4,0},{1,5},{5,1},{2,6},{6,2},{3,7},{7,3},{8,12},{12,8},{9,1... | collective-permute-start | bytes 24584 | tf_op jit(solution)/shard_map/ppermute | solution.py:114

commit v4 on v3

--- a/solution.py
+++ b/solution.py
@@ -41,14 +41,18 @@
     return pltpu.roll(value, shift, axis=1)
 
 
-def vmem_call(name, kernel, outs, scratch, limit_mib, flops, moved, operands, spaces=None):
+def vmem_call(
+    name, kernel, outs, scratch, limit_mib, flops, moved, operands, spaces=None, direct=1 << 60
+):
     spaces = spaces or [pltpu.VMEM] * len(operands)
     return pl.pallas_call(
         kernel,
         name=name,
         out_shape=outs,
         in_specs=[pl.BlockSpec(memory_space=space) for space in spaces],
-        out_specs=jax.tree.map(lambda _: pl.BlockSpec(memory_space=pltpu.VMEM), outs),
+        out_specs=jax.tree.map(
+            lambda out: pl.BlockSpec(memory_space=pl.ANY if out.size >= direct else pltpu.VMEM), outs
+        ),
         scratch_shapes=scratch,
         compiler_params=pltpu.CompilerParams(vmem_limit_bytes=limit_mib << 20),
         cost_estimate=pl.CostEstimate(flops=flops, bytes_accessed=moved, transcendentals=0),
@@ -154,7 +158,7 @@
 
 
 def make_pieces(
-    sz, count, rank, basis_in, res_in, after, message, split, wide, basis_rows, res_rows, sem
+    sz, count, rank, basis_in, res_in, after, message, wide, basis_rows, res_rows, sem
 ):
     del after
     slots, loads = sz.slots, sz.loads
@@ -182,8 +186,6 @@
             tile = index * 2 + half
             comp = tile // sz.cells
             hi, lo = split_hi_lo(basis[pl.ds(tile, slots, stride=sz.tiles), :])
-            split[tile, pl.ds(0, slots), :] = hi
-            split[tile, pl.ds(slots, slots), :] = lo
             value_hi, value_lo = split_hi_lo(own_rows(sz, res, comp, tile - comp * sz.cells))
             basis_hi.append(hi)
             basis_lo.append(lo)
@@ -316,13 +318,28 @@
         out[pl.ds(comp * sz.loads, sz.loads), :] = total.astype(BF16)
 
 
-def place_pieces(sz, starts, gathered, inverse, message, vector, wide):
+def place_pieces(
+    sz, gathered, inverse, after, message, starts_out, vector, wide, heads, starts, sem
+):
+    del after
+    devices = gathered.shape[0]
+    for device in range(devices):
+        heads[pl.ds(device, 1), :] = gathered[device].astype(F32)[0:1]
+    values = heads[...]
+    ranks = jnp.transpose(values)[sz.slots + 1 : sz.slots + 2, :]
+    earlier = values[:, sz.slots + 1 : sz.slots + 2] < ranks
+    total = jnp.sum(jnp.where(earlier, values[:, sz.slots : sz.slots + 1], 0.0), axis=0, keepdims=True)
+    starts_out[...] = jnp.zeros_like(starts_out)
+    starts_out[:, pl.ds(0, devices)] = jnp.broadcast_to(total.astype(jnp.int32), (8, devices))
+    copy = pltpu.make_async_copy(starts_out, starts, sem)
+    copy.start()
     half = sz.loads // 2
     lane = lane_ids(half)
     vector[...] = jnp.zeros_like(vector)
+    copy.wait()
 
     def place(device, carry):
-        start = starts[device]
+        start = starts[0, device]
         block = start // LANES
         offset = start - block * LANES
         packed = gathered[device].astype(F32)
@@ -392,7 +409,7 @@
 
 
 def spread_row(ref, index, row):
-    return jnp.broadcast_to(ref[index, pl.ds(row, 1), :], (8, LANES))
+    return ref[index, pl.ds(row, 8, stride=0), :]
 
 
 def make_coefs(sz, table, id_box, halo_ids, coefs, halo_coefs, own, mu_box, halo_mu):
@@ -474,11 +491,19 @@
     return jnp.where(even, down, roll_lanes(up, -2))
 
 
-def solve_and_direct(sz, starts, count, table, res, id_box, coarse, split, *refs):
+def solve_and_direct(sz, count, table, starts_in, res, id_box, coarse, basis_in, *refs):
     xhalo, yhalo, zhalo, refs = take_halos(refs, "gx", "gy", "col")
     direction, own, zface = refs[:3]
     xsend, ysend, refs = take_halos(refs[3:], "gx", "gy")
-    first, second, third, halos, inner, coefs, halo_coefs, mu_box, halo_mu, left, zedge = refs
+    first, second, third, halos, inner, coefs, halo_coefs, mu_box, halo_mu, left, zedge = refs[:11]
+    basis_rows, starts, sem = refs[11:]
+    copies = [
+        pltpu.make_async_copy(starts_in, starts, sem.at[0]),
+        pltpu.make_async_copy(basis_in, basis_rows, sem.at[1]),
+    ]
+    for copy in copies:
+        copy.start()
+    basis = basis_rows.reshape(sz.slots * sz.tiles, LANES)
     loads, comps = sz.loads, sz.comps
     groups = loads // 8
     lane8 = lane_ids(8)
@@ -504,7 +529,7 @@
                 place = x * sz.by + y
                 row = (x + 1) * sz.pitch + y + 1
                 tile = box_tile(sz, res, xhalo, yhalo, comp, x, y)
-                value = tile * jnp.broadcast_to(coefs[DINV, pl.ds(row, 1), :], (loads, LANES))
+                value = tile * coefs[DINV, pl.ds(row, loads, stride=0), :]
                 first[comp, place] = value
                 here = (((lane_k + 1) >> 1) & 63) == place
                 total = jnp.where(here, roll_lanes(value, 2 * place), total)
@@ -570,7 +595,9 @@
     sweep(first, second, 0)
     sweep(second, third, 1)
 
-    mine = own_coefs(sz, coarse, starts[own_index()])
+    for copy in copies:
+        copy.wait()
+    mine = own_coefs(sz, coarse, starts[0, own_index()])
     mine = jnp.where(lane_ids(loads) < jnp.minimum(count[0], sz.slots), mine, 0.0)
     left[...] = paired_left(mine, sz.slots, left)
     zedge[...] = jnp.zeros_like(zedge)
@@ -582,8 +609,11 @@
         result = relax(third, 2, place, (x + 2) * sz.pitch + y + 2)
         for comp in range(comps):
             tile = comp * sz.cells + cell
+            both = split_hi_lo(basis[pl.ds(tile, sz.slots, stride=sz.tiles), :])
             part = jnp.dot(
-                left[:, : 2 * sz.slots], split[tile], preferred_element_type=F32
+                left[:, : 2 * sz.slots],
+                jnp.concatenate(both, axis=0),
+                preferred_element_type=F32,
             )
             for group in range(groups):
                 rows = pl.ds(group * 8, 8)
@@ -613,7 +643,7 @@
 
 def make_image(sz, res, own, direction, *refs):
     xhalo, yhalo, zhalo, refs = take_halos(refs, "gx", "gy", "col")
-    dir_split, image_split, message, box, halo, sem = refs
+    dir_out, image_out, message, box, halo, dir_split, image_split, sem, out_sem = refs
     loads, comps = sz.loads, sz.comps
     groups = loads // 8
     copies = []
@@ -683,15 +713,25 @@
             )
         return total
 
-    total = lax.fori_loop(
-        0, sz.cells, at, jnp.zeros((2 * loads, 4 * loads), F32), unroll=4
-    )
+    total = jnp.zeros((2 * loads, 4 * loads), F32)
+    copies = []
+    for x in range(sz.cx):
+        total = lax.fori_loop(x * sz.cy, (x + 1) * sz.cy, at, total, unroll=4)
+        for comp in range(comps):
+            part = pl.ds(comp * sz.cells + x * sz.cy, sz.cy)
+            for j, (source, out) in enumerate(((dir_split, dir_out), (image_split, image_out))):
+                copies.append(
+                    pltpu.make_async_copy(source.at[part], out.at[part], out_sem.at[j, comp, x])
+                )
+                copies[-1].start()
     high, low = total[:loads], total[loads:]
     sums = high + roll_lanes(high, -loads) + low
     half = loads // 2
     lane = lane_ids(half)
     packed = jnp.where((lane & (2 * loads - 1)) < loads, sums[:half], roll_lanes(sums[half:], loads))
     message[...] = packed
+    for copy in copies:
+        copy.wait()
 
 
 def share_sums(sz, mine, *refs):
@@ -703,10 +743,21 @@
         message[device] = total
 
 
-def finish(
-    sz, sums, iterate, res, dir_split, image_split, new_iterate, new_residual, parts
-):
+def finish(sz, sums, *refs):
+    sources, outs, refs = refs[:4], refs[4:6], refs[6:]
+    locals_in, (new_iterate, new_residual), (parts, sem, out_sem) = refs[:4], refs[4:6], refs[6:]
+    iterate, res, dir_split, image_split = locals_in
     loads = sz.loads
+    copies = []
+    for comp in range(sz.comps):
+        copies.append([])
+        for j, (source, target) in enumerate(zip(sources, locals_in)):
+            length = source.shape[0] // sz.comps
+            part = pl.ds(comp * length, length)
+            copies[comp].append(
+                pltpu.make_async_copy(source.at[part], target.at[part], sem.at[j, comp])
+            )
+            copies[comp][-1].start()
     total = sums[0]
     for device in range(1, sums.shape[0]):
         total = total + sums[device]
@@ -733,8 +784,12 @@
     ) else step
     left = paired_left(padded, loads, parts)[:, : 2 * loads]
 
-    def at(cell, carry):
-        for comp in range(sz.comps):
+    writes = []
+    for comp in range(sz.comps):
+        for copy in copies[comp]:
+            copy.wait()
+
+        def at(cell, carry, comp=comp):
             tile = comp * sz.cells + cell
             right = jnp.concatenate([dir_split[tile], image_split[tile]], axis=1)
             part = jnp.dot(left, right, preferred_element_type=F32)
@@ -742,9 +797,17 @@
             rows = pl.ds(comp * loads * sz.cells + cell, loads, stride=sz.cells)
             new_iterate[rows, :] = iterate[rows, :] + part[:, :LANES]
             new_residual[rows, :] = res[rows, :] - part[:, LANES:]
-        return carry
-
-    lax.fori_loop(0, sz.cells, at, 0, unroll=4)
+            return carry
+
+        lax.fori_loop(0, sz.cells, at, 0, unroll=8)
+        part = pl.ds(comp * loads * sz.cells, loads * sz.cells)
+        for j, (source, target) in enumerate(zip((new_iterate, new_residual), outs)):
+            writes.append(
+                pltpu.make_async_copy(source.at[part], target.at[part], out_sem.at[j, comp])
+            )
+            writes[-1].start()
+    for copy in writes:
+        copy.wait()
 
 
 def body(
@@ -771,7 +834,7 @@
         [face] * swaps("gx"),
         [scratch((sz.comps * sz.loads, sz.cy, LANES), F32)] * 2
         + [scratch((sz.cells, LANES), jnp.int32), dma((3,))],
-        8,
+        60,
         1 << 20,
         2 << 20,
         [residual.reshape(-1, sz.cells, LANES), ids],
@@ -779,26 +842,24 @@
     )
     xhalo = exchange(faces, "gx")
 
-    packed, split = call(
+    vectors = eigen_basis.reshape(sz.slots, sz.tiles, LANES)
+    packed = call(
         "pieces",
         make_pieces,
-        [
-            shape((sz.loads // 2, LANES), BF16),
-            shape((sz.tiles, 2 * sz.slots, LANES), BF16),
-        ],
+        shape((sz.loads // 2, LANES), BF16),
         [
             scratch((sz.loads, LANES), F32),
             scratch((sz.slots, sz.tiles, LANES), F32),
             scratch((sz.comps, sz.loads * sz.cells, LANES), F32),
             dma((2, sz.comps)),
         ],
-        12,
+        60,
         1 << 27,
         7 << 20,
         [
             eigen_counts,
             coarse_rank,
-            eigen_basis.reshape(sz.slots, sz.tiles, LANES),
+            vectors,
             residual.reshape(sz.comps, -1, LANES),
             faces[0],
         ],
@@ -818,11 +879,6 @@
     )
     yhalo = exchange(faces, "gy")
     gathered = lax.all_to_all(message, AXES, 0, 0, tiled=True)
-    all_counts = gathered[:, 0, sz.slots].astype(jnp.int32)
-    all_ranks = gathered[:, 0, sz.slots + 1].astype(jnp.int32)
-    starts = jnp.sum(
-        all_counts[None, :] * (all_ranks[None, :] < all_ranks[:, None]).astype(jnp.int32), axis=1
-    )
     rows = (sz.cx + 4) * sz.pitch
     zmessage, id_box = call(
         "pack_z",
@@ -839,19 +895,23 @@
     tile = (1, sz.loads // 2, LANES)
     if sz.block_rows != 64:
         tile = (sz.block_rows // LANES, sz.loads, LANES)
-    partial = call(
+    wide = (8, max(LANES, devices))
+    partial, starts = call(
         "coarse",
         place_pieces,
-        shape((blocks,) + tile, F32),
+        [shape((blocks,) + tile, F32), shape(wide, jnp.int32)],
         [
             scratch((sz.total_rows // LANES + 1, sz.loads, LANES), F32),
             scratch((sz.loads, LANES), F32),
+            scratch((devices, LANES), F32),
+            smem(wide, jnp.int32),
+            dma,
         ],
         12,
         1 << 23,
         1 << 20,
-        [starts, gathered, coarse_inverse],
-        spaces=[smem, vmem, vmem],
+        [gathered, coarse_inverse, zmessage],
+        spaces=[vmem, vmem, pl.ANY],
     )
     coarse = lax.all_to_all(partial, ("gx", "col"), 0, 0, tiled=True)
     coarse = coarse.reshape((-1,) + tile[1:])
@@ -879,12 +939,16 @@
             scratch((rows, LANES), F32),
             scratch((2 * sz.loads, LANES), BF16),
             scratch((sz.face_z, LANES), F32),
+            scratch((sz.slots, sz.tiles, LANES), F32),
+            smem(starts.shape, jnp.int32),
+            dma((2,)),
         ],
-        20,
+        56,
         1 << 28,
         8 << 20,
-        [starts, eigen_counts, materials, res, id_box, coarse, split] + xhalo + yhalo + zhalo,
-        spaces=[smem, smem, smem] + [vmem] * (4 + len(xhalo + yhalo + zhalo)),
+        [eigen_counts, materials, starts, res, id_box, coarse, vectors] + xhalo + yhalo + zhalo,
+        spaces=[smem, smem, pl.ANY, vmem, vmem, vmem, pl.ANY]
+        + [vmem] * len(xhalo + yhalo + zhalo),
     )
     xhalo = exchange(faces[: swaps("gx")], "gx")
     yhalo = exchange(faces[swaps("gx") :], "gy")
@@ -898,12 +962,20 @@
             shape((sz.tiles, 2 * sz.loads, LANES), BF16),
             shape(sums_shape, F32),
         ],
-        [field, scratch((sz.comps, sz.loads, LANES), F32), dma((sz.comps, sz.cx))],
-        16,
+        [
+            field,
+            scratch((sz.comps, sz.loads, LANES), F32),
+            scratch((sz.tiles, 2 * sz.loads, LANES), BF16),
+            scratch((sz.tiles, 2 * sz.loads, LANES), BF16),
+            dma((sz.comps, sz.cx)),
+            dma((2, sz.comps, sz.cx)),
+        ],
+        56,
         1 << 28,
         8 << 20,
         [res, own, direction] + xhalo + yhalo + zhalo,
         spaces=[vmem, vmem, pl.ANY] + [vmem] * len(xhalo + yhalo + zhalo),
+        direct=1 << 16,
     )
     over, operands = AXES, [sums]
     if lax.axis_size("gy") == 2:
@@ -920,11 +992,16 @@
         "finish",
         finish,
         [flat, flat],
-        [scratch((2 * sz.loads, LANES), BF16)],
-        16,
+        [scratch(res.shape, F32)] * 2
+        + [scratch(dir_split.shape, BF16)] * 2
+        + [scratch(res.shape, F32)] * 2
+        + [scratch((2 * sz.loads, LANES), BF16), dma((4, sz.comps)), dma((2, sz.comps))],
+        60,
         1 << 27,
         9 << 20,
         [sums, old, res, dir_split, image_split],
+        spaces=[vmem] + [pl.ANY] * 4,
+        direct=1 << 16,
     )
     return (new_iterate.reshape(iterate.shape), new_residual.reshape(residual.shape))
 

time: 106 us -> 111 us (1.047)
  blocking collectives: 29 us -> 16.1 us
  Pallas kernels: 37.6 us -> 48.7 us
  waiting for transfers between devices: 6.19 us -> 13.4 us
  starting transfers between devices: 22.2 us -> 26.5 us
  local copies, waits for them, and re-layouts: 6.9 us -> 3.39 us
  other arithmetic: 1.48 us -> 0 us
    all_to_all x1 -> x0, blocking collectives: 13 us -> none  [body(): gathered = lax.all_to_all(message, AXES, 0, 0, tiled=True)]
    pallas_call x9, Pallas kernels: 37.6 us -> 48.7 us  [vmem_call(): pl.pallas_call(kernel, name=name, out_shape=outs, in_specs=[pl.BlockSpec(...]
    all_to_all x0 -> x1, waiting for transfers between devices: none -> 4.99 us  [body(): gathered = lax.all_to_all(message, AXES, 0, 0, tiled=True)]
    all_to_all x0 -> x1, starting transfers between devices: none -> 4.84 us  [body(): gathered = lax.all_to_all(message, AXES, 0, 0, tiled=True)]
    unnamed x20 -> x36, local copies, waits for them, and re-layouts: 6.9 us -> 3.39 us
    ppermute x11, waiting for transfers between devices: 6.19 us -> 7.67 us  [exchange(): result.append(lax.ppermute(faces[parity], axis, pairs))]
    convert_element_type x1 -> x0, other arithmetic: 1.3 us -> none  [body(): all_ranks = gathered[:, 0, sz.slots + 1].astype(jnp.int32)]
  transfers between devices with their start and end apart: 12 -> 13, of which waited for: 4 -> 7; matrix products, arithmetic and copies ran while one was open for 0% -> 0% of each run, Pallas kernels for 6% -> 7%
where the time goes in v4:
time: 111 us; the launch traced here: 110 us
  Pallas kernels  48.7 us (44%)
  starting transfers between devices  26.5 us (24%)
  blocking collectives  16.1 us (15%)
  waiting for transfers between devices  13.4 us (12%)
  local copies, waits for them, and re-layouts  3.39 us (3%)
  between operations  2.17 us (2%)
    pallas_call x9, Pallas kernels, vmem_call(): pl.pallas_call(kernel, name=name, out_shape=outs, in_specs=[pl.BlockSpec(...  48.7 us
    ppermute x11, starting transfers between devices, exchange(): result.append(lax.ppermute(faces[parity], axis, pairs))  18.1 us
    all_to_all x1, blocking collectives, body(): sums = lax.all_to_all(spread, over, 0, 0, tiled=True)  16.1 us
    ppermute x11, waiting for transfers between devices, exchange(): result.append(lax.ppermute(faces[parity], axis, pairs))  7.67 us
    all_to_all x1, waiting for transfers between devices, body(): gathered = lax.all_to_all(message, AXES, 0, 0, tiled=True)  4.99 us
    all_to_all x1, starting transfers between devices, body(): gathered = lax.all_to_all(message, AXES, 0, 0, tiled=True)  4.84 us
    all_to_all x1, starting transfers between devices, body(): coarse = lax.all_to_all(partial, ('gx', 'col'), 0, 0, tiled=True)  3.52 us
    unnamed x36, local copies, waits for them, and re-layouts  3.39 us
  transfers between devices with their start and end apart: 13, of which 7 were waited for; matrix products, arithmetic and copies ran while one was open for 0% of the time, Pallas kernels for 7%

profile of v4, /device:TPU:0, one launch (start us, length us, event | category | flops | bytes accessed | tf_op | source)
XLA Modules:
  0.0 110.2 jit_solution(17780263768634970667)
XLA Ops:
  0.6 2.0 %pack_x.1 = (bf16[784,128]{1,0:T(8,128)(2,1)}, bf16[784,128]{1,0:T(8,128)(2,1)}) custom-call(f32[96,32,128]{2,1,0:T(8,128)} %bitcast.9, s32[32,128]{1,0:T(8,128)} %bitcast.16), custom_call_target="tpu_custom_call" | custom-call | flops 1048576 | bytes 2097152 | tf_op jit(solution)/shard_map/pack_x/pallas_call | solution.py:48
  2.7 0.7 collective-permute-start.1
  3.3 5.7 %collective-permute-start = (bf16[784,128]{1,0:T(8,128)(2,1)}, bf16[784,128]{1,0:T(8,128)(2,1)S(1)}, u32[]{:S(2)}, u32[]{:S(2)}) collective-permute-start(bf16[784,128]{1,0:T(8,128)(2,1)} %get-tuple-element.21.refs_4_), channel_id=1, source_target_pairs={{0,8},{8,0},{16,24},{24,16},{1,9},{9,1},{17,25},{25,17},{2,10},{10... | collective-permute-start | bytes 602120 | tf_op jit(solution)/shard_map/ppermute | solution.py:118
  10.4 0.0 copy-start
  10.4 0.0 copy-start.4
  10.4 6.5 %pieces.1.refs_2_ = bf16[16,128]{1,0:T(8,128)(2,1)} custom-call(s32[1]{0:T(128)S(6)} %copy.11.refs_0_, s32[1]{0:T(128)S(6)} %copy.12.refs_1_, f32[48,96,128]{2,1,0:T(8,128)} %bitcast.19, f32[3,1024,128]{2,1,0:T(8,128)} %bitcast.10, bf16[784,128]{1,0:T(8,128)(2,1)} %get-tuple-element.21.refs_4_), custom_call_target="tpu_custom_call" | custom-call | flops 134217728 | bytes 7340032 | tf_op jit(solution)/shard_map/pieces/pallas_call | solution.py:48
  16.9 0.0 collective-permute-done.1.refs_4_.refs_3_.refs_8_
  16.9 0.0 copy-start.1
  16.9 1.3 %collective-permute-done.refs_3_.refs_2_.refs_7_ = bf16[784,128]{1,0:T(8,128)(2,1)S(1)} collective-permute-done((bf16[784,128]{1,0:T(8,128)(2,1)}, bf16[784,128]{1,0:T(8,128)(2,1)S(1)}, u32[]{:S(2)}, u32[]{:S(2)}) %collective-permute-start) | collective-permute-done | bytes 200736 | tf_op jit(solution)/shard_map/ppermute | solution.py:118
  18.2 0.0 copy-done
  18.2 0.0 copy-done.4
  18.2 0.0 copy-start.7
  18.2 0.7 copy-done.7
  18.9 0.9 pack_y.1
  19.8 0.0 copy-start.5
  19.8 4.8 %all-to-all-start = ((bf16[32,16,128]{2,1,0:T(8,128)(2,1)}), bf16[32,16,128]{2,1,0:T(8,128)(2,1)S(1)}, u32[]{:S(2)}, u32[]{:S(2)}) async-start(bf16[32,16,128]{2,1,0:T(8,128)(2,1)} %get-tuple-element.23), calls=%async_computation | async-start | bytes 262144 | tf_op jit(solution)/shard_map/all_to_all | solution.py:881
  24.6 0.3 collective-permute-start.2
  24.9 1.1 %collective-permute-done.2.refs_4_.refs_9_ = bf16[592,128]{1,0:T(8,128)(2,1)S(1)} collective-permute-done((bf16[592,128]{1,0:T(8,128)(2,1)S(1)}, bf16[592,128]{1,0:T(8,128)(2,1)S(1)}, u32[]{:S(2)}, u32[]{:S(2)}) %collective-permute-start.2) | collective-permute-done | bytes 151584 | tf_op jit(solution)/shard_map/ppermute | solution.py:118
  26.1 0.0 copy-start.3
  26.1 1.3 %pack_z.1 = (bf16[112,128]{1,0:T(8,128)(2,1)S(1)}, f32[128,128]{1,0:T(8,128)S(1)}) custom-call(f32[3072,128]{1,0:T(8,128)S(1)} %bitcast.15, s32[32,128]{1,0:T(8,128)S(1)} %bitcast.18, bf16[784,128]{1,0:T(8,128)(2,1)S(1)} %collective-permute-done.refs_3_.refs_2_.refs_7_, bf16[784,128]{1,0:T(8,128)(2,1)S(1)} %collective-permute-done.1.refs_4_.refs_3_.refs_8_, ...), custom_call_target="tpu_custom_call" | custom-call | flops 4194304 | bytes 3145728 | tf_op jit(solution)/shard_map/pack_z/pallas_call | solution.py:48
  27.4 0.0 copy-done.1
  27.4 0.0 copy-done.2
  27.4 0.0 copy-start.6
  27.4 0.6 copy-done.6
  28.0 5.0 %all-to-all-done.refs_0_ = bf16[32,16,128]{2,1,0:T(8,128)(2,1)S(1)} async-done(((bf16[32,16,128]{2,1,0:T(8,128)(2,1)}), bf16[32,16,128]{2,1,0:T(8,128)(2,1)S(1)}, u32[]{:S(2)}, u32[]{:S(2)}) %all-to-all-start) | async-done | bytes 131104 | tf_op jit(solution)/shard_map/all_to_all | solution.py:881
  33.0 0.0 copy-done.5
  33.0 2.2 %coarse.1 = (f32[16,1,16,128]{3,2,1,0:T(8,128)}, s32[8,128]{1,0:T(8,128)S(1)}) custom-call(bf16[32,16,128]{2,1,0:T(8,128)(2,1)S(1)} %all-to-all-done.refs_0_, bf16[64,1024]{1,0:T(8,128)(2,1)S(1)} %copy-done.5, bf16[112,128]{1,0:T(8,128)(2,1)S(1)} %get-tuple-element.25.refs_2_), custom_call_target="tpu_custom_call" | custom-call | flops 8388608 | bytes 1048576 | tf_op jit(solution)/shard_map/coarse/pallas_call | solution.py:48
  35.3 0.0 copy-start.9
  35.3 3.5 %all-to-all-start.1 = ((f32[16,1,16,128]{3,2,1,0:T(8,128)}), f32[16,1,16,128]{3,2,1,0:T(8,128)S(1)}, u32[]{:S(2)}, u32[]{:S(2)}) async-start(f32[16,1,16,128]{3,2,1,0:T(8,128)} %get-tuple-element.28), calls=%async_computation.1 | async-start | bytes 262144 | tf_op jit(solution)/shard_map/all_to_all | solution.py:916
  38.8 0.7 collective-permute-start.4
  39.5 4.6 %collective-permute-start.3 = (bf16[112,128]{1,0:T(8,128)(2,1)S(1)}, bf16[112,128]{1,0:T(8,128)(2,1)S(1)}, u32[]{:S(2)}, u32[]{:S(2)}) collective-permute-start(bf16[112,128]{1,0:T(8,128)(2,1)S(1)} %get-tuple-element.25.refs_2_), channel_id=1, source_target_pairs={{0,1},{1,0},{2,3},{3,2},{4,5},{5,4},{6,7},{7,6},{8,9},{9,8},{10,11... | collective-permute-start | bytes 86024 | tf_op jit(solution)/shard_map/ppermute | solution.py:118
  44.0 0.0 collective-permute-done.4.refs_11_
  44.0 0.0 copy-start.14
  44.0 1.8 %collective-permute-done.3.refs_10_ = bf16[112,128]{1,0:T(8,128)(2,1)S(1)} collective-permute-done((bf16[112,128]{1,0:T(8,128)(2,1)S(1)}, bf16[112,128]{1,0:T(8,128)(2,1)S(1)}, u32[]{:S(2)}, u32[]{:S(2)}) %collective-permute-start.3) | collective-permute-done | bytes 28704 | tf_op jit(solution)/shard_map/ppermute | solution.py:118
  45.9 0.8 all-to-all-done.1
  46.7 0.0 copy-done.3
  46.7 0.0 copy-done.9
  46.7 0.0 copy-done.14
  46.7 0.0 copy-done.15
  46.7 0.6 copy-done.10
  47.3 18.7 %solve.1 = (f32[3,32,32,128]{3,2,1,0:T(8,128)}, f32[8,32,128]{2,1,0:T(8,128)}, bf16[96,128]{1,0:T(8,128)(2,1)}, bf16[768,128]{1,0:T(8,128)(2,1)}, bf16[768,128]{1,0:T(8,128)(2,1)}, /*index=5*/bf16[384,128]{1,0:T(8,128)(2,1)}) custom-call(s32[1]{0:T(128)S(6)} %copy.11.refs_0_, f32[2,16]{1,0:T(2,128)} %refs_1_.4, s32[8,128]{1,0:T(8,128)} %copy-done.9, ...), custom_call_target="tpu_custom_call" | custom-call | flops 268435456 | bytes 8388608 | tf_op jit(solution)/shard_map/solve/pallas_call | solution.py:48
  66.0 0.9 collective-permute-start.5
  66.9 0.7 collective-permute-start.6
  67.6 0.1 collective-permute-start.7
  67.7 0.7 collective-permute-start.9
  68.4 3.7 %collective-permute-start.8 = (bf16[96,128]{1,0:T(8,128)(2,1)}, bf16[96,128]{1,0:T(8,128)(2,1)S(1)}, u32[]{:S(2)}, u32[]{:S(2)}) collective-permute-start(bf16[96,128]{1,0:T(8,128)(2,1)} %get-tuple-element.34), channel_id=1, source_target_pairs={{0,1},{1,0},{2,3},{3,2},{4,5},{5,4},{6,7},{7,6},{8,9},{9,8},{10,11... | collective-permute-start | bytes 73736 | tf_op jit(solution)/shard_map/ppermute | solution.py:118
  72.1 0.0 collective-permute-done.9.refs_7_
  72.1 2.0 %collective-permute-done.8.refs_6_ = bf16[96,128]{1,0:T(8,128)(2,1)S(1)} collective-permute-done((bf16[96,128]{1,0:T(8,128)(2,1)}, bf16[96,128]{1,0:T(8,128)(2,1)S(1)}, u32[]{:S(2)}, u32[]{:S(2)}) %collective-permute-start.8) | collective-permute-done | bytes 24608 | tf_op jit(solution)/shard_map/ppermute | solution.py:118
  74.1 0.0 collective-permute-done.7.refs_5_
  74.1 0.0 collective-permute-done.5.refs_3_
  74.1 0.0 copy-start.11
  74.1 0.0 collective-permute-done.6.refs_4_
  74.2 0.0 copy-start.12
  74.2 0.0 copy-done.16
  74.2 0.5 copy-done.17
  74.7 0.0 copy-done.13
  74.8 0.1 copy-done.11
  74.8 0.1 copy-done.12
  74.9 8.7 %image.1 = (bf16[96,64,128]{2,1,0:T(8,128)(2,1)}, bf16[96,64,128]{2,1,0:T(8,128)(2,1)}, f32[16,128]{1,0:T(8,128)}) custom-call(f32[3072,128]{1,0:T(8,128)} %bitcast.12, f32[8,32,128]{2,1,0:T(8,128)} %get-tuple-element.29.refs_1_, f32[3,32,32,128]{3,2,1,0:T(8,128)} %get-tuple-element.30.refs_2_, bf16[768,128]{1,0:T(8,128)(2,1)} %copy-done.11, ...), custom_call_target="tpu_custom_call" | custom-call | flops 268435456 | bytes 8388608 | tf_op jit(solution)/shard_map/image/pallas_call | solution.py:48
  83.6 0.1 collective-permute-start.10
  83.7 1.4 %collective-permute-done.10.refs_1_ = f32[16,128]{1,0:T(8,128)S(1)} collective-permute-done((f32[16,128]{1,0:T(8,128)}, f32[16,128]{1,0:T(8,128)S(1)}, u32[]{:S(2)}, u32[]{:S(2)}) %collective-permute-start.10) | collective-permute-done | bytes 8224 | tf_op jit(solution)/shard_map/ppermute | solution.py:118
  85.1 0.7 copy-done.8
  85.8 16.1 %all_to_all.15.refs_0_ = f32[16,16,128]{2,1,0:T(8,128)} all-to-all(f32[16,16,128]{2,1,0:T(8,128)S(1)} %share_sums.1), channel_id=1, replica_groups=mesh['gx'=4,'gy'=2,'col'=4] {'gx','col'}, dimensions={0} | all-to-all | bytes 262144 | tf_op jit(solution)/shard_map/all_to_all | solution.py:989
  101.9 8.4 %finish.1 = (f32[3072,128]{1,0:T(8,128)}, f32[3072,128]{1,0:T(8,128)}) custom-call(f32[16,16,128]{2,1,0:T(8,128)} %all_to_all.15.refs_0_, f32[3072,128]{1,0:T(8,128)} %bitcast.21, f32[3072,128]{1,0:T(8,128)} %bitcast.13, bf16[96,64,128]{2,1,0:T(8,128)(2,1)} %get-tuple-element.36.refs_3_, bf16[96,64,128]{2,1,0:T(8,128)(2,1)} %get-tuple-element.37.refs_4_), custom_call_target="tpu_custom_call" | custom-call | flops 134217728 | bytes 9437184 | tf_op jit(solution)/shard_map/finish/pallas_call | solution.py:48
  (8 shorter events, 0.0 us)
Async XLA Ops:
  2.7 14.2 %collective-permute-start.1 = (bf16[784,128]{1,0:T(8,128)(2,1)}, bf16[784,128]{1,0:T(8,128)(2,1)S(1)}, u32[]{:S(2)}, u32[]{:S(2)}) collective-permute-start(bf16[784,128]{1,0:T(8,128)(2,1)} %get-tuple-element.22), channel_id=1, source_target_pairs={{8,16},{16,8},{9,17},{17,9},{10,18},{18,10},{11,19},{19,11},{12,20... | collective-permute-start | bytes 602120 | tf_op jit(solution)/shard_map/ppermute | solution.py:118
  3.3 14.9 %collective-permute-start = (bf16[784,128]{1,0:T(8,128)(2,1)}, bf16[784,128]{1,0:T(8,128)(2,1)S(1)}, u32[]{:S(2)}, u32[]{:S(2)}) collective-permute-start(bf16[784,128]{1,0:T(8,128)(2,1)} %get-tuple-element.21.refs_4_), channel_id=1, source_target_pairs={{0,8},{8,0},{16,24},{24,16},{1,9},{9,1},{17,25},{25,17},{2,10},{10... | collective-permute-start | bytes 602120 | tf_op jit(solution)/shard_map/ppermute | solution.py:118
  10.4 7.8 %copy-start = (f32[3,32,4,8,128]{4,3,2,1,0:T(8,128)S(1)}, f32[3,32,4,8,128]{4,3,2,1,0:T(8,128)}, u32[]{:S(2)}) copy-start(f32[3,32,4,8,128]{4,3,2,1,0:T(8,128)} %param.9) | copy-start | bytes 4718596
  10.4 7.8 %copy-start.4 = (s32[4,8,128]{2,1,0:T(8,128)S(1)}, s32[4,8,128]{2,1,0:T(8,128)}, u32[]{:S(2)}) copy-start(s32[4,8,128]{2,1,0:T(8,128)} %param.10) | copy-start | bytes 49156
  16.9 10.5 %copy-start.1 = (bf16[784,128]{1,0:T(8,128)(2,1)}, bf16[784,128]{1,0:T(8,128)(2,1)S(1)}, u32[]{:S(2)}) copy-start(bf16[784,128]{1,0:T(8,128)(2,1)S(1)} %collective-permute-done.1.refs_4_.refs_3_.refs_8_) | copy-start | bytes 602116
  18.2 9.2 %copy-start.2 = (bf16[784,128]{1,0:T(8,128)(2,1)}, bf16[784,128]{1,0:T(8,128)(2,1)S(1)}, u32[]{:S(2)}) copy-start(bf16[784,128]{1,0:T(8,128)(2,1)S(1)} %collective-permute-done.refs_3_.refs_2_.refs_7_) | copy-start | bytes 602116
  18.2 0.7 copy-start.7
  19.8 13.3 %copy-start.5 = (bf16[64,1024]{1,0:T(8,128)(2,1)S(1)}, bf16[64,1024]{1,0:T(8,128)(2,1)}, u32[]{:S(2)}) copy-start(bf16[64,1024]{1,0:T(8,128)(2,1)} %refs_1_.3) | copy-start | bytes 393220
  19.8 13.2 %all-to-all-start = ((bf16[32,16,128]{2,1,0:T(8,128)(2,1)}), bf16[32,16,128]{2,1,0:T(8,128)(2,1)S(1)}, u32[]{:S(2)}, u32[]{:S(2)}) async-start(bf16[32,16,128]{2,1,0:T(8,128)(2,1)} %get-tuple-element.23), calls=%async_computation | async-start | bytes 262144 | tf_op jit(solution)/shard_map/all_to_all | solution.py:881
  24.6 1.4 %collective-permute-start.2 = (bf16[592,128]{1,0:T(8,128)(2,1)S(1)}, bf16[592,128]{1,0:T(8,128)(2,1)S(1)}, u32[]{:S(2)}, u32[]{:S(2)}) collective-permute-start(bf16[592,128]{1,0:T(8,128)(2,1)S(1)} %get-tuple-element.24), channel_id=1, source_target_pairs={{0,4},{4,0},{1,5},{5,1},{2,6},{6,2},{3,7},{7,3},{8,12},{12,8},{9,1... | collective-permute-start | bytes 454664 | tf_op jit(solution)/shard_map/ppermute | solution.py:118
  26.1 20.6 %copy-start.3 = (bf16[592,128]{1,0:T(8,128)(2,1)}, bf16[592,128]{1,0:T(8,128)(2,1)S(1)}, u32[]{:S(2)}) copy-start(bf16[592,128]{1,0:T(8,128)(2,1)S(1)} %collective-permute-done.2.refs_4_.refs_9_) | copy-start | bytes 454660
  27.4 0.6 copy-start.6
  35.3 11.4 %copy-start.9 = (s32[8,128]{1,0:T(8,128)}, s32[8,128]{1,0:T(8,128)S(1)}, u32[]{:S(2)}) copy-start(s32[8,128]{1,0:T(8,128)S(1)} %get-tuple-element.26.refs_2_) | copy-start | bytes 12292
  35.3 11.4 %all-to-all-start.1 = ((f32[16,1,16,128]{3,2,1,0:T(8,128)}), f32[16,1,16,128]{3,2,1,0:T(8,128)S(1)}, u32[]{:S(2)}, u32[]{:S(2)}) async-start(f32[16,1,16,128]{3,2,1,0:T(8,128)} %get-tuple-element.28), calls=%async_computation.1 | async-start | bytes 262144 | tf_op jit(solution)/shard_map/all_to_all | solution.py:916
  38.8 5.2 %collective-permute-start.4 = (bf16[112,128]{1,0:T(8,128)(2,1)S(1)}, bf16[112,128]{1,0:T(8,128)(2,1)S(1)}, u32[]{:S(2)}, u32[]{:S(2)}) collective-permute-start(bf16[112,128]{1,0:T(8,128)(2,1)S(1)} %get-tuple-element.25.refs_2_), channel_id=1, source_target_pairs={{1,2},{2,1},{5,6},{6,5},{9,10},{10,9},{13,14},{14,13},{17,18},{18,... | collective-permute-start | bytes 86024 | tf_op jit(solution)/shard_map/ppermute | solution.py:118
  39.5 6.4 %collective-permute-start.3 = (bf16[112,128]{1,0:T(8,128)(2,1)S(1)}, bf16[112,128]{1,0:T(8,128)(2,1)S(1)}, u32[]{:S(2)}, u32[]{:S(2)}) collective-permute-start(bf16[112,128]{1,0:T(8,128)(2,1)S(1)} %get-tuple-element.25.refs_2_), channel_id=1, source_target_pairs={{0,1},{1,0},{2,3},{3,2},{4,5},{5,4},{6,7},{7,6},{8,9},{9,8},{10,11... | collective-permute-start | bytes 86024 | tf_op jit(solution)/shard_map/ppermute | solution.py:118
  44.0 2.6 %copy-start.14 = (bf16[112,128]{1,0:T(8,128)(2,1)}, bf16[112,128]{1,0:T(8,128)(2,1)S(1)}, u32[]{:S(2)}) copy-start(bf16[112,128]{1,0:T(8,128)(2,1)S(1)} %collective-permute-done.4.refs_11_) | copy-start | bytes 86020
  45.9 0.8 copy-start.15
  46.7 0.7 copy-start.10
  66.0 8.1 %collective-permute-start.5 = (bf16[768,128]{1,0:T(8,128)(2,1)}, bf16[768,128]{1,0:T(8,128)(2,1)S(1)}, u32[]{:S(2)}, u32[]{:S(2)}) collective-permute-start(bf16[768,128]{1,0:T(8,128)(2,1)} %get-tuple-element.31), channel_id=1, source_target_pairs={{0,8},{8,0},{16,24},{24,16},{1,9},{9,1},{17,25},{25,17},{2,10},{10... | collective-permute-start | bytes 589832 | tf_op jit(solution)/shard_map/ppermute | solution.py:118
  66.9 7.2 %collective-permute-start.6 = (bf16[768,128]{1,0:T(8,128)(2,1)}, bf16[768,128]{1,0:T(8,128)(2,1)S(1)}, u32[]{:S(2)}, u32[]{:S(2)}) collective-permute-start(bf16[768,128]{1,0:T(8,128)(2,1)} %get-tuple-element.32), channel_id=1, source_target_pairs={{8,16},{16,8},{9,17},{17,9},{10,18},{18,10},{11,19},{19,11},{12,20... | collective-permute-start | bytes 589832 | tf_op jit(solution)/shard_map/ppermute | solution.py:118
  67.6 6.5 %collective-permute-start.7 = (bf16[384,128]{1,0:T(8,128)(2,1)}, bf16[384,128]{1,0:T(8,128)(2,1)S(1)}, u32[]{:S(2)}, u32[]{:S(2)}) collective-permute-start(bf16[384,128]{1,0:T(8,128)(2,1)} %get-tuple-element.33), channel_id=1, source_target_pairs={{0,4},{4,0},{1,5},{5,1},{2,6},{6,2},{3,7},{7,3},{8,12},{12,8},{9,1... | collective-permute-start | bytes 294920 | tf_op jit(solution)/shard_map/ppermute | solution.py:118
  67.7 4.4 %collective-permute-start.9 = (bf16[96,128]{1,0:T(8,128)(2,1)}, bf16[96,128]{1,0:T(8,128)(2,1)S(1)}, u32[]{:S(2)}, u32[]{:S(2)}) collective-permute-start(bf16[96,128]{1,0:T(8,128)(2,1)} %get-tuple-element.34), channel_id=1, source_target_pairs={{1,2},{2,1},{5,6},{6,5},{9,10},{10,9},{13,14},{14,13},{17,18},{18,... | collective-permute-start | bytes 73736 | tf_op jit(solution)/shard_map/ppermute | solution.py:118
  68.4 5.8 %collective-permute-start.8 = (bf16[96,128]{1,0:T(8,128)(2,1)}, bf16[96,128]{1,0:T(8,128)(2,1)S(1)}, u32[]{:S(2)}, u32[]{:S(2)}) collective-permute-start(bf16[96,128]{1,0:T(8,128)(2,1)} %get-tuple-element.34), channel_id=1, source_target_pairs={{0,1},{1,0},{2,3},{3,2},{4,5},{5,4},{6,7},{7,6},{8,9},{9,8},{10,11... | collective-permute-start | bytes 73736 | tf_op jit(solution)/shard_map/ppermute | solution.py:118
  72.1 2.1 %copy-start.16 = (bf16[96,128]{1,0:T(8,128)(2,1)}, bf16[96,128]{1,0:T(8,128)(2,1)S(1)}, u32[]{:S(2)}) copy-start(bf16[96,128]{1,0:T(8,128)(2,1)S(1)} %collective-permute-done.9.refs_7_) | copy-start | bytes 73732
  74.1 0.6 copy-start.17
  74.1 0.6 copy-start.13
  74.1 0.7 copy-start.11
  74.2 0.7 copy-start.12
  83.6 1.4 %collective-permute-start.10 = (f32[16,128]{1,0:T(8,128)}, f32[16,128]{1,0:T(8,128)S(1)}, u32[]{:S(2)}, u32[]{:S(2)}) collective-permute-start(f32[16,128]{1,0:T(8,128)} %get-tuple-element.35.refs_0_), channel_id=1, source_target_pairs={{0,4},{4,0},{1,5},{5,1},{2,6},{6,2},{3,7},{7,3},{8,12},{12,8},{9,1... | collective-permute-start | bytes 24584 | tf_op jit(solution)/shard_map/ppermute | solution.py:118
  85.1 0.7 copy-start.8

commit v5 on v3

--- a/solution.py
+++ b/solution.py
@@ -316,13 +316,28 @@
         out[pl.ds(comp * sz.loads, sz.loads), :] = total.astype(BF16)
 
 
-def place_pieces(sz, starts, gathered, inverse, message, vector, wide):
+def place_pieces(
+    sz, gathered, inverse, after, message, starts_out, vector, wide, heads, starts, sem
+):
+    del after
+    devices = gathered.shape[0]
+    for device in range(devices):
+        heads[pl.ds(device, 1), :] = gathered[device].astype(F32)[0:1]
+    values = heads[...]
+    ranks = jnp.transpose(values)[sz.slots + 1 : sz.slots + 2, :]
+    earlier = values[:, sz.slots + 1 : sz.slots + 2] < ranks
+    total = jnp.sum(jnp.where(earlier, values[:, sz.slots : sz.slots + 1], 0.0), axis=0, keepdims=True)
+    starts_out[...] = jnp.zeros_like(starts_out)
+    starts_out[:, pl.ds(0, devices)] = jnp.broadcast_to(total.astype(jnp.int32), (8, devices))
+    copy = pltpu.make_async_copy(starts_out, starts, sem)
+    copy.start()
     half = sz.loads // 2
     lane = lane_ids(half)
     vector[...] = jnp.zeros_like(vector)
+    copy.wait()
 
     def place(device, carry):
-        start = starts[device]
+        start = starts[0, device]
         block = start // LANES
         offset = start - block * LANES
         packed = gathered[device].astype(F32)
@@ -392,7 +407,7 @@
 
 
 def spread_row(ref, index, row):
-    return jnp.broadcast_to(ref[index, pl.ds(row, 1), :], (8, LANES))
+    return ref[index, pl.ds(row, 8, stride=0), :]
 
 
 def make_coefs(sz, table, id_box, halo_ids, coefs, halo_coefs, own, mu_box, halo_mu):
@@ -468,95 +483,137 @@
         halo_coefs[target] = jnp.where(keep[j], dinv * faces[j], 0.0)
 
 
+def neighbour_matrix(copies, spread):
+    width = (3 if spread else 2) * LANES
+    parts = []
+    for copy in range(copies + 1):
+        row = lax.broadcasted_iota(jnp.int32, (LANES, width), 0)
+        lane = lax.broadcasted_iota(jnp.int32, (LANES, width), 1)
+        even = (row & 1) == 0
+        if copy < copies:
+            hit = ((lane < LANES) & (row == lane - 1)) | (
+                (lane >= LANES) & (lane < 2 * LANES) & (row == lane - LANES + 1)
+            )
+            if spread:
+                source = jnp.where((lane & 1) == 0, 0, LANES - 1)
+                hit = hit | ((lane >= 2 * LANES) & (row == source))
+        else:
+            hit = ((lane == 0) & even) | ((lane == 2 * LANES - 1) & jnp.logical_not(even))
+        parts.append(jnp.where(hit, 1.0, 0.0).astype(BF16))
+    return jnp.concatenate(parts, axis=0)
+
+
 def z_halo(zhalo, rows):
     down, up = zhalo.below(rows), zhalo.above(rows)
     even = (lane_ids(down.shape[0]) & 1) == 0
     return jnp.where(even, down, roll_lanes(up, -2))
 
 
-def solve_and_direct(sz, starts, count, table, res, id_box, coarse, split, *refs):
+def solve_and_direct(sz, count, table, starts_in, res, id_box, coarse, split, *refs):
     xhalo, yhalo, zhalo, refs = take_halos(refs, "gx", "gy", "col")
     direction, own, zface = refs[:3]
     xsend, ysend, refs = take_halos(refs[3:], "gx", "gy")
-    first, second, third, halos, inner, coefs, halo_coefs, mu_box, halo_mu, left, zedge = refs
+    first, second, third, halos, inner, coefs, halo_coefs, mu_box, halo_mu, left, zedge = refs[:11]
+    wide, own_rows_coef, weights, lhs, near, starts, sem = refs[11:]
+    copy = pltpu.make_async_copy(starts_in, starts, sem)
+    copy.start()
     loads, comps = sz.loads, sz.comps
     groups = loads // 8
     lane8 = lane_ids(8)
 
     halo_mu[...] = jnp.zeros_like(halo_mu)
-    inner[1] = jnp.zeros((comps, loads, LANES), F32)
+    inner[...] = jnp.zeros_like(inner)
     make_coefs(
-        sz, table, id_box, z_halo(zhalo, pl.ds(sz.face_z, HALO_IDS))[:8], coefs, halo_coefs, own,
+        sz, table, id_box, z_halo(zhalo, pl.ds(sz.face_z, HALO_IDS))[:8], coefs, halo_coefs, own_rows_coef,
         mu_box, halo_mu,
     )
 
-    def here_of(place):
-        return (((lane8 + 1) >> 1) & 63) == place
+    weights[...] = neighbour_matrix(1, True)
+
+    def spread(place, carry):
+        x = place // sz.by
+        row = (x + 1) * sz.pitch + place - x * sz.by + 1
+        for j in range(9):
+            wide[j, place] = jnp.broadcast_to(coefs[j, pl.ds(row, 1), :], (8, LANES))
+        return carry
+
+    lax.fori_loop(0, sz.box, spread, 0, unroll=4)
+
+    def spread_own(cell, carry):
+        for j in range(8):
+            own[j, cell] = jnp.broadcast_to(own_rows_coef[j, pl.ds(cell, 1), :], (8, LANES))
+        return carry
+
+    lax.fori_loop(0, sz.cells, spread_own, 0, unroll=4)
 
     for comp in range(comps):
         halo = z_halo(zhalo, pl.ds(comp * loads, loads))
         dinv = jnp.concatenate([halo_coefs[DINV]] * groups, axis=0)
         halos[0, comp] = dinv * halo
-        total = jnp.zeros((loads, LANES), F32)
-        lane_k = lane_ids(loads)
         for x in range(sz.bx):
             for y in range(sz.by):
                 place = x * sz.by + y
-                row = (x + 1) * sz.pitch + y + 1
                 tile = box_tile(sz, res, xhalo, yhalo, comp, x, y)
-                value = tile * jnp.broadcast_to(coefs[DINV, pl.ds(row, 1), :], (loads, LANES))
-                first[comp, place] = value
-                here = (((lane_k + 1) >> 1) & 63) == place
-                total = jnp.where(here, roll_lanes(value, 2 * place), total)
-        inner[0, comp] = total
-
-    def relax(source, level, place, row):
-        coef = [spread_row(coefs, j, row) for j in range(9)]
-        xm, xp = jnp.maximum(place - sz.by, 0), jnp.minimum(place + sz.by, sz.box - 1)
-        ym, yp = jnp.maximum(place - 1, 0), jnp.minimum(place + 1, sz.box - 1)
-        back = lax.rem(LANES - 2 * place + LANES, LANES)
-        result = {}
-        for group in range(groups):
-            rows = pl.ds(group * 8, 8)
-            center = [source[comp, place, rows, :] for comp in range(comps)]
-            coupled = coef[DLAM] * sum(center)
+                first[comp, place] = tile * jnp.concatenate([wide[DINV, place]] * groups, axis=0)
+
+    lane_k = lane_ids(loads)
+
+    def relax(source, level, x, ys, put):
+        count = len(ys)
+        for j, y in enumerate(ys):
+            place = x * sz.by + y
+            here = (((lane_k + 1) >> 1) & 63) == place
             for comp in range(comps):
-                value = center[comp]
-                edge = pltpu.roll(halos[level, comp, rows, :], back, axis=1)
-                zm = jnp.where(lane8 == 0, edge, roll_lanes(value, 1))
-                zp = jnp.where(lane8 == LANES - 1, edge, roll_lanes(value, -1))
-                out = (first[comp, place, rows, :] - coupled) + coef[KEEP] * value
-                out = out + coef[WXM] * source[comp, xm, rows, :]
-                out = out + coef[WXP] * source[comp, xp, rows, :]
-                out = out + coef[WYM] * source[comp, ym, rows, :]
-                out = out + coef[WYP] * source[comp, yp, rows, :]
-                out = out + coef[WZM] * zm
-                out = out + coef[WZP] * zp
-                result[comp, group] = out
-        return result
+                rows = pl.ds((j * comps + comp) * loads, loads)
+                lhs[rows, pl.ds(0, LANES)] = source[comp, place].astype(BF16)
+                lhs[rows, pl.ds(LANES, LANES)] = jnp.where(here, halos[level, comp], 0.0).astype(BF16)
+        size = count * comps * loads
+        cut = 3 * LANES if level < 2 else 2 * LANES
+        near[pl.ds(0, size), pl.ds(0, cut)] = jnp.dot(
+            lhs[pl.ds(0, size), :], weights[:, pl.ds(0, cut)], preferred_element_type=F32
+        )
+        for j, y in enumerate(ys):
+            place = x * sz.by + y
+            coef = [wide[i, place] for i in range(9)]
+            here = (((lane8 + 1) >> 1) & 63) == place
+            xm, xp = jnp.maximum(place - sz.by, 0), jnp.minimum(place + sz.by, sz.box - 1)
+            ym, yp = jnp.maximum(place - 1, 0), jnp.minimum(place + 1, sz.box - 1)
+            for group in range(groups):
+                rows = pl.ds(group * 8, 8)
+                center = [source[comp, place, rows, :] for comp in range(comps)]
+                coupled = coef[DLAM] * (center[0] + center[1] + center[2])
+                for comp in range(comps):
+                    value = center[comp]
+                    at = pl.ds((j * comps + comp) * loads + group * 8, 8)
+                    out = (first[comp, place, rows, :] - coupled) + coef[KEEP] * value
+                    out = out + coef[WXM] * source[comp, xm, rows, :]
+                    out = out + coef[WXP] * source[comp, xp, rows, :]
+                    out = out + coef[WYM] * source[comp, ym, rows, :]
+                    out = out + coef[WYP] * source[comp, yp, rows, :]
+                    out = out + coef[WZM] * near[at, pl.ds(0, LANES)]
+                    out = out + coef[WZP] * near[at, pl.ds(LANES, LANES)]
+                    put(j, place, comp, group, out)
+                    if level < 2:
+                        pltpu.store(
+                            inner.at[level, comp, rows, :],
+                            near[at, pl.ds(2 * LANES, LANES)],
+                            mask=here,
+                        )
 
     def sweep(source, target, level):
-        def at(place, carry):
-            x = place // sz.by
-            row = (x + 1) * sz.pitch + place - x * sz.by + 1
-            result = relax(source, level, place, row)
-            for (comp, group), out in result.items():
-                rows = pl.ds(group * 8, 8)
-                target[comp, place, rows, :] = out
-                if level == 0:
-                    pltpu.store(
-                        inner.at[1, comp, rows, :],
-                        pltpu.roll(out, 2 * place, axis=1),
-                        mask=here_of(place),
-                    )
+        def put(j, place, comp, group, out):
+            target[comp, place, pl.ds(group * 8, 8), :] = out
+
+        def at(x, carry):
+            relax(source, level, x, range(sz.by), put)
             return carry
 
-        lax.fori_loop(0, sz.box, at, 0, unroll=6)
+        lax.fori_loop(0, sz.bx, at, 0)
         coef = [halo_coefs[j] for j in range(8)]
         for group in range(groups):
             rows = pl.ds(group * 8, 8)
             center = [halos[level, comp, rows, :] for comp in range(comps)]
-            coupled = coef[DLAM] * sum(center)
+            coupled = coef[DLAM] * (center[0] + center[1] + center[2])
             for comp in range(comps):
                 value = center[comp]
                 out = (halos[0, comp, rows, :] - coupled) + coef[KEEP] * value
@@ -570,37 +627,47 @@
     sweep(first, second, 0)
     sweep(second, third, 1)
 
-    mine = own_coefs(sz, coarse, starts[own_index()])
+    copy.wait()
+    mine = own_coefs(sz, coarse, starts[0, own_index()])
     mine = jnp.where(lane_ids(loads) < jnp.minimum(count[0], sz.slots), mine, 0.0)
     left[...] = paired_left(mine, sz.slots, left)
     zedge[...] = jnp.zeros_like(zedge)
 
-    def final(cell, carry):
-        x = cell // sz.cy
-        y = cell - x * sz.cy
-        place = (x + 1) * sz.by + y + 1
-        result = relax(third, 2, place, (x + 2) * sz.pitch + y + 2)
-        for comp in range(comps):
-            tile = comp * sz.cells + cell
-            part = jnp.dot(
-                left[:, : 2 * sz.slots], split[tile], preferred_element_type=F32
-            )
-            for group in range(groups):
-                rows = pl.ds(group * 8, 8)
-                value = result[comp, group] + (
-                    part[group * 8 : group * 8 + 8]
-                    + part[loads + group * 8 : loads + group * 8 + 8]
+    def final(x, carry):
+        def put(j, place, comp, group, out):
+            direction[comp, x * sz.cy + j, pl.ds(group * 8, 8), :] = out
+
+        relax(third, 2, x + 1, range(1, sz.cy + 1), put)
+        for y in range(sz.cy):
+            cell = x * sz.cy + y
+            place = (x + 1) * sz.by + y + 1
+            for comp in range(comps):
+                part = jnp.dot(
+                    left[:, : 2 * sz.slots],
+                    split[comp * sz.cells + cell],
+                    preferred_element_type=F32,
                 )
-                direction[comp, cell, rows, :] = value
-                zrows = pl.ds(comp * loads + group * 8, 8)
+                value = direction[comp, cell] + (part[:loads] + part[loads:])
+                direction[comp, cell] = value
+                lhs[pl.ds((y * comps + comp) * loads, loads), pl.ds(0, LANES)] = value.astype(BF16)
+        size = sz.cy * comps * loads
+        near[pl.ds(0, size), pl.ds(0, LANES)] = jnp.dot(
+            lhs[pl.ds(0, size), pl.ds(0, LANES)], edges, preferred_element_type=F32
+        )
+        for y in range(sz.cy):
+            place = (x + 1) * sz.by + y + 1
+            for comp in range(comps):
                 pltpu.store(
-                    zedge.at[zrows, :],
-                    pltpu.roll(value, 2 * place + 1, axis=1),
-                    mask=(lane8 >> 1) == place,
+                    zedge.at[pl.ds(comp * loads, loads), :],
+                    near[pl.ds((y * comps + comp) * loads, loads), pl.ds(0, LANES)],
+                    mask=(lane_k >> 1) == place,
                 )
         return carry
 
-    lax.fori_loop(0, sz.cells, final, 0, unroll=4)
+    edge_row = lax.broadcasted_iota(jnp.int32, (LANES, LANES), 0)
+    even_lane = (lane_ids(LANES) & 1) == 0
+    edges = jnp.where(jnp.where(even_lane, LANES - 1, 0) == edge_row, 1.0, 0.0).astype(BF16)
+    lax.fori_loop(0, sz.cx, final, 0)
     zface[...] = zedge[...].astype(BF16)
     for comp in range(comps):
         for y in range(sz.cy):
@@ -613,7 +680,8 @@
 
 def make_image(sz, res, own, direction, *refs):
     xhalo, yhalo, zhalo, refs = take_halos(refs, "gx", "gy", "col")
-    dir_split, image_split, message, box, halo, sem = refs
+    dir_split, image_split, message, box, halo, weights, lhs, near, sem = refs
+    weights[...] = neighbour_matrix(2, False)
     loads, comps = sz.loads, sz.comps
     groups = loads // 8
     copies = []
@@ -640,52 +708,57 @@
         halo[comp] = z_halo(zhalo, pl.ds(comp * loads, loads))
     for copy in copies:
         copy.wait()
-    lane8 = lane_ids(8)
-
-    def at(cell, total):
-        x = cell // sz.cy
-        y = cell - x * sz.cy
-        place = (x + 1) * sz.by + y + 1
-        back = lax.rem(LANES - 2 * place + LANES, LANES)
-        coef = [spread_row(own, j, cell) for j in range(8)]
-        parts = {}
-        for group in range(groups):
-            rows = pl.ds(group * 8, 8)
-            center = [box[comp, place, rows, :] for comp in range(comps)]
-            coupled = coef[1] * sum(center)
+    lane_k = lane_ids(loads)
+
+    def at(x, total):
+        for y in range(sz.cy):
+            cell = x * sz.cy + y
+            place = (x + 1) * sz.by + y + 1
+            here = (((lane_k + 1) >> 1) & 63) == place
             for comp in range(comps):
-                value = center[comp]
-                edge = pltpu.roll(halo[comp, rows, :], back, axis=1)
-                zm = jnp.where(lane8 == 0, edge, roll_lanes(value, 1))
-                zp = jnp.where(lane8 == LANES - 1, edge, roll_lanes(value, -1))
-                out = coef[0] * value + coupled
-                out = out - coef[2] * box[comp, place - sz.by, rows, :]
-                out = out - coef[3] * box[comp, place + sz.by, rows, :]
-                out = out - coef[4] * box[comp, place - 1, rows, :]
-                out = out - coef[5] * box[comp, place + 1, rows, :]
-                out = out - coef[6] * zm
-                parts[comp, group] = out - coef[7] * zp
-        for comp in range(comps):
-            tile = comp * sz.cells + cell
-            dir_hi, dir_lo = split_hi_lo(box[comp, place])
-            field = jnp.concatenate([parts[comp, group] for group in range(groups)], axis=0)
-            field_hi, field_lo = split_hi_lo(field)
-            res_hi, res_lo = split_hi_lo(own_rows(sz, res, comp, cell))
-            left = jnp.concatenate([dir_hi, dir_lo], axis=0)
-            field_both = jnp.concatenate([field_hi, field_lo], axis=0)
-            dir_split[tile] = left
-            image_split[tile] = field_both
-            total = total + lax.dot_general(
-                left,
-                jnp.concatenate([field_both, res_hi, res_lo], axis=0),
-                TRANSPOSED,
-                preferred_element_type=F32,
-            )
+                hi, lo = split_hi_lo(box[comp, place])
+                dir_split[comp * sz.cells + cell] = jnp.concatenate([hi, lo], axis=0)
+                rows = pl.ds((y * comps + comp) * loads, loads)
+                lhs[rows, pl.ds(0, LANES)] = hi
+                lhs[rows, pl.ds(LANES, LANES)] = lo
+                lhs[rows, pl.ds(2 * LANES, LANES)] = jnp.where(here, halo[comp], 0.0).astype(BF16)
+        near[...] = jnp.dot(lhs[...], weights[...], preferred_element_type=F32)
+        sides = {}
+        for y in range(sz.cy):
+            cell = x * sz.cy + y
+            place = (x + 1) * sz.by + y + 1
+            coef = [own[j, cell] for j in range(8)]
+            parts = {}
+            for group in range(groups):
+                rows = pl.ds(group * 8, 8)
+                center = [box[comp, place, rows, :] for comp in range(comps)]
+                coupled = coef[1] * (center[0] + center[1] + center[2])
+                for comp in range(comps):
+                    line = pl.ds((y * comps + comp) * loads + group * 8, 8)
+                    out = coef[0] * center[comp] + coupled
+                    out = out - coef[2] * box[comp, place - sz.by, rows, :]
+                    out = out - coef[3] * box[comp, place + sz.by, rows, :]
+                    out = out - coef[4] * box[comp, place - 1, rows, :]
+                    out = out - coef[5] * box[comp, place + 1, rows, :]
+                    out = out - coef[6] * near[line, pl.ds(0, LANES)]
+                    parts[comp, group] = out - coef[7] * near[line, pl.ds(LANES, LANES)]
+            for comp in range(comps):
+                tile = comp * sz.cells + cell
+                field = jnp.concatenate([parts[comp, group] for group in range(groups)], axis=0)
+                both = jnp.concatenate(split_hi_lo(field), axis=0)
+                image_split[tile] = both
+                right = jnp.concatenate((both,) + split_hi_lo(own_rows(sz, res, comp, cell)), axis=0)
+                sides[y, comp] = (dir_split[tile], right)
+            if y % 2 == 1:
+                for comp in range(comps):
+                    pair = zip(sides[y - 1, comp], sides[y, comp])
+                    left, right = (jnp.concatenate(items, axis=1) for items in pair)
+                    total = total + lax.dot_general(
+                        left, right, TRANSPOSED, preferred_element_type=F32
+                    )
         return total
 
-    total = lax.fori_loop(
-        0, sz.cells, at, jnp.zeros((2 * loads, 4 * loads), F32), unroll=4
-    )
+    total = lax.fori_loop(0, sz.cx, at, jnp.zeros((2 * loads, 4 * loads), F32))
     high, low = total[:loads], total[loads:]
     sums = high + roll_lanes(high, -loads) + low
     half = loads // 2
@@ -818,11 +891,6 @@
     )
     yhalo = exchange(faces, "gy")
     gathered = lax.all_to_all(message, AXES, 0, 0, tiled=True)
-    all_counts = gathered[:, 0, sz.slots].astype(jnp.int32)
-    all_ranks = gathered[:, 0, sz.slots + 1].astype(jnp.int32)
-    starts = jnp.sum(
-        all_counts[None, :] * (all_ranks[None, :] < all_ranks[:, None]).astype(jnp.int32), axis=1
-    )
     rows = (sz.cx + 4) * sz.pitch
     zmessage, id_box = call(
         "pack_z",
@@ -839,19 +907,23 @@
     tile = (1, sz.loads // 2, LANES)
     if sz.block_rows != 64:
         tile = (sz.block_rows // LANES, sz.loads, LANES)
-    partial = call(
+    wide = (8, max(LANES, devices))
+    partial, starts = call(
         "coarse",
         place_pieces,
-        shape((blocks,) + tile, F32),
+        [shape((blocks,) + tile, F32), shape(wide, jnp.int32)],
         [
             scratch((sz.total_rows // LANES + 1, sz.loads, LANES), F32),
             scratch((sz.loads, LANES), F32),
+            scratch((devices, LANES), F32),
+            smem(wide, jnp.int32),
+            dma,
         ],
         12,
         1 << 23,
         1 << 20,
-        [starts, gathered, coarse_inverse],
-        spaces=[smem, vmem, vmem],
+        [gathered, coarse_inverse, zmessage],
+        spaces=[vmem, vmem, pl.ANY],
     )
     coarse = lax.all_to_all(partial, ("gx", "col"), 0, 0, tiled=True)
     coarse = coarse.reshape((-1,) + tile[1:])
@@ -862,7 +934,7 @@
         solve_and_direct,
         [
             shape((sz.comps, sz.cells, sz.loads, LANES), F32),
-            shape((8, sz.cells, LANES), F32),
+            shape((8, sz.cells, 8, LANES), F32),
             shape((sz.face_z, LANES), BF16),
         ]
         + [shape((sz.face_x, LANES), BF16)] * swaps("gx")
@@ -879,12 +951,19 @@
             scratch((rows, LANES), F32),
             scratch((2 * sz.loads, LANES), BF16),
             scratch((sz.face_z, LANES), F32),
+            scratch((9, sz.box, 8, LANES), F32),
+            scratch((8, sz.cells, LANES), F32),
+            scratch((2 * LANES, 3 * LANES), BF16),
+            scratch((sz.by * sz.comps * sz.loads, 2 * LANES), BF16),
+            scratch((sz.by * sz.comps * sz.loads, 3 * LANES), F32),
+            smem(starts.shape, jnp.int32),
+            dma,
         ],
-        20,
+        26,
         1 << 28,
         8 << 20,
-        [starts, eigen_counts, materials, res, id_box, coarse, split] + xhalo + yhalo + zhalo,
-        spaces=[smem, smem, smem] + [vmem] * (4 + len(xhalo + yhalo + zhalo)),
+        [eigen_counts, materials, starts, res, id_box, coarse, split] + xhalo + yhalo + zhalo,
+        spaces=[smem, smem, pl.ANY] + [vmem] * (4 + len(xhalo + yhalo + zhalo)),
     )
     xhalo = exchange(faces[: swaps("gx")], "gx")
     yhalo = exchange(faces[swaps("gx") :], "gy")
@@ -898,8 +977,15 @@
             shape((sz.tiles, 2 * sz.loads, LANES), BF16),
             shape(sums_shape, F32),
         ],
-        [field, scratch((sz.comps, sz.loads, LANES), F32), dma((sz.comps, sz.cx))],
-        16,
+        [
+            field,
+            scratch((sz.comps, sz.loads, LANES), F32),
+            scratch((3 * LANES, 2 * LANES), BF16),
+            scratch((sz.cy * sz.comps * sz.loads, 3 * LANES), BF16),
+            scratch((sz.cy * sz.comps * sz.loads, 2 * LANES), F32),
+            dma((sz.comps, sz.cx)),
+        ],
+        20,
         1 << 28,
         8 << 20,
         [res, own, direction] + xhalo + yhalo + zhalo,

time: 106 us -> 99.1 us (0.935)
  blocking collectives: 29 us -> 16 us
  waiting for transfers between devices: 6.19 us -> 12.4 us
  starting transfers between devices: 22.2 us -> 26.6 us
  Pallas kernels: 37.6 us -> 34.7 us
  other arithmetic: 1.48 us -> 0 us
    all_to_all x1 -> x0, blocking collectives: 13 us -> none  [body(): gathered = lax.all_to_all(message, AXES, 0, 0, tiled=True)]
    all_to_all x0 -> x1, waiting for transfers between devices: none -> 5.62 us  [body(): gathered = lax.all_to_all(message, AXES, 0, 0, tiled=True)]
    all_to_all x0 -> x1, starting transfers between devices: none -> 4.84 us  [body(): gathered = lax.all_to_all(message, AXES, 0, 0, tiled=True)]
    pallas_call x9, Pallas kernels: 37.6 us -> 34.7 us  [vmem_call(): pl.pallas_call(kernel, name=name, out_shape=outs, in_specs=[pl.BlockSpec(...]
    convert_element_type x1 -> x0, other arithmetic: 1.3 us -> none  [body(): all_ranks = gathered[:, 0, sz.slots + 1].astype(jnp.int32)]
  transfers between devices with their start and end apart: 12 -> 13, of which waited for: 4 -> 6; matrix products, arithmetic and copies ran while one was open for 0% -> 0% of each run, Pallas kernels for 6% -> 6%
where the time goes in v5:
time: 99.1 us; the launch traced here: 98.6 us
  Pallas kernels  34.7 us (35%)
  starting transfers between devices  26.6 us (27%)
  blocking collectives  16 us (16%)
  waiting for transfers between devices  12.4 us (13%)
  local copies, waits for them, and re-layouts  6.87 us (7%)
  between operations  2.1 us (2%)
    pallas_call x9, Pallas kernels, vmem_call(): pl.pallas_call(kernel, name=name, out_shape=outs, in_specs=[pl.BlockSpec(...  34.7 us
    ppermute x11, starting transfers between devices, exchange(): result.append(lax.ppermute(faces[parity], axis, pairs))  18.2 us
    all_to_all x1, blocking collectives, body(): sums = lax.all_to_all(spread, over, 0, 0, tiled=True)  16 us
    unnamed x20, local copies, waits for them, and re-layouts  6.87 us
    ppermute x11, waiting for transfers between devices, exchange(): result.append(lax.ppermute(faces[parity], axis, pairs))  5.95 us
    all_to_all x1, waiting for transfers between devices, body(): gathered = lax.all_to_all(message, AXES, 0, 0, tiled=True)  5.62 us
    all_to_all x1, starting transfers between devices, body(): gathered = lax.all_to_all(message, AXES, 0, 0, tiled=True)  4.84 us
    all_to_all x1, starting transfers between devices, body(): coarse = lax.all_to_all(partial, ('gx', 'col'), 0, 0, tiled=True)  3.52 us
  transfers between devices with their start and end apart: 13, of which 6 were waited for; matrix products, arithmetic and copies ran while one was open for 0% of the time, Pallas kernels for 6%

profile of v5, /device:TPU:0, one launch (start us, length us, event | category | flops | bytes accessed | tf_op | source)
XLA Modules:
  0.0 98.6 jit_solution(10540987986995229040)
XLA Ops:
  0.6 0.0 copy-start
  0.6 1.4 %copy-done = f32[3,32,4,8,128]{4,3,2,1,0:T(8,128)S(1)} copy-done((f32[3,32,4,8,128]{4,3,2,1,0:T(8,128)S(1)}, f32[3,32,4,8,128]{4,3,2,1,0:T(8,128)}, u32[]{:S(2)}) %copy-start) | copy-done | bytes 1572888
  2.0 0.0 copy-start.6
  2.0 0.7 copy-done.6
  2.8 0.0 copy-start.1
  2.8 0.3 pack_x.1
  3.0 0.8 collective-permute-start.1
  3.9 5.7 %collective-permute-start = (bf16[784,128]{1,0:T(8,128)(2,1)S(1)}, bf16[784,128]{1,0:T(8,128)(2,1)S(1)}, u32[]{:S(2)}, u32[]{:S(2)}) collective-permute-start(bf16[784,128]{1,0:T(8,128)(2,1)S(1)} %get-tuple-element.23.refs_4_), channel_id=1, source_target_pairs={{0,8},{8,0},{16,24},{24,16},{1,9},{9,1},{17,25},{25,17},{2,10},{10... | collective-permute-start | bytes 602120 | tf_op jit(solution)/shard_map/ppermute | solution.py:114
  10.9 0.0 copy-done.1
  10.9 0.0 copy-start.2
  10.9 1.7 %copy-done.2 = f32[48,3,4,8,128]{4,3,2,1,0:T(8,128)S(1)} copy-done((f32[48,3,4,8,128]{4,3,2,1,0:T(8,128)S(1)}, f32[48,3,4,8,128]{4,3,2,1,0:T(8,128)}, u32[]{:S(2)}) %copy-start.2) | copy-done | bytes 2359320
  12.6 0.0 copy-start.7
  12.6 4.5 %pieces.1 = (bf16[16,128]{1,0:T(8,128)(2,1)S(1)}, bf16[96,96,128]{2,1,0:T(8,128)(2,1)S(1)}) custom-call(s32[1]{0:T(128)S(6)} %copy.11.refs_0_, s32[1]{0:T(128)S(6)} %copy.12.refs_1_, f32[48,96,128]{2,1,0:T(8,128)S(1)} %bitcast.16, f32[3,1024,128]{2,1,0:T(8,128)S(1)} %bitcast.10, bf16[784,128]{1,0:T(8,128)(2,1)S(1)} %get-tuple-element.23.refs_4_), custom_call_target="tpu_custom_call" | custom-call | flops 134217728 | bytes 7340032 | tf_op jit(solution)/shard_map/pieces/pallas_call | solution.py:46
  17.1 0.0 copy-start.3
  17.1 1.4 %copy-done.3 = bf16[96,96,128]{2,1,0:T(8,128)(2,1)} copy-done((bf16[96,96,128]{2,1,0:T(8,128)(2,1)}, bf16[96,96,128]{2,1,0:T(8,128)(2,1)S(1)}, u32[]{:S(2)}) %copy-start.3) | copy-done | bytes 2359320
  18.5 0.0 collective-permute-done.1.refs_4_.refs_3_.refs_8_
  18.5 0.0 collective-permute-done.refs_3_.refs_2_.refs_7_
  18.5 0.0 copy-done.7
  18.5 0.9 pack_y.1
  19.4 0.0 copy-start.8
  19.5 0.0 copy-start.9
  19.5 4.8 %all-to-all-start = ((bf16[32,16,128]{2,1,0:T(8,128)(2,1)}), bf16[32,16,128]{2,1,0:T(8,128)(2,1)S(1)}, u32[]{:S(2)}, u32[]{:S(2)}) async-start(bf16[32,16,128]{2,1,0:T(8,128)(2,1)} %get-tuple-element.26), calls=%async_computation | async-start | bytes 262144 | tf_op jit(solution)/shard_map/all_to_all | solution.py:893
  24.3 0.3 collective-permute-start.2
  24.6 1.1 %collective-permute-done.2.refs_4_.refs_9_ = bf16[592,128]{1,0:T(8,128)(2,1)S(1)} collective-permute-done((bf16[592,128]{1,0:T(8,128)(2,1)S(1)}, bf16[592,128]{1,0:T(8,128)(2,1)S(1)}, u32[]{:S(2)}, u32[]{:S(2)}) %collective-permute-start.2) | collective-permute-done | bytes 151584 | tf_op jit(solution)/shard_map/ppermute | solution.py:114
  25.7 1.3 %pack_z.1 = (bf16[112,128]{1,0:T(8,128)(2,1)S(1)}, f32[128,128]{1,0:T(8,128)S(1)}) custom-call(f32[3072,128]{1,0:T(8,128)S(1)} %bitcast.12, s32[32,128]{1,0:T(8,128)S(1)} %bitcast.21, bf16[784,128]{1,0:T(8,128)(2,1)S(1)} %collective-permute-done.refs_3_.refs_2_.refs_7_, bf16[784,128]{1,0:T(8,128)(2,1)S(1)} %collective-permute-done.1.refs_4_.refs_3_.refs_8_, ...), custom_call_target="tpu_custom_call" | custom-call | flops 4194304 | bytes 3145728 | tf_op jit(solution)/shard_map/pack_z/pallas_call | solution.py:46
  27.1 5.6 %all-to-all-done.refs_0_ = bf16[32,16,128]{2,1,0:T(8,128)(2,1)S(1)} async-done(((bf16[32,16,128]{2,1,0:T(8,128)(2,1)}), bf16[32,16,128]{2,1,0:T(8,128)(2,1)S(1)}, u32[]{:S(2)}, u32[]{:S(2)}) %all-to-all-start) | async-done | bytes 131104 | tf_op jit(solution)/shard_map/all_to_all | solution.py:893
  32.7 0.0 copy-done.8
  32.7 2.2 %coarse.1 = (f32[16,1,16,128]{3,2,1,0:T(8,128)}, s32[8,128]{1,0:T(8,128)S(1)}) custom-call(bf16[32,16,128]{2,1,0:T(8,128)(2,1)S(1)} %all-to-all-done.refs_0_, bf16[64,1024]{1,0:T(8,128)(2,1)S(1)} %copy-done.8, bf16[112,128]{1,0:T(8,128)(2,1)S(1)} %get-tuple-element.28.refs_2_), custom_call_target="tpu_custom_call" | custom-call | flops 8388608 | bytes 1048576 | tf_op jit(solution)/shard_map/coarse/pallas_call | solution.py:46
  34.9 3.5 %all-to-all-start.1 = ((f32[16,1,16,128]{3,2,1,0:T(8,128)}), f32[16,1,16,128]{3,2,1,0:T(8,128)S(1)}, u32[]{:S(2)}, u32[]{:S(2)}) async-start(f32[16,1,16,128]{3,2,1,0:T(8,128)} %get-tuple-element.31), calls=%async_computation.1 | async-start | bytes 262144 | tf_op jit(solution)/shard_map/all_to_all | solution.py:928
  38.5 0.7 collective-permute-start.4
  39.1 4.6 %collective-permute-start.3 = (bf16[112,128]{1,0:T(8,128)(2,1)S(1)}, bf16[112,128]{1,0:T(8,128)(2,1)S(1)}, u32[]{:S(2)}, u32[]{:S(2)}) collective-permute-start(bf16[112,128]{1,0:T(8,128)(2,1)S(1)} %get-tuple-element.28.refs_2_), channel_id=1, source_target_pairs={{0,1},{1,0},{2,3},{3,2},{4,5},{5,4},{6,7},{7,6},{8,9},{9,8},{10,11... | collective-permute-start | bytes 86024 | tf_op jit(solution)/shard_map/ppermute | solution.py:114
  43.7 0.0 collective-permute-done.4.refs_11_
  43.7 1.8 %collective-permute-done.3.refs_10_ = bf16[112,128]{1,0:T(8,128)(2,1)S(1)} collective-permute-done((bf16[112,128]{1,0:T(8,128)(2,1)S(1)}, bf16[112,128]{1,0:T(8,128)(2,1)S(1)}, u32[]{:S(2)}, u32[]{:S(2)}) %collective-permute-start.3) | collective-permute-done | bytes 28704 | tf_op jit(solution)/shard_map/ppermute | solution.py:114
  45.6 0.8 all-to-all-done.1
  46.3 0.0 copy-done.9
  46.3 0.0 copy-start.4
  46.3 1.7 %copy-done.4 = bf16[96,96,128]{2,1,0:T(8,128)(2,1)S(1)} copy-done((bf16[96,96,128]{2,1,0:T(8,128)(2,1)S(1)}, bf16[96,96,128]{2,1,0:T(8,128)(2,1)}, u32[]{:S(2)}) %copy-start.4) | copy-done | bytes 2359320
  48.0 10.9 %solve.1 = (f32[3,32,32,128]{3,2,1,0:T(8,128)S(1)}, f32[8,32,8,128]{3,2,1,0:T(8,128)S(1)}, bf16[96,128]{1,0:T(8,128)(2,1)S(1)}, bf16[768,128]{1,0:T(8,128)(2,1)S...) custom-call(s32[1]{0:T(128)S(6)} %copy.11.refs_0_, f32[2,16]{1,0:T(2,128)S(1)} %copy-done.9, ...), custom_call_target="tpu_custom_call" | custom-call | flops 268435456 | bytes 8388608 | tf_op jit(solution)/shard_map/solve/pallas_call | solution.py:46
  58.9 0.9 collective-permute-start.5
  59.9 0.7 collective-permute-start.6
  60.5 0.1 collective-permute-start.7
  60.6 0.7 collective-permute-start.9
  61.3 3.7 %collective-permute-start.8 = (bf16[96,128]{1,0:T(8,128)(2,1)S(1)}, bf16[96,128]{1,0:T(8,128)(2,1)S(1)}, u32[]{:S(2)}, u32[]{:S(2)}) collective-permute-start(bf16[96,128]{1,0:T(8,128)(2,1)S(1)} %get-tuple-element.38), channel_id=1, source_target_pairs={{0,1},{1,0},{2,3},{3,2},{4,5},{5,4},{6,7},{7,6},{8,9},{9,8},{10,11... | collective-permute-start | bytes 73736 | tf_op jit(solution)/shard_map/ppermute | solution.py:114
  65.0 0.0 collective-permute-done.9.refs_7_
  65.0 1.8 %collective-permute-done.8.refs_6_ = bf16[96,128]{1,0:T(8,128)(2,1)S(1)} collective-permute-done((bf16[96,128]{1,0:T(8,128)(2,1)S(1)}, bf16[96,128]{1,0:T(8,128)(2,1)S(1)}, u32[]{:S(2)}, u32[]{:S(2)}) %collective-permute-start.8) | collective-permute-done | bytes 24608 | tf_op jit(solution)/shard_map/ppermute | solution.py:114
  66.8 0.0 collective-permute-done.7.refs_5_
  66.8 0.0 collective-permute-done.5.refs_3_
  66.8 0.0 collective-permute-done.6.refs_4_
  66.8 0.0 copy-start.5
  66.9 6.7 %image.1 = (bf16[96,64,128]{2,1,0:T(8,128)(2,1)S(1)}, bf16[96,64,128]{2,1,0:T(8,128)(2,1)S(1)}, f32[16,128]{1,0:T(8,128)S(1)}) custom-call(f32[3072,128]{1,0:T(8,128)S(1)} %bitcast.14, f32[8,32,8,128]{3,2,1,0:T(8,128)S(1)} %get-tuple-element.33.refs_1_, f32[3,32,32,128]{3,2,1,0:T(8,128)S(1)} %get-tuple-element.34.refs_2_, ...), custom_call_target="tpu_custom_call" | custom-call | flops 268435456 | bytes 8388608 | tf_op jit(solution)/shard_map/image/pallas_call | solution.py:46
  73.6 0.1 collective-permute-start.10
  73.7 1.2 %collective-permute-done.10.refs_1_ = f32[16,128]{1,0:T(8,128)S(1)} collective-permute-done((f32[16,128]{1,0:T(8,128)S(1)}, f32[16,128]{1,0:T(8,128)S(1)}, u32[]{:S(2)}, u32[]{:S(2)}) %collective-permute-start.10) | collective-permute-done | bytes 8224 | tf_op jit(solution)/shard_map/ppermute | solution.py:114
  74.8 16.0 %all_to_all.15.refs_0_ = f32[16,16,128]{2,1,0:T(8,128)S(1)} all-to-all(f32[16,16,128]{2,1,0:T(8,128)S(1)} %share_sums.1), channel_id=1, replica_groups=mesh['gx'=4,'gy'=2,'col'=4] {'gx','col'}, dimensions={0} | all-to-all | bytes 262144 | tf_op jit(solution)/shard_map/all_to_all | solution.py:1003
  90.8 0.0 copy-done.5
  90.8 7.8 %finish.1 = (f32[3072,128]{1,0:T(8,128)}, f32[3072,128]{1,0:T(8,128)}) custom-call(f32[16,16,128]{2,1,0:T(8,128)S(1)} %all_to_all.15.refs_0_, f32[3072,128]{1,0:T(8,128)S(1)} %bitcast.17, f32[3072,128]{1,0:T(8,128)S(1)} %bitcast.15, bf16[96,64,128]{2,1,0:T(8,128)(2,1)S(1)} %get-tuple-element.40.refs_3_, bf16[96,64,128]{2,1,0:T(8,128)(2,1)S(1)} %get-tuple-element.41.refs_4_), custom_call_target="tpu_custom_call" | custom-call | flops 134217728 | bytes 9437184 | tf_op jit(solution)/shard_map/finish/pallas_call | solution.py:46
  (1 shorter events, 0.0 us)
Async XLA Ops:
  0.6 1.4 %copy-start = (f32[3,32,4,8,128]{4,3,2,1,0:T(8,128)S(1)}, f32[3,32,4,8,128]{4,3,2,1,0:T(8,128)}, u32[]{:S(2)}) copy-start(f32[3,32,4,8,128]{4,3,2,1,0:T(8,128)} %param.9) | copy-start | bytes 4718596
  2.0 0.7 copy-start.6
  2.8 8.1 %copy-start.1 = (f32[3,32,4,8,128]{4,3,2,1,0:T(8,128)S(1)}, f32[3,32,4,8,128]{4,3,2,1,0:T(8,128)}, u32[]{:S(2)}) copy-start(f32[3,32,4,8,128]{4,3,2,1,0:T(8,128)} %param.9) | copy-start | bytes 4718596
  3.0 15.5 %collective-permute-start.1 = (bf16[784,128]{1,0:T(8,128)(2,1)S(1)}, bf16[784,128]{1,0:T(8,128)(2,1)S(1)}, u32[]{:S(2)}, u32[]{:S(2)}) collective-permute-start(bf16[784,128]{1,0:T(8,128)(2,1)S(1)} %get-tuple-element.25), channel_id=1, source_target_pairs={{8,16},{16,8},{9,17},{17,9},{10,18},{18,10},{11,19},{19,11},{12,20... | collective-permute-start | bytes 602120 | tf_op jit(solution)/shard_map/ppermute | solution.py:114
  3.9 14.7 %collective-permute-start = (bf16[784,128]{1,0:T(8,128)(2,1)S(1)}, bf16[784,128]{1,0:T(8,128)(2,1)S(1)}, u32[]{:S(2)}, u32[]{:S(2)}) collective-permute-start(bf16[784,128]{1,0:T(8,128)(2,1)S(1)} %get-tuple-element.23.refs_4_), channel_id=1, source_target_pairs={{0,8},{8,0},{16,24},{24,16},{1,9},{9,1},{17,25},{25,17},{2,10},{10... | collective-permute-start | bytes 602120 | tf_op jit(solution)/shard_map/ppermute | solution.py:114
  10.9 1.7 %copy-start.2 = (f32[48,3,4,8,128]{4,3,2,1,0:T(8,128)S(1)}, f32[48,3,4,8,128]{4,3,2,1,0:T(8,128)}, u32[]{:S(2)}) copy-start(f32[48,3,4,8,128]{4,3,2,1,0:T(8,128)} %param.14) | copy-start | bytes 7077892
  12.6 6.0 %copy-start.7 = (s32[4,8,128]{2,1,0:T(8,128)S(1)}, s32[4,8,128]{2,1,0:T(8,128)}, u32[]{:S(2)}) copy-start(s32[4,8,128]{2,1,0:T(8,128)} %param.10) | copy-start | bytes 49156
  17.1 1.4 %copy-start.3 = (bf16[96,96,128]{2,1,0:T(8,128)(2,1)}, bf16[96,96,128]{2,1,0:T(8,128)(2,1)S(1)}, u32[]{:S(2)}) copy-start(bf16[96,96,128]{2,1,0:T(8,128)(2,1)S(1)} %get-tuple-element.32.refs_6_) | copy-start | bytes 7077892
  19.4 13.3 %copy-start.8 = (bf16[64,1024]{1,0:T(8,128)(2,1)S(1)}, bf16[64,1024]{1,0:T(8,128)(2,1)}, u32[]{:S(2)}) copy-start(bf16[64,1024]{1,0:T(8,128)(2,1)} %refs_1_.3) | copy-start | bytes 393220
  19.5 26.9 %copy-start.9 = (f32[2,16]{1,0:T(2,128)S(1)}, f32[2,16]{1,0:T(2,128)}, u32[]{:S(2)}) copy-start(f32[2,16]{1,0:T(2,128)} %refs_1_.4) | copy-start | bytes 388
  19.5 13.2 %all-to-all-start = ((bf16[32,16,128]{2,1,0:T(8,128)(2,1)}), bf16[32,16,128]{2,1,0:T(8,128)(2,1)S(1)}, u32[]{:S(2)}, u32[]{:S(2)}) async-start(bf16[32,16,128]{2,1,0:T(8,128)(2,1)} %get-tuple-element.26), calls=%async_computation | async-start | bytes 262144 | tf_op jit(solution)/shard_map/all_to_all | solution.py:893
  24.3 1.4 %collective-permute-start.2 = (bf16[592,128]{1,0:T(8,128)(2,1)S(1)}, bf16[592,128]{1,0:T(8,128)(2,1)S(1)}, u32[]{:S(2)}, u32[]{:S(2)}) collective-permute-start(bf16[592,128]{1,0:T(8,128)(2,1)S(1)} %get-tuple-element.27), channel_id=1, source_target_pairs={{0,4},{4,0},{1,5},{5,1},{2,6},{6,2},{3,7},{7,3},{8,12},{12,8},{9,1... | collective-permute-start | bytes 454664 | tf_op jit(solution)/shard_map/ppermute | solution.py:114
  34.9 11.4 %all-to-all-start.1 = ((f32[16,1,16,128]{3,2,1,0:T(8,128)}), f32[16,1,16,128]{3,2,1,0:T(8,128)S(1)}, u32[]{:S(2)}, u32[]{:S(2)}) async-start(f32[16,1,16,128]{3,2,1,0:T(8,128)} %get-tuple-element.31), calls=%async_computation.1 | async-start | bytes 262144 | tf_op jit(solution)/shard_map/all_to_all | solution.py:928
  38.5 5.2 %collective-permute-start.4 = (bf16[112,128]{1,0:T(8,128)(2,1)S(1)}, bf16[112,128]{1,0:T(8,128)(2,1)S(1)}, u32[]{:S(2)}, u32[]{:S(2)}) collective-permute-start(bf16[112,128]{1,0:T(8,128)(2,1)S(1)} %get-tuple-element.28.refs_2_), channel_id=1, source_target_pairs={{1,2},{2,1},{5,6},{6,5},{9,10},{10,9},{13,14},{14,13},{17,18},{18,... | collective-permute-start | bytes 86024 | tf_op jit(solution)/shard_map/ppermute | solution.py:114
  39.1 6.4 %collective-permute-start.3 = (bf16[112,128]{1,0:T(8,128)(2,1)S(1)}, bf16[112,128]{1,0:T(8,128)(2,1)S(1)}, u32[]{:S(2)}, u32[]{:S(2)}) collective-permute-start(bf16[112,128]{1,0:T(8,128)(2,1)S(1)} %get-tuple-element.28.refs_2_), channel_id=1, source_target_pairs={{0,1},{1,0},{2,3},{3,2},{4,5},{5,4},{6,7},{7,6},{8,9},{9,8},{10,11... | collective-permute-start | bytes 86024 | tf_op jit(solution)/shard_map/ppermute | solution.py:114
  46.3 1.7 %copy-start.4 = (bf16[96,96,128]{2,1,0:T(8,128)(2,1)S(1)}, bf16[96,96,128]{2,1,0:T(8,128)(2,1)}, u32[]{:S(2)}) copy-start(bf16[96,96,128]{2,1,0:T(8,128)(2,1)} %copy-done.3) | copy-start | bytes 7077892
  58.9 7.9 %collective-permute-start.5 = (bf16[768,128]{1,0:T(8,128)(2,1)S(1)}, bf16[768,128]{1,0:T(8,128)(2,1)S(1)}, u32[]{:S(2)}, u32[]{:S(2)}) collective-permute-start(bf16[768,128]{1,0:T(8,128)(2,1)S(1)} %get-tuple-element.35), channel_id=1, source_target_pairs={{0,8},{8,0},{16,24},{24,16},{1,9},{9,1},{17,25},{25,17},{2,10},{10... | collective-permute-start | bytes 589832 | tf_op jit(solution)/shard_map/ppermute | solution.py:114
  59.9 7.0 %collective-permute-start.6 = (bf16[768,128]{1,0:T(8,128)(2,1)S(1)}, bf16[768,128]{1,0:T(8,128)(2,1)S(1)}, u32[]{:S(2)}, u32[]{:S(2)}) collective-permute-start(bf16[768,128]{1,0:T(8,128)(2,1)S(1)} %get-tuple-element.36), channel_id=1, source_target_pairs={{8,16},{16,8},{9,17},{17,9},{10,18},{18,10},{11,19},{19,11},{12,20... | collective-permute-start | bytes 589832 | tf_op jit(solution)/shard_map/ppermute | solution.py:114
  60.5 6.3 %collective-permute-start.7 = (bf16[384,128]{1,0:T(8,128)(2,1)S(1)}, bf16[384,128]{1,0:T(8,128)(2,1)S(1)}, u32[]{:S(2)}, u32[]{:S(2)}) collective-permute-start(bf16[384,128]{1,0:T(8,128)(2,1)S(1)} %get-tuple-element.37), channel_id=1, source_target_pairs={{0,4},{4,0},{1,5},{5,1},{2,6},{6,2},{3,7},{7,3},{8,12},{12,8},{9,1... | collective-permute-start | bytes 294920 | tf_op jit(solution)/shard_map/ppermute | solution.py:114
  60.6 4.4 %collective-permute-start.9 = (bf16[96,128]{1,0:T(8,128)(2,1)S(1)}, bf16[96,128]{1,0:T(8,128)(2,1)S(1)}, u32[]{:S(2)}, u32[]{:S(2)}) collective-permute-start(bf16[96,128]{1,0:T(8,128)(2,1)S(1)} %get-tuple-element.38), channel_id=1, source_target_pairs={{1,2},{2,1},{5,6},{6,5},{9,10},{10,9},{13,14},{14,13},{17,18},{18,... | collective-permute-start | bytes 73736 | tf_op jit(solution)/shard_map/ppermute | solution.py:114
  61.3 5.6 %collective-permute-start.8 = (bf16[96,128]{1,0:T(8,128)(2,1)S(1)}, bf16[96,128]{1,0:T(8,128)(2,1)S(1)}, u32[]{:S(2)}, u32[]{:S(2)}) collective-permute-start(bf16[96,128]{1,0:T(8,128)(2,1)S(1)} %get-tuple-element.38), channel_id=1, source_target_pairs={{0,1},{1,0},{2,3},{3,2},{4,5},{5,4},{6,7},{7,6},{8,9},{9,8},{10,11... | collective-permute-start | bytes 73736 | tf_op jit(solution)/shard_map/ppermute | solution.py:114
  66.8 24.0 %copy-start.5 = (f32[3,32,4,8,128]{4,3,2,1,0:T(8,128)S(1)}, f32[3,32,4,8,128]{4,3,2,1,0:T(8,128)}, u32[]{:S(2)}) copy-start(f32[3,32,4,8,128]{4,3,2,1,0:T(8,128)} %param.8) | copy-start | bytes 4718596
  73.6 1.2 %collective-permute-start.10 = (f32[16,128]{1,0:T(8,128)S(1)}, f32[16,128]{1,0:T(8,128)S(1)}, u32[]{:S(2)}, u32[]{:S(2)}) collective-permute-start(f32[16,128]{1,0:T(8,128)S(1)} %get-tuple-element.39.refs_0_), channel_id=1, source_target_pairs={{0,4},{4,0},{1,5},{5,1},{2,6},{6,2},{3,7},{7,3},{8,12},{12,8},{9,1... | collective-permute-start | bytes 24584 | tf_op jit(solution)/shard_map/ppermute | solution.py:114

commit v6 on v5

--- a/solution.py
+++ b/solution.py
@@ -317,9 +317,9 @@
 
 
 def place_pieces(
-    sz, gathered, inverse, after, message, starts_out, vector, wide, heads, starts, sem
+    sz, gathered, inverse, *refs
 ):
-    del after
+    message, starts_out, vector, wide, heads, starts, sem = refs[-7:]
     devices = gathered.shape[0]
     for device in range(devices):
         heads[pl.ds(device, 1), :] = gathered[device].astype(F32)[0:1]
@@ -509,14 +509,11 @@
     return jnp.where(even, down, roll_lanes(up, -2))
 
 
-def solve_and_direct(sz, count, table, starts_in, res, id_box, coarse, split, *refs):
+def relax_box(sz, table, res, id_box, *refs):
     xhalo, yhalo, zhalo, refs = take_halos(refs, "gx", "gy", "col")
-    direction, own, zface = refs[:3]
-    xsend, ysend, refs = take_halos(refs[3:], "gx", "gy")
-    first, second, third, halos, inner, coefs, halo_coefs, mu_box, halo_mu, left, zedge = refs[:11]
-    wide, own_rows_coef, weights, lhs, near, starts, sem = refs[11:]
-    copy = pltpu.make_async_copy(starts_in, starts, sem)
-    copy.start()
+    near_part, own = refs[:2]
+    first, second, third, halos, inner, coefs, halo_coefs, mu_box, halo_mu = refs[2:11]
+    wide, own_rows_coef, weights, lhs, near = refs[11:]
     loads, comps = sz.loads, sz.comps
     groups = loads // 8
     lane8 = lane_ids(8)
@@ -627,6 +624,23 @@
     sweep(first, second, 0)
     sweep(second, third, 1)
 
+    def final(x, carry):
+        def put(j, place, comp, group, out):
+            near_part[comp, x * sz.cy + j, pl.ds(group * 8, 8), :] = out
+
+        relax(third, 2, x + 1, range(1, sz.cy + 1), put)
+        return carry
+
+    lax.fori_loop(0, sz.cx, final, 0)
+
+
+def make_direction(sz, count, starts_in, coarse, split, near_part, *refs):
+    direction, zface = refs[:2]
+    xsend, ysend, (left, zedge, lhs, near, starts, sem) = take_halos(refs[2:], "gx", "gy")
+    loads, comps = sz.loads, sz.comps
+    copy = pltpu.make_async_copy(starts_in, starts, sem)
+    copy.start()
+    lane_k = lane_ids(loads)
     copy.wait()
     mine = own_coefs(sz, coarse, starts[0, own_index()])
     mine = jnp.where(lane_ids(loads) < jnp.minimum(count[0], sz.slots), mine, 0.0)
@@ -634,10 +648,6 @@
     zedge[...] = jnp.zeros_like(zedge)
 
     def final(x, carry):
-        def put(j, place, comp, group, out):
-            direction[comp, x * sz.cy + j, pl.ds(group * 8, 8), :] = out
-
-        relax(third, 2, x + 1, range(1, sz.cy + 1), put)
         for y in range(sz.cy):
             cell = x * sz.cy + y
             place = (x + 1) * sz.by + y + 1
@@ -647,19 +657,16 @@
                     split[comp * sz.cells + cell],
                     preferred_element_type=F32,
                 )
-                value = direction[comp, cell] + (part[:loads] + part[loads:])
+                value = near_part[comp, cell] + (part[:loads] + part[loads:])
                 direction[comp, cell] = value
-                lhs[pl.ds((y * comps + comp) * loads, loads), pl.ds(0, LANES)] = value.astype(BF16)
-        size = sz.cy * comps * loads
-        near[pl.ds(0, size), pl.ds(0, LANES)] = jnp.dot(
-            lhs[pl.ds(0, size), pl.ds(0, LANES)], edges, preferred_element_type=F32
-        )
+                lhs[pl.ds((y * comps + comp) * loads, loads), :] = value.astype(BF16)
+        near[...] = jnp.dot(lhs[...], edges, preferred_element_type=F32)
         for y in range(sz.cy):
             place = (x + 1) * sz.by + y + 1
             for comp in range(comps):
                 pltpu.store(
                     zedge.at[pl.ds(comp * loads, loads), :],
-                    near[pl.ds((y * comps + comp) * loads, loads), pl.ds(0, LANES)],
+                    near[pl.ds((y * comps + comp) * loads, loads), :],
                     mask=(lane_k >> 1) == place,
                 )
         return carry
@@ -710,10 +717,14 @@
         copy.wait()
     lane_k = lane_ids(loads)
 
-    def at(x, total):
-        for y in range(sz.cy):
-            cell = x * sz.cy + y
-            place = (x + 1) * sz.by + y + 1
+    part_cells = sz.cy // 2
+
+    def at(step, total):
+        x = step // 2
+        first_y = (step - 2 * x) * part_cells
+        for y in range(part_cells):
+            cell = step * part_cells + y
+            place = (x + 1) * sz.by + first_y + y + 1
             here = (((lane_k + 1) >> 1) & 63) == place
             for comp in range(comps):
                 hi, lo = split_hi_lo(box[comp, place])
@@ -724,9 +735,9 @@
                 lhs[rows, pl.ds(2 * LANES, LANES)] = jnp.where(here, halo[comp], 0.0).astype(BF16)
         near[...] = jnp.dot(lhs[...], weights[...], preferred_element_type=F32)
         sides = {}
-        for y in range(sz.cy):
-            cell = x * sz.cy + y
-            place = (x + 1) * sz.by + y + 1
+        for y in range(part_cells):
+            cell = step * part_cells + y
+            place = (x + 1) * sz.by + first_y + y + 1
             coef = [own[j, cell] for j in range(8)]
             parts = {}
             for group in range(groups):
@@ -758,7 +769,7 @@
                     )
         return total
 
-    total = lax.fori_loop(0, sz.cx, at, jnp.zeros((2 * loads, 4 * loads), F32))
+    total = lax.fori_loop(0, 2 * sz.cx, at, jnp.zeros((2 * loads, 4 * loads), F32))
     high, low = total[:loads], total[loads:]
     sums = high + roll_lanes(high, -loads) + low
     half = loads // 2
@@ -817,7 +828,7 @@
             new_residual[rows, :] = res[rows, :] - part[:, LANES:]
         return carry
 
-    lax.fori_loop(0, sz.cells, at, 0, unroll=4)
+    lax.fori_loop(0, sz.cells, at, 0, unroll=2)
 
 
 def body(
@@ -922,23 +933,21 @@
         12,
         1 << 23,
         1 << 20,
-        [gathered, coarse_inverse, zmessage],
-        spaces=[vmem, vmem, pl.ANY],
+        [gathered, coarse_inverse] + zhalo,
+        spaces=[vmem, vmem] + [pl.ANY] * len(zhalo),
     )
     coarse = lax.all_to_all(partial, ("gx", "col"), 0, 0, tiled=True)
     coarse = coarse.reshape((-1,) + tile[1:])
 
     field = scratch((sz.comps, sz.box, sz.loads, LANES), F32)
-    direction, own, zface, *faces = call(
-        "solve",
-        solve_and_direct,
+    halos = xhalo + yhalo + zhalo
+    near_part, own = call(
+        "sweeps",
+        relax_box,
         [
             shape((sz.comps, sz.cells, sz.loads, LANES), F32),
             shape((8, sz.cells, 8, LANES), F32),
-            shape((sz.face_z, LANES), BF16),
-        ]
-        + [shape((sz.face_x, LANES), BF16)] * swaps("gx")
-        + [shape((sz.inner_y, LANES), BF16)] * swaps("gy"),
+        ],
         [
             field,
             field,
@@ -949,21 +958,41 @@
             scratch((9, 8, LANES), F32),
             scratch((rows, LANES), F32),
             scratch((rows, LANES), F32),
-            scratch((2 * sz.loads, LANES), BF16),
-            scratch((sz.face_z, LANES), F32),
             scratch((9, sz.box, 8, LANES), F32),
             scratch((8, sz.cells, LANES), F32),
             scratch((2 * LANES, 3 * LANES), BF16),
             scratch((sz.by * sz.comps * sz.loads, 2 * LANES), BF16),
             scratch((sz.by * sz.comps * sz.loads, 3 * LANES), F32),
+        ],
+        24,
+        1 << 28,
+        8 << 20,
+        [materials, res, id_box] + halos,
+        spaces=[smem] + [vmem] * (2 + len(halos)),
+    )
+    plane = sz.cy * sz.comps * sz.loads
+    direction, zface, *faces = call(
+        "direct",
+        make_direction,
+        [
+            shape((sz.comps, sz.cells, sz.loads, LANES), F32),
+            shape((sz.face_z, LANES), BF16),
+        ]
+        + [shape((sz.face_x, LANES), BF16)] * swaps("gx")
+        + [shape((sz.inner_y, LANES), BF16)] * swaps("gy"),
+        [
+            scratch((2 * sz.loads, LANES), BF16),
+            scratch((sz.face_z, LANES), F32),
+            scratch((plane, LANES), BF16),
+            scratch((plane, LANES), F32),
             smem(starts.shape, jnp.int32),
             dma,
         ],
-        26,
-        1 << 28,
+        14,
+        1 << 26,
         8 << 20,
-        [eigen_counts, materials, starts, res, id_box, coarse, split] + xhalo + yhalo + zhalo,
-        spaces=[smem, smem, pl.ANY] + [vmem] * (4 + len(xhalo + yhalo + zhalo)),
+        [eigen_counts, starts, coarse, split, near_part],
+        spaces=[smem, pl.ANY, vmem, vmem, vmem],
     )
     xhalo = exchange(faces[: swaps("gx")], "gx")
     yhalo = exchange(faces[swaps("gx") :], "gy")
@@ -981,8 +1010,8 @@
             field,
             scratch((sz.comps, sz.loads, LANES), F32),
             scratch((3 * LANES, 2 * LANES), BF16),
-            scratch((sz.cy * sz.comps * sz.loads, 3 * LANES), BF16),
-            scratch((sz.cy * sz.comps * sz.loads, 2 * LANES), F32),
+            scratch((plane // 2, 3 * LANES), BF16),
+            scratch((plane // 2, 2 * LANES), F32),
             dma((sz.comps, sz.cx)),
         ],
         20,

time: 99.1 us -> 107 us (1.080)
  waiting for transfers between devices: 12.4 us -> 5.91 us
  local copies, waits for them, and re-layouts: 6.87 us -> 12.4 us
  Pallas kernels: 34.7 us -> 38.9 us
  blocking collectives: 16 us -> 18.7 us
  starting transfers between devices: 26.6 us -> 27.8 us
    ppermute x11, starting transfers between devices: 18.2 us -> 11.3 us  [exchange(): result.append(lax.ppermute(faces[parity], axis, pairs))]
    unnamed x20 -> x40, local copies, waits for them, and re-layouts: 6.87 us -> 12.4 us
    all_to_all x1, starting transfers between devices: 3.52 us -> 8.89 us  [body(): coarse = lax.all_to_all(partial, ('gx', 'col'), 0, 0, tiled=True)]
    all_to_all x1, waiting for transfers between devices: 5.62 us -> 0.47 us  [body(): gathered = lax.all_to_all(message, AXES, 0, 0, tiled=True)]
    pallas_call x9 -> x10, Pallas kernels: 34.7 us -> 38.9 us  [vmem_call(): pl.pallas_call(kernel, name=name, out_shape=outs, in_specs=[pl.BlockSpec(...]
    all_to_all x1, starting transfers between devices: 4.84 us -> 7.62 us  [body(): gathered = lax.all_to_all(message, AXES, 0, 0, tiled=True)]
    all_to_all x1, blocking collectives: 16 us -> 18.7 us  [body(): sums = lax.all_to_all(spread, over, 0, 0, tiled=True)]
  transfers between devices with their start and end apart: 13 -> 13, of which waited for: 6 -> 5; matrix products, arithmetic and copies ran while one was open for 0% -> 0% of each run, Pallas kernels for 6% -> 15%
where the time goes in v6:
time: 107 us; the launch traced here: 106 us
  Pallas kernels  38.9 us (36%)
  starting transfers between devices  27.8 us (26%)
  blocking collectives  18.7 us (17%)
  local copies, waits for them, and re-layouts  12.4 us (12%)
  waiting for transfers between devices  5.91 us (6%)
  between operations  2.18 us (2%)
    pallas_call x10, Pallas kernels, vmem_call(): pl.pallas_call(kernel, name=name, out_shape=outs, in_specs=[pl.BlockSpec(...  38.9 us
    all_to_all x1, blocking collectives, body(): sums = lax.all_to_all(spread, over, 0, 0, tiled=True)  18.7 us
    unnamed x40, local copies, waits for them, and re-layouts  12.4 us
    ppermute x11, starting transfers between devices, exchange(): result.append(lax.ppermute(faces[parity], axis, pairs))  11.3 us
    all_to_all x1, starting transfers between devices, body(): coarse = lax.all_to_all(partial, ('gx', 'col'), 0, 0, tiled=True)  8.89 us
    all_to_all x1, starting transfers between devices, body(): gathered = lax.all_to_all(message, AXES, 0, 0, tiled=True)  7.62 us
    ppermute x11, waiting for transfers between devices, exchange(): result.append(lax.ppermute(faces[parity], axis, pairs))  5.44 us
  transfers between devices with their start and end apart: 13, of which 5 were waited for; matrix products, arithmetic and copies ran while one was open for 0% of the time, Pallas kernels for 15%

profile of v6, /device:TPU:0, one launch (start us, length us, event | category | flops | bytes accessed | tf_op | source)
XLA Modules:
  0.0 105.9 jit_solution(8305440498894939421)
XLA Ops:
  0.6 0.0 copy-start
  0.6 1.4 %copy-done = f32[3,32,4,8,128]{4,3,2,1,0:T(8,128)S(1)} copy-done((f32[3,32,4,8,128]{4,3,2,1,0:T(8,128)S(1)}, f32[3,32,4,8,128]{4,3,2,1,0:T(8,128)}, u32[]{:S(2)}) %copy-start) | copy-done | bytes 1572888
  2.0 0.0 copy-start.10
  2.0 0.7 copy-done.10
  2.8 0.3 pack_x.1
  3.0 3.0 %collective-permute-start = (bf16[784,128]{1,0:T(8,128)(2,1)S(1)}, bf16[784,128]{1,0:T(8,128)(2,1)S(1)}, u32[]{:S(2)}, u32[]{:S(2)}) collective-permute-start(bf16[784,128]{1,0:T(8,128)(2,1)S(1)} %get-tuple-element.24.refs_4_), channel_id=1, source_target_pairs={{0,8},{8,0},{16,24},{24,16},{1,9},{9,1},{17,25},{25,17},{2,10},{10... | collective-permute-start | bytes 602120 | tf_op jit(solution)/shard_map/ppermute | solution.py:114
  6.0 0.7 collective-permute-start.1
  8.0 0.0 copy-done.1
  8.0 0.0 copy-start.4
  8.0 1.7 %copy-done.4 = f32[48,3,4,8,128]{4,3,2,1,0:T(8,128)S(1)} copy-done((f32[48,3,4,8,128]{4,3,2,1,0:T(8,128)S(1)}, f32[48,3,4,8,128]{4,3,2,1,0:T(8,128)}, u32[]{:S(2)}) %copy-start.4) | copy-done | bytes 2359320
  9.7 4.5 %pieces.1 = (bf16[16,128]{1,0:T(8,128)(2,1)S(1)}, bf16[96,96,128]{2,1,0:T(8,128)(2,1)S(1)}) custom-call(s32[1]{0:T(128)S(6)} %copy.11.refs_0_, s32[1]{0:T(128)S(6)} %copy.12.refs_1_, f32[48,96,128]{2,1,0:T(8,128)S(1)} %bitcast.16, f32[3,1024,128]{2,1,0:T(8,128)S(1)} %bitcast.10, bf16[784,128]{1,0:T(8,128)(2,1)S(1)} %get-tuple-element.24.refs_4_), custom_call_target="tpu_custom_call" | custom-call | flops 134217728 | bytes 7340032 | tf_op jit(solution)/shard_map/pieces/pallas_call | solution.py:46
  14.2 0.0 copy-start.2
  14.3 1.4 %copy-done.2 = bf16[96,96,128]{2,1,0:T(8,128)(2,1)} copy-done((bf16[96,96,128]{2,1,0:T(8,128)(2,1)}, bf16[96,96,128]{2,1,0:T(8,128)(2,1)S(1)}, u32[]{:S(2)}) %copy-start.2) | copy-done | bytes 2359320
  15.7 0.0 collective-permute-done.refs_3_.refs_2_
  15.7 0.0 collective-permute-done.1.refs_4_.refs_3_
  15.7 0.0 copy-done.11
  15.7 0.9 pack_y.1
  16.6 7.6 %all-to-all-start = ((bf16[32,16,128]{2,1,0:T(8,128)(2,1)}), bf16[32,16,128]{2,1,0:T(8,128)(2,1)S(1)}, u32[]{:S(2)}, u32[]{:S(2)}) async-start(bf16[32,16,128]{2,1,0:T(8,128)(2,1)} %get-tuple-element.31), calls=%async_computation | async-start | bytes 262144 | tf_op jit(solution)/shard_map/all_to_all | solution.py:904
  24.2 0.3 collective-permute-start.2
  24.5 1.1 %collective-permute-done.2.refs_4_.refs_5_ = bf16[592,128]{1,0:T(8,128)(2,1)S(1)} collective-permute-done((bf16[592,128]{1,0:T(8,128)(2,1)S(1)}, bf16[592,128]{1,0:T(8,128)(2,1)S(1)}, u32[]{:S(2)}, u32[]{:S(2)}) %collective-permute-start.2) | collective-permute-done | bytes 151584 | tf_op jit(solution)/shard_map/ppermute | solution.py:114
  25.7 1.3 %pack_z.1 = (bf16[112,128]{1,0:T(8,128)(2,1)S(1)}, f32[128,128]{1,0:T(8,128)S(1)}) custom-call(f32[3072,128]{1,0:T(8,128)S(1)} %bitcast.12, s32[32,128]{1,0:T(8,128)S(1)} %bitcast.20, bf16[784,128]{1,0:T(8,128)(2,1)S(1)} %collective-permute-done.refs_3_.refs_2_, bf16[784,128]{1,0:T(8,128)(2,1)S(1)} %collective-permute-done.1.refs_4_.refs_3_, ...), custom_call_target="tpu_custom_call" | custom-call | flops 4194304 | bytes 3145728 | tf_op jit(solution)/shard_map/pack_z/pallas_call | solution.py:46
  27.0 0.0 copy-start.8
  27.0 0.7 copy-done.8
  27.7 0.6 copy-done.17
  28.3 1.8 %collective-permute-start.3 = (bf16[112,128]{1,0:T(8,128)(2,1)S(1)}, bf16[112,128]{1,0:T(8,128)(2,1)S(1)}, u32[]{:S(2)}, u32[]{:S(2)}) collective-permute-start(bf16[112,128]{1,0:T(8,128)(2,1)S(1)} %get-tuple-element.29), channel_id=1, source_target_pairs={{0,1},{1,0},{2,3},{3,2},{4,5},{5,4},{6,7},{7,6},{8,9},{9,8},{10,11... | collective-permute-start | bytes 86024 | tf_op jit(solution)/shard_map/ppermute | solution.py:114
  30.1 0.7 collective-permute-start.4
  30.7 1.4 %collective-permute-done.3.refs_6_.refs_2_ = bf16[112,128]{1,0:T(8,128)(2,1)S(1)} collective-permute-done((bf16[112,128]{1,0:T(8,128)(2,1)S(1)}, bf16[112,128]{1,0:T(8,128)(2,1)S(1)}, u32[]{:S(2)}, u32[]{:S(2)}) %collective-permute-start.3) | collective-permute-done | bytes 28704 | tf_op jit(solution)/shard_map/ppermute | solution.py:114
  32.2 0.0 collective-permute-done.4.refs_7_.refs_3_
  32.2 0.5 all-to-all-done.refs_0_
  32.6 0.0 copy-done.12
  32.6 2.2 %coarse.1 = (f32[16,1,16,128]{3,2,1,0:T(8,128)}, s32[8,128]{1,0:T(8,128)S(1)}) custom-call(bf16[32,16,128]{2,1,0:T(8,128)(2,1)S(1)} %all-to-all-done.refs_0_, bf16[64,1024]{1,0:T(8,128)(2,1)S(1)} %copy-done.12, bf16[112,128]{1,0:T(8,128)(2,1)S(1)} %collective-permute-done.3.refs_6_.refs_2_, bf16[112,128]{1,0:T(8,128)(2,1)S(1)} %collective-permute-done.4.refs_7_.refs_3_), custom_call_target="tpu_custom_call" | custom-call | flops 8388608 | bytes 1048576 | tf_op jit(solution)/shard_map/coarse/pallas_call | solution.py:46
  34.8 8.9 %all-to-all-start.1 = ((f32[16,1,16,128]{3,2,1,0:T(8,128)}), f32[16,1,16,128]{3,2,1,0:T(8,128)}, u32[]{:S(2)}, u32[]{:S(2)}) async-start(f32[16,1,16,128]{3,2,1,0:T(8,128)} %get-tuple-element.33), calls=%async_computation.1 | async-start | bytes 262144 | tf_op jit(solution)/shard_map/all_to_all | solution.py:939
  43.7 0.0 copy-done.13
  43.8 0.0 copy-done.15
  43.8 0.0 copy-done.19
  43.8 0.0 copy-start.9
  43.8 0.9 copy-done.9
  44.7 0.7 copy-done.14
  45.4 0.7 copy-done.16
  46.2 0.8 copy-done.18
  47.0 9.6 %sweeps.1 = (f32[3,32,32,128]{3,2,1,0:T(8,128)S(1)}, f32[8,32,8,128]{3,2,1,0:T(8,128)S(1)}) custom-call(f32[2,16]{1,0:T(2,128)S(1)} %copy-done.19, f32[3072,128]{1,0:T(8,128)S(1)} %bitcast.13, f32[128,128]{1,0:T(8,128)S(1)} %copy-done.18, bf16[784,128]{1,0:T(8,128)(2,1)S(1)} %collective-permute-done.refs_3_.refs_2_, ...), custom_call_target="tpu_custom_call" | custom-call | flops 268435456 | bytes 8388608 | tf_op jit(solution)/shard_map/sweeps/pallas_call | solution.py:46
  56.7 0.0 copy-start.6
  56.7 1.0 copy-done.6
  57.6 0.0 all-to-all-done.1
  57.6 1.7 %copy-done.3 = bf16[96,96,128]{2,1,0:T(8,128)(2,1)S(1)} copy-done((bf16[96,96,128]{2,1,0:T(8,128)(2,1)S(1)}, bf16[96,96,128]{2,1,0:T(8,128)(2,1)}, u32[]{:S(2)}) %copy-start.3) | copy-done | bytes 2359320
  59.3 3.7 %direct.1 = (f32[3,32,32,128]{3,2,1,0:T(8,128)S(1)}, bf16[96,128]{1,0:T(8,128)(2,1)S(1)}, bf16[768,128]{1,0:T(8,128)(2,1)S(1)}, bf16[768,128]{1,0:T(8,128)(2,1)S(1)}, bf16[384,128]{1,0:T(8,128)(2,1)S(1)}) custom-call(s32[1]{0:T(128)S(6)} %copy.11.refs_0_, s32[8,128]{1,0:T(8,128)S(1)} %get-tuple-element.32.refs_1_, f32[16,16,128]{2,1,0:T(8,128)} %bitcast.5.refs_2_, ...), custom_call_target="tpu_custom_call" | custom-call | flops 67108864 | bytes 8388608 | tf_op jit(solution)/shard_map/direct/pallas_call | solution.py:46
  63.0 1.9 %collective-permute-start.5 = (bf16[768,128]{1,0:T(8,128)(2,1)S(1)}, bf16[768,128]{1,0:T(8,128)(2,1)S(1)}, u32[]{:S(2)}, u32[]{:S(2)}) collective-permute-start(bf16[768,128]{1,0:T(8,128)(2,1)S(1)} %get-tuple-element.37), channel_id=1, source_target_pairs={{0,8},{8,0},{16,24},{24,16},{1,9},{9,1},{17,25},{25,17},{2,10},{10... | collective-permute-start | bytes 589832 | tf_op jit(solution)/shard_map/ppermute | solution.py:114
  65.0 0.7 collective-permute-start.6
  65.6 0.1 collective-permute-start.7
  65.7 1.5 %collective-permute-start.8 = (bf16[96,128]{1,0:T(8,128)(2,1)S(1)}, bf16[96,128]{1,0:T(8,128)(2,1)S(1)}, u32[]{:S(2)}, u32[]{:S(2)}) collective-permute-start(bf16[96,128]{1,0:T(8,128)(2,1)S(1)} %get-tuple-element.40), channel_id=1, source_target_pairs={{0,1},{1,0},{2,3},{3,2},{4,5},{5,4},{6,7},{7,6},{8,9},{9,8},{10,11... | collective-permute-start | bytes 73736 | tf_op jit(solution)/shard_map/ppermute | solution.py:114
  67.2 0.7 collective-permute-start.9
  67.9 1.7 %collective-permute-done.8.refs_6_ = bf16[96,128]{1,0:T(8,128)(2,1)S(1)} collective-permute-done((bf16[96,128]{1,0:T(8,128)(2,1)S(1)}, bf16[96,128]{1,0:T(8,128)(2,1)S(1)}, u32[]{:S(2)}, u32[]{:S(2)}) %collective-permute-start.8) | collective-permute-done | bytes 24608 | tf_op jit(solution)/shard_map/ppermute | solution.py:114
  69.6 0.0 collective-permute-done.9.refs_7_
  69.6 0.0 collective-permute-done.7.refs_5_
  69.6 0.0 collective-permute-done.5.refs_3_
  69.6 0.0 collective-permute-done.6.refs_4_
  69.6 0.0 copy-done.7
  69.6 0.0 copy-start.5
  69.6 7.6 %image.1 = (bf16[96,64,128]{2,1,0:T(8,128)(2,1)S(1)}, bf16[96,64,128]{2,1,0:T(8,128)(2,1)S(1)}, f32[16,128]{1,0:T(8,128)S(1)}) custom-call(f32[3072,128]{1,0:T(8,128)S(1)} %bitcast.14, f32[8,32,8,128]{3,2,1,0:T(8,128)S(1)} %copy-done.7, f32[3,32,32,128]{3,2,1,0:T(8,128)S(1)} %get-tuple-element.36.refs_2_, ...), custom_call_target="tpu_custom_call" | custom-call | flops 268435456 | bytes 8388608 | tf_op jit(solution)/shard_map/image/pallas_call | solution.py:46
  77.3 0.1 collective-permute-start.10
  77.3 1.2 %collective-permute-done.10.refs_1_ = f32[16,128]{1,0:T(8,128)S(1)} collective-permute-done((f32[16,128]{1,0:T(8,128)S(1)}, f32[16,128]{1,0:T(8,128)S(1)}, u32[]{:S(2)}, u32[]{:S(2)}) %collective-permute-start.10) | collective-permute-done | bytes 8224 | tf_op jit(solution)/shard_map/ppermute | solution.py:114
  78.5 18.7 %all_to_all.15.refs_0_ = f32[16,16,128]{2,1,0:T(8,128)S(1)} all-to-all(f32[16,16,128]{2,1,0:T(8,128)S(1)} %share_sums.1), channel_id=1, replica_groups=mesh['gx'=4,'gy'=2,'col'=4] {'gx','col'}, dimensions={0} | all-to-all | bytes 262144 | tf_op jit(solution)/shard_map/all_to_all | solution.py:1032
  97.2 0.0 copy-done.5
  97.2 8.7 %finish.1 = (f32[3072,128]{1,0:T(8,128)}, f32[3072,128]{1,0:T(8,128)}) custom-call(f32[16,16,128]{2,1,0:T(8,128)S(1)} %all_to_all.15.refs_0_, f32[3072,128]{1,0:T(8,128)S(1)} %bitcast.17, f32[3072,128]{1,0:T(8,128)S(1)} %bitcast.15, bf16[96,64,128]{2,1,0:T(8,128)(2,1)S(1)} %get-tuple-element.42.refs_3_, bf16[96,64,128]{2,1,0:T(8,128)(2,1)S(1)} %get-tuple-element.43.refs_4_), custom_call_target="tpu_custom_call" | custom-call | flops 134217728 | bytes 9437184 | tf_op jit(solution)/shard_map/finish/pallas_call | solution.py:46
  (13 shorter events, 0.0 us)
Async XLA Ops:
  0.6 1.4 %copy-start = (f32[3,32,4,8,128]{4,3,2,1,0:T(8,128)S(1)}, f32[3,32,4,8,128]{4,3,2,1,0:T(8,128)}, u32[]{:S(2)}) copy-start(f32[3,32,4,8,128]{4,3,2,1,0:T(8,128)} %param.9) | copy-start | bytes 4718596
  2.0 0.7 copy-start.10
  2.8 5.3 %copy-start.1 = (f32[3,32,4,8,128]{4,3,2,1,0:T(8,128)S(1)}, f32[3,32,4,8,128]{4,3,2,1,0:T(8,128)}, u32[]{:S(2)}) copy-start(f32[3,32,4,8,128]{4,3,2,1,0:T(8,128)} %param.9) | copy-start | bytes 4718596
  3.0 12.6 %collective-permute-start = (bf16[784,128]{1,0:T(8,128)(2,1)S(1)}, bf16[784,128]{1,0:T(8,128)(2,1)S(1)}, u32[]{:S(2)}, u32[]{:S(2)}) collective-permute-start(bf16[784,128]{1,0:T(8,128)(2,1)S(1)} %get-tuple-element.24.refs_4_), channel_id=1, source_target_pairs={{0,8},{8,0},{16,24},{24,16},{1,9},{9,1},{17,25},{25,17},{2,10},{10... | collective-permute-start | bytes 602120 | tf_op jit(solution)/shard_map/ppermute | solution.py:114
  6.0 9.6 %collective-permute-start.1 = (bf16[784,128]{1,0:T(8,128)(2,1)S(1)}, bf16[784,128]{1,0:T(8,128)(2,1)S(1)}, u32[]{:S(2)}, u32[]{:S(2)}) collective-permute-start(bf16[784,128]{1,0:T(8,128)(2,1)S(1)} %get-tuple-element.25), channel_id=1, source_target_pairs={{8,16},{16,8},{9,17},{17,9},{10,18},{18,10},{11,19},{19,11},{12,20... | collective-permute-start | bytes 602120 | tf_op jit(solution)/shard_map/ppermute | solution.py:114
  8.0 1.7 %copy-start.4 = (f32[48,3,4,8,128]{4,3,2,1,0:T(8,128)S(1)}, f32[48,3,4,8,128]{4,3,2,1,0:T(8,128)}, u32[]{:S(2)}) copy-start(f32[48,3,4,8,128]{4,3,2,1,0:T(8,128)} %param.14) | copy-start | bytes 7077892
  9.7 6.0 %copy-start.11 = (s32[4,8,128]{2,1,0:T(8,128)S(1)}, s32[4,8,128]{2,1,0:T(8,128)}, u32[]{:S(2)}) copy-start(s32[4,8,128]{2,1,0:T(8,128)} %param.10) | copy-start | bytes 49156
  14.2 1.4 %copy-start.2 = (bf16[96,96,128]{2,1,0:T(8,128)(2,1)}, bf16[96,96,128]{2,1,0:T(8,128)(2,1)S(1)}, u32[]{:S(2)}) copy-start(bf16[96,96,128]{2,1,0:T(8,128)(2,1)S(1)} %get-tuple-element.34.refs_3_) | copy-start | bytes 7077892
  16.6 16.0 %copy-start.12 = (bf16[64,1024]{1,0:T(8,128)(2,1)S(1)}, bf16[64,1024]{1,0:T(8,128)(2,1)}, u32[]{:S(2)}) copy-start(bf16[64,1024]{1,0:T(8,128)(2,1)} %refs_1_.2) | copy-start | bytes 393220
  16.6 27.2 %copy-start.19 = (f32[2,16]{1,0:T(2,128)S(1)}, f32[2,16]{1,0:T(2,128)}, u32[]{:S(2)}) copy-start(f32[2,16]{1,0:T(2,128)} %refs_0_.3) | copy-start | bytes 388
  16.6 16.0 %all-to-all-start = ((bf16[32,16,128]{2,1,0:T(8,128)(2,1)}), bf16[32,16,128]{2,1,0:T(8,128)(2,1)S(1)}, u32[]{:S(2)}, u32[]{:S(2)}) async-start(bf16[32,16,128]{2,1,0:T(8,128)(2,1)} %get-tuple-element.31), calls=%async_computation | async-start | bytes 262144 | tf_op jit(solution)/shard_map/all_to_all | solution.py:904
  24.2 1.4 %collective-permute-start.2 = (bf16[592,128]{1,0:T(8,128)(2,1)S(1)}, bf16[592,128]{1,0:T(8,128)(2,1)S(1)}, u32[]{:S(2)}, u32[]{:S(2)}) collective-permute-start(bf16[592,128]{1,0:T(8,128)(2,1)S(1)} %get-tuple-element.27), channel_id=1, source_target_pairs={{0,4},{4,0},{1,5},{5,1},{2,6},{6,2},{3,7},{7,3},{8,12},{12,8},{9,1... | collective-permute-start | bytes 454664 | tf_op jit(solution)/shard_map/ppermute | solution.py:114
  27.0 0.7 copy-start.8
  27.7 0.6 copy-start.17
  28.3 3.9 %collective-permute-start.3 = (bf16[112,128]{1,0:T(8,128)(2,1)S(1)}, bf16[112,128]{1,0:T(8,128)(2,1)S(1)}, u32[]{:S(2)}, u32[]{:S(2)}) collective-permute-start(bf16[112,128]{1,0:T(8,128)(2,1)S(1)} %get-tuple-element.29), channel_id=1, source_target_pairs={{0,1},{1,0},{2,3},{3,2},{4,5},{5,4},{6,7},{7,6},{8,9},{9,8},{10,11... | collective-permute-start | bytes 86024 | tf_op jit(solution)/shard_map/ppermute | solution.py:114
  30.1 2.1 %collective-permute-start.4 = (bf16[112,128]{1,0:T(8,128)(2,1)S(1)}, bf16[112,128]{1,0:T(8,128)(2,1)S(1)}, u32[]{:S(2)}, u32[]{:S(2)}) collective-permute-start(bf16[112,128]{1,0:T(8,128)(2,1)S(1)} %get-tuple-element.29), channel_id=1, source_target_pairs={{1,2},{2,1},{5,6},{6,5},{9,10},{10,9},{13,14},{14,13},{17,18},{18,... | collective-permute-start | bytes 86024 | tf_op jit(solution)/shard_map/ppermute | solution.py:114
  32.2 11.6 %copy-start.13 = (bf16[112,128]{1,0:T(8,128)(2,1)}, bf16[112,128]{1,0:T(8,128)(2,1)S(1)}, u32[]{:S(2)}) copy-start(bf16[112,128]{1,0:T(8,128)(2,1)S(1)} %collective-permute-done.3.refs_6_.refs_2_) | copy-start | bytes 86020
  32.2 11.6 %copy-start.15 = (bf16[112,128]{1,0:T(8,128)(2,1)}, bf16[112,128]{1,0:T(8,128)(2,1)S(1)}, u32[]{:S(2)}) copy-start(bf16[112,128]{1,0:T(8,128)(2,1)S(1)} %collective-permute-done.4.refs_7_.refs_3_) | copy-start | bytes 86020
  34.8 22.8 %all-to-all-start.1 = ((f32[16,1,16,128]{3,2,1,0:T(8,128)}), f32[16,1,16,128]{3,2,1,0:T(8,128)}, u32[]{:S(2)}, u32[]{:S(2)}) async-start(f32[16,1,16,128]{3,2,1,0:T(8,128)} %get-tuple-element.33), calls=%async_computation.1 | async-start | bytes 262144 | tf_op jit(solution)/shard_map/all_to_all | solution.py:939
  43.8 0.9 copy-start.9
  44.7 0.7 copy-start.14
  45.4 0.7 copy-start.16
  46.2 0.8 copy-start.18
  56.7 1.0 copy-start.6
  57.6 1.7 %copy-start.3 = (bf16[96,96,128]{2,1,0:T(8,128)(2,1)S(1)}, bf16[96,96,128]{2,1,0:T(8,128)(2,1)}, u32[]{:S(2)}) copy-start(bf16[96,96,128]{2,1,0:T(8,128)(2,1)} %copy-done.2) | copy-start | bytes 7077892
  59.3 10.3 %copy-start.7 = (f32[8,32,8,128]{3,2,1,0:T(8,128)S(1)}, f32[8,32,8,128]{3,2,1,0:T(8,128)}, u32[]{:S(2)}) copy-start(f32[8,32,8,128]{3,2,1,0:T(8,128)} %copy-done.6) | copy-start | bytes 3145732
  63.0 6.6 %collective-permute-start.5 = (bf16[768,128]{1,0:T(8,128)(2,1)S(1)}, bf16[768,128]{1,0:T(8,128)(2,1)S(1)}, u32[]{:S(2)}, u32[]{:S(2)}) collective-permute-start(bf16[768,128]{1,0:T(8,128)(2,1)S(1)} %get-tuple-element.37), channel_id=1, source_target_pairs={{0,8},{8,0},{16,24},{24,16},{1,9},{9,1},{17,25},{25,17},{2,10},{10... | collective-permute-start | bytes 589832 | tf_op jit(solution)/shard_map/ppermute | solution.py:114
  65.0 4.7 %collective-permute-start.6 = (bf16[768,128]{1,0:T(8,128)(2,1)S(1)}, bf16[768,128]{1,0:T(8,128)(2,1)S(1)}, u32[]{:S(2)}, u32[]{:S(2)}) collective-permute-start(bf16[768,128]{1,0:T(8,128)(2,1)S(1)} %get-tuple-element.38), channel_id=1, source_target_pairs={{8,16},{16,8},{9,17},{17,9},{10,18},{18,10},{11,19},{19,11},{12,20... | collective-permute-start | bytes 589832 | tf_op jit(solution)/shard_map/ppermute | solution.py:114
  65.6 4.0 %collective-permute-start.7 = (bf16[384,128]{1,0:T(8,128)(2,1)S(1)}, bf16[384,128]{1,0:T(8,128)(2,1)S(1)}, u32[]{:S(2)}, u32[]{:S(2)}) collective-permute-start(bf16[384,128]{1,0:T(8,128)(2,1)S(1)} %get-tuple-element.39), channel_id=1, source_target_pairs={{0,4},{4,0},{1,5},{5,1},{2,6},{6,2},{3,7},{7,3},{8,12},{12,8},{9,1... | collective-permute-start | bytes 294920 | tf_op jit(solution)/shard_map/ppermute | solution.py:114
  65.7 3.9 %collective-permute-start.8 = (bf16[96,128]{1,0:T(8,128)(2,1)S(1)}, bf16[96,128]{1,0:T(8,128)(2,1)S(1)}, u32[]{:S(2)}, u32[]{:S(2)}) collective-permute-start(bf16[96,128]{1,0:T(8,128)(2,1)S(1)} %get-tuple-element.40), channel_id=1, source_target_pairs={{0,1},{1,0},{2,3},{3,2},{4,5},{5,4},{6,7},{7,6},{8,9},{9,8},{10,11... | collective-permute-start | bytes 73736 | tf_op jit(solution)/shard_map/ppermute | solution.py:114
  67.2 2.4 %collective-permute-start.9 = (bf16[96,128]{1,0:T(8,128)(2,1)S(1)}, bf16[96,128]{1,0:T(8,128)(2,1)S(1)}, u32[]{:S(2)}, u32[]{:S(2)}) collective-permute-start(bf16[96,128]{1,0:T(8,128)(2,1)S(1)} %get-tuple-element.40), channel_id=1, source_target_pairs={{1,2},{2,1},{5,6},{6,5},{9,10},{10,9},{13,14},{14,13},{17,18},{18,... | collective-permute-start | bytes 73736 | tf_op jit(solution)/shard_map/ppermute | solution.py:114
  69.6 27.6 %copy-start.5 = (f32[3,32,4,8,128]{4,3,2,1,0:T(8,128)S(1)}, f32[3,32,4,8,128]{4,3,2,1,0:T(8,128)}, u32[]{:S(2)}) copy-start(f32[3,32,4,8,128]{4,3,2,1,0:T(8,128)} %param.8) | copy-start | bytes 4718596
  77.3 1.2 %collective-permute-start.10 = (f32[16,128]{1,0:T(8,128)S(1)}, f32[16,128]{1,0:T(8,128)S(1)}, u32[]{:S(2)}, u32[]{:S(2)}) collective-permute-start(f32[16,128]{1,0:T(8,128)S(1)} %get-tuple-element.41.refs_0_), channel_id=1, source_target_pairs={{0,4},{4,0},{1,5},{5,1},{2,6},{6,2},{3,7},{7,3},{8,12},{12,8},{9,1... | collective-permute-start | bytes 24584 | tf_op jit(solution)/shard_map/ppermute | solution.py:114

commit v7 on v5

--- a/solution.py
+++ b/solution.py
@@ -182,8 +182,7 @@
             tile = index * 2 + half
             comp = tile // sz.cells
             hi, lo = split_hi_lo(basis[pl.ds(tile, slots, stride=sz.tiles), :])
-            split[tile, pl.ds(0, slots), :] = hi
-            split[tile, pl.ds(slots, slots), :] = lo
+            split[tile] = hi
             value_hi, value_lo = split_hi_lo(own_rows(sz, res, comp, tile - comp * sz.cells))
             basis_hi.append(hi)
             basis_lo.append(lo)
@@ -208,7 +207,7 @@
         for copy in copies[comp]:
             copy.wait()
         carry = lax.fori_loop(
-            comp * sz.cells // 2, (comp + 1) * sz.cells // 2, step, carry, unroll=4
+            comp * sz.cells // 2, (comp + 1) * sz.cells // 2, step, carry, unroll=8
         )
     both, low = carry
     pieces = both[:loads] + both[loads:] + low
@@ -514,7 +513,7 @@
     direction, own, zface = refs[:3]
     xsend, ysend, refs = take_halos(refs[3:], "gx", "gy")
     first, second, third, halos, inner, coefs, halo_coefs, mu_box, halo_mu, left, zedge = refs[:11]
-    wide, own_rows_coef, weights, lhs, near, starts, sem = refs[11:]
+    wide, own_rows_coef, weights, both_lhs, both_near, starts, sem = refs[11:]
     copy = pltpu.make_async_copy(starts_in, starts, sem)
     copy.start()
     loads, comps = sz.loads, sz.comps
@@ -558,8 +557,9 @@
 
     lane_k = lane_ids(loads)
 
-    def relax(source, level, x, ys, put):
+    def relax(source, level, x, ys, put, buffer):
         count = len(ys)
+        lhs, near = both_lhs.at[buffer], both_near.at[buffer]
         for j, y in enumerate(ys):
             place = x * sz.by + y
             here = (((lane_k + 1) >> 1) & 63) == place
@@ -604,11 +604,12 @@
         def put(j, place, comp, group, out):
             target[comp, place, pl.ds(group * 8, 8), :] = out
 
-        def at(x, carry):
-            relax(source, level, x, range(sz.by), put)
+        def at(pair, carry):
+            for buffer in range(2):
+                relax(source, level, 2 * pair + buffer, range(sz.by), put, buffer)
             return carry
 
-        lax.fori_loop(0, sz.bx, at, 0)
+        lax.fori_loop(0, sz.bx // 2, at, 0)
         coef = [halo_coefs[j] for j in range(8)]
         for group in range(groups):
             rows = pl.ds(group * 8, 8)
@@ -633,17 +634,23 @@
     left[...] = paired_left(mine, sz.slots, left)
     zedge[...] = jnp.zeros_like(zedge)
 
-    def final(x, carry):
+    def final(pair, carry):
+        for buffer in range(2):
+            finish_plane(2 * pair + buffer, buffer)
+        return carry
+
+    def finish_plane(x, buffer):
+        lhs, near = both_lhs.at[buffer], both_near.at[buffer]
+
         def put(j, place, comp, group, out):
             direction[comp, x * sz.cy + j, pl.ds(group * 8, 8), :] = out
 
-        relax(third, 2, x + 1, range(1, sz.cy + 1), put)
+        relax(third, 2, x + 1, range(1, sz.cy + 1), put, buffer)
         for y in range(sz.cy):
             cell = x * sz.cy + y
-            place = (x + 1) * sz.by + y + 1
             for comp in range(comps):
                 part = jnp.dot(
-                    left[:, : 2 * sz.slots],
+                    left[:, : sz.slots],
                     split[comp * sz.cells + cell],
                     preferred_element_type=F32,
                 )
@@ -662,12 +669,11 @@
                     near[pl.ds((y * comps + comp) * loads, loads), pl.ds(0, LANES)],
                     mask=(lane_k >> 1) == place,
                 )
-        return carry
 
     edge_row = lax.broadcasted_iota(jnp.int32, (LANES, LANES), 0)
     even_lane = (lane_ids(LANES) & 1) == 0
     edges = jnp.where(jnp.where(even_lane, LANES - 1, 0) == edge_row, 1.0, 0.0).astype(BF16)
-    lax.fori_loop(0, sz.cx, final, 0)
+    lax.fori_loop(0, sz.cx // 2, final, 0)
     zface[...] = zedge[...].astype(BF16)
     for comp in range(comps):
         for y in range(sz.cy):
@@ -680,43 +686,31 @@
 
 def make_image(sz, res, own, direction, *refs):
     xhalo, yhalo, zhalo, refs = take_halos(refs, "gx", "gy", "col")
-    dir_split, image_split, message, box, halo, weights, lhs, near, sem = refs
+    dir_split, image_split, message, halo, weights, both_lhs, both_near = refs
     weights[...] = neighbour_matrix(2, False)
     loads, comps = sz.loads, sz.comps
     groups = loads // 8
-    copies = []
     for comp in range(comps):
-        for x in range(sz.cx):
-            copies.append(
-                pltpu.make_async_copy(
-                    direction.at[comp, pl.ds(x * sz.cy, sz.cy)],
-                    box.at[comp, pl.ds((x + 1) * sz.by + 1, sz.cy)],
-                    sem.at[comp, x],
-                )
-            )
-    for copy in copies:
-        copy.start()
-    for comp in range(comps):
-        for y in range(sz.cy):
-            rows = pl.ds((comp * sz.cy + y) * loads, loads)
-            box[comp, y + 1] = xhalo.below(rows)
-            box[comp, (sz.bx - 1) * sz.by + y + 1] = xhalo.above(rows)
-        for x in range(sz.cx):
-            rows = pl.ds((comp * sz.cx + x) * loads, loads)
-            box[comp, (x + 1) * sz.by] = yhalo.below(rows)
-            box[comp, (x + 1) * sz.by + sz.by - 1] = yhalo.above(rows)
         halo[comp] = z_halo(zhalo, pl.ds(comp * loads, loads))
-    for copy in copies:
-        copy.wait()
     lane_k = lane_ids(loads)
-
-    def at(x, total):
+    total = jnp.zeros((2 * loads, 4 * loads), F32)
+
+    def field_at(comp, x, y):
+        if x < 0 or x == sz.cx:
+            side = xhalo.below if x < 0 else xhalo.above
+            return side(pl.ds((comp * sz.cy + y) * loads, loads))
+        if y < 0 or y == sz.cy:
+            side = yhalo.below if y < 0 else yhalo.above
+            return side(pl.ds((comp * sz.cx + x) * loads, loads))
+        return direction[comp, x * sz.cy + y]
+
+    for x in range(sz.cx):
+        lhs, near = both_lhs.at[x % 2], both_near.at[x % 2]
         for y in range(sz.cy):
             cell = x * sz.cy + y
-            place = (x + 1) * sz.by + y + 1
-            here = (((lane_k + 1) >> 1) & 63) == place
+            here = (((lane_k + 1) >> 1) & 63) == (x + 1) * sz.by + y + 1
             for comp in range(comps):
-                hi, lo = split_hi_lo(box[comp, place])
+                hi, lo = split_hi_lo(direction[comp, cell])
                 dir_split[comp * sz.cells + cell] = jnp.concatenate([hi, lo], axis=0)
                 rows = pl.ds((y * comps + comp) * loads, loads)
                 lhs[rows, pl.ds(0, LANES)] = hi
@@ -726,26 +720,20 @@
         sides = {}
         for y in range(sz.cy):
             cell = x * sz.cy + y
-            place = (x + 1) * sz.by + y + 1
-            coef = [own[j, cell] for j in range(8)]
-            parts = {}
-            for group in range(groups):
-                rows = pl.ds(group * 8, 8)
-                center = [box[comp, place, rows, :] for comp in range(comps)]
-                coupled = coef[1] * (center[0] + center[1] + center[2])
-                for comp in range(comps):
-                    line = pl.ds((y * comps + comp) * loads + group * 8, 8)
-                    out = coef[0] * center[comp] + coupled
-                    out = out - coef[2] * box[comp, place - sz.by, rows, :]
-                    out = out - coef[3] * box[comp, place + sz.by, rows, :]
-                    out = out - coef[4] * box[comp, place - 1, rows, :]
-                    out = out - coef[5] * box[comp, place + 1, rows, :]
-                    out = out - coef[6] * near[line, pl.ds(0, LANES)]
-                    parts[comp, group] = out - coef[7] * near[line, pl.ds(LANES, LANES)]
+            coef = [jnp.concatenate([own[j, cell]] * groups, axis=0) for j in range(8)]
+            center = [field_at(comp, x, y) for comp in range(comps)]
+            coupled = coef[1] * (center[0] + center[1] + center[2])
             for comp in range(comps):
                 tile = comp * sz.cells + cell
-                field = jnp.concatenate([parts[comp, group] for group in range(groups)], axis=0)
-                both = jnp.concatenate(split_hi_lo(field), axis=0)
+                line = pl.ds((y * comps + comp) * loads, loads)
+                out = coef[0] * center[comp] + coupled
+                out = out - coef[2] * field_at(comp, x - 1, y)
+                out = out - coef[3] * field_at(comp, x + 1, y)
+                out = out - coef[4] * field_at(comp, x, y - 1)
+                out = out - coef[5] * field_at(comp, x, y + 1)
+                out = out - coef[6] * near[line, pl.ds(0, LANES)]
+                out = out - coef[7] * near[line, pl.ds(LANES, LANES)]
+                both = jnp.concatenate(split_hi_lo(out), axis=0)
                 image_split[tile] = both
                 right = jnp.concatenate((both,) + split_hi_lo(own_rows(sz, res, comp, cell)), axis=0)
                 sides[y, comp] = (dir_split[tile], right)
@@ -756,9 +744,6 @@
                     total = total + lax.dot_general(
                         left, right, TRANSPOSED, preferred_element_type=F32
                     )
-        return total
-
-    total = lax.fori_loop(0, sz.cx, at, jnp.zeros((2 * loads, 4 * loads), F32))
     high, low = total[:loads], total[loads:]
     sums = high + roll_lanes(high, -loads) + low
     half = loads // 2
@@ -817,7 +802,7 @@
             new_residual[rows, :] = res[rows, :] - part[:, LANES:]
         return carry
 
-    lax.fori_loop(0, sz.cells, at, 0, unroll=4)
+    lax.fori_loop(0, sz.cells, at, 0, unroll=8)
 
 
 def body(
@@ -857,7 +842,7 @@
         make_pieces,
         [
             shape((sz.loads // 2, LANES), BF16),
-            shape((sz.tiles, 2 * sz.slots, LANES), BF16),
+            shape((sz.tiles, sz.slots, LANES), BF16),
         ],
         [
             scratch((sz.loads, LANES), F32),
@@ -954,12 +939,12 @@
             scratch((9, sz.box, 8, LANES), F32),
             scratch((8, sz.cells, LANES), F32),
             scratch((2 * LANES, 3 * LANES), BF16),
-            scratch((sz.by * sz.comps * sz.loads, 2 * LANES), BF16),
-            scratch((sz.by * sz.comps * sz.loads, 3 * LANES), F32),
+            scratch((2, sz.by * sz.comps * sz.loads, 2 * LANES), BF16),
+            scratch((2, sz.by * sz.comps * sz.loads, 3 * LANES), F32),
             smem(starts.shape, jnp.int32),
             dma,
         ],
-        26,
+        28,
         1 << 28,
         8 << 20,
         [eigen_counts, materials, starts, res, id_box, coarse, split] + xhalo + yhalo + zhalo,
@@ -978,18 +963,16 @@
             shape(sums_shape, F32),
         ],
         [
-            field,
             scratch((sz.comps, sz.loads, LANES), F32),
             scratch((3 * LANES, 2 * LANES), BF16),
-            scratch((sz.cy * sz.comps * sz.loads, 3 * LANES), BF16),
-            scratch((sz.cy * sz.comps * sz.loads, 2 * LANES), F32),
-            dma((sz.comps, sz.cx)),
+            scratch((2, sz.cy * sz.comps * sz.loads, 3 * LANES), BF16),
+            scratch((2, sz.cy * sz.comps * sz.loads, 2 * LANES), F32),
         ],
         20,
         1 << 28,
         8 << 20,
         [res, own, direction] + xhalo + yhalo + zhalo,
-        spaces=[vmem, vmem, pl.ANY] + [vmem] * len(xhalo + yhalo + zhalo),
+        spaces=[vmem] * (3 + len(xhalo + yhalo + zhalo)),
     )
     over, operands = AXES, [sums]
     if lax.axis_size("gy") == 2:

time: 99.1 us -> 97.3 us (0.982)
  Pallas kernels: 34.7 us -> 28.7 us
  local copies, waits for them, and re-layouts: 6.87 us -> 9.37 us
    pallas_call x9, Pallas kernels: 34.7 us -> 28.7 us  [vmem_call(): pl.pallas_call(kernel, name=name, out_shape=outs, in_specs=[pl.BlockSpec(...]
    unnamed x20 -> x30, local copies, waits for them, and re-layouts: 6.87 us -> 9.37 us
    ppermute x11, waiting for transfers between devices: 5.95 us -> 7.6 us  [exchange(): result.append(lax.ppermute(faces[parity], axis, pairs))]
  transfers between devices with their start and end apart: 13 -> 13, of which waited for: 6 -> 7; matrix products, arithmetic and copies ran while one was open for 0% -> 0% of each run, Pallas kernels for 6% -> 5%
where the time goes in v7:
time: 97.3 us; the launch traced here: 96.6 us
  Pallas kernels  28.7 us (29%)
  starting transfers between devices  27.3 us (28%)
  blocking collectives  16 us (16%)
  waiting for transfers between devices  13.2 us (14%)
  local copies, waits for them, and re-layouts  9.37 us (10%)
  between operations  2.11 us (2%)
    pallas_call x9, Pallas kernels, vmem_call(): pl.pallas_call(kernel, name=name, out_shape=outs, in_specs=[pl.BlockSpec(...  28.7 us
    ppermute x11, starting transfers between devices, exchange(): result.append(lax.ppermute(faces[parity], axis, pairs))  19 us
    all_to_all x1, blocking collectives, body(): sums = lax.all_to_all(spread, over, 0, 0, tiled=True)  16 us
    unnamed x30, local copies, waits for them, and re-layouts  9.37 us
    ppermute x11, waiting for transfers between devices, exchange(): result.append(lax.ppermute(faces[parity], axis, pairs))  7.6 us
    all_to_all x1, waiting for transfers between devices, body(): gathered = lax.all_to_all(message, AXES, 0, 0, tiled=True)  5.42 us
    all_to_all x1, starting transfers between devices, body(): gathered = lax.all_to_all(message, AXES, 0, 0, tiled=True)  4.84 us
    all_to_all x1, starting transfers between devices, body(): coarse = lax.all_to_all(partial, ('gx', 'col'), 0, 0, tiled=True)  3.51 us
  transfers between devices with their start and end apart: 13, of which 7 were waited for; matrix products, arithmetic and copies ran while one was open for 0% of the time, Pallas kernels for 5%

profile of v7, /device:TPU:0, one launch (start us, length us, event | category | flops | bytes accessed | tf_op | source)
XLA Modules:
  0.0 96.6 jit_solution(15688674440270365459)
XLA Ops:
  0.6 0.0 copy-start
  0.6 1.4 %copy-done = f32[3,32,4,8,128]{4,3,2,1,0:T(8,128)S(1)} copy-done((f32[3,32,4,8,128]{4,3,2,1,0:T(8,128)S(1)}, f32[3,32,4,8,128]{4,3,2,1,0:T(8,128)}, u32[]{:S(2)}) %copy-start) | copy-done | bytes 1572888
  2.0 0.0 copy-start.4
  2.0 0.7 copy-done.4
  2.8 0.0 copy-start.1
  2.8 0.3 pack_x.1
  3.0 0.8 collective-permute-start.1
  3.9 5.7 %collective-permute-start = (bf16[784,128]{1,0:T(8,128)(2,1)S(1)}, bf16[784,128]{1,0:T(8,128)(2,1)S(1)}, u32[]{:S(2)}, u32[]{:S(2)}) collective-permute-start(bf16[784,128]{1,0:T(8,128)(2,1)S(1)} %get-tuple-element.23.refs_4_), channel_id=1, source_target_pairs={{0,8},{8,0},{16,24},{24,16},{1,9},{9,1},{17,25},{25,17},{2,10},{10... | collective-permute-start | bytes 602120 | tf_op jit(solution)/shard_map/ppermute | solution.py:114
  10.9 0.0 copy-done.1
  10.9 0.0 copy-start.2
  10.9 1.7 %copy-done.2 = f32[48,3,4,8,128]{4,3,2,1,0:T(8,128)S(1)} copy-done((f32[48,3,4,8,128]{4,3,2,1,0:T(8,128)S(1)}, f32[48,3,4,8,128]{4,3,2,1,0:T(8,128)}, u32[]{:S(2)}) %copy-start.2) | copy-done | bytes 2359320
  12.6 0.0 copy-start.5
  12.6 3.9 %pieces.1 = (bf16[16,128]{1,0:T(8,128)(2,1)S(1)}, bf16[96,48,128]{2,1,0:T(8,128)(2,1)S(1)}) custom-call(s32[1]{0:T(128)S(6)} %copy.11.refs_0_, s32[1]{0:T(128)S(6)} %copy.12.refs_1_, f32[48,96,128]{2,1,0:T(8,128)S(1)} %bitcast.16, f32[3,1024,128]{2,1,0:T(8,128)S(1)} %bitcast.10, bf16[784,128]{1,0:T(8,128)(2,1)S(1)} %get-tuple-element.23.refs_4_), custom_call_target="tpu_custom_call" | custom-call | flops 134217728 | bytes 7340032 | tf_op jit(solution)/shard_map/pieces/pallas_call | solution.py:46
  16.5 0.0 collective-permute-done.1.refs_4_.refs_3_.refs_8_
  16.5 2.0 %collective-permute-done.refs_3_.refs_2_.refs_7_ = bf16[784,128]{1,0:T(8,128)(2,1)S(1)} collective-permute-done((bf16[784,128]{1,0:T(8,128)(2,1)S(1)}, bf16[784,128]{1,0:T(8,128)(2,1)S(1)}, u32[]{:S(2)}, u32[]{:S(2)}) %collective-permute-start) | collective-permute-done | bytes 200736 | tf_op jit(solution)/shard_map/ppermute | solution.py:114
  18.5 0.0 copy-done.5
  18.5 0.3 pack_y.1
  18.8 0.0 copy-start.8
  18.8 0.6 copy-done.8
  19.4 0.0 copy-start.14
  19.4 0.7 copy-done.14
  20.1 0.0 copy-start.13
  20.1 4.8 %all-to-all-start = ((bf16[32,16,128]{2,1,0:T(8,128)(2,1)}), bf16[32,16,128]{2,1,0:T(8,128)(2,1)S(1)}, u32[]{:S(2)}, u32[]{:S(2)}) async-start(bf16[32,16,128]{2,1,0:T(8,128)(2,1)} %copy-done.8), calls=%async_computation | async-start | bytes 262144 | tf_op jit(solution)/shard_map/all_to_all | solution.py:878
  24.9 0.3 collective-permute-start.2
  25.2 1.3 %collective-permute-done.2.refs_4_.refs_9_ = bf16[592,128]{1,0:T(8,128)(2,1)S(1)} collective-permute-done((bf16[592,128]{1,0:T(8,128)(2,1)}, bf16[592,128]{1,0:T(8,128)(2,1)S(1)}, u32[]{:S(2)}, u32[]{:S(2)}) %collective-permute-start.2) | collective-permute-done | bytes 151584 | tf_op jit(solution)/shard_map/ppermute | solution.py:114
  26.6 1.3 %pack_z.1 = (bf16[112,128]{1,0:T(8,128)(2,1)S(1)}, f32[128,128]{1,0:T(8,128)S(1)}) custom-call(f32[3072,128]{1,0:T(8,128)S(1)} %bitcast.12, s32[32,128]{1,0:T(8,128)S(1)} %bitcast.21, bf16[784,128]{1,0:T(8,128)(2,1)S(1)} %collective-permute-done.refs_3_.refs_2_.refs_7_, bf16[784,128]{1,0:T(8,128)(2,1)S(1)} %collective-permute-done.1.refs_4_.refs_3_.refs_8_, ...), custom_call_target="tpu_custom_call" | custom-call | flops 4194304 | bytes 3145728 | tf_op jit(solution)/shard_map/pack_z/pallas_call | solution.py:46
  27.9 5.4 %all-to-all-done.refs_0_ = bf16[32,16,128]{2,1,0:T(8,128)(2,1)S(1)} async-done(((bf16[32,16,128]{2,1,0:T(8,128)(2,1)}), bf16[32,16,128]{2,1,0:T(8,128)(2,1)S(1)}, u32[]{:S(2)}, u32[]{:S(2)}) %all-to-all-start) | async-done | bytes 131104 | tf_op jit(solution)/shard_map/all_to_all | solution.py:878
  33.3 0.0 copy-start.6
  33.3 0.9 copy-done.6
  34.2 1.5 %coarse.1 = (f32[16,1,16,128]{3,2,1,0:T(8,128)S(1)}, s32[8,128]{1,0:T(8,128)S(1)}) custom-call(bf16[32,16,128]{2,1,0:T(8,128)(2,1)S(1)} %all-to-all-done.refs_0_, bf16[64,1024]{1,0:T(8,128)(2,1)S(1)} %copy-done.6, bf16[112,128]{1,0:T(8,128)(2,1)S(1)} %get-tuple-element.28.refs_2_), custom_call_target="tpu_custom_call" | custom-call | flops 8388608 | bytes 1048576 | tf_op jit(solution)/shard_map/coarse/pallas_call | solution.py:46
  35.8 0.0 copy-start.7
  35.8 0.6 copy-done.7
  36.4 3.5 %all-to-all-start.1 = ((f32[16,1,16,128]{3,2,1,0:T(8,128)}), f32[16,1,16,128]{3,2,1,0:T(8,128)S(1)}, u32[]{:S(2)}, u32[]{:S(2)}) async-start(f32[16,1,16,128]{3,2,1,0:T(8,128)} %copy-done.7), calls=%async_computation.1 | async-start | bytes 262144 | tf_op jit(solution)/shard_map/all_to_all | solution.py:913
  40.0 0.7 collective-permute-start.4
  40.6 4.6 %collective-permute-start.3 = (bf16[112,128]{1,0:T(8,128)(2,1)S(1)}, bf16[112,128]{1,0:T(8,128)(2,1)S(1)}, u32[]{:S(2)}, u32[]{:S(2)}) collective-permute-start(bf16[112,128]{1,0:T(8,128)(2,1)S(1)} %get-tuple-element.28.refs_2_), channel_id=1, source_target_pairs={{0,1},{1,0},{2,3},{3,2},{4,5},{5,4},{6,7},{7,6},{8,9},{9,8},{10,11... | collective-permute-start | bytes 86024 | tf_op jit(solution)/shard_map/ppermute | solution.py:114
  45.2 0.0 collective-permute-done.4.refs_11_
  45.2 0.0 copy-start.9
  45.2 0.6 copy-done.9
  45.8 1.2 %collective-permute-done.3.refs_10_ = bf16[112,128]{1,0:T(8,128)(2,1)S(1)} collective-permute-done((bf16[112,128]{1,0:T(8,128)(2,1)S(1)}, bf16[112,128]{1,0:T(8,128)(2,1)S(1)}, u32[]{:S(2)}, u32[]{:S(2)}) %collective-permute-start.3) | collective-permute-done | bytes 28704 | tf_op jit(solution)/shard_map/ppermute | solution.py:114
  47.1 0.0 copy-start.11
  47.1 0.6 copy-done.11
  47.7 0.2 all-to-all-done.1
  47.8 0.0 copy-done.13
  47.8 0.0 copy-start.10
  47.8 0.7 copy-done.10
  48.6 0.7 copy-done.12
  49.3 10.9 %solve.1 = (f32[3,32,32,128]{3,2,1,0:T(8,128)S(1)}, f32[8,32,8,128]{3,2,1,0:T(8,128)S(1)}, bf16[96,128]{1,0:T(8,128)(2,1)S(1)}, bf16[768,128]{1,0:T(8,128)(2,1)S...) custom-call(s32[1]{0:T(128)S(6)} %copy.11.refs_0_, f32[2,16]{1,0:T(2,128)S(1)} %copy-done.13, ...), custom_call_target="tpu_custom_call" | custom-call | flops 268435456 | bytes 8388608 | tf_op jit(solution)/shard_map/solve/pallas_call | solution.py:46
  60.2 1.4 %collective-permute-start.5 = (bf16[768,128]{1,0:T(8,128)(2,1)S(1)}, bf16[768,128]{1,0:T(8,128)(2,1)S(1)}, u32[]{:S(2)}, u32[]{:S(2)}) collective-permute-start(bf16[768,128]{1,0:T(8,128)(2,1)S(1)} %get-tuple-element.35), channel_id=1, source_target_pairs={{0,8},{8,0},{16,24},{24,16},{1,9},{9,1},{17,25},{25,17},{2,10},{10... | collective-permute-start | bytes 589832 | tf_op jit(solution)/shard_map/ppermute | solution.py:114
  61.6 0.7 collective-permute-start.6
  62.3 0.1 collective-permute-start.7
  62.4 0.8 collective-permute-start.9
  63.2 3.9 %collective-permute-start.8 = (bf16[96,128]{1,0:T(8,128)(2,1)S(1)}, bf16[96,128]{1,0:T(8,128)(2,1)S(1)}, u32[]{:S(2)}, u32[]{:S(2)}) collective-permute-start(bf16[96,128]{1,0:T(8,128)(2,1)S(1)} %get-tuple-element.38), channel_id=1, source_target_pairs={{0,1},{1,0},{2,3},{3,2},{4,5},{5,4},{6,7},{7,6},{8,9},{9,8},{10,11... | collective-permute-start | bytes 73736 | tf_op jit(solution)/shard_map/ppermute | solution.py:114
  67.1 0.0 collective-permute-done.9.refs_7_
  67.1 1.8 %collective-permute-done.8.refs_6_ = bf16[96,128]{1,0:T(8,128)(2,1)S(1)} collective-permute-done((bf16[96,128]{1,0:T(8,128)(2,1)S(1)}, bf16[96,128]{1,0:T(8,128)(2,1)S(1)}, u32[]{:S(2)}, u32[]{:S(2)}) %collective-permute-start.8) | collective-permute-done | bytes 24608 | tf_op jit(solution)/shard_map/ppermute | solution.py:114
  68.9 0.0 collective-permute-done.7.refs_5_
  68.9 0.0 collective-permute-done.5.refs_3_
  68.9 0.0 collective-permute-done.6.refs_4_
  68.9 0.0 copy-start.3
  68.9 3.3 %image.1 = (bf16[96,64,128]{2,1,0:T(8,128)(2,1)S(1)}, bf16[96,64,128]{2,1,0:T(8,128)(2,1)S(1)}, f32[16,128]{1,0:T(8,128)S(1)}) custom-call(f32[3072,128]{1,0:T(8,128)S(1)} %bitcast.14, f32[8,32,8,128]{3,2,1,0:T(8,128)S(1)} %get-tuple-element.33.refs_1_, f32[3,32,32,128]{3,2,1,0:T(8,128)S(1)} %get-tuple-element.34.refs_2_, ...), custom_call_target="tpu_custom_call" | custom-call | flops 268435456 | bytes 8388608 | tf_op jit(solution)/shard_map/image/pallas_call | solution.py:46
  72.3 0.0 collective-permute-start.10
  72.3 1.2 %collective-permute-done.10.refs_1_ = f32[16,128]{1,0:T(8,128)S(1)} collective-permute-done((f32[16,128]{1,0:T(8,128)S(1)}, f32[16,128]{1,0:T(8,128)S(1)}, u32[]{:S(2)}, u32[]{:S(2)}) %collective-permute-start.10) | collective-permute-done | bytes 8224 | tf_op jit(solution)/shard_map/ppermute | solution.py:114
  73.5 16.0 %all_to_all.15.refs_0_ = f32[16,16,128]{2,1,0:T(8,128)S(1)} all-to-all(f32[16,16,128]{2,1,0:T(8,128)S(1)} %share_sums.1), channel_id=1, replica_groups=mesh['gx'=4,'gy'=2,'col'=4] {'gx','col'}, dimensions={0} | all-to-all | bytes 262144 | tf_op jit(solution)/shard_map/all_to_all | solution.py:986
  89.5 0.0 copy-done.3
  89.5 7.2 %finish.1 = (f32[3072,128]{1,0:T(8,128)}, f32[3072,128]{1,0:T(8,128)}) custom-call(f32[16,16,128]{2,1,0:T(8,128)S(1)} %all_to_all.15.refs_0_, f32[3072,128]{1,0:T(8,128)S(1)} %bitcast.17, f32[3072,128]{1,0:T(8,128)S(1)} %bitcast.15, bf16[96,64,128]{2,1,0:T(8,128)(2,1)S(1)} %get-tuple-element.40.refs_3_, bf16[96,64,128]{2,1,0:T(8,128)(2,1)S(1)} %get-tuple-element.41.refs_4_), custom_call_target="tpu_custom_call" | custom-call | flops 134217728 | bytes 9437184 | tf_op jit(solution)/shard_map/finish/pallas_call | solution.py:46
  (2 shorter events, 0.0 us)
Async XLA Ops:
  0.6 1.4 %copy-start = (f32[3,32,4,8,128]{4,3,2,1,0:T(8,128)S(1)}, f32[3,32,4,8,128]{4,3,2,1,0:T(8,128)}, u32[]{:S(2)}) copy-start(f32[3,32,4,8,128]{4,3,2,1,0:T(8,128)} %param.9) | copy-start | bytes 4718596
  2.0 0.7 copy-start.4
  2.8 8.1 %copy-start.1 = (f32[3,32,4,8,128]{4,3,2,1,0:T(8,128)S(1)}, f32[3,32,4,8,128]{4,3,2,1,0:T(8,128)}, u32[]{:S(2)}) copy-start(f32[3,32,4,8,128]{4,3,2,1,0:T(8,128)} %param.9) | copy-start | bytes 4718596
  3.0 13.4 %collective-permute-start.1 = (bf16[784,128]{1,0:T(8,128)(2,1)S(1)}, bf16[784,128]{1,0:T(8,128)(2,1)S(1)}, u32[]{:S(2)}, u32[]{:S(2)}) collective-permute-start(bf16[784,128]{1,0:T(8,128)(2,1)S(1)} %get-tuple-element.25), channel_id=1, source_target_pairs={{8,16},{16,8},{9,17},{17,9},{10,18},{18,10},{11,19},{19,11},{12,20... | collective-permute-start | bytes 602120 | tf_op jit(solution)/shard_map/ppermute | solution.py:114
  3.9 14.6 %collective-permute-start = (bf16[784,128]{1,0:T(8,128)(2,1)S(1)}, bf16[784,128]{1,0:T(8,128)(2,1)S(1)}, u32[]{:S(2)}, u32[]{:S(2)}) collective-permute-start(bf16[784,128]{1,0:T(8,128)(2,1)S(1)} %get-tuple-element.23.refs_4_), channel_id=1, source_target_pairs={{0,8},{8,0},{16,24},{24,16},{1,9},{9,1},{17,25},{25,17},{2,10},{10... | collective-permute-start | bytes 602120 | tf_op jit(solution)/shard_map/ppermute | solution.py:114
  10.9 1.7 %copy-start.2 = (f32[48,3,4,8,128]{4,3,2,1,0:T(8,128)S(1)}, f32[48,3,4,8,128]{4,3,2,1,0:T(8,128)}, u32[]{:S(2)}) copy-start(f32[48,3,4,8,128]{4,3,2,1,0:T(8,128)} %param.14) | copy-start | bytes 7077892
  12.6 5.9 %copy-start.5 = (s32[4,8,128]{2,1,0:T(8,128)S(1)}, s32[4,8,128]{2,1,0:T(8,128)}, u32[]{:S(2)}) copy-start(s32[4,8,128]{2,1,0:T(8,128)} %param.10) | copy-start | bytes 49156
  18.8 0.7 copy-start.8
  19.4 0.7 copy-start.14
  20.1 27.8 %copy-start.13 = (f32[2,16]{1,0:T(2,128)S(1)}, f32[2,16]{1,0:T(2,128)}, u32[]{:S(2)}) copy-start(f32[2,16]{1,0:T(2,128)} %refs_1_.4) | copy-start | bytes 388
  20.1 13.2 %all-to-all-start = ((bf16[32,16,128]{2,1,0:T(8,128)(2,1)}), bf16[32,16,128]{2,1,0:T(8,128)(2,1)S(1)}, u32[]{:S(2)}, u32[]{:S(2)}) async-start(bf16[32,16,128]{2,1,0:T(8,128)(2,1)} %copy-done.8), calls=%async_computation | async-start | bytes 262144 | tf_op jit(solution)/shard_map/all_to_all | solution.py:878
  24.9 1.7 %collective-permute-start.2 = (bf16[592,128]{1,0:T(8,128)(2,1)}, bf16[592,128]{1,0:T(8,128)(2,1)S(1)}, u32[]{:S(2)}, u32[]{:S(2)}) collective-permute-start(bf16[592,128]{1,0:T(8,128)(2,1)} %copy-done.14), channel_id=1, source_target_pairs={{0,4},{4,0},{1,5},{5,1},{2,6},{6,2},{3,7},{7,3},{8,12},{12,8},{9,1... | collective-permute-start | bytes 454664 | tf_op jit(solution)/shard_map/ppermute | solution.py:114
  33.3 0.9 copy-start.6
  35.8 0.7 copy-start.7
  36.4 11.4 %all-to-all-start.1 = ((f32[16,1,16,128]{3,2,1,0:T(8,128)}), f32[16,1,16,128]{3,2,1,0:T(8,128)S(1)}, u32[]{:S(2)}, u32[]{:S(2)}) async-start(f32[16,1,16,128]{3,2,1,0:T(8,128)} %copy-done.7), calls=%async_computation.1 | async-start | bytes 262144 | tf_op jit(solution)/shard_map/all_to_all | solution.py:913
  40.0 5.2 %collective-permute-start.4 = (bf16[112,128]{1,0:T(8,128)(2,1)S(1)}, bf16[112,128]{1,0:T(8,128)(2,1)S(1)}, u32[]{:S(2)}, u32[]{:S(2)}) collective-permute-start(bf16[112,128]{1,0:T(8,128)(2,1)S(1)} %get-tuple-element.28.refs_2_), channel_id=1, source_target_pairs={{1,2},{2,1},{5,6},{6,5},{9,10},{10,9},{13,14},{14,13},{17,18},{18,... | collective-permute-start | bytes 86024 | tf_op jit(solution)/shard_map/ppermute | solution.py:114
  40.6 6.4 %collective-permute-start.3 = (bf16[112,128]{1,0:T(8,128)(2,1)S(1)}, bf16[112,128]{1,0:T(8,128)(2,1)S(1)}, u32[]{:S(2)}, u32[]{:S(2)}) collective-permute-start(bf16[112,128]{1,0:T(8,128)(2,1)S(1)} %get-tuple-element.28.refs_2_), channel_id=1, source_target_pairs={{0,1},{1,0},{2,3},{3,2},{4,5},{5,4},{6,7},{7,6},{8,9},{9,8},{10,11... | collective-permute-start | bytes 86024 | tf_op jit(solution)/shard_map/ppermute | solution.py:114
  45.2 0.6 copy-start.9
  47.1 0.6 copy-start.11
  47.8 0.7 copy-start.10
  48.6 0.7 copy-start.12
  60.2 8.7 %collective-permute-start.5 = (bf16[768,128]{1,0:T(8,128)(2,1)S(1)}, bf16[768,128]{1,0:T(8,128)(2,1)S(1)}, u32[]{:S(2)}, u32[]{:S(2)}) collective-permute-start(bf16[768,128]{1,0:T(8,128)(2,1)S(1)} %get-tuple-element.35), channel_id=1, source_target_pairs={{0,8},{8,0},{16,24},{24,16},{1,9},{9,1},{17,25},{25,17},{2,10},{10... | collective-permute-start | bytes 589832 | tf_op jit(solution)/shard_map/ppermute | solution.py:114
  61.6 7.3 %collective-permute-start.6 = (bf16[768,128]{1,0:T(8,128)(2,1)S(1)}, bf16[768,128]{1,0:T(8,128)(2,1)S(1)}, u32[]{:S(2)}, u32[]{:S(2)}) collective-permute-start(bf16[768,128]{1,0:T(8,128)(2,1)S(1)} %get-tuple-element.36), channel_id=1, source_target_pairs={{8,16},{16,8},{9,17},{17,9},{10,18},{18,10},{11,19},{19,11},{12,20... | collective-permute-start | bytes 589832 | tf_op jit(solution)/shard_map/ppermute | solution.py:114
  62.3 6.6 %collective-permute-start.7 = (bf16[384,128]{1,0:T(8,128)(2,1)S(1)}, bf16[384,128]{1,0:T(8,128)(2,1)S(1)}, u32[]{:S(2)}, u32[]{:S(2)}) collective-permute-start(bf16[384,128]{1,0:T(8,128)(2,1)S(1)} %get-tuple-element.37), channel_id=1, source_target_pairs={{0,4},{4,0},{1,5},{5,1},{2,6},{6,2},{3,7},{7,3},{8,12},{12,8},{9,1... | collective-permute-start | bytes 294920 | tf_op jit(solution)/shard_map/ppermute | solution.py:114
  62.4 4.7 %collective-permute-start.9 = (bf16[96,128]{1,0:T(8,128)(2,1)S(1)}, bf16[96,128]{1,0:T(8,128)(2,1)S(1)}, u32[]{:S(2)}, u32[]{:S(2)}) collective-permute-start(bf16[96,128]{1,0:T(8,128)(2,1)S(1)} %get-tuple-element.38), channel_id=1, source_target_pairs={{1,2},{2,1},{5,6},{6,5},{9,10},{10,9},{13,14},{14,13},{17,18},{18,... | collective-permute-start | bytes 73736 | tf_op jit(solution)/shard_map/ppermute | solution.py:114
  63.2 5.7 %collective-permute-start.8 = (bf16[96,128]{1,0:T(8,128)(2,1)S(1)}, bf16[96,128]{1,0:T(8,128)(2,1)S(1)}, u32[]{:S(2)}, u32[]{:S(2)}) collective-permute-start(bf16[96,128]{1,0:T(8,128)(2,1)S(1)} %get-tuple-element.38), channel_id=1, source_target_pairs={{0,1},{1,0},{2,3},{3,2},{4,5},{5,4},{6,7},{7,6},{8,9},{9,8},{10,11... | collective-permute-start | bytes 73736 | tf_op jit(solution)/shard_map/ppermute | solution.py:114
  68.9 20.5 %copy-start.3 = (f32[3,32,4,8,128]{4,3,2,1,0:T(8,128)S(1)}, f32[3,32,4,8,128]{4,3,2,1,0:T(8,128)}, u32[]{:S(2)}) copy-start(f32[3,32,4,8,128]{4,3,2,1,0:T(8,128)} %param.8) | copy-start | bytes 4718596
  72.3 1.2 %collective-permute-start.10 = (f32[16,128]{1,0:T(8,128)S(1)}, f32[16,128]{1,0:T(8,128)S(1)}, u32[]{:S(2)}, u32[]{:S(2)}) collective-permute-start(f32[16,128]{1,0:T(8,128)S(1)} %get-tuple-element.39.refs_0_), channel_id=1, source_target_pairs={{0,4},{4,0},{1,5},{5,1},{2,6},{6,2},{3,7},{7,3},{8,12},{12,8},{9,1... | collective-permute-start | bytes 24584 | tf_op jit(solution)/shard_map/ppermute | solution.py:114

commit v8 on v7

--- a/solution.py
+++ b/solution.py
@@ -41,14 +41,17 @@
     return pltpu.roll(value, shift, axis=1)
 
 
-def vmem_call(name, kernel, outs, scratch, limit_mib, flops, moved, operands, spaces=None):
+def vmem_call(
+    name, kernel, outs, scratch, limit_mib, flops, moved, operands, spaces=None,
+    out_space=pltpu.VMEM,
+):
     spaces = spaces or [pltpu.VMEM] * len(operands)
     return pl.pallas_call(
         kernel,
         name=name,
         out_shape=outs,
         in_specs=[pl.BlockSpec(memory_space=space) for space in spaces],
-        out_specs=jax.tree.map(lambda _: pl.BlockSpec(memory_space=pltpu.VMEM), outs),
+        out_specs=jax.tree.map(lambda _: pl.BlockSpec(memory_space=out_space), outs),
         scratch_shapes=scratch,
         compiler_params=pltpu.CompilerParams(vmem_limit_bytes=limit_mib << 20),
         cost_estimate=pl.CostEstimate(flops=flops, bytes_accessed=moved, transcendentals=0),
@@ -182,7 +185,8 @@
             tile = index * 2 + half
             comp = tile // sz.cells
             hi, lo = split_hi_lo(basis[pl.ds(tile, slots, stride=sz.tiles), :])
-            split[tile] = hi
+            split[tile, pl.ds(0, slots), :] = hi
+            split[tile, pl.ds(slots, slots), :] = lo
             value_hi, value_lo = split_hi_lo(own_rows(sz, res, comp, tile - comp * sz.cells))
             basis_hi.append(hi)
             basis_lo.append(lo)
@@ -206,9 +210,8 @@
     for comp in range(sz.comps):
         for copy in copies[comp]:
             copy.wait()
-        carry = lax.fori_loop(
-            comp * sz.cells // 2, (comp + 1) * sz.cells // 2, step, carry, unroll=8
-        )
+        for index in range(comp * sz.cells // 2, (comp + 1) * sz.cells // 2):
+            carry = step(index, carry)
     both, low = carry
     pieces = both[:loads] + both[loads:] + low
     slot = lax.broadcasted_iota(jnp.int32, pieces.shape, 1)
@@ -482,8 +485,8 @@
         halo_coefs[target] = jnp.where(keep[j], dinv * faces[j], 0.0)
 
 
-def neighbour_matrix(copies, spread):
-    width = (3 if spread else 2) * LANES
+def neighbour_matrix(copies):
+    width = 2 * LANES
     parts = []
     for copy in range(copies + 1):
         row = lax.broadcasted_iota(jnp.int32, (LANES, width), 0)
@@ -491,13 +494,10 @@
         even = (row & 1) == 0
         if copy < copies:
             hit = ((lane < LANES) & (row == lane - 1)) | (
-                (lane >= LANES) & (lane < 2 * LANES) & (row == lane - LANES + 1)
+                (lane >= LANES) & (row == lane - LANES + 1)
             )
-            if spread:
-                source = jnp.where((lane & 1) == 0, 0, LANES - 1)
-                hit = hit | ((lane >= 2 * LANES) & (row == source))
         else:
-            hit = ((lane == 0) & even) | ((lane == 2 * LANES - 1) & jnp.logical_not(even))
+            hit = ((lane == 0) & even) | ((lane == width - 1) & jnp.logical_not(even))
         parts.append(jnp.where(hit, 1.0, 0.0).astype(BF16))
     return jnp.concatenate(parts, axis=0)
 
@@ -527,7 +527,7 @@
         mu_box, halo_mu,
     )
 
-    weights[...] = neighbour_matrix(1, True)
+    weights[...] = neighbour_matrix(1)
 
     def spread(place, carry):
         x = place // sz.by
@@ -568,9 +568,8 @@
                 lhs[rows, pl.ds(0, LANES)] = source[comp, place].astype(BF16)
                 lhs[rows, pl.ds(LANES, LANES)] = jnp.where(here, halos[level, comp], 0.0).astype(BF16)
         size = count * comps * loads
-        cut = 3 * LANES if level < 2 else 2 * LANES
-        near[pl.ds(0, size), pl.ds(0, cut)] = jnp.dot(
-            lhs[pl.ds(0, size), :], weights[:, pl.ds(0, cut)], preferred_element_type=F32
+        near[pl.ds(0, size), :] = jnp.dot(
+            lhs[pl.ds(0, size), :], weights[...], preferred_element_type=F32
         )
         for j, y in enumerate(ys):
             place = x * sz.by + y
@@ -596,7 +595,7 @@
                     if level < 2:
                         pltpu.store(
                             inner.at[level, comp, rows, :],
-                            near[at, pl.ds(2 * LANES, LANES)],
+                            pltpu.roll(value, 2 * place, axis=1),
                             mask=here,
                         )
 
@@ -650,7 +649,7 @@
             cell = x * sz.cy + y
             for comp in range(comps):
                 part = jnp.dot(
-                    left[:, : sz.slots],
+                    left[:, : 2 * sz.slots],
                     split[comp * sz.cells + cell],
                     preferred_element_type=F32,
                 )
@@ -687,7 +686,7 @@
 def make_image(sz, res, own, direction, *refs):
     xhalo, yhalo, zhalo, refs = take_halos(refs, "gx", "gy", "col")
     dir_split, image_split, message, halo, weights, both_lhs, both_near = refs
-    weights[...] = neighbour_matrix(2, False)
+    weights[...] = neighbour_matrix(2)
     loads, comps = sz.loads, sz.comps
     groups = loads // 8
     for comp in range(comps):
@@ -762,7 +761,8 @@
 
 
 def finish(
-    sz, sums, iterate, res, dir_split, image_split, new_iterate, new_residual, parts
+    sz, sums, iterate, res, dir_split, image_split, iterate_out, residual_out, parts, new_iterate,
+    new_residual, sem,
 ):
     loads = sz.loads
     total = sums[0]
@@ -791,8 +791,9 @@
     ) else step
     left = paired_left(padded, loads, parts)[:, : 2 * loads]
 
-    def at(cell, carry):
-        for comp in range(sz.comps):
+    writes = []
+    for comp in range(sz.comps):
+        for cell in range(sz.cells):
             tile = comp * sz.cells + cell
             right = jnp.concatenate([dir_split[tile], image_split[tile]], axis=1)
             part = jnp.dot(left, right, preferred_element_type=F32)
@@ -800,9 +801,14 @@
             rows = pl.ds(comp * loads * sz.cells + cell, loads, stride=sz.cells)
             new_iterate[rows, :] = iterate[rows, :] + part[:, :LANES]
             new_residual[rows, :] = res[rows, :] - part[:, LANES:]
-        return carry
-
-    lax.fori_loop(0, sz.cells, at, 0, unroll=8)
+        done = pl.ds(comp * loads * sz.cells, loads * sz.cells)
+        for j, (source, out) in enumerate(
+            ((new_iterate, iterate_out), (new_residual, residual_out))
+        ):
+            writes.append(pltpu.make_async_copy(source.at[done], out.at[done], sem.at[j, comp]))
+            writes[-1].start()
+    for copy in writes:
+        copy.wait()
 
 
 def body(
@@ -842,7 +848,7 @@
         make_pieces,
         [
             shape((sz.loads // 2, LANES), BF16),
-            shape((sz.tiles, sz.slots, LANES), BF16),
+            shape((sz.tiles, 2 * sz.slots, LANES), BF16),
         ],
         [
             scratch((sz.loads, LANES), F32),
@@ -938,9 +944,9 @@
             scratch((sz.face_z, LANES), F32),
             scratch((9, sz.box, 8, LANES), F32),
             scratch((8, sz.cells, LANES), F32),
-            scratch((2 * LANES, 3 * LANES), BF16),
+            scratch((2 * LANES, 2 * LANES), BF16),
             scratch((2, sz.by * sz.comps * sz.loads, 2 * LANES), BF16),
-            scratch((2, sz.by * sz.comps * sz.loads, 3 * LANES), F32),
+            scratch((2, sz.by * sz.comps * sz.loads, 2 * LANES), F32),
             smem(starts.shape, jnp.int32),
             dma,
         ],
@@ -989,11 +995,17 @@
         "finish",
         finish,
         [flat, flat],
-        [scratch((2 * sz.loads, LANES), BF16)],
-        16,
+        [
+            scratch((2 * sz.loads, LANES), BF16),
+            scratch(res.shape, F32),
+            scratch(res.shape, F32),
+            dma((2, sz.comps)),
+        ],
+        20,
         1 << 27,
         9 << 20,
         [sums, old, res, dir_split, image_split],
+        out_space=pl.ANY,
     )
     return (new_iterate.reshape(iterate.shape), new_residual.reshape(residual.shape))
 

time: 97.3 us -> 94.3 us (0.969)
  local copies, waits for them, and re-layouts: 9.37 us -> 6.87 us
    unnamed x30 -> x20, local copies, waits for them, and re-layouts: 9.37 us -> 6.87 us
where the time goes in v8:
time: 94.3 us; the launch traced here: 93.8 us
  Pallas kernels  28.3 us (30%)
  starting transfers between devices  26.7 us (28%)
  blocking collectives  16 us (17%)
  waiting for transfers between devices  13.8 us (15%)
  local copies, waits for them, and re-layouts  6.87 us (7%)
  between operations  2.25 us (2%)
    pallas_call x9, Pallas kernels, vmem_call(): pl.pallas_call(kernel, name=name, out_shape=outs, in_specs=[pl.BlockSpec(...  28.3 us
    ppermute x11, starting transfers between devices, exchange(): result.append(lax.ppermute(faces[parity], axis, pairs))  18.3 us
    all_to_all x1, blocking collectives, body(): sums = lax.all_to_all(spread, over, 0, 0, tiled=True)  16 us
    ppermute x11, waiting for transfers between devices, exchange(): result.append(lax.ppermute(faces[parity], axis, pairs))  7.35 us
    unnamed x20, local copies, waits for them, and re-layouts  6.87 us
    all_to_all x1, waiting for transfers between devices, body(): gathered = lax.all_to_all(message, AXES, 0, 0, tiled=True)  5.62 us
    all_to_all x1, starting transfers between devices, body(): gathered = lax.all_to_all(message, AXES, 0, 0, tiled=True)  4.84 us
    all_to_all x1, starting transfers between devices, body(): coarse = lax.all_to_all(partial, ('gx', 'col'), 0, 0, tiled=True)  3.52 us
  transfers between devices with their start and end apart: 13, of which 7 were waited for; matrix products, arithmetic and copies ran while one was open for 0% of the time, Pallas kernels for 5%

profile of v8, /device:TPU:0, one launch (start us, length us, event | category | flops | bytes accessed | tf_op | source)
XLA Modules:
  0.0 93.8 jit_solution(3443843606095126079)
XLA Ops:
  0.6 0.0 copy-start
  0.6 1.4 %copy-done = f32[3,32,4,8,128]{4,3,2,1,0:T(8,128)S(1)} copy-done((f32[3,32,4,8,128]{4,3,2,1,0:T(8,128)S(1)}, f32[3,32,4,8,128]{4,3,2,1,0:T(8,128)}, u32[]{:S(2)}) %copy-start) | copy-done | bytes 1572888
  2.0 0.0 copy-start.6
  2.0 0.7 copy-done.6
  2.8 0.0 copy-start.1
  2.8 0.3 pack_x.1
  3.0 0.8 collective-permute-start.1
  3.9 5.7 %collective-permute-start = (bf16[784,128]{1,0:T(8,128)(2,1)S(1)}, bf16[784,128]{1,0:T(8,128)(2,1)S(1)}, u32[]{:S(2)}, u32[]{:S(2)}) collective-permute-start(bf16[784,128]{1,0:T(8,128)(2,1)S(1)} %get-tuple-element.23.refs_4_), channel_id=1, source_target_pairs={{0,8},{8,0},{16,24},{24,16},{1,9},{9,1},{17,25},{25,17},{2,10},{10... | collective-permute-start | bytes 602120 | tf_op jit(solution)/shard_map/ppermute | solution.py:117
  10.9 0.0 copy-done.1
  10.9 0.0 copy-start.2
  10.9 1.7 %copy-done.2 = f32[48,3,4,8,128]{4,3,2,1,0:T(8,128)S(1)} copy-done((f32[48,3,4,8,128]{4,3,2,1,0:T(8,128)S(1)}, f32[48,3,4,8,128]{4,3,2,1,0:T(8,128)}, u32[]{:S(2)}) %copy-start.2) | copy-done | bytes 2359320
  12.6 0.0 copy-start.7
  12.6 3.1 %pieces.1 = (bf16[16,128]{1,0:T(8,128)(2,1)S(1)}, bf16[96,96,128]{2,1,0:T(8,128)(2,1)S(1)}) custom-call(s32[1]{0:T(128)S(6)} %copy.11.refs_0_, s32[1]{0:T(128)S(6)} %copy.12.refs_1_, f32[48,96,128]{2,1,0:T(8,128)S(1)} %bitcast.16, f32[3,1024,128]{2,1,0:T(8,128)S(1)} %bitcast.10, bf16[784,128]{1,0:T(8,128)(2,1)S(1)} %get-tuple-element.23.refs_4_), custom_call_target="tpu_custom_call" | custom-call | flops 134217728 | bytes 7340032 | tf_op jit(solution)/shard_map/pieces/pallas_call | solution.py:49
  15.7 0.0 copy-start.3
  15.7 1.4 %copy-done.3 = bf16[96,96,128]{2,1,0:T(8,128)(2,1)} copy-done((bf16[96,96,128]{2,1,0:T(8,128)(2,1)}, bf16[96,96,128]{2,1,0:T(8,128)(2,1)S(1)}, u32[]{:S(2)}) %copy-start.3) | copy-done | bytes 2359320
  17.1 0.0 collective-permute-done.1.refs_4_.refs_3_.refs_8_
  17.1 1.4 %collective-permute-done.refs_3_.refs_2_.refs_7_ = bf16[784,128]{1,0:T(8,128)(2,1)S(1)} collective-permute-done((bf16[784,128]{1,0:T(8,128)(2,1)S(1)}, bf16[784,128]{1,0:T(8,128)(2,1)S(1)}, u32[]{:S(2)}, u32[]{:S(2)}) %collective-permute-start) | collective-permute-done | bytes 200736 | tf_op jit(solution)/shard_map/ppermute | solution.py:117
  18.5 0.0 copy-done.7
  18.5 0.9 pack_y.1
  19.4 0.0 copy-start.8
  19.4 0.0 copy-start.9
  19.4 4.8 %all-to-all-start = ((bf16[32,16,128]{2,1,0:T(8,128)(2,1)}), bf16[32,16,128]{2,1,0:T(8,128)(2,1)S(1)}, u32[]{:S(2)}, u32[]{:S(2)}) async-start(bf16[32,16,128]{2,1,0:T(8,128)(2,1)} %get-tuple-element.26), calls=%async_computation | async-start | bytes 262144 | tf_op jit(solution)/shard_map/all_to_all | solution.py:884
  24.3 0.3 collective-permute-start.2
  24.6 1.1 %collective-permute-done.2.refs_4_.refs_9_ = bf16[592,128]{1,0:T(8,128)(2,1)S(1)} collective-permute-done((bf16[592,128]{1,0:T(8,128)(2,1)S(1)}, bf16[592,128]{1,0:T(8,128)(2,1)S(1)}, u32[]{:S(2)}, u32[]{:S(2)}) %collective-permute-start.2) | collective-permute-done | bytes 151584 | tf_op jit(solution)/shard_map/ppermute | solution.py:117
  25.7 1.3 %pack_z.1 = (bf16[112,128]{1,0:T(8,128)(2,1)S(1)}, f32[128,128]{1,0:T(8,128)S(1)}) custom-call(f32[3072,128]{1,0:T(8,128)S(1)} %bitcast.12, s32[32,128]{1,0:T(8,128)S(1)} %bitcast.21, bf16[784,128]{1,0:T(8,128)(2,1)S(1)} %collective-permute-done.refs_3_.refs_2_.refs_7_, bf16[784,128]{1,0:T(8,128)(2,1)S(1)} %collective-permute-done.1.refs_4_.refs_3_.refs_8_, ...), custom_call_target="tpu_custom_call" | custom-call | flops 4194304 | bytes 3145728 | tf_op jit(solution)/shard_map/pack_z/pallas_call | solution.py:49
  27.0 5.6 %all-to-all-done.refs_0_ = bf16[32,16,128]{2,1,0:T(8,128)(2,1)S(1)} async-done(((bf16[32,16,128]{2,1,0:T(8,128)(2,1)}), bf16[32,16,128]{2,1,0:T(8,128)(2,1)S(1)}, u32[]{:S(2)}, u32[]{:S(2)}) %all-to-all-start) | async-done | bytes 131104 | tf_op jit(solution)/shard_map/all_to_all | solution.py:884
  32.7 0.0 copy-done.8
  32.7 2.2 %coarse.1 = (f32[16,1,16,128]{3,2,1,0:T(8,128)}, s32[8,128]{1,0:T(8,128)S(1)}) custom-call(bf16[32,16,128]{2,1,0:T(8,128)(2,1)S(1)} %all-to-all-done.refs_0_, bf16[64,1024]{1,0:T(8,128)(2,1)S(1)} %copy-done.8, bf16[112,128]{1,0:T(8,128)(2,1)S(1)} %get-tuple-element.28.refs_2_), custom_call_target="tpu_custom_call" | custom-call | flops 8388608 | bytes 1048576 | tf_op jit(solution)/shard_map/coarse/pallas_call | solution.py:49
  34.9 3.5 %all-to-all-start.1 = ((f32[16,1,16,128]{3,2,1,0:T(8,128)}), f32[16,1,16,128]{3,2,1,0:T(8,128)S(1)}, u32[]{:S(2)}, u32[]{:S(2)}) async-start(f32[16,1,16,128]{3,2,1,0:T(8,128)} %get-tuple-element.31), calls=%async_computation.1 | async-start | bytes 262144 | tf_op jit(solution)/shard_map/all_to_all | solution.py:919
  38.4 0.7 collective-permute-start.4
  39.1 4.6 %collective-permute-start.3 = (bf16[112,128]{1,0:T(8,128)(2,1)S(1)}, bf16[112,128]{1,0:T(8,128)(2,1)S(1)}, u32[]{:S(2)}, u32[]{:S(2)}) collective-permute-start(bf16[112,128]{1,0:T(8,128)(2,1)S(1)} %get-tuple-element.28.refs_2_), channel_id=1, source_target_pairs={{0,1},{1,0},{2,3},{3,2},{4,5},{5,4},{6,7},{7,6},{8,9},{9,8},{10,11... | collective-permute-start | bytes 86024 | tf_op jit(solution)/shard_map/ppermute | solution.py:117
  43.7 0.0 collective-permute-done.4.refs_11_
  43.7 1.8 %collective-permute-done.3.refs_10_ = bf16[112,128]{1,0:T(8,128)(2,1)S(1)} collective-permute-done((bf16[112,128]{1,0:T(8,128)(2,1)S(1)}, bf16[112,128]{1,0:T(8,128)(2,1)S(1)}, u32[]{:S(2)}, u32[]{:S(2)}) %collective-permute-start.3) | collective-permute-done | bytes 28704 | tf_op jit(solution)/shard_map/ppermute | solution.py:117
  45.5 0.8 all-to-all-done.1
  46.3 0.0 copy-done.9
  46.3 0.0 copy-start.4
  46.3 1.7 %copy-done.4 = bf16[96,96,128]{2,1,0:T(8,128)(2,1)S(1)} copy-done((bf16[96,96,128]{2,1,0:T(8,128)(2,1)S(1)}, bf16[96,96,128]{2,1,0:T(8,128)(2,1)}, u32[]{:S(2)}) %copy-start.4) | copy-done | bytes 2359320
  47.9 10.9 %solve.1 = (f32[3,32,32,128]{3,2,1,0:T(8,128)S(1)}, f32[8,32,8,128]{3,2,1,0:T(8,128)S(1)}, bf16[96,128]{1,0:T(8,128)(2,1)S(1)}, bf16[768,128]{1,0:T(8,128)(2,1)S...) custom-call(s32[1]{0:T(128)S(6)} %copy.11.refs_0_, f32[2,16]{1,0:T(2,128)S(1)} %copy-done.9, ...), custom_call_target="tpu_custom_call" | custom-call | flops 268435456 | bytes 8388608 | tf_op jit(solution)/shard_map/solve/pallas_call | solution.py:49
  58.9 0.9 collective-permute-start.5
  59.8 0.7 collective-permute-start.6
  60.5 0.1 collective-permute-start.7
  60.6 0.8 collective-permute-start.9
  61.4 3.7 %collective-permute-start.8 = (bf16[96,128]{1,0:T(8,128)(2,1)S(1)}, bf16[96,128]{1,0:T(8,128)(2,1)S(1)}, u32[]{:S(2)}, u32[]{:S(2)}) collective-permute-start(bf16[96,128]{1,0:T(8,128)(2,1)S(1)} %get-tuple-element.38), channel_id=1, source_target_pairs={{0,1},{1,0},{2,3},{3,2},{4,5},{5,4},{6,7},{7,6},{8,9},{9,8},{10,11... | collective-permute-start | bytes 73736 | tf_op jit(solution)/shard_map/ppermute | solution.py:117
  65.2 0.0 collective-permute-done.9.refs_7_
  65.2 1.8 %collective-permute-done.8.refs_6_ = bf16[96,128]{1,0:T(8,128)(2,1)S(1)} collective-permute-done((bf16[96,128]{1,0:T(8,128)(2,1)S(1)}, bf16[96,128]{1,0:T(8,128)(2,1)S(1)}, u32[]{:S(2)}, u32[]{:S(2)}) %collective-permute-start.8) | collective-permute-done | bytes 24608 | tf_op jit(solution)/shard_map/ppermute | solution.py:117
  67.0 0.0 collective-permute-done.7.refs_5_
  67.0 0.0 collective-permute-done.5.refs_3_
  67.0 0.0 collective-permute-done.6.refs_4_
  67.0 0.0 copy-start.5
  67.0 3.3 %image.1 = (bf16[96,64,128]{2,1,0:T(8,128)(2,1)S(1)}, bf16[96,64,128]{2,1,0:T(8,128)(2,1)S(1)}, f32[16,128]{1,0:T(8,128)S(1)}) custom-call(f32[3072,128]{1,0:T(8,128)S(1)} %bitcast.14, f32[8,32,8,128]{3,2,1,0:T(8,128)S(1)} %get-tuple-element.33.refs_1_, f32[3,32,32,128]{3,2,1,0:T(8,128)S(1)} %get-tuple-element.34.refs_2_, ...), custom_call_target="tpu_custom_call" | custom-call | flops 268435456 | bytes 8388608 | tf_op jit(solution)/shard_map/image/pallas_call | solution.py:49
  70.3 0.0 collective-permute-start.10
  70.3 1.2 %collective-permute-done.10.refs_1_ = f32[16,128]{1,0:T(8,128)S(1)} collective-permute-done((f32[16,128]{1,0:T(8,128)S(1)}, f32[16,128]{1,0:T(8,128)S(1)}, u32[]{:S(2)}, u32[]{:S(2)}) %collective-permute-start.10) | collective-permute-done | bytes 8224 | tf_op jit(solution)/shard_map/ppermute | solution.py:117
  71.5 16.0 %all_to_all.15.refs_0_ = f32[16,16,128]{2,1,0:T(8,128)S(1)} all-to-all(f32[16,16,128]{2,1,0:T(8,128)S(1)} %share_sums.1), channel_id=1, replica_groups=mesh['gx'=4,'gy'=2,'col'=4] {'gx','col'}, dimensions={0} | all-to-all | bytes 262144 | tf_op jit(solution)/shard_map/all_to_all | solution.py:992
  87.5 0.0 copy-done.5
  87.5 6.2 %finish.1 = (f32[3072,128]{1,0:T(8,128)}, f32[3072,128]{1,0:T(8,128)}) custom-call(f32[16,16,128]{2,1,0:T(8,128)S(1)} %all_to_all.15.refs_0_, f32[3072,128]{1,0:T(8,128)S(1)} %bitcast.17, f32[3072,128]{1,0:T(8,128)S(1)} %bitcast.15, bf16[96,64,128]{2,1,0:T(8,128)(2,1)S(1)} %get-tuple-element.40.refs_3_, bf16[96,64,128]{2,1,0:T(8,128)(2,1)S(1)} %get-tuple-element.41.refs_4_), custom_call_target="tpu_custom_call" | custom-call | flops 134217728 | bytes 9437184 | tf_op jit(solution)/shard_map/finish/pallas_call | solution.py:49
  (1 shorter events, 0.0 us)
Async XLA Ops:
  0.6 1.4 %copy-start = (f32[3,32,4,8,128]{4,3,2,1,0:T(8,128)S(1)}, f32[3,32,4,8,128]{4,3,2,1,0:T(8,128)}, u32[]{:S(2)}) copy-start(f32[3,32,4,8,128]{4,3,2,1,0:T(8,128)} %param.9) | copy-start | bytes 4718596
  2.0 0.7 copy-start.6
  2.8 8.1 %copy-start.1 = (f32[3,32,4,8,128]{4,3,2,1,0:T(8,128)S(1)}, f32[3,32,4,8,128]{4,3,2,1,0:T(8,128)}, u32[]{:S(2)}) copy-start(f32[3,32,4,8,128]{4,3,2,1,0:T(8,128)} %param.9) | copy-start | bytes 4718596
  3.0 14.1 %collective-permute-start.1 = (bf16[784,128]{1,0:T(8,128)(2,1)S(1)}, bf16[784,128]{1,0:T(8,128)(2,1)S(1)}, u32[]{:S(2)}, u32[]{:S(2)}) collective-permute-start(bf16[784,128]{1,0:T(8,128)(2,1)S(1)} %get-tuple-element.25), channel_id=1, source_target_pairs={{8,16},{16,8},{9,17},{17,9},{10,18},{18,10},{11,19},{19,11},{12,20... | collective-permute-start | bytes 602120 | tf_op jit(solution)/shard_map/ppermute | solution.py:117
  3.9 14.6 %collective-permute-start = (bf16[784,128]{1,0:T(8,128)(2,1)S(1)}, bf16[784,128]{1,0:T(8,128)(2,1)S(1)}, u32[]{:S(2)}, u32[]{:S(2)}) collective-permute-start(bf16[784,128]{1,0:T(8,128)(2,1)S(1)} %get-tuple-element.23.refs_4_), channel_id=1, source_target_pairs={{0,8},{8,0},{16,24},{24,16},{1,9},{9,1},{17,25},{25,17},{2,10},{10... | collective-permute-start | bytes 602120 | tf_op jit(solution)/shard_map/ppermute | solution.py:117
  10.9 1.7 %copy-start.2 = (f32[48,3,4,8,128]{4,3,2,1,0:T(8,128)S(1)}, f32[48,3,4,8,128]{4,3,2,1,0:T(8,128)}, u32[]{:S(2)}) copy-start(f32[48,3,4,8,128]{4,3,2,1,0:T(8,128)} %param.14) | copy-start | bytes 7077892
  12.6 5.9 %copy-start.7 = (s32[4,8,128]{2,1,0:T(8,128)S(1)}, s32[4,8,128]{2,1,0:T(8,128)}, u32[]{:S(2)}) copy-start(s32[4,8,128]{2,1,0:T(8,128)} %param.10) | copy-start | bytes 49156
  15.7 1.4 %copy-start.3 = (bf16[96,96,128]{2,1,0:T(8,128)(2,1)}, bf16[96,96,128]{2,1,0:T(8,128)(2,1)S(1)}, u32[]{:S(2)}) copy-start(bf16[96,96,128]{2,1,0:T(8,128)(2,1)S(1)} %get-tuple-element.32.refs_6_) | copy-start | bytes 7077892
  19.4 13.3 %copy-start.8 = (bf16[64,1024]{1,0:T(8,128)(2,1)S(1)}, bf16[64,1024]{1,0:T(8,128)(2,1)}, u32[]{:S(2)}) copy-start(bf16[64,1024]{1,0:T(8,128)(2,1)} %refs_1_.3) | copy-start | bytes 393220
  19.4 26.9 %copy-start.9 = (f32[2,16]{1,0:T(2,128)S(1)}, f32[2,16]{1,0:T(2,128)}, u32[]{:S(2)}) copy-start(f32[2,16]{1,0:T(2,128)} %refs_1_.4) | copy-start | bytes 388
  19.4 13.2 %all-to-all-start = ((bf16[32,16,128]{2,1,0:T(8,128)(2,1)}), bf16[32,16,128]{2,1,0:T(8,128)(2,1)S(1)}, u32[]{:S(2)}, u32[]{:S(2)}) async-start(bf16[32,16,128]{2,1,0:T(8,128)(2,1)} %get-tuple-element.26), calls=%async_computation | async-start | bytes 262144 | tf_op jit(solution)/shard_map/all_to_all | solution.py:884
  24.3 1.4 %collective-permute-start.2 = (bf16[592,128]{1,0:T(8,128)(2,1)S(1)}, bf16[592,128]{1,0:T(8,128)(2,1)S(1)}, u32[]{:S(2)}, u32[]{:S(2)}) collective-permute-start(bf16[592,128]{1,0:T(8,128)(2,1)S(1)} %get-tuple-element.27), channel_id=1, source_target_pairs={{0,4},{4,0},{1,5},{5,1},{2,6},{6,2},{3,7},{7,3},{8,12},{12,8},{9,1... | collective-permute-start | bytes 454664 | tf_op jit(solution)/shard_map/ppermute | solution.py:117
  34.9 11.4 %all-to-all-start.1 = ((f32[16,1,16,128]{3,2,1,0:T(8,128)}), f32[16,1,16,128]{3,2,1,0:T(8,128)S(1)}, u32[]{:S(2)}, u32[]{:S(2)}) async-start(f32[16,1,16,128]{3,2,1,0:T(8,128)} %get-tuple-element.31), calls=%async_computation.1 | async-start | bytes 262144 | tf_op jit(solution)/shard_map/all_to_all | solution.py:919
  38.4 5.2 %collective-permute-start.4 = (bf16[112,128]{1,0:T(8,128)(2,1)S(1)}, bf16[112,128]{1,0:T(8,128)(2,1)S(1)}, u32[]{:S(2)}, u32[]{:S(2)}) collective-permute-start(bf16[112,128]{1,0:T(8,128)(2,1)S(1)} %get-tuple-element.28.refs_2_), channel_id=1, source_target_pairs={{1,2},{2,1},{5,6},{6,5},{9,10},{10,9},{13,14},{14,13},{17,18},{18,... | collective-permute-start | bytes 86024 | tf_op jit(solution)/shard_map/ppermute | solution.py:117
  39.1 6.4 %collective-permute-start.3 = (bf16[112,128]{1,0:T(8,128)(2,1)S(1)}, bf16[112,128]{1,0:T(8,128)(2,1)S(1)}, u32[]{:S(2)}, u32[]{:S(2)}) collective-permute-start(bf16[112,128]{1,0:T(8,128)(2,1)S(1)} %get-tuple-element.28.refs_2_), channel_id=1, source_target_pairs={{0,1},{1,0},{2,3},{3,2},{4,5},{5,4},{6,7},{7,6},{8,9},{9,8},{10,11... | collective-permute-start | bytes 86024 | tf_op jit(solution)/shard_map/ppermute | solution.py:117
  46.3 1.7 %copy-start.4 = (bf16[96,96,128]{2,1,0:T(8,128)(2,1)S(1)}, bf16[96,96,128]{2,1,0:T(8,128)(2,1)}, u32[]{:S(2)}) copy-start(bf16[96,96,128]{2,1,0:T(8,128)(2,1)} %copy-done.3) | copy-start | bytes 7077892
  58.9 8.1 %collective-permute-start.5 = (bf16[768,128]{1,0:T(8,128)(2,1)S(1)}, bf16[768,128]{1,0:T(8,128)(2,1)S(1)}, u32[]{:S(2)}, u32[]{:S(2)}) collective-permute-start(bf16[768,128]{1,0:T(8,128)(2,1)S(1)} %get-tuple-element.35), channel_id=1, source_target_pairs={{0,8},{8,0},{16,24},{24,16},{1,9},{9,1},{17,25},{25,17},{2,10},{10... | collective-permute-start | bytes 589832 | tf_op jit(solution)/shard_map/ppermute | solution.py:117
  59.8 7.2 %collective-permute-start.6 = (bf16[768,128]{1,0:T(8,128)(2,1)S(1)}, bf16[768,128]{1,0:T(8,128)(2,1)S(1)}, u32[]{:S(2)}, u32[]{:S(2)}) collective-permute-start(bf16[768,128]{1,0:T(8,128)(2,1)S(1)} %get-tuple-element.36), channel_id=1, source_target_pairs={{8,16},{16,8},{9,17},{17,9},{10,18},{18,10},{11,19},{19,11},{12,20... | collective-permute-start | bytes 589832 | tf_op jit(solution)/shard_map/ppermute | solution.py:117
  60.5 6.5 %collective-permute-start.7 = (bf16[384,128]{1,0:T(8,128)(2,1)S(1)}, bf16[384,128]{1,0:T(8,128)(2,1)S(1)}, u32[]{:S(2)}, u32[]{:S(2)}) collective-permute-start(bf16[384,128]{1,0:T(8,128)(2,1)S(1)} %get-tuple-element.37), channel_id=1, source_target_pairs={{0,4},{4,0},{1,5},{5,1},{2,6},{6,2},{3,7},{7,3},{8,12},{12,8},{9,1... | collective-permute-start | bytes 294920 | tf_op jit(solution)/shard_map/ppermute | solution.py:117
  60.6 4.6 %collective-permute-start.9 = (bf16[96,128]{1,0:T(8,128)(2,1)S(1)}, bf16[96,128]{1,0:T(8,128)(2,1)S(1)}, u32[]{:S(2)}, u32[]{:S(2)}) collective-permute-start(bf16[96,128]{1,0:T(8,128)(2,1)S(1)} %get-tuple-element.38), channel_id=1, source_target_pairs={{1,2},{2,1},{5,6},{6,5},{9,10},{10,9},{13,14},{14,13},{17,18},{18,... | collective-permute-start | bytes 73736 | tf_op jit(solution)/shard_map/ppermute | solution.py:117
  61.4 5.5 %collective-permute-start.8 = (bf16[96,128]{1,0:T(8,128)(2,1)S(1)}, bf16[96,128]{1,0:T(8,128)(2,1)S(1)}, u32[]{:S(2)}, u32[]{:S(2)}) collective-permute-start(bf16[96,128]{1,0:T(8,128)(2,1)S(1)} %get-tuple-element.38), channel_id=1, source_target_pairs={{0,1},{1,0},{2,3},{3,2},{4,5},{5,4},{6,7},{7,6},{8,9},{9,8},{10,11... | collective-permute-start | bytes 73736 | tf_op jit(solution)/shard_map/ppermute | solution.py:117
  67.0 20.5 %copy-start.5 = (f32[3,32,4,8,128]{4,3,2,1,0:T(8,128)S(1)}, f32[3,32,4,8,128]{4,3,2,1,0:T(8,128)}, u32[]{:S(2)}) copy-start(f32[3,32,4,8,128]{4,3,2,1,0:T(8,128)} %param.8) | copy-start | bytes 4718596
  70.3 1.2 %collective-permute-start.10 = (f32[16,128]{1,0:T(8,128)S(1)}, f32[16,128]{1,0:T(8,128)S(1)}, u32[]{:S(2)}, u32[]{:S(2)}) collective-permute-start(f32[16,128]{1,0:T(8,128)S(1)} %get-tuple-element.39.refs_0_), channel_id=1, source_target_pairs={{0,4},{4,0},{1,5},{5,1},{2,6},{6,2},{3,7},{7,3},{8,12},{12,8},{9,1... | collective-permute-start | bytes 24584 | tf_op jit(solution)/shard_map/ppermute | solution.py:117

commit v9 on v8

--- a/solution.py
+++ b/solution.py
@@ -575,8 +575,12 @@
             place = x * sz.by + y
             coef = [wide[i, place] for i in range(9)]
             here = (((lane8 + 1) >> 1) & 63) == place
-            xm, xp = jnp.maximum(place - sz.by, 0), jnp.minimum(place + sz.by, sz.box - 1)
-            ym, yp = jnp.maximum(place - 1, 0), jnp.minimum(place + 1, sz.box - 1)
+            sides = [
+                (WXM, place - sz.by, x > 0),
+                (WXP, place + sz.by, x < sz.bx - 1),
+                (WYM, place - 1, y > 0),
+                (WYP, place + 1, y < sz.by - 1),
+            ]
             for group in range(groups):
                 rows = pl.ds(group * 8, 8)
                 center = [source[comp, place, rows, :] for comp in range(comps)]
@@ -585,17 +589,16 @@
                     value = center[comp]
                     at = pl.ds((j * comps + comp) * loads + group * 8, 8)
                     out = (first[comp, place, rows, :] - coupled) + coef[KEEP] * value
-                    out = out + coef[WXM] * source[comp, xm, rows, :]
-                    out = out + coef[WXP] * source[comp, xp, rows, :]
-                    out = out + coef[WYM] * source[comp, ym, rows, :]
-                    out = out + coef[WYP] * source[comp, yp, rows, :]
+                    for weight, other, inside in sides:
+                        if inside:
+                            out = out + coef[weight] * source[comp, other, rows, :]
                     out = out + coef[WZM] * near[at, pl.ds(0, LANES)]
                     out = out + coef[WZP] * near[at, pl.ds(LANES, LANES)]
                     put(j, place, comp, group, out)
                     if level < 2:
                         pltpu.store(
                             inner.at[level, comp, rows, :],
-                            pltpu.roll(value, 2 * place, axis=1),
+                            roll_lanes(value, 2 * place),
                             mask=here,
                         )
 
@@ -603,12 +606,8 @@
         def put(j, place, comp, group, out):
             target[comp, place, pl.ds(group * 8, 8), :] = out
 
-        def at(pair, carry):
-            for buffer in range(2):
-                relax(source, level, 2 * pair + buffer, range(sz.by), put, buffer)
-            return carry
-
-        lax.fori_loop(0, sz.bx // 2, at, 0)
+        for x in range(sz.bx):
+            relax(source, level, x, range(sz.by), put, x % 2)
         coef = [halo_coefs[j] for j in range(8)]
         for group in range(groups):
             rows = pl.ds(group * 8, 8)
@@ -632,11 +631,6 @@
     mine = jnp.where(lane_ids(loads) < jnp.minimum(count[0], sz.slots), mine, 0.0)
     left[...] = paired_left(mine, sz.slots, left)
     zedge[...] = jnp.zeros_like(zedge)
-
-    def final(pair, carry):
-        for buffer in range(2):
-            finish_plane(2 * pair + buffer, buffer)
-        return carry
 
     def finish_plane(x, buffer):
         lhs, near = both_lhs.at[buffer], both_near.at[buffer]
@@ -672,7 +666,8 @@
     edge_row = lax.broadcasted_iota(jnp.int32, (LANES, LANES), 0)
     even_lane = (lane_ids(LANES) & 1) == 0
     edges = jnp.where(jnp.where(even_lane, LANES - 1, 0) == edge_row, 1.0, 0.0).astype(BF16)
-    lax.fori_loop(0, sz.cx // 2, final, 0)
+    for x in range(sz.cx):
+        finish_plane(x, x % 2)
     zface[...] = zedge[...].astype(BF16)
     for comp in range(comps):
         for y in range(sz.cy):

time: 94.3 us -> 93.8 us (level)
  no operation moved by 1% of the time
where the time goes in v9:
time: 93.8 us; the launch traced here: 93.3 us
  Pallas kernels  27.5 us (29%)
  starting transfers between devices  26.8 us (29%)
  blocking collectives  16.2 us (17%)
  waiting for transfers between devices  13.6 us (14%)
  local copies, waits for them, and re-layouts  6.87 us (7%)
  between operations  2.27 us (2%)
    pallas_call x9, Pallas kernels, vmem_call(): pl.pallas_call(kernel, name=name, out_shape=outs, in_specs=[pl.BlockSpec(...  27.5 us
    ppermute x11, starting transfers between devices, exchange(): result.append(lax.ppermute(faces[parity], axis, pairs))  18.4 us
    all_to_all x1, blocking collectives, body(): sums = lax.all_to_all(spread, over, 0, 0, tiled=True)  16.2 us
    ppermute x11, waiting for transfers between devices, exchange(): result.append(lax.ppermute(faces[parity], axis, pairs))  7.35 us
    unnamed x20, local copies, waits for them, and re-layouts  6.87 us
    all_to_all x1, waiting for transfers between devices, body(): gathered = lax.all_to_all(message, AXES, 0, 0, tiled=True)  5.62 us
    all_to_all x1, starting transfers between devices, body(): gathered = lax.all_to_all(message, AXES, 0, 0, tiled=True)  4.84 us
    all_to_all x1, starting transfers between devices, body(): coarse = lax.all_to_all(partial, ('gx', 'col'), 0, 0, tiled=True)  3.52 us
  transfers between devices with their start and end apart: 13, of which 7 were waited for; matrix products, arithmetic and copies ran while one was open for 0% of the time, Pallas kernels for 5%

profile of v9, /device:TPU:0, one launch (start us, length us, event | category | flops | bytes accessed | tf_op | source)
XLA Modules:
  0.0 93.3 jit_solution(6045786554778757059)
XLA Ops:
  0.6 0.0 copy-start
  0.6 1.4 %copy-done = f32[3,32,4,8,128]{4,3,2,1,0:T(8,128)S(1)} copy-done((f32[3,32,4,8,128]{4,3,2,1,0:T(8,128)S(1)}, f32[3,32,4,8,128]{4,3,2,1,0:T(8,128)}, u32[]{:S(2)}) %copy-start) | copy-done | bytes 1572888
  2.0 0.0 copy-start.6
  2.0 0.7 copy-done.6
  2.8 0.0 copy-start.1
  2.8 0.3 pack_x.1
  3.0 0.8 collective-permute-start.1
  3.9 5.7 %collective-permute-start = (bf16[784,128]{1,0:T(8,128)(2,1)S(1)}, bf16[784,128]{1,0:T(8,128)(2,1)S(1)}, u32[]{:S(2)}, u32[]{:S(2)}) collective-permute-start(bf16[784,128]{1,0:T(8,128)(2,1)S(1)} %get-tuple-element.23.refs_4_), channel_id=1, source_target_pairs={{0,8},{8,0},{16,24},{24,16},{1,9},{9,1},{17,25},{25,17},{2,10},{10... | collective-permute-start | bytes 602120 | tf_op jit(solution)/shard_map/ppermute | solution.py:117
  10.9 0.0 copy-done.1
  10.9 0.0 copy-start.2
  10.9 1.7 %copy-done.2 = f32[48,3,4,8,128]{4,3,2,1,0:T(8,128)S(1)} copy-done((f32[48,3,4,8,128]{4,3,2,1,0:T(8,128)S(1)}, f32[48,3,4,8,128]{4,3,2,1,0:T(8,128)}, u32[]{:S(2)}) %copy-start.2) | copy-done | bytes 2359320
  12.6 0.0 copy-start.7
  12.6 3.1 %pieces.1 = (bf16[16,128]{1,0:T(8,128)(2,1)S(1)}, bf16[96,96,128]{2,1,0:T(8,128)(2,1)S(1)}) custom-call(s32[1]{0:T(128)S(6)} %copy.11.refs_0_, s32[1]{0:T(128)S(6)} %copy.12.refs_1_, f32[48,96,128]{2,1,0:T(8,128)S(1)} %bitcast.16, f32[3,1024,128]{2,1,0:T(8,128)S(1)} %bitcast.10, bf16[784,128]{1,0:T(8,128)(2,1)S(1)} %get-tuple-element.23.refs_4_), custom_call_target="tpu_custom_call" | custom-call | flops 134217728 | bytes 7340032 | tf_op jit(solution)/shard_map/pieces/pallas_call | solution.py:49
  15.7 0.0 copy-start.3
  15.7 1.4 %copy-done.3 = bf16[96,96,128]{2,1,0:T(8,128)(2,1)} copy-done((bf16[96,96,128]{2,1,0:T(8,128)(2,1)}, bf16[96,96,128]{2,1,0:T(8,128)(2,1)S(1)}, u32[]{:S(2)}) %copy-start.3) | copy-done | bytes 2359320
  17.1 0.0 collective-permute-done.1.refs_4_.refs_3_.refs_8_
  17.1 1.4 %collective-permute-done.refs_3_.refs_2_.refs_7_ = bf16[784,128]{1,0:T(8,128)(2,1)S(1)} collective-permute-done((bf16[784,128]{1,0:T(8,128)(2,1)S(1)}, bf16[784,128]{1,0:T(8,128)(2,1)S(1)}, u32[]{:S(2)}, u32[]{:S(2)}) %collective-permute-start) | collective-permute-done | bytes 200736 | tf_op jit(solution)/shard_map/ppermute | solution.py:117
  18.5 0.0 copy-done.7
  18.5 0.9 pack_y.1
  19.4 0.0 copy-start.8
  19.4 0.0 copy-start.9
  19.4 4.8 %all-to-all-start = ((bf16[32,16,128]{2,1,0:T(8,128)(2,1)}), bf16[32,16,128]{2,1,0:T(8,128)(2,1)S(1)}, u32[]{:S(2)}, u32[]{:S(2)}) async-start(bf16[32,16,128]{2,1,0:T(8,128)(2,1)} %get-tuple-element.26), calls=%async_computation | async-start | bytes 262144 | tf_op jit(solution)/shard_map/all_to_all | solution.py:879
  24.3 0.3 collective-permute-start.2
  24.6 1.1 %collective-permute-done.2.refs_4_.refs_9_ = bf16[592,128]{1,0:T(8,128)(2,1)S(1)} collective-permute-done((bf16[592,128]{1,0:T(8,128)(2,1)S(1)}, bf16[592,128]{1,0:T(8,128)(2,1)S(1)}, u32[]{:S(2)}, u32[]{:S(2)}) %collective-permute-start.2) | collective-permute-done | bytes 151584 | tf_op jit(solution)/shard_map/ppermute | solution.py:117
  25.7 1.3 %pack_z.1 = (bf16[112,128]{1,0:T(8,128)(2,1)S(1)}, f32[128,128]{1,0:T(8,128)S(1)}) custom-call(f32[3072,128]{1,0:T(8,128)S(1)} %bitcast.12, s32[32,128]{1,0:T(8,128)S(1)} %bitcast.21, bf16[784,128]{1,0:T(8,128)(2,1)S(1)} %collective-permute-done.refs_3_.refs_2_.refs_7_, bf16[784,128]{1,0:T(8,128)(2,1)S(1)} %collective-permute-done.1.refs_4_.refs_3_.refs_8_, ...), custom_call_target="tpu_custom_call" | custom-call | flops 4194304 | bytes 3145728 | tf_op jit(solution)/shard_map/pack_z/pallas_call | solution.py:49
  27.0 5.6 %all-to-all-done.refs_0_ = bf16[32,16,128]{2,1,0:T(8,128)(2,1)S(1)} async-done(((bf16[32,16,128]{2,1,0:T(8,128)(2,1)}), bf16[32,16,128]{2,1,0:T(8,128)(2,1)S(1)}, u32[]{:S(2)}, u32[]{:S(2)}) %all-to-all-start) | async-done | bytes 131104 | tf_op jit(solution)/shard_map/all_to_all | solution.py:879
  32.7 0.0 copy-done.8
  32.7 2.2 %coarse.1 = (f32[16,1,16,128]{3,2,1,0:T(8,128)}, s32[8,128]{1,0:T(8,128)S(1)}) custom-call(bf16[32,16,128]{2,1,0:T(8,128)(2,1)S(1)} %all-to-all-done.refs_0_, bf16[64,1024]{1,0:T(8,128)(2,1)S(1)} %copy-done.8, bf16[112,128]{1,0:T(8,128)(2,1)S(1)} %get-tuple-element.28.refs_2_), custom_call_target="tpu_custom_call" | custom-call | flops 8388608 | bytes 1048576 | tf_op jit(solution)/shard_map/coarse/pallas_call | solution.py:49
  34.9 3.5 %all-to-all-start.1 = ((f32[16,1,16,128]{3,2,1,0:T(8,128)}), f32[16,1,16,128]{3,2,1,0:T(8,128)S(1)}, u32[]{:S(2)}, u32[]{:S(2)}) async-start(f32[16,1,16,128]{3,2,1,0:T(8,128)} %get-tuple-element.31), calls=%async_computation.1 | async-start | bytes 262144 | tf_op jit(solution)/shard_map/all_to_all | solution.py:914
  38.4 0.8 collective-permute-start.4
  39.3 4.6 %collective-permute-start.3 = (bf16[112,128]{1,0:T(8,128)(2,1)S(1)}, bf16[112,128]{1,0:T(8,128)(2,1)S(1)}, u32[]{:S(2)}, u32[]{:S(2)}) collective-permute-start(bf16[112,128]{1,0:T(8,128)(2,1)S(1)} %get-tuple-element.28.refs_2_), channel_id=1, source_target_pairs={{0,1},{1,0},{2,3},{3,2},{4,5},{5,4},{6,7},{7,6},{8,9},{9,8},{10,11... | collective-permute-start | bytes 86024 | tf_op jit(solution)/shard_map/ppermute | solution.py:117
  43.8 0.0 collective-permute-done.4.refs_11_
  43.8 1.8 %collective-permute-done.3.refs_10_ = bf16[112,128]{1,0:T(8,128)(2,1)S(1)} collective-permute-done((bf16[112,128]{1,0:T(8,128)(2,1)S(1)}, bf16[112,128]{1,0:T(8,128)(2,1)S(1)}, u32[]{:S(2)}, u32[]{:S(2)}) %collective-permute-start.3) | collective-permute-done | bytes 28704 | tf_op jit(solution)/shard_map/ppermute | solution.py:117
  45.7 0.7 all-to-all-done.1
  46.3 0.0 copy-done.9
  46.3 0.0 copy-start.4
  46.4 1.7 %copy-done.4 = bf16[96,96,128]{2,1,0:T(8,128)(2,1)S(1)} copy-done((bf16[96,96,128]{2,1,0:T(8,128)(2,1)S(1)}, bf16[96,96,128]{2,1,0:T(8,128)(2,1)}, u32[]{:S(2)}) %copy-start.4) | copy-done | bytes 2359320
  48.0 10.2 %solve.1 = (f32[3,32,32,128]{3,2,1,0:T(8,128)S(1)}, f32[8,32,8,128]{3,2,1,0:T(8,128)S(1)}, bf16[96,128]{1,0:T(8,128)(2,1)S(1)}, bf16[768,128]{1,0:T(8,128)(2,1)S...) custom-call(s32[1]{0:T(128)S(6)} %copy.11.refs_0_, f32[2,16]{1,0:T(2,128)S(1)} %copy-done.9, ...), custom_call_target="tpu_custom_call" | custom-call | flops 268435456 | bytes 8388608 | tf_op jit(solution)/shard_map/solve/pallas_call | solution.py:49
  58.2 0.9 collective-permute-start.5
  59.1 0.7 collective-permute-start.6
  59.8 0.1 collective-permute-start.7
  59.8 0.7 collective-permute-start.9
  60.5 3.9 %collective-permute-start.8 = (bf16[96,128]{1,0:T(8,128)(2,1)S(1)}, bf16[96,128]{1,0:T(8,128)(2,1)S(1)}, u32[]{:S(2)}, u32[]{:S(2)}) collective-permute-start(bf16[96,128]{1,0:T(8,128)(2,1)S(1)} %get-tuple-element.38), channel_id=1, source_target_pairs={{0,1},{1,0},{2,3},{3,2},{4,5},{5,4},{6,7},{7,6},{8,9},{9,8},{10,11... | collective-permute-start | bytes 73736 | tf_op jit(solution)/shard_map/ppermute | solution.py:117
  64.4 0.0 collective-permute-done.9.refs_7_
  64.4 1.8 %collective-permute-done.8.refs_6_ = bf16[96,128]{1,0:T(8,128)(2,1)S(1)} collective-permute-done((bf16[96,128]{1,0:T(8,128)(2,1)S(1)}, bf16[96,128]{1,0:T(8,128)(2,1)S(1)}, u32[]{:S(2)}, u32[]{:S(2)}) %collective-permute-start.8) | collective-permute-done | bytes 24608 | tf_op jit(solution)/shard_map/ppermute | solution.py:117
  66.2 0.0 collective-permute-done.7.refs_5_
  66.2 0.0 collective-permute-done.5.refs_3_
  66.2 0.0 collective-permute-done.6.refs_4_
  66.2 0.0 copy-start.5
  66.2 3.3 %image.1 = (bf16[96,64,128]{2,1,0:T(8,128)(2,1)S(1)}, bf16[96,64,128]{2,1,0:T(8,128)(2,1)S(1)}, f32[16,128]{1,0:T(8,128)S(1)}) custom-call(f32[3072,128]{1,0:T(8,128)S(1)} %bitcast.14, f32[8,32,8,128]{3,2,1,0:T(8,128)S(1)} %get-tuple-element.33.refs_1_, f32[3,32,32,128]{3,2,1,0:T(8,128)S(1)} %get-tuple-element.34.refs_2_, ...), custom_call_target="tpu_custom_call" | custom-call | flops 268435456 | bytes 8388608 | tf_op jit(solution)/shard_map/image/pallas_call | solution.py:49
  69.5 0.0 collective-permute-start.10
  69.5 1.2 %collective-permute-done.10.refs_1_ = f32[16,128]{1,0:T(8,128)S(1)} collective-permute-done((f32[16,128]{1,0:T(8,128)S(1)}, f32[16,128]{1,0:T(8,128)S(1)}, u32[]{:S(2)}, u32[]{:S(2)}) %collective-permute-start.10) | collective-permute-done | bytes 8224 | tf_op jit(solution)/shard_map/ppermute | solution.py:117
  70.8 16.2 %all_to_all.15.refs_0_ = f32[16,16,128]{2,1,0:T(8,128)S(1)} all-to-all(f32[16,16,128]{2,1,0:T(8,128)S(1)} %share_sums.1), channel_id=1, replica_groups=mesh['gx'=4,'gy'=2,'col'=4] {'gx','col'}, dimensions={0} | all-to-all | bytes 262144 | tf_op jit(solution)/shard_map/all_to_all | solution.py:987
  86.9 0.0 copy-done.5
  86.9 6.2 %finish.1 = (f32[3072,128]{1,0:T(8,128)}, f32[3072,128]{1,0:T(8,128)}) custom-call(f32[16,16,128]{2,1,0:T(8,128)S(1)} %all_to_all.15.refs_0_, f32[3072,128]{1,0:T(8,128)S(1)} %bitcast.17, f32[3072,128]{1,0:T(8,128)S(1)} %bitcast.15, bf16[96,64,128]{2,1,0:T(8,128)(2,1)S(1)} %get-tuple-element.40.refs_3_, bf16[96,64,128]{2,1,0:T(8,128)(2,1)S(1)} %get-tuple-element.41.refs_4_), custom_call_target="tpu_custom_call" | custom-call | flops 134217728 | bytes 9437184 | tf_op jit(solution)/shard_map/finish/pallas_call | solution.py:49
  (1 shorter events, 0.0 us)
Async XLA Ops:
  0.6 1.4 %copy-start = (f32[3,32,4,8,128]{4,3,2,1,0:T(8,128)S(1)}, f32[3,32,4,8,128]{4,3,2,1,0:T(8,128)}, u32[]{:S(2)}) copy-start(f32[3,32,4,8,128]{4,3,2,1,0:T(8,128)} %param.9) | copy-start | bytes 4718596
  2.0 0.7 copy-start.6
  2.8 8.1 %copy-start.1 = (f32[3,32,4,8,128]{4,3,2,1,0:T(8,128)S(1)}, f32[3,32,4,8,128]{4,3,2,1,0:T(8,128)}, u32[]{:S(2)}) copy-start(f32[3,32,4,8,128]{4,3,2,1,0:T(8,128)} %param.9) | copy-start | bytes 4718596
  3.0 14.1 %collective-permute-start.1 = (bf16[784,128]{1,0:T(8,128)(2,1)S(1)}, bf16[784,128]{1,0:T(8,128)(2,1)S(1)}, u32[]{:S(2)}, u32[]{:S(2)}) collective-permute-start(bf16[784,128]{1,0:T(8,128)(2,1)S(1)} %get-tuple-element.25), channel_id=1, source_target_pairs={{8,16},{16,8},{9,17},{17,9},{10,18},{18,10},{11,19},{19,11},{12,20... | collective-permute-start | bytes 602120 | tf_op jit(solution)/shard_map/ppermute | solution.py:117
  3.9 14.6 %collective-permute-start = (bf16[784,128]{1,0:T(8,128)(2,1)S(1)}, bf16[784,128]{1,0:T(8,128)(2,1)S(1)}, u32[]{:S(2)}, u32[]{:S(2)}) collective-permute-start(bf16[784,128]{1,0:T(8,128)(2,1)S(1)} %get-tuple-element.23.refs_4_), channel_id=1, source_target_pairs={{0,8},{8,0},{16,24},{24,16},{1,9},{9,1},{17,25},{25,17},{2,10},{10... | collective-permute-start | bytes 602120 | tf_op jit(solution)/shard_map/ppermute | solution.py:117
  10.9 1.7 %copy-start.2 = (f32[48,3,4,8,128]{4,3,2,1,0:T(8,128)S(1)}, f32[48,3,4,8,128]{4,3,2,1,0:T(8,128)}, u32[]{:S(2)}) copy-start(f32[48,3,4,8,128]{4,3,2,1,0:T(8,128)} %param.14) | copy-start | bytes 7077892
  12.6 5.9 %copy-start.7 = (s32[4,8,128]{2,1,0:T(8,128)S(1)}, s32[4,8,128]{2,1,0:T(8,128)}, u32[]{:S(2)}) copy-start(s32[4,8,128]{2,1,0:T(8,128)} %param.10) | copy-start | bytes 49156
  15.7 1.4 %copy-start.3 = (bf16[96,96,128]{2,1,0:T(8,128)(2,1)}, bf16[96,96,128]{2,1,0:T(8,128)(2,1)S(1)}, u32[]{:S(2)}) copy-start(bf16[96,96,128]{2,1,0:T(8,128)(2,1)S(1)} %get-tuple-element.32.refs_6_) | copy-start | bytes 7077892
  19.4 13.3 %copy-start.8 = (bf16[64,1024]{1,0:T(8,128)(2,1)S(1)}, bf16[64,1024]{1,0:T(8,128)(2,1)}, u32[]{:S(2)}) copy-start(bf16[64,1024]{1,0:T(8,128)(2,1)} %refs_1_.3) | copy-start | bytes 393220
  19.4 26.9 %copy-start.9 = (f32[2,16]{1,0:T(2,128)S(1)}, f32[2,16]{1,0:T(2,128)}, u32[]{:S(2)}) copy-start(f32[2,16]{1,0:T(2,128)} %refs_1_.4) | copy-start | bytes 388
  19.4 13.2 %all-to-all-start = ((bf16[32,16,128]{2,1,0:T(8,128)(2,1)}), bf16[32,16,128]{2,1,0:T(8,128)(2,1)S(1)}, u32[]{:S(2)}, u32[]{:S(2)}) async-start(bf16[32,16,128]{2,1,0:T(8,128)(2,1)} %get-tuple-element.26), calls=%async_computation | async-start | bytes 262144 | tf_op jit(solution)/shard_map/all_to_all | solution.py:879
  24.3 1.4 %collective-permute-start.2 = (bf16[592,128]{1,0:T(8,128)(2,1)S(1)}, bf16[592,128]{1,0:T(8,128)(2,1)S(1)}, u32[]{:S(2)}, u32[]{:S(2)}) collective-permute-start(bf16[592,128]{1,0:T(8,128)(2,1)S(1)} %get-tuple-element.27), channel_id=1, source_target_pairs={{0,4},{4,0},{1,5},{5,1},{2,6},{6,2},{3,7},{7,3},{8,12},{12,8},{9,1... | collective-permute-start | bytes 454664 | tf_op jit(solution)/shard_map/ppermute | solution.py:117
  34.9 11.5 %all-to-all-start.1 = ((f32[16,1,16,128]{3,2,1,0:T(8,128)}), f32[16,1,16,128]{3,2,1,0:T(8,128)S(1)}, u32[]{:S(2)}, u32[]{:S(2)}) async-start(f32[16,1,16,128]{3,2,1,0:T(8,128)} %get-tuple-element.31), calls=%async_computation.1 | async-start | bytes 262144 | tf_op jit(solution)/shard_map/all_to_all | solution.py:914
  38.4 5.4 %collective-permute-start.4 = (bf16[112,128]{1,0:T(8,128)(2,1)S(1)}, bf16[112,128]{1,0:T(8,128)(2,1)S(1)}, u32[]{:S(2)}, u32[]{:S(2)}) collective-permute-start(bf16[112,128]{1,0:T(8,128)(2,1)S(1)} %get-tuple-element.28.refs_2_), channel_id=1, source_target_pairs={{1,2},{2,1},{5,6},{6,5},{9,10},{10,9},{13,14},{14,13},{17,18},{18,... | collective-permute-start | bytes 86024 | tf_op jit(solution)/shard_map/ppermute | solution.py:117
  39.3 6.4 %collective-permute-start.3 = (bf16[112,128]{1,0:T(8,128)(2,1)S(1)}, bf16[112,128]{1,0:T(8,128)(2,1)S(1)}, u32[]{:S(2)}, u32[]{:S(2)}) collective-permute-start(bf16[112,128]{1,0:T(8,128)(2,1)S(1)} %get-tuple-element.28.refs_2_), channel_id=1, source_target_pairs={{0,1},{1,0},{2,3},{3,2},{4,5},{5,4},{6,7},{7,6},{8,9},{9,8},{10,11... | collective-permute-start | bytes 86024 | tf_op jit(solution)/shard_map/ppermute | solution.py:117
  46.3 1.7 %copy-start.4 = (bf16[96,96,128]{2,1,0:T(8,128)(2,1)S(1)}, bf16[96,96,128]{2,1,0:T(8,128)(2,1)}, u32[]{:S(2)}) copy-start(bf16[96,96,128]{2,1,0:T(8,128)(2,1)} %copy-done.3) | copy-start | bytes 7077892
  58.2 8.0 %collective-permute-start.5 = (bf16[768,128]{1,0:T(8,128)(2,1)S(1)}, bf16[768,128]{1,0:T(8,128)(2,1)S(1)}, u32[]{:S(2)}, u32[]{:S(2)}) collective-permute-start(bf16[768,128]{1,0:T(8,128)(2,1)S(1)} %get-tuple-element.35), channel_id=1, source_target_pairs={{0,8},{8,0},{16,24},{24,16},{1,9},{9,1},{17,25},{25,17},{2,10},{10... | collective-permute-start | bytes 589832 | tf_op jit(solution)/shard_map/ppermute | solution.py:117
  59.1 7.1 %collective-permute-start.6 = (bf16[768,128]{1,0:T(8,128)(2,1)S(1)}, bf16[768,128]{1,0:T(8,128)(2,1)S(1)}, u32[]{:S(2)}, u32[]{:S(2)}) collective-permute-start(bf16[768,128]{1,0:T(8,128)(2,1)S(1)} %get-tuple-element.36), channel_id=1, source_target_pairs={{8,16},{16,8},{9,17},{17,9},{10,18},{18,10},{11,19},{19,11},{12,20... | collective-permute-start | bytes 589832 | tf_op jit(solution)/shard_map/ppermute | solution.py:117
  59.8 6.4 %collective-permute-start.7 = (bf16[384,128]{1,0:T(8,128)(2,1)S(1)}, bf16[384,128]{1,0:T(8,128)(2,1)S(1)}, u32[]{:S(2)}, u32[]{:S(2)}) collective-permute-start(bf16[384,128]{1,0:T(8,128)(2,1)S(1)} %get-tuple-element.37), channel_id=1, source_target_pairs={{0,4},{4,0},{1,5},{5,1},{2,6},{6,2},{3,7},{7,3},{8,12},{12,8},{9,1... | collective-permute-start | bytes 294920 | tf_op jit(solution)/shard_map/ppermute | solution.py:117
  59.8 4.6 %collective-permute-start.9 = (bf16[96,128]{1,0:T(8,128)(2,1)S(1)}, bf16[96,128]{1,0:T(8,128)(2,1)S(1)}, u32[]{:S(2)}, u32[]{:S(2)}) collective-permute-start(bf16[96,128]{1,0:T(8,128)(2,1)S(1)} %get-tuple-element.38), channel_id=1, source_target_pairs={{1,2},{2,1},{5,6},{6,5},{9,10},{10,9},{13,14},{14,13},{17,18},{18,... | collective-permute-start | bytes 73736 | tf_op jit(solution)/shard_map/ppermute | solution.py:117
  60.5 5.7 %collective-permute-start.8 = (bf16[96,128]{1,0:T(8,128)(2,1)S(1)}, bf16[96,128]{1,0:T(8,128)(2,1)S(1)}, u32[]{:S(2)}, u32[]{:S(2)}) collective-permute-start(bf16[96,128]{1,0:T(8,128)(2,1)S(1)} %get-tuple-element.38), channel_id=1, source_target_pairs={{0,1},{1,0},{2,3},{3,2},{4,5},{5,4},{6,7},{7,6},{8,9},{9,8},{10,11... | collective-permute-start | bytes 73736 | tf_op jit(solution)/shard_map/ppermute | solution.py:117
  66.2 20.7 %copy-start.5 = (f32[3,32,4,8,128]{4,3,2,1,0:T(8,128)S(1)}, f32[3,32,4,8,128]{4,3,2,1,0:T(8,128)}, u32[]{:S(2)}) copy-start(f32[3,32,4,8,128]{4,3,2,1,0:T(8,128)} %param.8) | copy-start | bytes 4718596
  69.5 1.2 %collective-permute-start.10 = (f32[16,128]{1,0:T(8,128)S(1)}, f32[16,128]{1,0:T(8,128)S(1)}, u32[]{:S(2)}, u32[]{:S(2)}) collective-permute-start(f32[16,128]{1,0:T(8,128)S(1)} %get-tuple-element.39.refs_0_), channel_id=1, source_target_pairs={{0,4},{4,0},{1,5},{5,1},{2,6},{6,2},{3,7},{7,3},{8,12},{12,8},{9,1... | collective-permute-start | bytes 24584 | tf_op jit(solution)/shard_map/ppermute | solution.py:117

commit v10 on v9

--- a/solution.py
+++ b/solution.py
@@ -357,7 +357,7 @@
         vector[block + 1] = vector[block + 1] + jnp.where(wide_lane < offset, both, 0.0)
         return carry
 
-    lax.fori_loop(0, gathered.shape[0], place, 0, unroll=8)
+    lax.fori_loop(0, gathered.shape[0], place, 0, unroll=32)
     total = jnp.zeros((sz.loads, sz.block_rows), F32)
     for block in range(sz.total_rows // LANES):
         total = total + lax.dot_general(

time: 93.8 us -> 93.6 us (level)
  no operation moved by 1% of the time
where the time goes in v10:
time: 93.6 us; the launch traced here: 93.1 us
  Pallas kernels  27.3 us (29%)
  starting transfers between devices  26.8 us (29%)
  blocking collectives  16.2 us (17%)
  waiting for transfers between devices  13.6 us (15%)
  local copies, waits for them, and re-layouts  6.87 us (7%)
  between operations  2.27 us (2%)
    pallas_call x9, Pallas kernels, vmem_call(): pl.pallas_call(kernel, name=name, out_shape=outs, in_specs=[pl.BlockSpec(...  27.3 us
    ppermute x11, starting transfers between devices, exchange(): result.append(lax.ppermute(faces[parity], axis, pairs))  18.4 us
    all_to_all x1, blocking collectives, body(): sums = lax.all_to_all(spread, over, 0, 0, tiled=True)  16.2 us
    ppermute x11, waiting for transfers between devices, exchange(): result.append(lax.ppermute(faces[parity], axis, pairs))  7.35 us
    unnamed x20, local copies, waits for them, and re-layouts  6.87 us
    all_to_all x1, waiting for transfers between devices, body(): gathered = lax.all_to_all(message, AXES, 0, 0, tiled=True)  5.62 us
    all_to_all x1, starting transfers between devices, body(): gathered = lax.all_to_all(message, AXES, 0, 0, tiled=True)  4.84 us
    all_to_all x1, starting transfers between devices, body(): coarse = lax.all_to_all(partial, ('gx', 'col'), 0, 0, tiled=True)  3.52 us
  transfers between devices with their start and end apart: 13, of which 7 were waited for; matrix products, arithmetic and copies ran while one was open for 0% of the time, Pallas kernels for 5%

profile of v10, /device:TPU:0, one launch (start us, length us, event | category | flops | bytes accessed | tf_op | source)
XLA Modules:
  0.0 93.1 jit_solution(10544870474782972742)
XLA Ops:
  0.6 0.0 copy-start
  0.6 1.4 %copy-done = f32[3,32,4,8,128]{4,3,2,1,0:T(8,128)S(1)} copy-done((f32[3,32,4,8,128]{4,3,2,1,0:T(8,128)S(1)}, f32[3,32,4,8,128]{4,3,2,1,0:T(8,128)}, u32[]{:S(2)}) %copy-start) | copy-done | bytes 1572888
  2.0 0.0 copy-start.6
  2.0 0.7 copy-done.6
  2.8 0.0 copy-start.1
  2.8 0.3 pack_x.1
  3.0 0.8 collective-permute-start.1
  3.9 5.7 %collective-permute-start = (bf16[784,128]{1,0:T(8,128)(2,1)S(1)}, bf16[784,128]{1,0:T(8,128)(2,1)S(1)}, u32[]{:S(2)}, u32[]{:S(2)}) collective-permute-start(bf16[784,128]{1,0:T(8,128)(2,1)S(1)} %get-tuple-element.23.refs_4_), channel_id=1, source_target_pairs={{0,8},{8,0},{16,24},{24,16},{1,9},{9,1},{17,25},{25,17},{2,10},{10... | collective-permute-start | bytes 602120 | tf_op jit(solution)/shard_map/ppermute | solution.py:117
  10.9 0.0 copy-done.1
  10.9 0.0 copy-start.2
  10.9 1.7 %copy-done.2 = f32[48,3,4,8,128]{4,3,2,1,0:T(8,128)S(1)} copy-done((f32[48,3,4,8,128]{4,3,2,1,0:T(8,128)S(1)}, f32[48,3,4,8,128]{4,3,2,1,0:T(8,128)}, u32[]{:S(2)}) %copy-start.2) | copy-done | bytes 2359320
  12.6 0.0 copy-start.7
  12.6 3.1 %pieces.1 = (bf16[16,128]{1,0:T(8,128)(2,1)S(1)}, bf16[96,96,128]{2,1,0:T(8,128)(2,1)S(1)}) custom-call(s32[1]{0:T(128)S(6)} %copy.11.refs_0_, s32[1]{0:T(128)S(6)} %copy.12.refs_1_, f32[48,96,128]{2,1,0:T(8,128)S(1)} %bitcast.16, f32[3,1024,128]{2,1,0:T(8,128)S(1)} %bitcast.10, bf16[784,128]{1,0:T(8,128)(2,1)S(1)} %get-tuple-element.23.refs_4_), custom_call_target="tpu_custom_call" | custom-call | flops 134217728 | bytes 7340032 | tf_op jit(solution)/shard_map/pieces/pallas_call | solution.py:49
  15.7 0.0 copy-start.3
  15.7 1.4 %copy-done.3 = bf16[96,96,128]{2,1,0:T(8,128)(2,1)} copy-done((bf16[96,96,128]{2,1,0:T(8,128)(2,1)}, bf16[96,96,128]{2,1,0:T(8,128)(2,1)S(1)}, u32[]{:S(2)}) %copy-start.3) | copy-done | bytes 2359320
  17.1 0.0 collective-permute-done.1.refs_4_.refs_3_.refs_8_
  17.1 1.4 %collective-permute-done.refs_3_.refs_2_.refs_7_ = bf16[784,128]{1,0:T(8,128)(2,1)S(1)} collective-permute-done((bf16[784,128]{1,0:T(8,128)(2,1)S(1)}, bf16[784,128]{1,0:T(8,128)(2,1)S(1)}, u32[]{:S(2)}, u32[]{:S(2)}) %collective-permute-start) | collective-permute-done | bytes 200736 | tf_op jit(solution)/shard_map/ppermute | solution.py:117
  18.5 0.0 copy-done.7
  18.5 0.9 pack_y.1
  19.4 0.0 copy-start.8
  19.4 0.0 copy-start.9
  19.4 4.8 %all-to-all-start = ((bf16[32,16,128]{2,1,0:T(8,128)(2,1)}), bf16[32,16,128]{2,1,0:T(8,128)(2,1)S(1)}, u32[]{:S(2)}, u32[]{:S(2)}) async-start(bf16[32,16,128]{2,1,0:T(8,128)(2,1)} %get-tuple-element.26), calls=%async_computation | async-start | bytes 262144 | tf_op jit(solution)/shard_map/all_to_all | solution.py:879
  24.3 0.3 collective-permute-start.2
  24.6 1.1 %collective-permute-done.2.refs_4_.refs_9_ = bf16[592,128]{1,0:T(8,128)(2,1)S(1)} collective-permute-done((bf16[592,128]{1,0:T(8,128)(2,1)S(1)}, bf16[592,128]{1,0:T(8,128)(2,1)S(1)}, u32[]{:S(2)}, u32[]{:S(2)}) %collective-permute-start.2) | collective-permute-done | bytes 151584 | tf_op jit(solution)/shard_map/ppermute | solution.py:117
  25.7 1.3 %pack_z.1 = (bf16[112,128]{1,0:T(8,128)(2,1)S(1)}, f32[128,128]{1,0:T(8,128)S(1)}) custom-call(f32[3072,128]{1,0:T(8,128)S(1)} %bitcast.12, s32[32,128]{1,0:T(8,128)S(1)} %bitcast.21, bf16[784,128]{1,0:T(8,128)(2,1)S(1)} %collective-permute-done.refs_3_.refs_2_.refs_7_, bf16[784,128]{1,0:T(8,128)(2,1)S(1)} %collective-permute-done.1.refs_4_.refs_3_.refs_8_, ...), custom_call_target="tpu_custom_call" | custom-call | flops 4194304 | bytes 3145728 | tf_op jit(solution)/shard_map/pack_z/pallas_call | solution.py:49
  27.0 5.6 %all-to-all-done.refs_0_ = bf16[32,16,128]{2,1,0:T(8,128)(2,1)S(1)} async-done(((bf16[32,16,128]{2,1,0:T(8,128)(2,1)}), bf16[32,16,128]{2,1,0:T(8,128)(2,1)S(1)}, u32[]{:S(2)}, u32[]{:S(2)}) %all-to-all-start) | async-done | bytes 131104 | tf_op jit(solution)/shard_map/all_to_all | solution.py:879
  32.7 0.0 copy-done.8
  32.7 2.0 %coarse.1 = (f32[16,1,16,128]{3,2,1,0:T(8,128)}, s32[8,128]{1,0:T(8,128)S(1)}) custom-call(bf16[32,16,128]{2,1,0:T(8,128)(2,1)S(1)} %all-to-all-done.refs_0_, bf16[64,1024]{1,0:T(8,128)(2,1)S(1)} %copy-done.8, bf16[112,128]{1,0:T(8,128)(2,1)S(1)} %get-tuple-element.28.refs_2_), custom_call_target="tpu_custom_call" | custom-call | flops 8388608 | bytes 1048576 | tf_op jit(solution)/shard_map/coarse/pallas_call | solution.py:49
  34.7 3.5 %all-to-all-start.1 = ((f32[16,1,16,128]{3,2,1,0:T(8,128)}), f32[16,1,16,128]{3,2,1,0:T(8,128)S(1)}, u32[]{:S(2)}, u32[]{:S(2)}) async-start(f32[16,1,16,128]{3,2,1,0:T(8,128)} %get-tuple-element.31), calls=%async_computation.1 | async-start | bytes 262144 | tf_op jit(solution)/shard_map/all_to_all | solution.py:914
  38.2 0.8 collective-permute-start.4
  39.1 4.6 %collective-permute-start.3 = (bf16[112,128]{1,0:T(8,128)(2,1)S(1)}, bf16[112,128]{1,0:T(8,128)(2,1)S(1)}, u32[]{:S(2)}, u32[]{:S(2)}) collective-permute-start(bf16[112,128]{1,0:T(8,128)(2,1)S(1)} %get-tuple-element.28.refs_2_), channel_id=1, source_target_pairs={{0,1},{1,0},{2,3},{3,2},{4,5},{5,4},{6,7},{7,6},{8,9},{9,8},{10,11... | collective-permute-start | bytes 86024 | tf_op jit(solution)/shard_map/ppermute | solution.py:117
  43.7 0.0 collective-permute-done.4.refs_11_
  43.7 1.8 %collective-permute-done.3.refs_10_ = bf16[112,128]{1,0:T(8,128)(2,1)S(1)} collective-permute-done((bf16[112,128]{1,0:T(8,128)(2,1)S(1)}, bf16[112,128]{1,0:T(8,128)(2,1)S(1)}, u32[]{:S(2)}, u32[]{:S(2)}) %collective-permute-start.3) | collective-permute-done | bytes 28704 | tf_op jit(solution)/shard_map/ppermute | solution.py:117
  45.5 0.7 all-to-all-done.1
  46.2 0.0 copy-done.9
  46.2 0.0 copy-start.4
  46.2 1.7 %copy-done.4 = bf16[96,96,128]{2,1,0:T(8,128)(2,1)S(1)} copy-done((bf16[96,96,128]{2,1,0:T(8,128)(2,1)S(1)}, bf16[96,96,128]{2,1,0:T(8,128)(2,1)}, u32[]{:S(2)}) %copy-start.4) | copy-done | bytes 2359320
  47.8 10.2 %solve.1 = (f32[3,32,32,128]{3,2,1,0:T(8,128)S(1)}, f32[8,32,8,128]{3,2,1,0:T(8,128)S(1)}, bf16[96,128]{1,0:T(8,128)(2,1)S(1)}, bf16[768,128]{1,0:T(8,128)(2,1)S...) custom-call(s32[1]{0:T(128)S(6)} %copy.11.refs_0_, f32[2,16]{1,0:T(2,128)S(1)} %copy-done.9, ...), custom_call_target="tpu_custom_call" | custom-call | flops 268435456 | bytes 8388608 | tf_op jit(solution)/shard_map/solve/pallas_call | solution.py:49
  58.0 0.9 collective-permute-start.5
  58.9 0.7 collective-permute-start.6
  59.6 0.1 collective-permute-start.7
  59.7 0.7 collective-permute-start.9
  60.3 3.9 %collective-permute-start.8 = (bf16[96,128]{1,0:T(8,128)(2,1)S(1)}, bf16[96,128]{1,0:T(8,128)(2,1)S(1)}, u32[]{:S(2)}, u32[]{:S(2)}) collective-permute-start(bf16[96,128]{1,0:T(8,128)(2,1)S(1)} %get-tuple-element.38), channel_id=1, source_target_pairs={{0,1},{1,0},{2,3},{3,2},{4,5},{5,4},{6,7},{7,6},{8,9},{9,8},{10,11... | collective-permute-start | bytes 73736 | tf_op jit(solution)/shard_map/ppermute | solution.py:117
  64.2 0.0 collective-permute-done.9.refs_7_
  64.2 1.8 %collective-permute-done.8.refs_6_ = bf16[96,128]{1,0:T(8,128)(2,1)S(1)} collective-permute-done((bf16[96,128]{1,0:T(8,128)(2,1)S(1)}, bf16[96,128]{1,0:T(8,128)(2,1)S(1)}, u32[]{:S(2)}, u32[]{:S(2)}) %collective-permute-start.8) | collective-permute-done | bytes 24608 | tf_op jit(solution)/shard_map/ppermute | solution.py:117
  66.0 0.0 collective-permute-done.7.refs_5_
  66.0 0.0 collective-permute-done.5.refs_3_
  66.0 0.0 collective-permute-done.6.refs_4_
  66.0 0.0 copy-start.5
  66.0 3.3 %image.1 = (bf16[96,64,128]{2,1,0:T(8,128)(2,1)S(1)}, bf16[96,64,128]{2,1,0:T(8,128)(2,1)S(1)}, f32[16,128]{1,0:T(8,128)S(1)}) custom-call(f32[3072,128]{1,0:T(8,128)S(1)} %bitcast.14, f32[8,32,8,128]{3,2,1,0:T(8,128)S(1)} %get-tuple-element.33.refs_1_, f32[3,32,32,128]{3,2,1,0:T(8,128)S(1)} %get-tuple-element.34.refs_2_, ...), custom_call_target="tpu_custom_call" | custom-call | flops 268435456 | bytes 8388608 | tf_op jit(solution)/shard_map/image/pallas_call | solution.py:49
  69.4 0.0 collective-permute-start.10
  69.4 1.2 %collective-permute-done.10.refs_1_ = f32[16,128]{1,0:T(8,128)S(1)} collective-permute-done((f32[16,128]{1,0:T(8,128)S(1)}, f32[16,128]{1,0:T(8,128)S(1)}, u32[]{:S(2)}, u32[]{:S(2)}) %collective-permute-start.10) | collective-permute-done | bytes 8224 | tf_op jit(solution)/shard_map/ppermute | solution.py:117
  70.6 16.2 %all_to_all.15.refs_0_ = f32[16,16,128]{2,1,0:T(8,128)S(1)} all-to-all(f32[16,16,128]{2,1,0:T(8,128)S(1)} %share_sums.1), channel_id=1, replica_groups=mesh['gx'=4,'gy'=2,'col'=4] {'gx','col'}, dimensions={0} | all-to-all | bytes 262144 | tf_op jit(solution)/shard_map/all_to_all | solution.py:987
  86.8 0.0 copy-done.5
  86.8 6.2 %finish.1 = (f32[3072,128]{1,0:T(8,128)}, f32[3072,128]{1,0:T(8,128)}) custom-call(f32[16,16,128]{2,1,0:T(8,128)S(1)} %all_to_all.15.refs_0_, f32[3072,128]{1,0:T(8,128)S(1)} %bitcast.17, f32[3072,128]{1,0:T(8,128)S(1)} %bitcast.15, bf16[96,64,128]{2,1,0:T(8,128)(2,1)S(1)} %get-tuple-element.40.refs_3_, bf16[96,64,128]{2,1,0:T(8,128)(2,1)S(1)} %get-tuple-element.41.refs_4_), custom_call_target="tpu_custom_call" | custom-call | flops 134217728 | bytes 9437184 | tf_op jit(solution)/shard_map/finish/pallas_call | solution.py:49
  (1 shorter events, 0.0 us)
Async XLA Ops:
  0.6 1.4 %copy-start = (f32[3,32,4,8,128]{4,3,2,1,0:T(8,128)S(1)}, f32[3,32,4,8,128]{4,3,2,1,0:T(8,128)}, u32[]{:S(2)}) copy-start(f32[3,32,4,8,128]{4,3,2,1,0:T(8,128)} %param.9) | copy-start | bytes 4718596
  2.0 0.7 copy-start.6
  2.8 8.1 %copy-start.1 = (f32[3,32,4,8,128]{4,3,2,1,0:T(8,128)S(1)}, f32[3,32,4,8,128]{4,3,2,1,0:T(8,128)}, u32[]{:S(2)}) copy-start(f32[3,32,4,8,128]{4,3,2,1,0:T(8,128)} %param.9) | copy-start | bytes 4718596
  3.0 14.1 %collective-permute-start.1 = (bf16[784,128]{1,0:T(8,128)(2,1)S(1)}, bf16[784,128]{1,0:T(8,128)(2,1)S(1)}, u32[]{:S(2)}, u32[]{:S(2)}) collective-permute-start(bf16[784,128]{1,0:T(8,128)(2,1)S(1)} %get-tuple-element.25), channel_id=1, source_target_pairs={{8,16},{16,8},{9,17},{17,9},{10,18},{18,10},{11,19},{19,11},{12,20... | collective-permute-start | bytes 602120 | tf_op jit(solution)/shard_map/ppermute | solution.py:117
  3.9 14.6 %collective-permute-start = (bf16[784,128]{1,0:T(8,128)(2,1)S(1)}, bf16[784,128]{1,0:T(8,128)(2,1)S(1)}, u32[]{:S(2)}, u32[]{:S(2)}) collective-permute-start(bf16[784,128]{1,0:T(8,128)(2,1)S(1)} %get-tuple-element.23.refs_4_), channel_id=1, source_target_pairs={{0,8},{8,0},{16,24},{24,16},{1,9},{9,1},{17,25},{25,17},{2,10},{10... | collective-permute-start | bytes 602120 | tf_op jit(solution)/shard_map/ppermute | solution.py:117
  10.9 1.7 %copy-start.2 = (f32[48,3,4,8,128]{4,3,2,1,0:T(8,128)S(1)}, f32[48,3,4,8,128]{4,3,2,1,0:T(8,128)}, u32[]{:S(2)}) copy-start(f32[48,3,4,8,128]{4,3,2,1,0:T(8,128)} %param.14) | copy-start | bytes 7077892
  12.6 5.9 %copy-start.7 = (s32[4,8,128]{2,1,0:T(8,128)S(1)}, s32[4,8,128]{2,1,0:T(8,128)}, u32[]{:S(2)}) copy-start(s32[4,8,128]{2,1,0:T(8,128)} %param.10) | copy-start | bytes 49156
  15.7 1.4 %copy-start.3 = (bf16[96,96,128]{2,1,0:T(8,128)(2,1)}, bf16[96,96,128]{2,1,0:T(8,128)(2,1)S(1)}, u32[]{:S(2)}) copy-start(bf16[96,96,128]{2,1,0:T(8,128)(2,1)S(1)} %get-tuple-element.32.refs_6_) | copy-start | bytes 7077892
  19.4 13.3 %copy-start.8 = (bf16[64,1024]{1,0:T(8,128)(2,1)S(1)}, bf16[64,1024]{1,0:T(8,128)(2,1)}, u32[]{:S(2)}) copy-start(bf16[64,1024]{1,0:T(8,128)(2,1)} %refs_1_.3) | copy-start | bytes 393220
  19.4 26.8 %copy-start.9 = (f32[2,16]{1,0:T(2,128)S(1)}, f32[2,16]{1,0:T(2,128)}, u32[]{:S(2)}) copy-start(f32[2,16]{1,0:T(2,128)} %refs_1_.4) | copy-start | bytes 388
  19.4 13.2 %all-to-all-start = ((bf16[32,16,128]{2,1,0:T(8,128)(2,1)}), bf16[32,16,128]{2,1,0:T(8,128)(2,1)S(1)}, u32[]{:S(2)}, u32[]{:S(2)}) async-start(bf16[32,16,128]{2,1,0:T(8,128)(2,1)} %get-tuple-element.26), calls=%async_computation | async-start | bytes 262144 | tf_op jit(solution)/shard_map/all_to_all | solution.py:879
  24.3 1.4 %collective-permute-start.2 = (bf16[592,128]{1,0:T(8,128)(2,1)S(1)}, bf16[592,128]{1,0:T(8,128)(2,1)S(1)}, u32[]{:S(2)}, u32[]{:S(2)}) collective-permute-start(bf16[592,128]{1,0:T(8,128)(2,1)S(1)} %get-tuple-element.27), channel_id=1, source_target_pairs={{0,4},{4,0},{1,5},{5,1},{2,6},{6,2},{3,7},{7,3},{8,12},{12,8},{9,1... | collective-permute-start | bytes 454664 | tf_op jit(solution)/shard_map/ppermute | solution.py:117
  34.7 11.5 %all-to-all-start.1 = ((f32[16,1,16,128]{3,2,1,0:T(8,128)}), f32[16,1,16,128]{3,2,1,0:T(8,128)S(1)}, u32[]{:S(2)}, u32[]{:S(2)}) async-start(f32[16,1,16,128]{3,2,1,0:T(8,128)} %get-tuple-element.31), calls=%async_computation.1 | async-start | bytes 262144 | tf_op jit(solution)/shard_map/all_to_all | solution.py:914
  38.2 5.4 %collective-permute-start.4 = (bf16[112,128]{1,0:T(8,128)(2,1)S(1)}, bf16[112,128]{1,0:T(8,128)(2,1)S(1)}, u32[]{:S(2)}, u32[]{:S(2)}) collective-permute-start(bf16[112,128]{1,0:T(8,128)(2,1)S(1)} %get-tuple-element.28.refs_2_), channel_id=1, source_target_pairs={{1,2},{2,1},{5,6},{6,5},{9,10},{10,9},{13,14},{14,13},{17,18},{18,... | collective-permute-start | bytes 86024 | tf_op jit(solution)/shard_map/ppermute | solution.py:117
  39.1 6.4 %collective-permute-start.3 = (bf16[112,128]{1,0:T(8,128)(2,1)S(1)}, bf16[112,128]{1,0:T(8,128)(2,1)S(1)}, u32[]{:S(2)}, u32[]{:S(2)}) collective-permute-start(bf16[112,128]{1,0:T(8,128)(2,1)S(1)} %get-tuple-element.28.refs_2_), channel_id=1, source_target_pairs={{0,1},{1,0},{2,3},{3,2},{4,5},{5,4},{6,7},{7,6},{8,9},{9,8},{10,11... | collective-permute-start | bytes 86024 | tf_op jit(solution)/shard_map/ppermute | solution.py:117
  46.2 1.7 %copy-start.4 = (bf16[96,96,128]{2,1,0:T(8,128)(2,1)S(1)}, bf16[96,96,128]{2,1,0:T(8,128)(2,1)}, u32[]{:S(2)}) copy-start(bf16[96,96,128]{2,1,0:T(8,128)(2,1)} %copy-done.3) | copy-start | bytes 7077892
  58.0 8.0 %collective-permute-start.5 = (bf16[768,128]{1,0:T(8,128)(2,1)S(1)}, bf16[768,128]{1,0:T(8,128)(2,1)S(1)}, u32[]{:S(2)}, u32[]{:S(2)}) collective-permute-start(bf16[768,128]{1,0:T(8,128)(2,1)S(1)} %get-tuple-element.35), channel_id=1, source_target_pairs={{0,8},{8,0},{16,24},{24,16},{1,9},{9,1},{17,25},{25,17},{2,10},{10... | collective-permute-start | bytes 589832 | tf_op jit(solution)/shard_map/ppermute | solution.py:117
  58.9 7.1 %collective-permute-start.6 = (bf16[768,128]{1,0:T(8,128)(2,1)S(1)}, bf16[768,128]{1,0:T(8,128)(2,1)S(1)}, u32[]{:S(2)}, u32[]{:S(2)}) collective-permute-start(bf16[768,128]{1,0:T(8,128)(2,1)S(1)} %get-tuple-element.36), channel_id=1, source_target_pairs={{8,16},{16,8},{9,17},{17,9},{10,18},{18,10},{11,19},{19,11},{12,20... | collective-permute-start | bytes 589832 | tf_op jit(solution)/shard_map/ppermute | solution.py:117
  59.6 6.4 %collective-permute-start.7 = (bf16[384,128]{1,0:T(8,128)(2,1)S(1)}, bf16[384,128]{1,0:T(8,128)(2,1)S(1)}, u32[]{:S(2)}, u32[]{:S(2)}) collective-permute-start(bf16[384,128]{1,0:T(8,128)(2,1)S(1)} %get-tuple-element.37), channel_id=1, source_target_pairs={{0,4},{4,0},{1,5},{5,1},{2,6},{6,2},{3,7},{7,3},{8,12},{12,8},{9,1... | collective-permute-start | bytes 294920 | tf_op jit(solution)/shard_map/ppermute | solution.py:117
  59.7 4.6 %collective-permute-start.9 = (bf16[96,128]{1,0:T(8,128)(2,1)S(1)}, bf16[96,128]{1,0:T(8,128)(2,1)S(1)}, u32[]{:S(2)}, u32[]{:S(2)}) collective-permute-start(bf16[96,128]{1,0:T(8,128)(2,1)S(1)} %get-tuple-element.38), channel_id=1, source_target_pairs={{1,2},{2,1},{5,6},{6,5},{9,10},{10,9},{13,14},{14,13},{17,18},{18,... | collective-permute-start | bytes 73736 | tf_op jit(solution)/shard_map/ppermute | solution.py:117
  60.3 5.7 %collective-permute-start.8 = (bf16[96,128]{1,0:T(8,128)(2,1)S(1)}, bf16[96,128]{1,0:T(8,128)(2,1)S(1)}, u32[]{:S(2)}, u32[]{:S(2)}) collective-permute-start(bf16[96,128]{1,0:T(8,128)(2,1)S(1)} %get-tuple-element.38), channel_id=1, source_target_pairs={{0,1},{1,0},{2,3},{3,2},{4,5},{5,4},{6,7},{7,6},{8,9},{9,8},{10,11... | collective-permute-start | bytes 73736 | tf_op jit(solution)/shard_map/ppermute | solution.py:117
  66.0 20.7 %copy-start.5 = (f32[3,32,4,8,128]{4,3,2,1,0:T(8,128)S(1)}, f32[3,32,4,8,128]{4,3,2,1,0:T(8,128)}, u32[]{:S(2)}) copy-start(f32[3,32,4,8,128]{4,3,2,1,0:T(8,128)} %param.8) | copy-start | bytes 4718596
  69.4 1.2 %collective-permute-start.10 = (f32[16,128]{1,0:T(8,128)S(1)}, f32[16,128]{1,0:T(8,128)S(1)}, u32[]{:S(2)}, u32[]{:S(2)}) collective-permute-start(f32[16,128]{1,0:T(8,128)S(1)} %get-tuple-element.39.refs_0_), channel_id=1, source_target_pairs={{0,4},{4,0},{1,5},{5,1},{2,6},{6,2},{3,7},{7,3},{8,12},{12,8},{9,1... | collective-permute-start | bytes 24584 | tf_op jit(solution)/shard_map/ppermute | solution.py:117
